TPU v7x, 32 devices: a whole 2x2x4 slice. The times are simulated.
32 devices in a mesh: section: 4 (over y, x), tensor: 8 (over z, core).
Axes of the slice: x: 2, y: 2, z: 4, core: 2. Of those that a mesh axis runs over, the one named last changes fastest.
Arguments:
- tokens: bfloat16 [512, 8192], P('section'), may hold values from -6 to 6
- cotangent: bfloat16 [512, 8192], P('section'), may hold values from -0.3125 to 0.3125
- gate_weight: bfloat16 [640, 8192], P(('section', 'tensor')), may hold values from -0.0625 to 0.0625
- up_weight: bfloat16 [640, 8192], P(('section', 'tensor')), may hold values from -0.0625 to 0.0625
- down_weight: bfloat16 [640, 8192], P(('section', 'tensor')), may hold values from -0.25 to 0.25
Outputs:
- output: bfloat16 [512, 8192], P('section', 'tensor')
- grad_gate: float32 [640, 8192], P(('section', 'tensor'))
- grad_up: float32 [640, 8192], P(('section', 'tensor'))
- grad_down: float32 [640, 8192], P(('section', 'tensor'))
All inputs are finite; a program needn't handle non-finite values.
Results may differ from a plain program's by a relative error of at most 0.005.
Values may be sent and summed in bfloat16 or wider, within the bound.
No kernel may reach another device: no remote copies, remote signals or barrier semaphores. Data moves between devices by JAX's collectives and lax.ppermute only.
A program may use at most 64 MiB of HBM per device.

v0:
```python
import jax
import jax.numpy as jnp
from jax import lax
from jax.sharding import PartitionSpec as P

STEPS = 3


def passed_along(value, axis, steps):
    count = lax.axis_size(axis)
    pairs = [(source, (source + steps) % count) for source in range(count)]
    return lax.ppermute(value, axis, pairs)


def forward_block(inputs, gate_rows, up_rows, down_rows):
    along_rows = (((1,), (1,)), ((), ()))
    gate_proj = lax.dot_general(inputs, gate_rows, along_rows, preferred_element_type=jnp.float32)
    up_proj = lax.dot_general(inputs, up_rows, along_rows, preferred_element_type=jnp.float32)
    activated = jax.nn.silu(gate_proj)
    hidden = (activated * up_proj).astype(jnp.bfloat16)
    partial_value = jnp.dot(hidden, down_rows, preferred_element_type=jnp.float32)
    return (partial_value, gate_proj, up_proj, hidden)


def backward_block(inputs, cot_rows, down_rows, gate_proj, up_proj, hidden):
    along_rows = (((1,), (1,)), ((), ()))
    along_tokens = (((0,), (0,)), ((), ()))
    hidden_grad = lax.dot_general(
        cot_rows, down_rows, along_rows, preferred_element_type=jnp.float32
    )
    sigmoid_gate = jax.nn.sigmoid(gate_proj)
    activated = jax.nn.silu(gate_proj)
    gate_grad = (
        hidden_grad * up_proj * sigmoid_gate * (1.0 + gate_proj * (1.0 - sigmoid_gate))
    ).astype(jnp.bfloat16)
    up_grad = (hidden_grad * activated).astype(jnp.bfloat16)
    grad_gate = lax.dot_general(gate_grad, inputs, along_tokens, preferred_element_type=jnp.float32)
    grad_up = lax.dot_general(up_grad, inputs, along_tokens, preferred_element_type=jnp.float32)
    grad_down = lax.dot_general(hidden, cot_rows, along_tokens, preferred_element_type=jnp.float32)
    return (grad_gate, grad_up, grad_down)


def add_terms(earlier, later):
    return (earlier[0] + later[0], earlier[1] + later[1], earlier[2] + later[2])


def on_device(tokens, cotangent, gate_weight, up_weight, down_weight):
    weights = (gate_weight, up_weight, down_weight)
    total = jnp.zeros(tokens.shape, jnp.float32)
    stored = []
    gradient_sum = None
    for offset in range(STEPS):
        if offset > 0:
            weights = passed_along((weights[0], weights[1], weights[2]), "section", 1)
        partial_value, gate_proj, up_proj, hidden = forward_block(
            tokens, weights[0], weights[1], weights[2]
        )
        total = total + partial_value
        stored.append((weights[2], gate_proj, up_proj, hidden))
    for offset in reversed(range(STEPS)):
        saved = stored[offset]
        terms = backward_block(tokens, cotangent, saved[0], saved[1], saved[2], saved[3])
        if gradient_sum is None:
            gradient_sum = terms
        else:
            gradient_sum = add_terms(passed_along(gradient_sum, "section", -1), terms)
    output = lax.psum_scatter(total, "tensor", scatter_dimension=1, tiled=True).astype(jnp.bfloat16)
    return (output, gradient_sum[0], gradient_sum[1], gradient_sum[2])


def solution(mesh):
    placed = (
        P("section", None),
        P("section", None),
        P(("section", "tensor"), None),
        P(("section", "tensor"), None),
        P(("section", "tensor"), None),
    )
    return jax.shard_map(
        on_device,
        mesh=mesh,
        in_specs=placed,
        out_specs=(
            P("section", "tensor"),
            P(("section", "tensor"), None),
            P(("section", "tensor"), None),
            P(("section", "tensor"), None),
        ),
        check_vma=False,
    )
```

profile of v0, /device:TPU:0, one launch (start us, length us, event | category | flops | bytes accessed | tf_op | source)
XLA Modules:
  0.0 181.3 jit_solution(7101062222092680567)
XLA Ops:
  7.2 3.0 %collective-permute-start = (bf16[20,8192]{1,0:T(8,128)(2,1)}, bf16[20,8192]{1,0:T(8,128)(2,1)S(1)}, u32[]{:S(2)}, u32[]{:S(2)}) collective-permute-start(bf16[20,8192]{1,0:T(8,128)(2,1)} %param.7), channel_id=1, source_target_pairs={{0,8},{8,16},{16,24},{24,0},{1,9},{9,17},{17,25},{25,1},{2,10},{10... | collective-permute-start | bytes 983048 | tf_op jit(solution)/shard_map/ppermute | solution.py:12
  10.2 1.5 collective-permute-start.1
  11.7 1.5 collective-permute-start.2
  13.2 1.6 fusion.19
  15.6 0.7 fusion.20
  16.3 5.0 %collective-permute-done = bf16[20,8192]{1,0:T(8,128)(2,1)S(1)} collective-permute-done((bf16[20,8192]{1,0:T(8,128)(2,1)}, bf16[20,8192]{1,0:T(8,128)(2,1)S(1)}, u32[]{:S(2)}, u32[]{:S(2)}) %collective-permute-start) | collective-permute-done | bytes 327712 | tf_op jit(solution)/shard_map/ppermute | solution.py:12
  22.0 1.1 collective-permute-start.3
  23.1 6.6 %collective-permute-done.1 = bf16[20,8192]{1,0:T(8,128)(2,1)S(1)} collective-permute-done((bf16[20,8192]{1,0:T(8,128)(2,1)}, bf16[20,8192]{1,0:T(8,128)(2,1)S(1)}, u32[]{:S(2)}, u32[]{:S(2)}) %collective-permute-start.1) | collective-permute-done | bytes 327712 | tf_op jit(solution)/shard_map/ppermute | solution.py:12
  29.8 1.1 collective-permute-start.4
  31.6 6.6 %collective-permute-done.2 = bf16[20,8192]{1,0:T(8,128)(2,1)S(1)} collective-permute-done((bf16[20,8192]{1,0:T(8,128)(2,1)}, bf16[20,8192]{1,0:T(8,128)(2,1)S(1)}, u32[]{:S(2)}, u32[]{:S(2)}) %collective-permute-start.2) | collective-permute-done | bytes 327712 | tf_op jit(solution)/shard_map/ppermute | solution.py:12
  38.2 1.1 collective-permute-start.5
  39.3 0.7 convolution_add_fusion.1
  40.0 6.6 %collective-permute-done.3 = bf16[20,8192]{1,0:T(8,128)(2,1)S(1)} collective-permute-done((bf16[20,8192]{1,0:T(8,128)(2,1)S(1)}, bf16[20,8192]{1,0:T(8,128)(2,1)S(1)}, u32[]{:S(2)}, u32[]{:S(2)}) %collective-permute-start.3) | collective-permute-done | bytes 327712 | tf_op jit(solution)/shard_map/ppermute | solution.py:12
  47.3 7.7 %collective-permute-done.4 = bf16[20,8192]{1,0:T(8,128)(2,1)S(1)} collective-permute-done((bf16[20,8192]{1,0:T(8,128)(2,1)S(1)}, bf16[20,8192]{1,0:T(8,128)(2,1)S(1)}, u32[]{:S(2)}, u32[]{:S(2)}) %collective-permute-start.4) | collective-permute-done | bytes 327712 | tf_op jit(solution)/shard_map/ppermute | solution.py:12
  55.7 6.9 %collective-permute-done.5 = bf16[20,8192]{1,0:T(8,128)(2,1)S(1)} collective-permute-done((bf16[20,8192]{1,0:T(8,128)(2,1)S(1)}, bf16[20,8192]{1,0:T(8,128)(2,1)S(1)}, u32[]{:S(2)}, u32[]{:S(2)}) %collective-permute-start.5) | collective-permute-done | bytes 327712 | tf_op jit(solution)/shard_map/ppermute | solution.py:12
  62.6 2.7 %convolution_add_fusion = f32[128,8192]{1,0:T(8,128)} fusion(f32[128,8192]{1,0:T(8,128)S(1)} %convolution_add_fusion.1, bf16[128,20]{0,1:T(8,128)(2,1)S(1)} %get-tuple-element.8, bf16[20,8192]{1,0:T(8,128)(2,1)S(1)} %collective-permute-done.5), kind=kOutput, calls=%fused_computation | convolution fusion | flops 42991616 | bytes 8721408 | tf_op jit(solution)/shard_map/dot_general | solution.py:21
  65.4 2.1 %fusion.27 = f32[20,8192]{1,0:T(8,128)S(1)} fusion(bf16[128,20]{0,1:T(8,128)(2,1)S(1)} %get-tuple-element.4, bf16[128,8192]{1,0:T(8,128)(2,1)} %param.6), kind=kOutput, calls=%fused_computation.41 | convolution fusion | flops 41943040 | bytes 2757632 | tf_op jit(solution)/shard_map/dot_general | solution.py:39
  68.7 1.8 collective-permute-start.6
  70.9 1.5 collective-permute-start.8
  74.0 15.2 %collective-permute-done.6 = f32[20,8192]{1,0:T(8,128)S(1)} collective-permute-done((f32[20,8192]{1,0:T(8,128)S(1)}, f32[20,8192]{1,0:T(8,128)S(1)}, u32[]{:S(2)}, u32[]{:S(2)}) %collective-permute-start.6) | collective-permute-done | bytes 655392 | tf_op jit(solution)/shard_map/ppermute | solution.py:12
  89.6 2.7 %collective-permute-start.7 = (f32[20,8192]{1,0:T(8,128)S(1)}, f32[20,8192]{1,0:T(8,128)S(1)}, u32[]{:S(2)}, u32[]{:S(2)}) collective-permute-start(f32[20,8192]{1,0:T(8,128)S(1)} %convolution_add_fusion.4), channel_id=1, source_target_pairs={{0,24},{8,0},{16,8},{24,16},{1,25},{9,1},{17,9},{25,17},{2,26},{10... | collective-permute-start | bytes 1966088 | tf_op jit(solution)/shard_map/ppermute | solution.py:12
  92.3 13.8 %collective-permute-done.8 = f32[20,8192]{1,0:T(8,128)S(1)} collective-permute-done((f32[20,8192]{1,0:T(8,128)S(1)}, f32[20,8192]{1,0:T(8,128)S(1)}, u32[]{:S(2)}, u32[]{:S(2)}) %collective-permute-start.8) | collective-permute-done | bytes 655392 | tf_op jit(solution)/shard_map/ppermute | solution.py:12
  106.4 2.7 %collective-permute-start.9 = (f32[20,8192]{1,0:T(8,128)S(1)}, f32[20,8192]{1,0:T(8,128)S(1)}, u32[]{:S(2)}, u32[]{:S(2)}) collective-permute-start(f32[20,8192]{1,0:T(8,128)S(1)} %convolution_add_fusion.3), channel_id=1, source_target_pairs={{0,24},{8,0},{16,8},{24,16},{1,25},{9,1},{17,9},{25,17},{2,26},{10... | collective-permute-start | bytes 1966088 | tf_op jit(solution)/shard_map/ppermute | solution.py:12
  109.1 13.8 %collective-permute-done.10 = f32[20,8192]{1,0:T(8,128)S(1)} collective-permute-done((f32[20,8192]{1,0:T(8,128)S(1)}, f32[20,8192]{1,0:T(8,128)S(1)}, u32[]{:S(2)}, u32[]{:S(2)}) %collective-permute-start.10) | collective-permute-done | bytes 655392 | tf_op jit(solution)/shard_map/ppermute | solution.py:12
  123.3 2.7 %collective-permute-start.11 = (f32[20,8192]{1,0:T(8,128)S(1)}, f32[20,8192]{1,0:T(8,128)S(1)}, u32[]{:S(2)}, u32[]{:S(2)}) collective-permute-start(f32[20,8192]{1,0:T(8,128)S(1)} %convolution_add_fusion.2), channel_id=1, source_target_pairs={{0,24},{8,0},{16,8},{24,16},{1,25},{9,1},{17,9},{25,17},{2,26},{10... | collective-permute-start | bytes 1966088 | tf_op jit(solution)/shard_map/ppermute | solution.py:12
  127.5 12.3 %collective-permute-done.7 = f32[20,8192]{1,0:T(8,128)S(1)} collective-permute-done((f32[20,8192]{1,0:T(8,128)S(1)}, f32[20,8192]{1,0:T(8,128)S(1)}, u32[]{:S(2)}, u32[]{:S(2)}) %collective-permute-start.7) | collective-permute-done | bytes 655392 | tf_op jit(solution)/shard_map/ppermute | solution.py:12
  139.8 1.0 add.60
  140.7 15.9 %collective-permute-done.9 = f32[20,8192]{1,0:T(8,128)S(1)} collective-permute-done((f32[20,8192]{1,0:T(8,128)S(1)}, f32[20,8192]{1,0:T(8,128)S(1)}, u32[]{:S(2)}, u32[]{:S(2)}) %collective-permute-start.9) | collective-permute-done | bytes 655392 | tf_op jit(solution)/shard_map/ppermute | solution.py:12
  156.6 1.0 add.62
  157.6 14.1 %collective-permute-done.11 = f32[20,8192]{1,0:T(8,128)S(1)} collective-permute-done((f32[20,8192]{1,0:T(8,128)S(1)}, f32[20,8192]{1,0:T(8,128)S(1)}, u32[]{:S(2)}, u32[]{:S(2)}) %collective-permute-start.11) | collective-permute-done | bytes 655392 | tf_op jit(solution)/shard_map/ppermute | solution.py:12
  171.7 1.0 add.64
  172.7 1.8 convert_element_type.33
  (28 shorter events, 9.3 us)
Async XLA Ops:
  7.2 6.1 %copy-start = (bf16[128,8192]{1,0:T(8,128)(2,1)S(1)}, bf16[128,8192]{1,0:T(8,128)(2,1)}, u32[]{:S(2)}) copy-start(bf16[128,8192]{1,0:T(8,128)(2,1)} %param.5) | copy-start | bytes 6291460
  7.2 7.7 %copy-start.3 = (bf16[20,8192]{1,0:T(8,128)(2,1)S(1)}, bf16[20,8192]{1,0:T(8,128)(2,1)}, u32[]{:S(2)}) copy-start(bf16[20,8192]{1,0:T(8,128)(2,1)} %param.8) | copy-start | bytes 983044
  7.2 8.4 %copy-start.2 = (bf16[20,8192]{1,0:T(8,128)(2,1)S(1)}, bf16[20,8192]{1,0:T(8,128)(2,1)}, u32[]{:S(2)}) copy-start(bf16[20,8192]{1,0:T(8,128)(2,1)} %param.9) | copy-start | bytes 983044
  7.2 165.5 %reduce-scatter.2.cloned.1.call-start = ((), (), s32[]{:S(2)}) async-start(), calls=%async_computation.1 | async-start | bytes 4718592 | tf_op jit(solution)/shard_map/reduce_scatter | solution.py:67
  7.2 14.1 %collective-permute-start = (bf16[20,8192]{1,0:T(8,128)(2,1)}, bf16[20,8192]{1,0:T(8,128)(2,1)S(1)}, u32[]{:S(2)}, u32[]{:S(2)}) collective-permute-start(bf16[20,8192]{1,0:T(8,128)(2,1)} %param.7), channel_id=1, source_target_pairs={{0,8},{8,16},{16,24},{24,0},{1,9},{9,17},{17,25},{25,1},{2,10},{10... | collective-permute-start | bytes 983048 | tf_op jit(solution)/shard_map/ppermute | solution.py:12
  10.2 19.5 %collective-permute-start.1 = (bf16[20,8192]{1,0:T(8,128)(2,1)}, bf16[20,8192]{1,0:T(8,128)(2,1)S(1)}, u32[]{:S(2)}, u32[]{:S(2)}) collective-permute-start(bf16[20,8192]{1,0:T(8,128)(2,1)} %param.8), channel_id=1, source_target_pairs={{0,8},{8,16},{16,24},{24,0},{1,9},{9,17},{17,25},{25,1},{2,10},{10... | collective-permute-start | bytes 983048 | tf_op jit(solution)/shard_map/ppermute | solution.py:12
  11.7 26.5 %collective-permute-start.2 = (bf16[20,8192]{1,0:T(8,128)(2,1)}, bf16[20,8192]{1,0:T(8,128)(2,1)S(1)}, u32[]{:S(2)}, u32[]{:S(2)}) collective-permute-start(bf16[20,8192]{1,0:T(8,128)(2,1)} %param.9), channel_id=1, source_target_pairs={{0,8},{8,16},{16,24},{24,0},{1,9},{9,17},{17,25},{25,1},{2,10},{10... | collective-permute-start | bytes 983048 | tf_op jit(solution)/shard_map/ppermute | solution.py:12
  22.0 24.6 %collective-permute-start.3 = (bf16[20,8192]{1,0:T(8,128)(2,1)S(1)}, bf16[20,8192]{1,0:T(8,128)(2,1)S(1)}, u32[]{:S(2)}, u32[]{:S(2)}) collective-permute-start(bf16[20,8192]{1,0:T(8,128)(2,1)S(1)} %collective-permute-done), channel_id=1, source_target_pairs={{0,8},{8,16},{16,24},{24,0},{1,9},{9,17},{17,25},{25,1},{2,10},{10... | collective-permute-start | bytes 983048 | tf_op jit(solution)/shard_map/ppermute | solution.py:12
  29.8 25.3 %collective-permute-start.4 = (bf16[20,8192]{1,0:T(8,128)(2,1)S(1)}, bf16[20,8192]{1,0:T(8,128)(2,1)S(1)}, u32[]{:S(2)}, u32[]{:S(2)}) collective-permute-start(bf16[20,8192]{1,0:T(8,128)(2,1)S(1)} %collective-permute-done.1), channel_id=1, source_target_pairs={{0,8},{8,16},{16,24},{24,0},{1,9},{9,17},{17,25},{25,1},{2,10},{10... | collective-permute-start | bytes 983048 | tf_op jit(solution)/shard_map/ppermute | solution.py:12
  38.2 24.5 %collective-permute-start.5 = (bf16[20,8192]{1,0:T(8,128)(2,1)S(1)}, bf16[20,8192]{1,0:T(8,128)(2,1)S(1)}, u32[]{:S(2)}, u32[]{:S(2)}) collective-permute-start(bf16[20,8192]{1,0:T(8,128)(2,1)S(1)} %collective-permute-done.2), channel_id=1, source_target_pairs={{0,8},{8,16},{16,24},{24,0},{1,9},{9,17},{17,25},{25,1},{2,10},{10... | collective-permute-start | bytes 983048 | tf_op jit(solution)/shard_map/ppermute | solution.py:12
  65.4 2.2 %copy-start.1 = (bf16[128,8192]{1,0:T(8,128)(2,1)S(1)}, bf16[128,8192]{1,0:T(8,128)(2,1)}, u32[]{:S(2)}) copy-start(bf16[128,8192]{1,0:T(8,128)(2,1)} %param.6) | copy-start | bytes 6291460
  68.7 20.5 %collective-permute-start.6 = (f32[20,8192]{1,0:T(8,128)S(1)}, f32[20,8192]{1,0:T(8,128)S(1)}, u32[]{:S(2)}, u32[]{:S(2)}) collective-permute-start(f32[20,8192]{1,0:T(8,128)S(1)} %fusion.3), channel_id=1, source_target_pairs={{0,24},{8,0},{16,8},{24,16},{1,25},{9,1},{17,9},{25,17},{2,26},{10... | collective-permute-start | bytes 1966088 | tf_op jit(solution)/shard_map/ppermute | solution.py:12
  70.9 35.2 %collective-permute-start.8 = (f32[20,8192]{1,0:T(8,128)S(1)}, f32[20,8192]{1,0:T(8,128)S(1)}, u32[]{:S(2)}, u32[]{:S(2)}) collective-permute-start(f32[20,8192]{1,0:T(8,128)S(1)} %fusion.5), channel_id=1, source_target_pairs={{0,24},{8,0},{16,8},{24,16},{1,25},{9,1},{17,9},{25,17},{2,26},{10... | collective-permute-start | bytes 1966088 | tf_op jit(solution)/shard_map/ppermute | solution.py:12
  72.7 50.2 %collective-permute-start.10 = (f32[20,8192]{1,0:T(8,128)S(1)}, f32[20,8192]{1,0:T(8,128)S(1)}, u32[]{:S(2)}, u32[]{:S(2)}) collective-permute-start(f32[20,8192]{1,0:T(8,128)S(1)} %fusion.26), channel_id=1, source_target_pairs={{0,24},{8,0},{16,8},{24,16},{1,25},{9,1},{17,9},{25,17},{2,26},{10... | collective-permute-start | bytes 1966088 | tf_op jit(solution)/shard_map/ppermute | solution.py:12
  89.6 50.2 %collective-permute-start.7 = (f32[20,8192]{1,0:T(8,128)S(1)}, f32[20,8192]{1,0:T(8,128)S(1)}, u32[]{:S(2)}, u32[]{:S(2)}) collective-permute-start(f32[20,8192]{1,0:T(8,128)S(1)} %convolution_add_fusion.4), channel_id=1, source_target_pairs={{0,24},{8,0},{16,8},{24,16},{1,25},{9,1},{17,9},{25,17},{2,26},{10... | collective-permute-start | bytes 1966088 | tf_op jit(solution)/shard_map/ppermute | solution.py:12
  106.4 50.2 %collective-permute-start.9 = (f32[20,8192]{1,0:T(8,128)S(1)}, f32[20,8192]{1,0:T(8,128)S(1)}, u32[]{:S(2)}, u32[]{:S(2)}) collective-permute-start(f32[20,8192]{1,0:T(8,128)S(1)} %convolution_add_fusion.3), channel_id=1, source_target_pairs={{0,24},{8,0},{16,8},{24,16},{1,25},{9,1},{17,9},{25,17},{2,26},{10... | collective-permute-start | bytes 1966088 | tf_op jit(solution)/shard_map/ppermute | solution.py:12
  123.3 48.4 %collective-permute-start.11 = (f32[20,8192]{1,0:T(8,128)S(1)}, f32[20,8192]{1,0:T(8,128)S(1)}, u32[]{:S(2)}, u32[]{:S(2)}) collective-permute-start(f32[20,8192]{1,0:T(8,128)S(1)} %convolution_add_fusion.2), channel_id=1, source_target_pairs={{0,24},{8,0},{16,8},{24,16},{1,25},{9,1},{17,9},{25,17},{2,26},{10... | collective-permute-start | bytes 1966088 | tf_op jit(solution)/shard_map/ppermute | solution.py:12
Sparse Core Ops, SparseCore 0:
  65.5 50.5 reduce-scatter.1
where the time goes:
time: 182 us; the launch traced here: 181 us
  waiting for transfers between devices  125 us (69%)
  starting transfers between devices  21.3 us (12%)
  matrix products  16.5 us (9%)
  between operations  14.1 us (8%)
  other arithmetic  4.66 us (3%)
    ppermute x12, waiting for transfers between devices, passed_along(): return lax.ppermute(value, axis, pairs)  125 us
    ppermute x12, starting transfers between devices, passed_along(): return lax.ppermute(value, axis, pairs)  21.2 us
    dot_general x3, matrix products, forward_block(): jnp.dot(hidden, down_rows, preferred_element_type=jnp.float32)  4.18 us
  transfers between devices with their start and end apart: 13, of which 12 were waited for; matrix products, arithmetic and copies ran while one was open for 9% of the time, Pallas kernels for 0%

commit v1 on v0

v1 whole, which is shorter than its diff:
```python
import jax
import jax.numpy as jnp
from jax import lax
from jax.sharding import PartitionSpec as P

STEPS = 3
BF = jnp.bfloat16
F32 = jnp.float32


def rows_dot(inputs, rows):
    return lax.dot_general(inputs, rows, (((1,), (1,)), ((), ())), preferred_element_type=F32)


def tokens_dot(left, right):
    return lax.dot_general(left, right, (((0,), (0,)), ((), ())), preferred_element_type=F32)


def exchanged(value, axis, bit):
    count = lax.axis_size(axis)
    return lax.ppermute(value, axis, [(source, source ^ bit) for source in range(count)])


def ring_passed(value, steps):
    count = lax.axis_size("section")
    return lax.ppermute(value, "section", [(source, (source + steps) % count) for source in range(count)])


def packed_weights(gate, up, down):
    half = gate.shape[1] // 2
    return (
        jnp.concatenate([gate[:, :half], up[:, :half]], 0),
        jnp.concatenate([gate[:, half:], up[:, half:]], 0),
        jnp.concatenate([down[:, :half], down[:, half:]], 0),
    )


def block_work(inputs, cot, weights):
    first, second, down = weights
    rows = down.shape[0] // 2
    half = down.shape[1]
    both = rows_dot(inputs[:, :half], first) + rows_dot(inputs[:, half:], second)
    gate, up = both[:, :rows], both[:, rows:]
    sig = jax.nn.sigmoid(gate)
    activated = gate * sig
    hidden = (activated * up).astype(BF)
    dhid = rows_dot(cot[:, :half], down[:rows]) + rows_dot(cot[:, half:], down[rows:])
    dgate = (dhid * up * sig * (1.0 + gate * (1.0 - sig))).astype(BF)
    dup = (dhid * activated).astype(BF)
    pair = jnp.concatenate([dgate, dup], 1)
    return hidden, pair


def block_grads(inputs, cot, hidden, pair):
    half = inputs.shape[1] // 2
    return (
        tokens_dot(pair, inputs[:, :half]),
        tokens_dot(pair, inputs[:, half:]),
        jnp.concatenate([tokens_dot(hidden, cot[:, :half]), tokens_dot(hidden, cot[:, half:])], 0),
    )


def scattered_sum(total):
    count = lax.axis_size("tensor")
    if count & (count - 1):
        return lax.psum_scatter(total, "tensor", scatter_dimension=1, tiled=True).astype(BF)
    me = lax.axis_index("tensor")
    width = total.shape[1] // count
    parts = [total[:, k * width : (k + 1) * width] for k in range(count)]
    bit = 1
    while bit < count:
        mine = (me & bit) != 0
        low, high = parts[0::2], parts[1::2]
        keep = [jnp.where(mine, b, a) for a, b in zip(low, high)]
        send = jnp.concatenate([jnp.where(mine, a, b).astype(BF) for a, b in zip(low, high)], 1)
        got = exchanged(send, "tensor", bit).astype(F32)
        parts = [k + got[:, i * width : (i + 1) * width] for i, k in enumerate(keep)]
        bit *= 2
    return parts[0].astype(BF)


def on_device(tokens, cotangent, gate_weight, up_weight, down_weight):
    own = packed_weights(gate_weight, up_weight, down_weight)
    four = lax.axis_size("section") == 4
    odd = (lax.axis_index("section") & 1) != 0
    if four:
        far = tuple(exchanged(piece, "section", 2) for piece in own)
        near = tuple(exchanged(jnp.where(odd, f, o), "section", 1) for f, o in zip(far, own))
    else:
        near = tuple(ring_passed(piece, 1) for piece in own)
        far = tuple(ring_passed(piece, 1) for piece in near)
    work = [block_work(tokens, cotangent, w) for w in (own, near, far)]
    hidden = jnp.concatenate([w[0] for w in work], 1)
    rows = gate_weight.shape[0]
    down_low = jnp.concatenate([w[2][:rows] for w in (own, near, far)], 0)
    down_high = jnp.concatenate([w[2][rows:] for w in (own, near, far)], 0)
    total = jnp.concatenate(
        [jnp.dot(hidden, down_low, preferred_element_type=F32), jnp.dot(hidden, down_high, preferred_element_type=F32)], 1
    )
    output = scattered_sum(total)
    grads = [block_grads(tokens, cotangent, *w) for w in work]
    zero = jnp.zeros((), F32)
    sums = []
    for k in (2, 0, 1):
        g_own, g_near, g_far = (g[k] for g in grads)
        if four:
            side = exchanged(g_near.astype(BF), "section", 1).astype(F32)
            back = exchanged((g_far + jnp.where(odd, side, zero)).astype(BF), "section", 2).astype(F32)
            sums.append(g_own + back + jnp.where(odd, zero, side))
        else:
            side = ring_passed(g_far.astype(BF), -1).astype(F32)
            back = ring_passed((g_near + side).astype(BF), -1).astype(F32)
            sums.append(g_own + back)
    down_sum, low, high = sums
    grad_gate = jnp.concatenate([low[:rows], high[:rows]], 1)
    grad_up = jnp.concatenate([low[rows:], high[rows:]], 1)
    grad_down = jnp.concatenate([down_sum[:rows], down_sum[rows:]], 1)
    return (output, grad_gate, grad_up, grad_down)


def solution(mesh):
    placed = (
        P("section", None),
        P("section", None),
        P(("section", "tensor"), None),
        P(("section", "tensor"), None),
        P(("section", "tensor"), None),
    )
    return jax.shard_map(
        on_device,
        mesh=mesh,
        in_specs=placed,
        out_specs=(
            P("section", "tensor"),
            P(("section", "tensor"), None),
            P(("section", "tensor"), None),
            P(("section", "tensor"), None),
        ),
        check_vma=False,
    )
```

time: 182 us -> 108 us (0.59)
  waiting for transfers between devices: 125 us -> 53.2 us
  between operations: 14.1 us -> 1.04 us
  other arithmetic: 4.66 us -> 8.87 us
  local copies, waits for them, and re-layouts: 0.12 us -> 3.8 us
  starting transfers between devices: 21.3 us -> 23.4 us
    ppermute x12 -> x15, waiting for transfers between devices: 125 us -> 53.2 us  [exchanged(): lax.ppermute(value, axis, [(source, source ^ bit) for source in range(cou...]
    concatenate x0 -> x9, other arithmetic: none -> 5.37 us  [the longest x1 0.93 us: on_device(): grad_gate = jnp.concatenate([low[:rows], high[:rows]], 1)]
    slice x0 -> x7, local copies, waits for them, and re-layouts: none -> 3.75 us  [the longest x1 1.27 us: packed_weights(): gate[:, :half]]
    add x3, other arithmetic: 2.88 us -> 0.39 us  [on_device(): sums.append(g_own + back + jnp.where(odd, zero, side))]
    ppermute x12 -> x15, starting transfers between devices: 21.2 us -> 23.4 us  [exchanged(): lax.ppermute(value, axis, [(source, source ^ bit) for source in range(cou...]
    dot_general x21 -> x26, matrix products: 16.5 us -> 17.4 us  [the longest x12 10.9 us: rows_dot(): lax.dot_general(inputs, rows, (((1,), (1,)), ((), ())), preferred_element...]
  transfers between devices with their start and end apart: 13 -> 15, of which waited for: 12 -> 10; matrix products, arithmetic and copies ran while one was open for 9% -> 21% of each run, Pallas kernels for 0% -> 0%
where the time goes in v1:
time: 108 us
  waiting for transfers between devices  53.2 us (49%)
  starting transfers between devices  23.4 us (22%)
  matrix products  17.4 us (16%)
  other arithmetic  8.87 us (8%)
  local copies, waits for them, and re-layouts  3.8 us (4%)
    ppermute x15, waiting for transfers between devices, exchanged(): lax.ppermute(value, axis, [(source, source ^ bit) for source in range(cou...  53.2 us
    ppermute x15, starting transfers between devices, exchanged(): lax.ppermute(value, axis, [(source, source ^ bit) for source in range(cou...  23.4 us
    dot_general x12, matrix products, rows_dot(): lax.dot_general(inputs, rows, (((1,), (1,)), ((), ())), preferred_element...  10.9 us
    dot_general x12, matrix products, tokens_dot(): lax.dot_general(left, right, (((0,), (0,)), ((), ())), preferred_element_...  5.54 us
  transfers between devices with their start and end apart: 15, of which 10 were waited for; matrix products, arithmetic and copies ran while one was open for 21% of the time, Pallas kernels for 0%

profile of v1, /device:TPU:0, one launch (start us, length us, event | category | flops | bytes accessed | tf_op | source)
XLA Modules:
  0.0 107.7 jit_solution(9448401368833982484)
XLA Ops:
  0.6 1.2 %fusion.90 = (bf16[20,4096]{1,0:T(8,128)(2,1)S(1)}, bf16[20,4096]{1,0:T(8,128)(2,1)S(1)}) fusion(bf16[20,8192]{1,0:T(8,128)(2,1)} %param.9), kind=kLoop, calls=%fused_computation.145 | loop fusion | bytes 655360 | tf_op jit(solution)/shard_map/slice | solution.py:34
  2.6 3.0 %collective-permute-start.4 = (bf16[40,4096]{1,0:T(8,128)(2,1)}, bf16[40,4096]{1,0:T(8,128)(2,1)}, u32[]{:S(2)}, u32[]{:S(2)}) collective-permute-start(bf16[40,4096]{1,0:T(8,128)(2,1)} %pad_maximum_fusion.7), channel_id=1, source_target_pairs={{0,16},{8,24},{16,0},{24,8},{1,17},{9,25},{17,1},{25,9},{2,18},{10... | collective-permute-start | bytes 983048 | tf_op jit(solution)/shard_map/ppermute | solution.py:21
  5.6 1.3 %fusion.88 = (bf16[20,4096]{1,0:T(8,128)(2,1)S(1)}, bf16[20,4096]{1,0:T(8,128)(2,1)S(1)}, bf16[20,4096]{1,0:T(8,128)(2,1)S(1)}, bf16[20,4096]{1,0:T(8,128)(2,1)S(1)}) fusion(bf16[20,8192]{1,0:T(8,128)(2,1)} %param.7, bf16[20,8192]{1,0:T(8,128)(2,1)} %param.8), kind=kLoop, calls=%fused_computation.143 | loop fusion | bytes 1310720 | tf_op jit(solution)/shard_map/slice | solution.py:32
  8.5 2.0 %collective-permute-start = (bf16[40,4096]{1,0:T(8,128)(2,1)}, bf16[40,4096]{1,0:T(8,128)(2,1)}, u32[]{:S(2)}, u32[]{:S(2)}) collective-permute-start(bf16[40,4096]{1,0:T(8,128)(2,1)} %pad_maximum_fusion.5), channel_id=1, source_target_pairs={{0,16},{8,24},{16,0},{24,8},{1,17},{9,25},{17,1},{25,9},{2,18},{10... | collective-permute-start | bytes 983048 | tf_op jit(solution)/shard_map/ppermute | solution.py:21
  10.6 1.5 %fusion.64 = f32[40,128]{1,0:T(8,128)S(1)} fusion(bf16[40,4096]{1,0:T(8,128)(2,1)} %pad_maximum_fusion.5, bf16[128,8192]{1,0:T(8,128)(2,1)S(1)} %copy-done), kind=kOutput, calls=%fused_computation.98 | convolution fusion | flops 41943040 | bytes 1396736 | tf_op jit(solution)/shard_map/dot_general | solution.py:12
  12.0 1.4 %fusion.2 = f32[128,40]{0,1:T(8,128)S(1)} fusion(f32[40,128]{1,0:T(8,128)S(1)} %fusion.64, bf16[40,4096]{1,0:T(8,128)(2,1)} %pad_maximum_fusion.6, bf16[128,8192]{1,0:T(8,128)(2,1)S(1)} %copy-done), kind=kOutput, calls=%fused_computation.9 | convolution fusion | flops 41948160 | bytes 1417216 | tf_op jit(solution)/shard_map/dot_general | solution.py:12
  14.4 1.0 fusion.29
  15.6 1.0 fusion.39
  16.7 1.1 %fusion.60 = f32[40,4096]{1,0:T(8,128)S(1)} fusion(bf16[128,8192]{1,0:T(8,128)(2,1)S(1)} %copy-done, bf16[128,20]{0,1:T(8,128)(2,1)} %copy-done.10, bf16[128,20]{0,1:T(8,128)(2,1)S(1)} %get-tuple-element.38), kind=kOutput, calls=%fused_computation.94 | convolution fusion | flops 41963520 | bytes 1715200 | tf_op jit(solution)/shard_map/dot_general | solution.py:16
  17.9 2.5 %collective-permute-start.5 = (bf16[40,4096]{1,0:T(8,128)(2,1)S(1)}, bf16[40,4096]{1,0:T(8,128)(2,1)S(1)}, u32[]{:S(2)}, u32[]{:S(2)}) collective-permute-start(bf16[40,4096]{1,0:T(8,128)(2,1)S(1)} %broadcast_select_fusion), channel_id=1, source_target_pairs={{0,8},{8,0},{16,24},{24,16},{1,9},{9,1},{17,25},{25,17},{2,10},{10... | collective-permute-start | bytes 983048 | tf_op jit(solution)/shard_map/ppermute | solution.py:21
  20.4 1.0 collective-permute-done.2
  21.6 3.1 %collective-permute-start.3 = (bf16[40,4096]{1,0:T(8,128)(2,1)S(1)}, bf16[40,4096]{1,0:T(8,128)(2,1)S(1)}, u32[]{:S(2)}, u32[]{:S(2)}) collective-permute-start(bf16[40,4096]{1,0:T(8,128)(2,1)S(1)} %broadcast_select_fusion.1), channel_id=1, source_target_pairs={{0,8},{8,0},{16,24},{24,16},{1,9},{9,1},{17,25},{25,17},{2,10},{10... | collective-permute-start | bytes 983048 | tf_op jit(solution)/shard_map/ppermute | solution.py:21
  24.7 1.1 fusion.92
  25.8 1.3 %fusion.33 = f32[20,128]{1,0:T(8,128)S(1)} fusion(bf16[128,8192]{1,0:T(8,128)(2,1)S(1)} %copy-done.2, bf16[40,4096]{1,0:T(8,128)(2,1)} %collective-permute-done.4), kind=kOutput, calls=%fused_computation.69 | convolution fusion | flops 20971520 | bytes 1255424 | tf_op jit(solution)/shard_map/dot_general | solution.py:12
  27.1 1.5 %fusion.50 = f32[40,128]{1,0:T(8,128)S(1)} fusion(bf16[40,4096]{1,0:T(8,128)(2,1)} %collective-permute-done.2, bf16[128,8192]{1,0:T(8,128)(2,1)S(1)} %copy-done), kind=kOutput, calls=%fused_computation.86 | convolution fusion | flops 41943040 | bytes 1396736 | tf_op jit(solution)/shard_map/dot_general | solution.py:12
  28.7 1.4 %fusion = f32[128,40]{0,1:T(8,128)S(1)} fusion(f32[40,128]{1,0:T(8,128)S(1)} %fusion.50, bf16[40,4096]{1,0:T(8,128)(2,1)} %collective-permute-done, bf16[128,8192]{1,0:T(8,128)(2,1)S(1)} %copy-done), kind=kOutput, calls=%fused_computation.5 | convolution fusion | flops 41948160 | bytes 1417216 | tf_op jit(solution)/shard_map/dot_general | solution.py:12
  30.1 1.3 %multiply_convert_fusion.3 = (bf16[128,20]{0,1:T(8,128)(2,1)S(1)}, bf16[128,20]{0,1:T(8,128)(2,1)S(1)}, bf16[128,20]{0,1:T(8,128)(2,1)S(1)}) fusion(f32[128,40]{0,1:T(8,128)S(1)} %fusion, f32[20,128]{1,0:T(8,128)S(1)} %fusion.33, bf16[128,8192]{1,0:T(8,128)(2,1)S(1)} %copy-done.2, bf16[40,4096]{1,0:T(8,128)(2,1)} %collective-permute-done.4), kind=kOutput, calls=%fused_computation.111 | convolution fusion | flops 21012480 | bytes 1297408 | tf_op jit(solution)/shard_map/dot_general | solution.py:12
  32.0 1.9 %collective-permute-start.1 = (bf16[40,4096]{1,0:T(8,128)(2,1)S(1)}, bf16[40,4096]{1,0:T(8,128)(2,1)S(1)}, u32[]{:S(2)}, u32[]{:S(2)}) collective-permute-start(bf16[40,4096]{1,0:T(8,128)(2,1)S(1)} %broadcast_select_fusion.2), channel_id=1, source_target_pairs={{0,8},{8,0},{16,24},{24,16},{1,9},{9,1},{17,25},{25,17},{2,10},{10... | collective-permute-start | bytes 983048 | tf_op jit(solution)/shard_map/ppermute | solution.py:21
  35.4 5.9 %collective-permute-done.1 = bf16[40,4096]{1,0:T(8,128)(2,1)S(1)} collective-permute-done((bf16[40,4096]{1,0:T(8,128)(2,1)S(1)}, bf16[40,4096]{1,0:T(8,128)(2,1)S(1)}, u32[]{:S(2)}, u32[]{:S(2)}) %collective-permute-start.1) | collective-permute-done | bytes 327712 | tf_op jit(solution)/shard_map/ppermute | solution.py:21
  44.7 1.8 %collective-permute-start.11 = (bf16[40,4096]{1,0:T(8,128)(2,1)S(1)}, bf16[40,4096]{1,0:T(8,128)(2,1)S(1)}, u32[]{:S(2)}, u32[]{:S(2)}) collective-permute-start(bf16[40,4096]{1,0:T(8,128)(2,1)S(1)} %convolution_convert_fusion), channel_id=1, source_target_pairs={{0,8},{8,0},{16,24},{24,16},{1,9},{9,1},{17,25},{25,17},{2,10},{10... | collective-permute-start | bytes 983048 | tf_op jit(solution)/shard_map/ppermute | solution.py:21
  46.8 1.8 %collective-permute-start.13 = (bf16[40,4096]{1,0:T(8,128)(2,1)S(1)}, bf16[40,4096]{1,0:T(8,128)(2,1)S(1)}, u32[]{:S(2)}, u32[]{:S(2)}) collective-permute-start(bf16[40,4096]{1,0:T(8,128)(2,1)S(1)} %pad_maximum_fusion.8), channel_id=1, source_target_pairs={{0,8},{8,0},{16,24},{24,16},{1,9},{9,1},{17,25},{25,17},{2,10},{10... | collective-permute-start | bytes 983048 | tf_op jit(solution)/shard_map/ppermute | solution.py:21
  48.6 6.6 %collective-permute-done.11 = bf16[40,4096]{1,0:T(8,128)(2,1)S(1)} collective-permute-done((bf16[40,4096]{1,0:T(8,128)(2,1)S(1)}, bf16[40,4096]{1,0:T(8,128)(2,1)S(1)}, u32[]{:S(2)}, u32[]{:S(2)}) %collective-permute-start.11) | collective-permute-done | bytes 327712 | tf_op jit(solution)/shard_map/ppermute | solution.py:21
  56.4 5.8 %collective-permute-done.9 = bf16[40,4096]{1,0:T(8,128)(2,1)S(1)} collective-permute-done((bf16[40,4096]{1,0:T(8,128)(2,1)S(1)}, bf16[40,4096]{1,0:T(8,128)(2,1)S(1)}, u32[]{:S(2)}, u32[]{:S(2)}) %collective-permute-start.9) | collective-permute-done | bytes 327712 | tf_op jit(solution)/shard_map/ppermute | solution.py:21
  63.5 5.4 %collective-permute-done.13 = bf16[40,4096]{1,0:T(8,128)(2,1)S(1)} collective-permute-done((bf16[40,4096]{1,0:T(8,128)(2,1)S(1)}, bf16[40,4096]{1,0:T(8,128)(2,1)S(1)}, u32[]{:S(2)}, u32[]{:S(2)}) %collective-permute-start.13) | collective-permute-done | bytes 327712 | tf_op jit(solution)/shard_map/ppermute | solution.py:21
  70.1 1.5 %collective-permute-done.10 = bf16[40,4096]{1,0:T(8,128)(2,1)S(1)} collective-permute-done((bf16[40,4096]{1,0:T(8,128)(2,1)S(1)}, bf16[40,4096]{1,0:T(8,128)(2,1)S(1)}, u32[]{:S(2)}, u32[]{:S(2)}) %collective-permute-start.10) | collective-permute-done | bytes 327712 | tf_op jit(solution)/shard_map/ppermute | solution.py:21
  71.7 6.7 %collective-permute-done.14 = bf16[40,4096]{1,0:T(8,128)(2,1)S(1)} collective-permute-done((bf16[40,4096]{1,0:T(8,128)(2,1)S(1)}, bf16[40,4096]{1,0:T(8,128)(2,1)S(1)}, u32[]{:S(2)}, u32[]{:S(2)}) %collective-permute-start.14) | collective-permute-done | bytes 327712 | tf_op jit(solution)/shard_map/ppermute | solution.py:21
  78.6 0.9 pad_maximum_fusion.1
  79.8 1.0 select_convert_fusion.2
  80.9 1.6 %collective-permute-start.7 = (bf16[128,2048]{1,0:T(8,128)(2,1)S(1)}, bf16[128,2048]{1,0:T(8,128)(2,1)S(1)}, u32[]{:S(2)}, u32[]{:S(2)}) collective-permute-start(bf16[128,2048]{1,0:T(8,128)(2,1)S(1)} %pad_maximum_fusion.4), channel_id=1, source_target_pairs={{0,2},{1,3},{2,0},{3,1},{4,6},{5,7},{6,4},{7,5},{8,10},{9,11},{10,... | collective-permute-start | bytes 1572872 | tf_op jit(solution)/shard_map/ppermute | solution.py:21
  83.4 10.2 %collective-permute-done.7 = bf16[128,2048]{1,0:T(8,128)(2,1)S(1)} collective-permute-done((bf16[128,2048]{1,0:T(8,128)(2,1)S(1)}, bf16[128,2048]{1,0:T(8,128)(2,1)S(1)}, u32[]{:S(2)}, u32[]{:S(2)}) %collective-permute-start.7) | collective-permute-done | bytes 524320 | tf_op jit(solution)/shard_map/ppermute | solution.py:21
  94.1 2.6 %collective-permute-start.8 = (bf16[128,1024]{1,0:T(8,128)(2,1)S(1)}, bf16[128,1024]{1,0:T(8,128)(2,1)S(1)}, u32[]{:S(2)}, u32[]{:S(2)}) collective-permute-start(bf16[128,1024]{1,0:T(8,128)(2,1)S(1)} %get-tuple-element.4), channel_id=1, source_target_pairs={{0,4},{1,5},{2,6},{3,7},{4,0},{5,1},{6,2},{7,3},{8,12},{9,13},{10,... | collective-permute-start | bytes 786440 | tf_op jit(solution)/shard_map/ppermute | solution.py:21
  97.7 9.2 %collective-permute-done.8 = bf16[128,1024]{1,0:T(8,128)(2,1)S(1)} collective-permute-done((bf16[128,1024]{1,0:T(8,128)(2,1)S(1)}, bf16[128,1024]{1,0:T(8,128)(2,1)S(1)}, u32[]{:S(2)}, u32[]{:S(2)}) %collective-permute-start.8) | collective-permute-done | bytes 262176 | tf_op jit(solution)/shard_map/ppermute | solution.py:21
  (76 shorter events, 16.9 us)
Async XLA Ops:
  0.6 9.9 %copy-start = (bf16[128,8192]{1,0:T(8,128)(2,1)S(1)}, bf16[128,8192]{1,0:T(8,128)(2,1)}, u32[]{:S(2)}) copy-start(bf16[128,8192]{1,0:T(8,128)(2,1)} %param.5) | copy-start | bytes 6291460
  2.6 15.1 %collective-permute-start.4 = (bf16[40,4096]{1,0:T(8,128)(2,1)}, bf16[40,4096]{1,0:T(8,128)(2,1)}, u32[]{:S(2)}, u32[]{:S(2)}) collective-permute-start(bf16[40,4096]{1,0:T(8,128)(2,1)} %pad_maximum_fusion.7), channel_id=1, source_target_pairs={{0,16},{8,24},{16,0},{24,8},{1,17},{9,25},{17,1},{25,9},{2,18},{10... | collective-permute-start | bytes 983048 | tf_op jit(solution)/shard_map/ppermute | solution.py:21
  6.9 6.6 %copy-start.3 = (bf16[20,4096]{1,0:T(8,128)(2,1)}, bf16[20,4096]{1,0:T(8,128)(2,1)S(1)}, u32[]{:S(2)}) copy-start(bf16[20,4096]{1,0:T(8,128)(2,1)S(1)} %get-tuple-element.27) | copy-start | bytes 491524
  6.9 6.6 %copy-start.5 = (bf16[20,4096]{1,0:T(8,128)(2,1)}, bf16[20,4096]{1,0:T(8,128)(2,1)S(1)}, u32[]{:S(2)}) copy-start(bf16[20,4096]{1,0:T(8,128)(2,1)S(1)} %get-tuple-element.45) | copy-start | bytes 491524
  6.9 6.6 %copy-start.1 = (bf16[128,8192]{1,0:T(8,128)(2,1)S(1)}, bf16[128,8192]{1,0:T(8,128)(2,1)}, u32[]{:S(2)}) copy-start(bf16[128,8192]{1,0:T(8,128)(2,1)} %param.6) | copy-start | bytes 6291460
  6.9 6.6 %copy-start.9 = (bf16[20,8192]{1,0:T(8,128)(2,1)S(1)}, bf16[20,8192]{1,0:T(8,128)(2,1)}, u32[]{:S(2)}) copy-start(bf16[20,8192]{1,0:T(8,128)(2,1)} %param.9) | copy-start | bytes 983044
  7.7 13.8 %collective-permute-start.2 = (bf16[40,4096]{1,0:T(8,128)(2,1)}, bf16[40,4096]{1,0:T(8,128)(2,1)}, u32[]{:S(2)}, u32[]{:S(2)}) collective-permute-start(bf16[40,4096]{1,0:T(8,128)(2,1)} %pad_maximum_fusion.6), channel_id=1, source_target_pairs={{0,16},{8,24},{16,0},{24,8},{1,17},{9,25},{17,1},{25,9},{2,18},{10... | collective-permute-start | bytes 983048 | tf_op jit(solution)/shard_map/ppermute | solution.py:21
  8.5 20.0 %collective-permute-start = (bf16[40,4096]{1,0:T(8,128)(2,1)}, bf16[40,4096]{1,0:T(8,128)(2,1)}, u32[]{:S(2)}, u32[]{:S(2)}) collective-permute-start(bf16[40,4096]{1,0:T(8,128)(2,1)} %pad_maximum_fusion.5), channel_id=1, source_target_pairs={{0,16},{8,24},{16,0},{24,8},{1,17},{9,25},{17,1},{25,9},{2,18},{10... | collective-permute-start | bytes 983048 | tf_op jit(solution)/shard_map/ppermute | solution.py:21
  14.3 2.3 %copy-start.10 = (bf16[128,20]{0,1:T(8,128)(2,1)}, bf16[128,20]{0,1:T(8,128)(2,1)S(1)}, u32[]{:S(2)}) copy-start(bf16[128,20]{0,1:T(8,128)(2,1)S(1)} %get-tuple-element.39) | copy-start | bytes 15364
  16.6 4.8 %copy-start.4 = (bf16[20,4096]{1,0:T(8,128)(2,1)S(1)}, bf16[20,4096]{1,0:T(8,128)(2,1)}, u32[]{:S(2)}) copy-start(bf16[20,4096]{1,0:T(8,128)(2,1)} %copy-done.3) | copy-start | bytes 491524
  16.6 4.8 %copy-start.6 = (bf16[20,4096]{1,0:T(8,128)(2,1)S(1)}, bf16[20,4096]{1,0:T(8,128)(2,1)}, u32[]{:S(2)}) copy-start(bf16[20,4096]{1,0:T(8,128)(2,1)} %copy-done.5) | copy-start | bytes 491524
  16.6 9.1 %copy-start.2 = (bf16[128,8192]{1,0:T(8,128)(2,1)S(1)}, bf16[128,8192]{1,0:T(8,128)(2,1)}, u32[]{:S(2)}) copy-start(bf16[128,8192]{1,0:T(8,128)(2,1)} %param.6) | copy-start | bytes 6291460
  17.9 15.9 %collective-permute-start.5 = (bf16[40,4096]{1,0:T(8,128)(2,1)S(1)}, bf16[40,4096]{1,0:T(8,128)(2,1)S(1)}, u32[]{:S(2)}, u32[]{:S(2)}) collective-permute-start(bf16[40,4096]{1,0:T(8,128)(2,1)S(1)} %broadcast_select_fusion), channel_id=1, source_target_pairs={{0,8},{8,0},{16,24},{24,16},{1,9},{9,1},{17,25},{25,17},{2,10},{10... | collective-permute-start | bytes 983048 | tf_op jit(solution)/shard_map/ppermute | solution.py:21
  21.6 13.3 %collective-permute-start.3 = (bf16[40,4096]{1,0:T(8,128)(2,1)S(1)}, bf16[40,4096]{1,0:T(8,128)(2,1)S(1)}, u32[]{:S(2)}, u32[]{:S(2)}) collective-permute-start(bf16[40,4096]{1,0:T(8,128)(2,1)S(1)} %broadcast_select_fusion.1), channel_id=1, source_target_pairs={{0,8},{8,0},{16,24},{24,16},{1,9},{9,1},{17,25},{25,17},{2,10},{10... | collective-permute-start | bytes 983048 | tf_op jit(solution)/shard_map/ppermute | solution.py:21
  32.0 9.4 %collective-permute-start.1 = (bf16[40,4096]{1,0:T(8,128)(2,1)S(1)}, bf16[40,4096]{1,0:T(8,128)(2,1)S(1)}, u32[]{:S(2)}, u32[]{:S(2)}) collective-permute-start(bf16[40,4096]{1,0:T(8,128)(2,1)S(1)} %broadcast_select_fusion.2), channel_id=1, source_target_pairs={{0,8},{8,0},{16,24},{24,16},{1,9},{9,1},{17,25},{25,17},{2,10},{10... | collective-permute-start | bytes 983048 | tf_op jit(solution)/shard_map/ppermute | solution.py:21
  44.6 35.0 %collective-permute-start.6 = (bf16[128,4096]{1,0:T(8,128)(2,1)S(1)}, bf16[128,4096]{1,0:T(8,128)(2,1)S(1)}, u32[]{:S(2)}, u32[]{:S(2)}) collective-permute-start(bf16[128,4096]{1,0:T(8,128)(2,1)S(1)} %pad_maximum_fusion), channel_id=1, source_target_pairs={{0,1},{1,0},{2,3},{3,2},{4,5},{5,4},{6,7},{7,6},{8,9},{9,8},{10,11... | collective-permute-start | bytes 3145736 | tf_op jit(solution)/shard_map/ppermute | solution.py:21
  44.7 10.6 %collective-permute-start.11 = (bf16[40,4096]{1,0:T(8,128)(2,1)S(1)}, bf16[40,4096]{1,0:T(8,128)(2,1)S(1)}, u32[]{:S(2)}, u32[]{:S(2)}) collective-permute-start(bf16[40,4096]{1,0:T(8,128)(2,1)S(1)} %convolution_convert_fusion), channel_id=1, source_target_pairs={{0,8},{8,0},{16,24},{24,16},{1,9},{9,1},{17,25},{25,17},{2,10},{10... | collective-permute-start | bytes 983048 | tf_op jit(solution)/shard_map/ppermute | solution.py:21
  46.5 15.8 %collective-permute-start.9 = (bf16[40,4096]{1,0:T(8,128)(2,1)S(1)}, bf16[40,4096]{1,0:T(8,128)(2,1)S(1)}, u32[]{:S(2)}, u32[]{:S(2)}) collective-permute-start(bf16[40,4096]{1,0:T(8,128)(2,1)S(1)} %convolution_convert_fusion.1), channel_id=1, source_target_pairs={{0,8},{8,0},{16,24},{24,16},{1,9},{9,1},{17,25},{25,17},{2,10},{10... | collective-permute-start | bytes 983048 | tf_op jit(solution)/shard_map/ppermute | solution.py:21
  46.8 22.0 %collective-permute-start.13 = (bf16[40,4096]{1,0:T(8,128)(2,1)S(1)}, bf16[40,4096]{1,0:T(8,128)(2,1)S(1)}, u32[]{:S(2)}, u32[]{:S(2)}) collective-permute-start(bf16[40,4096]{1,0:T(8,128)(2,1)S(1)} %pad_maximum_fusion.8), channel_id=1, source_target_pairs={{0,8},{8,0},{16,24},{24,16},{1,9},{9,1},{17,25},{25,17},{2,10},{10... | collective-permute-start | bytes 983048 | tf_op jit(solution)/shard_map/ppermute | solution.py:21
  55.5 14.3 %collective-permute-start.12 = (bf16[40,4096]{1,0:T(8,128)(2,1)S(1)}, bf16[40,4096]{1,0:T(8,128)(2,1)S(1)}, u32[]{:S(2)}, u32[]{:S(2)}) collective-permute-start(bf16[40,4096]{1,0:T(8,128)(2,1)S(1)} %fusion.9), channel_id=1, source_target_pairs={{0,16},{8,24},{16,0},{24,8},{1,17},{9,25},{17,1},{25,9},{2,18},{10... | collective-permute-start | bytes 983048 | tf_op jit(solution)/shard_map/ppermute | solution.py:21
  62.6 9.0 %collective-permute-start.10 = (bf16[40,4096]{1,0:T(8,128)(2,1)S(1)}, bf16[40,4096]{1,0:T(8,128)(2,1)S(1)}, u32[]{:S(2)}, u32[]{:S(2)}) collective-permute-start(bf16[40,4096]{1,0:T(8,128)(2,1)S(1)} %fusion.6), channel_id=1, source_target_pairs={{0,16},{8,24},{16,0},{24,8},{1,17},{9,25},{17,1},{25,9},{2,18},{10... | collective-permute-start | bytes 983048 | tf_op jit(solution)/shard_map/ppermute | solution.py:21
  69.0 9.5 %collective-permute-start.14 = (bf16[40,4096]{1,0:T(8,128)(2,1)S(1)}, bf16[40,4096]{1,0:T(8,128)(2,1)S(1)}, u32[]{:S(2)}, u32[]{:S(2)}) collective-permute-start(bf16[40,4096]{1,0:T(8,128)(2,1)S(1)} %fusion.12), channel_id=1, source_target_pairs={{0,16},{8,24},{16,0},{24,8},{1,17},{9,25},{17,1},{25,9},{2,18},{10... | collective-permute-start | bytes 983048 | tf_op jit(solution)/shard_map/ppermute | solution.py:21
  70.1 8.4 %copy-start.7 = (f32[20,4096]{1,0:T(8,128)S(1)}, f32[20,4096]{1,0:T(8,128)}, u32[]{:S(2)}) copy-start(f32[20,4096]{1,0:T(8,128)} %fusion.29) | copy-start | bytes 983044
  70.1 8.4 %copy-start.8 = (f32[20,4096]{1,0:T(8,128)S(1)}, f32[20,4096]{1,0:T(8,128)}, u32[]{:S(2)}) copy-start(f32[20,4096]{1,0:T(8,128)} %fusion.39) | copy-start | bytes 983044
  80.9 12.8 %collective-permute-start.7 = (bf16[128,2048]{1,0:T(8,128)(2,1)S(1)}, bf16[128,2048]{1,0:T(8,128)(2,1)S(1)}, u32[]{:S(2)}, u32[]{:S(2)}) collective-permute-start(bf16[128,2048]{1,0:T(8,128)(2,1)S(1)} %pad_maximum_fusion.4), channel_id=1, source_target_pairs={{0,2},{1,3},{2,0},{3,1},{4,6},{5,7},{6,4},{7,5},{8,10},{9,11},{10,... | collective-permute-start | bytes 1572872 | tf_op jit(solution)/shard_map/ppermute | solution.py:21
  94.1 12.8 %collective-permute-start.8 = (bf16[128,1024]{1,0:T(8,128)(2,1)S(1)}, bf16[128,1024]{1,0:T(8,128)(2,1)S(1)}, u32[]{:S(2)}, u32[]{:S(2)}) collective-permute-start(bf16[128,1024]{1,0:T(8,128)(2,1)S(1)} %get-tuple-element.4), channel_id=1, source_target_pairs={{0,4},{1,5},{2,6},{3,7},{4,0},{5,1},{6,2},{7,3},{8,12},{9,13},{10,... | collective-permute-start | bytes 786440 | tf_op jit(solution)/shard_map/ppermute | solution.py:21

commit v2 on v0

v2 whole, which is shorter than its diff:
```python
import jax
import jax.numpy as jnp
from jax import lax
from jax.experimental import pallas as pl
from jax.experimental.pallas import tpu as pltpu
from jax.sharding import PartitionSpec as P

BF = jnp.bfloat16
F32 = jnp.float32
NN = (((1,), (0,)), ((), ()))
NT = (((1,), (1,)), ((), ()))
TN = (((0,), (0,)), ((), ()))
TILE = 512


def dot(left, right, dims):
    return lax.dot_general(left, right, dims, preferred_element_type=F32)


class Steps:
    def __init__(self):
        self.mark = None

    def __call__(self, body, outs, ins, also=()):
        marks = [*also] if self.mark is None else [*also, self.mark]
        count = len(ins)

        def kernel(*refs):
            body(*refs[:count], *refs[count + len(marks) : -1])
            refs[-1][...] = jnp.zeros_like(refs[-1])

        single = isinstance(outs, tuple)
        shapes = ([outs] if single else list(outs)) + [((8, 128), F32)]
        *got, self.mark = pl.pallas_call(
            kernel,
            out_shape=[jax.ShapeDtypeStruct(*s) for s in shapes],
            in_specs=[pl.BlockSpec(memory_space=pltpu.VMEM)] * (count + len(marks)),
            out_specs=[pl.BlockSpec(memory_space=pltpu.VMEM)] * len(shapes),
            compiler_params=pltpu.CompilerParams(vmem_limit_bytes=24 * 1024 * 1024),
            cost_estimate=pl.CostEstimate(flops=1, bytes_accessed=1, transcendentals=0),
        )(*ins, *marks)
        return got[0] if single else got


def is_odd():
    return lax.rem(lax.axis_index("section"), 2) == 1


def project(x, low, high, both, hid_a, hid_b):
    rows, half = low.shape[0] // 2, low.shape[1]
    total = jnp.zeros(both.shape, F32)
    for at in range(0, half, 1024):
        cut = slice(at, at + 1024)
        total += dot(low[:, cut], x[:, cut], NT)
        total += dot(high[:, cut], x[:, half + at : half + at + 1024], NT)
    both[...] = total
    up = pltpu.roll(total, rows, 0)
    hidden = total * jax.nn.sigmoid(total) * up
    first = lax.broadcasted_iota(jnp.int32, total.shape, 0) < rows
    hidden = jnp.where(first, hidden, 0.0)
    hid_a[...] = hidden.astype(BF)
    hid_b[...] = pltpu.roll(hidden, rows, 0).astype(BF)


def derive(g, down, both, pair):
    rows, half = down.shape[0] // 2, down.shape[1]
    low = jnp.zeros(both.shape, F32)
    high = jnp.zeros(both.shape, F32)
    for at in range(0, half, 1024):
        cut = slice(at, at + 1024)
        low += dot(down[:, cut], g[:, cut], NT)
        high += dot(down[:, cut], g[:, half + at : half + at + 1024], NT)
    dhid = low + pltpu.roll(high, rows, 0)
    gate = both[...]
    up = pltpu.roll(gate, rows, 0)
    sig = jax.nn.sigmoid(gate)
    dgate = dhid * up * sig * (1.0 + gate * (1.0 - sig))
    dup = pltpu.roll(dhid * (gate * sig), rows, 0)
    first = lax.broadcasted_iota(jnp.int32, gate.shape, 0) < rows
    pair[...] = jnp.where(first, dgate, dup).astype(BF)


def down_columns(g, hid_a, hid_b, at, half):
    cut = slice(at, at + TILE)
    return dot(hid_a[...], g[:, cut], NN) + dot(hid_b[...], g[:, half + at : half + at + TILE], NN)


def own_grads(x, g, hid_a, hid_b, pair, low, high, down):
    half = low.shape[1]
    for at in range(0, half, TILE):
        cut = slice(at, at + TILE)
        low[:, cut] = dot(pair[...], x[:, cut], NN)
        high[:, cut] = dot(pair[...], x[:, half + at : half + at + TILE], NN)
        down[:, cut] = down_columns(g, hid_a, hid_b, at, half)


def sent_down(g, hid_a, hid_b, out):
    half = out.shape[1]
    for at in range(0, half, TILE):
        out[:, at : at + TILE] = down_columns(g, hid_a, hid_b, at, half).astype(BF)


def sent_pair(x, pair, low, high):
    half = low.shape[1]
    for at in range(0, half, TILE):
        cut = slice(at, at + TILE)
        low[:, cut] = dot(pair[...], x[:, cut], NN).astype(BF)
        high[:, cut] = dot(pair[...], x[:, half + at : half + at + TILE], NN).astype(BF)


def kept(side, odd, four, wanted):
    value = side.astype(F32)
    return jnp.where(odd == wanted, value, 0.0) if four else value


def either(bit, run):
    for value in range(2):
        pl.when(bit == value)(lambda value=value: run(value))


def picked(here, piece, out):
    @pl.when(is_odd())
    def _():
        out[...] = here[...]

    @pl.when(jnp.logical_not(is_odd()))
    def _():
        out[...] = piece[...]


def output_sums(count, tokens_half, *refs):
    hids, downs, outs = refs[:6], refs[6:9], refs[9:]
    half = downs[0].shape[1]
    width = 2 * half // count
    mine = lax.rem(lax.axis_index("tensor"), 2)
    tile = min(width, TILE)
    def run(mine):
        for pair in range(count // 2):
            which = 0 if 4 * pair < count else 1
            local = 2 * pair - which * (count // 2)
            for kind in range(2):
                base = (local + (mine if kind else 1 - mine)) * width
                for at in range(0, width, tile):
                    cols = slice(base + at, base + at + tile)
                    total = sum(dot(hids[2 * b + which][...], downs[b][:, cols], TN) for b in range(3))
                    here = slice(pair * width + at, pair * width + at + tile)
                    for part in range(2):
                        rows = slice(part * tokens_half, (part + 1) * tokens_half)
                        out = outs[2 * part + kind]
                        out[:, here] = total[rows].astype(out.dtype)

    either(mine, run)


def halved(bit, width, keep, got, send, left):
    mine = lax.rem(lax.div(lax.axis_index("tensor"), bit), 2)
    tile = min(width, TILE)

    def run(mine):
        for block in range(left.shape[1] // width):
            for kind, out in enumerate((send, left)):
                base = (2 * block + (mine if kind else 1 - mine)) * width
                for at in range(0, width, tile):
                    cols = slice(base + at, base + at + tile)
                    here = slice(block * width + at, block * width + at + tile)
                    out[:, here] = (keep[:, cols] + got[:, cols].astype(F32)).astype(out.dtype)

    either(mine, run)


def final_output(keep_a, got_a, keep_b, got_b, out):
    part = keep_a.shape[0]
    out[:part, :] = (keep_a[...] + got_a[...].astype(F32)).astype(BF)
    out[part:, :] = (keep_b[...] + got_b[...].astype(F32)).astype(BF)


def exchanged(value, axis, bit):
    count = lax.axis_size(axis)
    return lax.ppermute(value, axis, [(source, source ^ bit) for source in range(count)])


def ring_passed(value, steps):
    count = lax.axis_size("section")
    return lax.ppermute(value, "section", [(source, (source + steps) % count) for source in range(count)])


def packed_weights(gate, up, down):
    half = gate.shape[1] // 2
    low = jnp.concatenate([gate[:, :half], up[:, :half]], 0)
    low, gate, up = lax.optimization_barrier((low, gate, up))
    high = jnp.concatenate([gate[:, half:], up[:, half:]], 0)
    high, down = lax.optimization_barrier((high, down))
    return low, high, jnp.concatenate([down[:, :half], down[:, half:]], 0)


def on_device(x, g, gate_weight, up_weight, down_weight):
    rows, wide = gate_weight.shape
    half, both_rows, tokens = wide // 2, 2 * rows, x.shape[0]
    count = lax.axis_size("tensor")
    four = lax.axis_size("section") == 4
    piece = ((both_rows, half), BF)
    step = Steps()
    small, small_bf = ((both_rows, tokens), F32), ((both_rows, tokens), BF)

    def one_hop(value):
        return exchanged(value, "section", 2) if four else ring_passed(value, 1)

    def relay(here, value):
        if not four:
            return ring_passed(here, 1)
        return exchanged(step(picked, piece, [here, value]), "section", 1)

    own = packed_weights(gate_weight, up_weight, down_weight)
    first = [one_hop(value) for value in own]
    second = [None] * 3
    both_own, *hid_own = step(project, [small, small_bf, small_bf], [x, own[0], own[1]])
    pair_own = step(derive, small_bf, [g, own[2], both_own])
    grads_f32 = [((both_rows, half), F32)] * 3
    own_low, own_high, own_down = step(own_grads, grads_f32, [x, g, *hid_own, pair_own])
    second[0] = relay(first[0], own[0])
    second[1] = relay(first[1], own[1])
    both_first, *hid_first = step(project, [small, small_bf, small_bf], [x, first[0], first[1]])
    second[2] = relay(first[2], own[2])
    pair_first = step(derive, small_bf, [g, first[2], both_first], also=[second[0]])
    both_second, *hid_second = step(project, [small, small_bf, small_bf], [x, second[0], second[1]])

    def outward(value):
        return exchanged(value, "section", 1) if four else ring_passed(value, -1)

    def backward(value):
        return exchanged(value, "section", 2) if four else ring_passed(value, -1)

    far = hid_second if four else hid_first
    tail = step(sent_down, piece, [g, *far])
    side_down = outward(tail)

    part = tokens // 2
    if count & (count - 1) == 0 and count > 1:
        shapes = [((part, wide // 2), BF), ((part, wide // 2), F32)] * 2
        hids = [*hid_own, *hid_first, *hid_second]

        def sums(*refs):
            output_sums(count, part, *refs)

        send_a, keep_a, send_b, keep_b = step(sums, shapes, [*hids, own[2], first[2], second[2]])
        got_a, got_b = exchanged(send_a, "tensor", 1), exchanged(send_b, "tensor", 1)
    pair_second = step(derive, small_bf, [g, second[2], both_second])
    far = pair_second if four else pair_first
    near = pair_first if four else pair_second
    near_hid = hid_first if four else hid_second
    low, high = step(sent_pair, [piece, piece], [x, far])
    side_low, side_high = outward(low), outward(high)

    width = wide // count

    def next_half(keep, got, bit):
        cols = keep.shape[1] // 2

        def body(*refs):
            halved(bit, width, *refs)

        send, keep = step(body, [((part, cols), BF), ((part, cols), F32)], [keep, got])
        return exchanged(send, "tensor", bit), keep

    def back_down(gr, a, b, side, out):
        odd = is_odd()
        for at in range(0, half, TILE):
            value = down_columns(gr, a, b, at, half) + kept(side[:, at : at + TILE], odd, four, True)
            out[:, at : at + TILE] = value.astype(BF)

    def back_pair(offset):
        def body(xr, pair, side, out):
            odd = is_odd()
            for at in range(0, half, TILE):
                value = dot(pair[...], xr[:, offset + at : offset + at + TILE], NN)
                value += kept(side[:, at : at + TILE], odd, four, True)
                out[:, at : at + TILE] = value.astype(BF)

        return body

    got_a, keep_a = next_half(keep_a, got_a, 2)
    got_b, keep_b = next_half(keep_b, got_b, 2)
    last = step(back_down, piece, [g, *near_hid, side_down])
    back_of_down = backward(last)
    bit = 4
    got_a, keep_a = next_half(keep_a, got_a, bit)
    last = step(back_pair(0), piece, [x, near, side_low])
    back_of_low = backward(last)
    got_b, keep_b = next_half(keep_b, got_b, bit)
    last = step(back_pair(half), piece, [x, near, side_high], also=[got_a])
    back_of_high = backward(last)
    bit *= 2
    while bit < count:
        got_a, keep_a = next_half(keep_a, got_a, bit)
        got_b, keep_b = next_half(keep_b, got_b, bit)
        bit *= 2

    def finished(own_ref, back, side, odd, cut):
        value = own_ref[:, cut] + back[:, cut].astype(F32)
        return value + kept(side[:, cut], odd, four, False) if four else value

    def final_down(own_ref, back, side, out):
        odd = is_odd()
        for at in range(0, half, TILE):
            cut = slice(at, at + TILE)
            value = finished(own_ref, back, side, odd, cut)
            out[:, cut] = value[:rows]
            out[:, half + at : half + at + TILE] = value[rows:]

    def final_pair(low_ref, high_ref, low_back, high_back, low_side, high_side, out_gate, out_up):
        odd = is_odd()
        for offset, refs in ((0, (low_ref, low_back, low_side)), (half, (high_ref, high_back, high_side))):
            for at in range(0, half, TILE):
                value = finished(*refs, odd, slice(at, at + TILE))
                out_gate[:, offset + at : offset + at + TILE] = value[:rows]
                out_up[:, offset + at : offset + at + TILE] = value[rows:]

    whole = ((rows, wide), F32)
    grad_down = step(final_down, whole, [own_down, back_of_down, side_down])
    output = step(final_output, ((tokens, width), BF), [keep_a, got_a, keep_b, got_b])
    grad_gate, grad_up = step(
        final_pair, [whole, whole], [own_low, own_high, back_of_low, back_of_high, side_low, side_high]
    )
    return (output, grad_gate, grad_up, grad_down)


def solution(mesh):
    placed = (
        P("section", None),
        P("section", None),
        P(("section", "tensor"), None),
        P(("section", "tensor"), None),
        P(("section", "tensor"), None),
    )
    return jax.shard_map(
        on_device,
        mesh=mesh,
        in_specs=placed,
        out_specs=(
            P("section", "tensor"),
            P(("section", "tensor"), None),
            P(("section", "tensor"), None),
            P(("section", "tensor"), None),
        ),
        check_vma=False,
    )
```

time: 182 us -> 83.6 us (0.46)
  waiting for transfers between devices: 125 us -> 42.3 us
  matrix products: 16.5 us -> 0 us
  between operations: 14.1 us -> 0.87 us
  Pallas kernels: 0 us -> 12.9 us
  other arithmetic: 4.66 us -> 0.2 us
  starting transfers between devices: 21.3 us -> 25 us
  local copies, waits for them, and re-layouts: 0.12 us -> 2.16 us
    ppermute x12 -> x18, waiting for transfers between devices: 125 us -> 42.3 us  [exchanged(): lax.ppermute(value, axis, [(source, source ^ bit) for source in range(cou...]
    dot_general x21 -> x0, matrix products: 16.5 us -> none  [the longest x3 4.18 us: forward_block(): jnp.dot(hidden, down_rows, preferred_element_type=jnp.float32)]
    pallas_call x0 -> x23, Pallas kernels: none -> 12.9 us  [__call__(): pl.pallas_call(kernel, out_shape=[jax.ShapeDtypeStruct(*s) for s in shape...]
    ppermute x12 -> x18, starting transfers between devices: 21.2 us -> 25 us  [exchanged(): lax.ppermute(value, axis, [(source, source ^ bit) for source in range(cou...]
    add x3 -> x0, other arithmetic: 2.88 us -> none  [add_terms(): return (earlier[0] + later[0], earlier[1] + later[1], earlier[2] + later[2])]
    slice x0 -> x7, local copies, waits for them, and re-layouts: none -> 2.14 us  [the longest x2 2.1 us: packed_weights(): low = jnp.concatenate([gate[:, :half], up[:, :half]], 0)]
  transfers between devices with their start and end apart: 13 -> 18, of which waited for: 12 -> 11; matrix products, arithmetic and copies ran while one was open for 9% -> 0% of each run, Pallas kernels for 0% -> 12%
where the time goes in v2:
time: 83.6 us; the launch traced here: 83.5 us
  waiting for transfers between devices  42.3 us (51%)
  starting transfers between devices  25 us (30%)
  Pallas kernels  12.9 us (15%)
  local copies, waits for them, and re-layouts  2.16 us (3%)
  between operations  0.87 us (1%)
    ppermute x18, waiting for transfers between devices, exchanged(): lax.ppermute(value, axis, [(source, source ^ bit) for source in range(cou...  42.3 us
    ppermute x18, starting transfers between devices, exchanged(): lax.ppermute(value, axis, [(source, source ^ bit) for source in range(cou...  25 us
    pallas_call x23, Pallas kernels, __call__(): pl.pallas_call(kernel, out_shape=[jax.ShapeDtypeStruct(*s) for s in shape...  12.9 us
    slice x2, local copies, waits for them, and re-layouts, packed_weights(): low = jnp.concatenate([gate[:, :half], up[:, :half]], 0)  2.1 us
  transfers between devices with their start and end apart: 18, of which 11 were waited for; matrix products, arithmetic and copies ran while one was open for 0% of the time, Pallas kernels for 12%

profile of v2, /device:TPU:0, one launch (start us, length us, event | category | flops | bytes accessed | tf_op | source)
XLA Modules:
  0.0 83.5 jit_solution(927397356810566967)
XLA Ops:
  0.7 1.0 %slice.18 = bf16[20,4096]{1,0:T(8,128)(2,1)S(1)} slice(bf16[20,8192]{1,0:T(8,128)(2,1)} %param.7), slice={[0:20], [0:4096]} | slice | bytes 327680 | tf_op jit(solution)/shard_map/slice | solution.py:189
  1.7 1.1 %slice.19 = bf16[20,4096]{1,0:T(8,128)(2,1)S(1)} slice(bf16[20,8192]{1,0:T(8,128)(2,1)} %param.8), slice={[0:20], [0:4096]} | slice | bytes 327680 | tf_op jit(solution)/shard_map/slice | solution.py:189
  3.0 3.0 %collective-permute-start.1 = (bf16[40,4096]{1,0:T(8,128)(2,1)S(1)}, bf16[40,4096]{1,0:T(8,128)(2,1)S(1)}, u32[]{:S(2)}, u32[]{:S(2)}) collective-permute-start(bf16[40,4096]{1,0:T(8,128)(2,1)S(1)} %pad_maximum_fusion.1.refs_2_.refs_1_), channel_id=1, source_target_pairs={{0,16},{8,24},{16,0},{24,8},{1,17},{9,25},{17,1},{25,9},{2,18},{10... | collective-permute-start | bytes 983048 | tf_op jit(solution)/shard_map/ppermute | solution.py:179
  6.2 2.0 %collective-permute-start.4 = (bf16[40,4096]{1,0:T(8,128)(2,1)S(1)}, bf16[40,4096]{1,0:T(8,128)(2,1)S(1)}, u32[]{:S(2)}, u32[]{:S(2)}) collective-permute-start(bf16[40,4096]{1,0:T(8,128)(2,1)S(1)} %pad_maximum_fusion.2.refs_1_.refs_6_), channel_id=1, source_target_pairs={{0,16},{8,24},{16,0},{24,8},{1,17},{9,25},{17,1},{25,9},{2,18},{10... | collective-permute-start | bytes 983048 | tf_op jit(solution)/shard_map/ppermute | solution.py:179
  8.2 0.8 shard_map.84
  9.0 0.8 %shard_map.85 = (bf16[40,128]{1,0:T(8,128)(2,1)S(1)}, f32[8,128]{1,0:T(8,128)S(1)}) custom-call(bf16[128,8192]{1,0:T(8,128)(2,1)S(1)} %copy-done.1, bf16[40,4096]{1,0:T(8,128)(2,1)S(1)} %pad_maximum_fusion.2.refs_1_.refs_6_, f32[40,128]{1,0:T(8,128)S(1)} %get-tuple-element.78.refs_2_, f32[8,128]{1,0:T(8,128)S(1)} %get-tuple-element.79.refs_3_), custom_call_target="tpu_custom_call" | custom-call | flops 1 | bytes 1 | tf_op jit(solution)/shard_map/pallas_call | solution.py:34
  10.6 11.0 %collective-permute-done.refs_0_.refs_1_ = bf16[40,4096]{1,0:T(8,128)(2,1)S(1)} collective-permute-done((bf16[40,4096]{1,0:T(8,128)(2,1)S(1)}, bf16[40,4096]{1,0:T(8,128)(2,1)S(1)}, u32[]{:S(2)}, u32[]{:S(2)}) %collective-permute-start) | collective-permute-done | bytes 327712 | tf_op jit(solution)/shard_map/ppermute | solution.py:179
  21.6 2.1 %collective-permute-start.2 = (bf16[40,4096]{1,0:T(8,128)(2,1)S(1)}, bf16[40,4096]{1,0:T(8,128)(2,1)S(1)}, u32[]{:S(2)}, u32[]{:S(2)}) collective-permute-start(bf16[40,4096]{1,0:T(8,128)(2,1)S(1)} %get-tuple-element.87), channel_id=1, source_target_pairs={{0,8},{8,0},{16,24},{24,16},{1,9},{9,1},{17,25},{25,17},{2,10},{10... | collective-permute-start | bytes 983048 | tf_op jit(solution)/shard_map/ppermute | solution.py:179
  24.7 3.1 %collective-permute-done.4.refs_0_.refs_1_.refs_7_ = bf16[40,4096]{1,0:T(8,128)(2,1)S(1)} collective-permute-done((bf16[40,4096]{1,0:T(8,128)(2,1)S(1)}, bf16[40,4096]{1,0:T(8,128)(2,1)S(1)}, u32[]{:S(2)}, u32[]{:S(2)}) %collective-permute-start.4) | collective-permute-done | bytes 327712 | tf_op jit(solution)/shard_map/ppermute | solution.py:179
  27.8 1.8 %collective-permute-start.5 = (bf16[40,4096]{1,0:T(8,128)(2,1)S(1)}, bf16[40,4096]{1,0:T(8,128)(2,1)S(1)}, u32[]{:S(2)}, u32[]{:S(2)}) collective-permute-start(bf16[40,4096]{1,0:T(8,128)(2,1)S(1)} %get-tuple-element.95), channel_id=1, source_target_pairs={{0,8},{8,0},{16,24},{24,16},{1,9},{9,1},{17,25},{25,17},{2,10},{10... | collective-permute-start | bytes 983048 | tf_op jit(solution)/shard_map/ppermute | solution.py:179
  29.6 2.8 %collective-permute-done.2.refs_3_.refs_1_ = bf16[40,4096]{1,0:T(8,128)(2,1)S(1)} collective-permute-done((bf16[40,4096]{1,0:T(8,128)(2,1)S(1)}, bf16[40,4096]{1,0:T(8,128)(2,1)S(1)}, u32[]{:S(2)}, u32[]{:S(2)}) %collective-permute-start.2) | collective-permute-done | bytes 327712 | tf_op jit(solution)/shard_map/ppermute | solution.py:179
  32.3 0.8 %shard_map.91 = (bf16[40,128]{1,0:T(8,128)(2,1)S(1)}, f32[8,128]{1,0:T(8,128)S(1)}) custom-call(bf16[128,8192]{1,0:T(8,128)(2,1)S(1)} %copy-done.1, bf16[40,4096]{1,0:T(8,128)(2,1)S(1)} %collective-permute-done.4.refs_0_.refs_1_.refs_7_, f32[40,128]{1,0:T(8,128)S(1)} %get-tuple-element.89.refs_2_, ...), custom_call_target="tpu_custom_call" | custom-call | flops 1 | bytes 1 | tf_op jit(solution)/shard_map/pallas_call | solution.py:34
  33.2 6.2 %collective-permute-done.3.refs_2_ = bf16[40,4096]{1,0:T(8,128)(2,1)S(1)} collective-permute-done((bf16[40,4096]{1,0:T(8,128)(2,1)S(1)}, bf16[40,4096]{1,0:T(8,128)(2,1)S(1)}, u32[]{:S(2)}, u32[]{:S(2)}) %collective-permute-start.3) | collective-permute-done | bytes 327712 | tf_op jit(solution)/shard_map/ppermute | solution.py:179
  40.6 3.2 %collective-permute-done.5.refs_8_.refs_1_ = bf16[40,4096]{1,0:T(8,128)(2,1)S(1)} collective-permute-done((bf16[40,4096]{1,0:T(8,128)(2,1)S(1)}, bf16[40,4096]{1,0:T(8,128)(2,1)S(1)}, u32[]{:S(2)}, u32[]{:S(2)}) %collective-permute-start.5) | collective-permute-done | bytes 327712 | tf_op jit(solution)/shard_map/ppermute | solution.py:179
  43.8 1.8 %shard_map.94 = (bf16[64,4096]{1,0:T(8,128)(2,1)S(1)}, f32[64,4096]{1,0:T(8,128)S(1)}, bf16[64,4096]{1,0:T(8,128)(2,1)S(1)}, f32[64,4096]{1,0:T(8,128)S(1)}, f32[8,128]{1,0:T(8,128)S(1)}) custom-call(bf16[40,128]{1,0:T(8,128)(2,1)S(1)} %get-tuple-element.75.refs_2_.refs_0_, bf16[40,128]{1,0:T(8,128)(2,1)S(1)} %get-tuple-element.76.refs_3_.refs_1_, ...), custom_call_target="tpu_custom_call" | custom-call | flops 1 | bytes 1 | tf_op jit(solution)/shard_map/pallas_call | solution.py:34
  46.2 1.4 %collective-permute-start.8 = (bf16[40,4096]{1,0:T(8,128)(2,1)S(1)}, bf16[40,4096]{1,0:T(8,128)(2,1)S(1)}, u32[]{:S(2)}, u32[]{:S(2)}) collective-permute-start(bf16[40,4096]{1,0:T(8,128)(2,1)S(1)} %get-tuple-element.107), channel_id=1, source_target_pairs={{0,8},{8,0},{16,24},{24,16},{1,9},{9,1},{17,25},{25,17},{2,10},{10... | collective-permute-start | bytes 983048 | tf_op jit(solution)/shard_map/ppermute | solution.py:179
  47.6 0.8 %shard_map.95 = (bf16[40,128]{1,0:T(8,128)(2,1)S(1)}, f32[8,128]{1,0:T(8,128)S(1)}) custom-call(bf16[128,8192]{1,0:T(8,128)(2,1)S(1)} %copy-done.1, bf16[40,4096]{1,0:T(8,128)(2,1)S(1)} %collective-permute-done.5.refs_8_.refs_1_, f32[40,128]{1,0:T(8,128)S(1)} %get-tuple-element.100.refs_2_, f32[8,128]{1,0:T(8,128)S(1)} %get-tuple-element.101.refs_3_), custom_call_target="tpu_custom_call" | custom-call | flops 1 | bytes 1 | tf_op jit(solution)/shard_map/pallas_call | solution.py:34
  49.0 1.6 %collective-permute-start.7 = (bf16[64,2048]{1,0:T(8,128)(2,1)S(1)}, bf16[64,2048]{1,0:T(8,128)(2,1)S(1)}, u32[]{:S(2)}, u32[]{:S(2)}) collective-permute-start(bf16[64,2048]{1,0:T(8,128)(2,1)S(1)} %get-tuple-element.106), channel_id=1, source_target_pairs={{0,2},{1,3},{2,0},{3,1},{4,6},{5,7},{6,4},{7,5},{8,10},{9,11},{10,... | collective-permute-start | bytes 786440 | tf_op jit(solution)/shard_map/ppermute | solution.py:179
  51.2 1.5 %collective-permute-start.15 = (bf16[40,4096]{1,0:T(8,128)(2,1)S(1)}, bf16[40,4096]{1,0:T(8,128)(2,1)S(1)}, u32[]{:S(2)}, u32[]{:S(2)}) collective-permute-start(bf16[40,4096]{1,0:T(8,128)(2,1)S(1)} %get-tuple-element.125), channel_id=1, source_target_pairs={{0,8},{8,0},{16,24},{24,16},{1,9},{9,1},{17,25},{25,17},{2,10},{10... | collective-permute-start | bytes 983048 | tf_op jit(solution)/shard_map/ppermute | solution.py:179
  53.3 3.4 %collective-permute-done.8.refs_3_.refs_2_ = bf16[40,4096]{1,0:T(8,128)(2,1)S(1)} collective-permute-done((bf16[40,4096]{1,0:T(8,128)(2,1)S(1)}, bf16[40,4096]{1,0:T(8,128)(2,1)S(1)}, u32[]{:S(2)}, u32[]{:S(2)}) %collective-permute-start.8) | collective-permute-done | bytes 327712 | tf_op jit(solution)/shard_map/ppermute | solution.py:179
  57.2 1.1 %collective-permute-done.7.refs_1_ = bf16[64,2048]{1,0:T(8,128)(2,1)S(1)} collective-permute-done((bf16[64,2048]{1,0:T(8,128)(2,1)S(1)}, bf16[64,2048]{1,0:T(8,128)(2,1)S(1)}, u32[]{:S(2)}, u32[]{:S(2)}) %collective-permute-start.7) | collective-permute-done | bytes 262176 | tf_op jit(solution)/shard_map/ppermute | solution.py:179
  58.3 2.6 %collective-permute-start.10 = (bf16[64,1024]{1,0:T(8,128)(2,1)S(1)}, bf16[64,1024]{1,0:T(8,128)(2,1)S(1)}, u32[]{:S(2)}, u32[]{:S(2)}) collective-permute-start(bf16[64,1024]{1,0:T(8,128)(2,1)S(1)} %get-tuple-element.114), channel_id=1, source_target_pairs={{0,4},{1,5},{2,6},{3,7},{4,0},{5,1},{6,2},{7,3},{8,12},{9,13},{10,... | collective-permute-start | bytes 393224 | tf_op jit(solution)/shard_map/ppermute | solution.py:179
  61.0 1.5 %collective-permute-start.14 = (bf16[40,4096]{1,0:T(8,128)(2,1)S(1)}, bf16[40,4096]{1,0:T(8,128)(2,1)S(1)}, u32[]{:S(2)}, u32[]{:S(2)}) collective-permute-start(bf16[40,4096]{1,0:T(8,128)(2,1)S(1)} %get-tuple-element.124), channel_id=1, source_target_pairs={{0,16},{8,24},{16,0},{24,8},{1,17},{9,25},{17,1},{25,9},{2,18},{10... | collective-permute-start | bytes 983048 | tf_op jit(solution)/shard_map/ppermute | solution.py:179
  62.5 1.3 %collective-permute-done.12.refs_2_.refs_4_ = bf16[40,4096]{1,0:T(8,128)(2,1)S(1)} collective-permute-done((bf16[40,4096]{1,0:T(8,128)(2,1)S(1)}, bf16[40,4096]{1,0:T(8,128)(2,1)S(1)}, u32[]{:S(2)}, u32[]{:S(2)}) %collective-permute-start.12) | collective-permute-done | bytes 327712 | tf_op jit(solution)/shard_map/ppermute | solution.py:179
  64.1 1.5 %collective-permute-start.16 = (bf16[40,4096]{1,0:T(8,128)(2,1)S(1)}, bf16[40,4096]{1,0:T(8,128)(2,1)S(1)}, u32[]{:S(2)}, u32[]{:S(2)}) collective-permute-start(bf16[40,4096]{1,0:T(8,128)(2,1)S(1)} %get-tuple-element.132), channel_id=1, source_target_pairs={{0,16},{8,24},{16,0},{24,8},{1,17},{9,25},{17,1},{25,9},{2,18},{10... | collective-permute-start | bytes 983048 | tf_op jit(solution)/shard_map/ppermute | solution.py:179
  65.6 4.3 %collective-permute-done.15.refs_2_.refs_5_ = bf16[40,4096]{1,0:T(8,128)(2,1)S(1)} collective-permute-done((bf16[40,4096]{1,0:T(8,128)(2,1)S(1)}, bf16[40,4096]{1,0:T(8,128)(2,1)S(1)}, u32[]{:S(2)}, u32[]{:S(2)}) %collective-permute-start.15) | collective-permute-done | bytes 327712 | tf_op jit(solution)/shard_map/ppermute | solution.py:179
  70.2 1.5 %collective-permute-start.17 = (bf16[40,4096]{1,0:T(8,128)(2,1)S(1)}, bf16[40,4096]{1,0:T(8,128)(2,1)S(1)}, u32[]{:S(2)}, u32[]{:S(2)}) collective-permute-start(bf16[40,4096]{1,0:T(8,128)(2,1)S(1)} %get-tuple-element.133), channel_id=1, source_target_pairs={{0,16},{8,24},{16,0},{24,8},{1,17},{9,25},{17,1},{25,9},{2,18},{10... | collective-permute-start | bytes 983048 | tf_op jit(solution)/shard_map/ppermute | solution.py:179
  71.7 2.6 %collective-permute-start.13 = (bf16[64,1024]{1,0:T(8,128)(2,1)S(1)}, bf16[64,1024]{1,0:T(8,128)(2,1)S(1)}, u32[]{:S(2)}, u32[]{:S(2)}) collective-permute-start(bf16[64,1024]{1,0:T(8,128)(2,1)S(1)} %get-tuple-element.122), channel_id=1, source_target_pairs={{0,4},{1,5},{2,6},{3,7},{4,0},{5,1},{6,2},{7,3},{8,12},{9,13},{10,... | collective-permute-start | bytes 393224 | tf_op jit(solution)/shard_map/ppermute | solution.py:179
  74.3 1.0 %shard_map.104 = (f32[20,8192]{1,0:T(8,128)}, f32[8,128]{1,0:T(8,128)S(1)}) custom-call(f32[40,4096]{1,0:T(8,128)S(1)} %get-tuple-element.123.refs_0_, bf16[40,4096]{1,0:T(8,128)(2,1)S(1)} %collective-permute-done.14.refs_1_, bf16[40,4096]{1,0:T(8,128)(2,1)S(1)} %collective-permute-done.8.refs_3_.refs_2_, f32[8,128]{1,0:T(8,128)S(1)} %get-tuple-element.127.refs_3_), custom_call_target="tpu_custom_call" | custom-call | flops 1 | bytes 1 | tf_op jit(solution)/shard_map/pallas_call | solution.py:34
  75.3 4.4 %collective-permute-done.13.refs_3_ = bf16[64,1024]{1,0:T(8,128)(2,1)S(1)} collective-permute-done((bf16[64,1024]{1,0:T(8,128)(2,1)S(1)}, bf16[64,1024]{1,0:T(8,128)(2,1)S(1)}, u32[]{:S(2)}, u32[]{:S(2)}) %collective-permute-start.13) | collective-permute-done | bytes 131104 | tf_op jit(solution)/shard_map/ppermute | solution.py:179
  80.5 1.6 %collective-permute-done.17.refs_3_ = bf16[40,4096]{1,0:T(8,128)(2,1)S(1)} collective-permute-done((bf16[40,4096]{1,0:T(8,128)(2,1)S(1)}, bf16[40,4096]{1,0:T(8,128)(2,1)S(1)}, u32[]{:S(2)}, u32[]{:S(2)}) %collective-permute-start.17) | collective-permute-done | bytes 327712 | tf_op jit(solution)/shard_map/ppermute | solution.py:179
  82.1 1.4 %shard_map.106 = (f32[20,8192]{1,0:T(8,128)}, f32[20,8192]{1,0:T(8,128)}, f32[8,128]{1,0:T(8,128)}) custom-call(f32[40,4096]{1,0:T(8,128)S(1)} %get-tuple-element.130.refs_0_, f32[40,4096]{1,0:T(8,128)S(1)} %get-tuple-element.131.refs_1_, bf16[40,4096]{1,0:T(8,128)(2,1)S(1)} %collective-permute-done.16.refs_2_, ...), custom_call_target="tpu_custom_call" | custom-call | flops 1 | bytes 1 | tf_op jit(solution)/shard_map/pallas_call | solution.py:34
  (43 shorter events, 7.4 us)
Async XLA Ops:
  0.6 2.2 %slice-start = ((bf16[20,8192]{1,0:T(8,128)(2,1)}), bf16[20,4096]{1,0:T(8,128)(2,1)S(1)}, s32[]{:S(2)}) async-start(bf16[20,8192]{1,0:T(8,128)(2,1)} %param.7), calls=%async_computation | async-start | bytes 393216 | tf_op jit(solution)/shard_map/slice | solution.py:191
  0.6 2.2 %slice-start.1 = ((bf16[20,8192]{1,0:T(8,128)(2,1)}), bf16[20,4096]{1,0:T(8,128)(2,1)S(1)}, s32[]{:S(2)}) async-start(bf16[20,8192]{1,0:T(8,128)(2,1)} %param.8), calls=%async_computation.1 | async-start | bytes 393216 | tf_op jit(solution)/shard_map/slice | solution.py:191
  0.7 5.4 %copy-start.2 = (bf16[20,8192]{1,0:T(8,128)(2,1)S(1)}, bf16[20,8192]{1,0:T(8,128)(2,1)}, u32[]{:S(2)}) copy-start(bf16[20,8192]{1,0:T(8,128)(2,1)} %param.9) | copy-start | bytes 983044
  1.7 6.5 %copy-start = (bf16[128,8192]{1,0:T(8,128)(2,1)S(1)}, bf16[128,8192]{1,0:T(8,128)(2,1)}, u32[]{:S(2)}) copy-start(bf16[128,8192]{1,0:T(8,128)(2,1)} %refs_0_.23) | copy-start | bytes 6291460
  3.0 6.1 %copy-start.1 = (bf16[128,8192]{1,0:T(8,128)(2,1)S(1)}, bf16[128,8192]{1,0:T(8,128)(2,1)}, u32[]{:S(2)}) copy-start(bf16[128,8192]{1,0:T(8,128)(2,1)} %refs_0_.21) | copy-start | bytes 6291460
  3.0 20.7 %collective-permute-start.1 = (bf16[40,4096]{1,0:T(8,128)(2,1)S(1)}, bf16[40,4096]{1,0:T(8,128)(2,1)S(1)}, u32[]{:S(2)}, u32[]{:S(2)}) collective-permute-start(bf16[40,4096]{1,0:T(8,128)(2,1)S(1)} %pad_maximum_fusion.1.refs_2_.refs_1_), channel_id=1, source_target_pairs={{0,16},{8,24},{16,0},{24,8},{1,17},{9,25},{17,1},{25,9},{2,18},{10... | collective-permute-start | bytes 983048 | tf_op jit(solution)/shard_map/ppermute | solution.py:179
  6.0 15.6 %collective-permute-start = (bf16[40,4096]{1,0:T(8,128)(2,1)S(1)}, bf16[40,4096]{1,0:T(8,128)(2,1)S(1)}, u32[]{:S(2)}, u32[]{:S(2)}) collective-permute-start(bf16[40,4096]{1,0:T(8,128)(2,1)S(1)} %pad_maximum_fusion.refs_1_), channel_id=1, source_target_pairs={{0,16},{8,24},{16,0},{24,8},{1,17},{9,25},{17,1},{25,9},{2,18},{10... | collective-permute-start | bytes 983048 | tf_op jit(solution)/shard_map/ppermute | solution.py:179
  6.2 21.6 %collective-permute-start.4 = (bf16[40,4096]{1,0:T(8,128)(2,1)S(1)}, bf16[40,4096]{1,0:T(8,128)(2,1)S(1)}, u32[]{:S(2)}, u32[]{:S(2)}) collective-permute-start(bf16[40,4096]{1,0:T(8,128)(2,1)S(1)} %pad_maximum_fusion.2.refs_1_.refs_6_), channel_id=1, source_target_pairs={{0,16},{8,24},{16,0},{24,8},{1,17},{9,25},{17,1},{25,9},{2,18},{10... | collective-permute-start | bytes 983048 | tf_op jit(solution)/shard_map/ppermute | solution.py:179
  21.6 10.7 %collective-permute-start.2 = (bf16[40,4096]{1,0:T(8,128)(2,1)S(1)}, bf16[40,4096]{1,0:T(8,128)(2,1)S(1)}, u32[]{:S(2)}, u32[]{:S(2)}) collective-permute-start(bf16[40,4096]{1,0:T(8,128)(2,1)S(1)} %get-tuple-element.87), channel_id=1, source_target_pairs={{0,8},{8,0},{16,24},{24,16},{1,9},{9,1},{17,25},{25,17},{2,10},{10... | collective-permute-start | bytes 983048 | tf_op jit(solution)/shard_map/ppermute | solution.py:179
  23.7 15.6 %collective-permute-start.3 = (bf16[40,4096]{1,0:T(8,128)(2,1)S(1)}, bf16[40,4096]{1,0:T(8,128)(2,1)S(1)}, u32[]{:S(2)}, u32[]{:S(2)}) collective-permute-start(bf16[40,4096]{1,0:T(8,128)(2,1)S(1)} %get-tuple-element.88), channel_id=1, source_target_pairs={{0,8},{8,0},{16,24},{24,16},{1,9},{9,1},{17,25},{25,17},{2,10},{10... | collective-permute-start | bytes 983048 | tf_op jit(solution)/shard_map/ppermute | solution.py:179
  27.8 16.0 %collective-permute-start.5 = (bf16[40,4096]{1,0:T(8,128)(2,1)S(1)}, bf16[40,4096]{1,0:T(8,128)(2,1)S(1)}, u32[]{:S(2)}, u32[]{:S(2)}) collective-permute-start(bf16[40,4096]{1,0:T(8,128)(2,1)S(1)} %get-tuple-element.95), channel_id=1, source_target_pairs={{0,8},{8,0},{16,24},{24,16},{1,9},{9,1},{17,25},{25,17},{2,10},{10... | collective-permute-start | bytes 983048 | tf_op jit(solution)/shard_map/ppermute | solution.py:179
  45.6 3.3 %collective-permute-start.6 = (bf16[64,4096]{1,0:T(8,128)(2,1)S(1)}, bf16[64,4096]{1,0:T(8,128)(2,1)S(1)}, u32[]{:S(2)}, u32[]{:S(2)}) collective-permute-start(bf16[64,4096]{1,0:T(8,128)(2,1)S(1)} %get-tuple-element.99), channel_id=1, source_target_pairs={{0,1},{1,0},{2,3},{3,2},{4,5},{5,4},{6,7},{7,6},{8,9},{9,8},{10,11... | collective-permute-start | bytes 1572872 | tf_op jit(solution)/shard_map/ppermute | solution.py:179
  45.7 7.0 %collective-permute-start.9 = (bf16[64,4096]{1,0:T(8,128)(2,1)S(1)}, bf16[64,4096]{1,0:T(8,128)(2,1)S(1)}, u32[]{:S(2)}, u32[]{:S(2)}) collective-permute-start(bf16[64,4096]{1,0:T(8,128)(2,1)S(1)} %get-tuple-element.109), channel_id=1, source_target_pairs={{0,1},{1,0},{2,3},{3,2},{4,5},{5,4},{6,7},{7,6},{8,9},{9,8},{10,11... | collective-permute-start | bytes 1572872 | tf_op jit(solution)/shard_map/ppermute | solution.py:179
  46.2 10.6 %collective-permute-start.8 = (bf16[40,4096]{1,0:T(8,128)(2,1)S(1)}, bf16[40,4096]{1,0:T(8,128)(2,1)S(1)}, u32[]{:S(2)}, u32[]{:S(2)}) collective-permute-start(bf16[40,4096]{1,0:T(8,128)(2,1)S(1)} %get-tuple-element.107), channel_id=1, source_target_pairs={{0,8},{8,0},{16,24},{24,16},{1,9},{9,1},{17,25},{25,17},{2,10},{10... | collective-permute-start | bytes 983048 | tf_op jit(solution)/shard_map/ppermute | solution.py:179
  49.0 9.3 %collective-permute-start.7 = (bf16[64,2048]{1,0:T(8,128)(2,1)S(1)}, bf16[64,2048]{1,0:T(8,128)(2,1)S(1)}, u32[]{:S(2)}, u32[]{:S(2)}) collective-permute-start(bf16[64,2048]{1,0:T(8,128)(2,1)S(1)} %get-tuple-element.106), channel_id=1, source_target_pairs={{0,2},{1,3},{2,0},{3,1},{4,6},{5,7},{6,4},{7,5},{8,10},{9,11},{10,... | collective-permute-start | bytes 786440 | tf_op jit(solution)/shard_map/ppermute | solution.py:179
  50.6 13.1 %collective-permute-start.12 = (bf16[40,4096]{1,0:T(8,128)(2,1)S(1)}, bf16[40,4096]{1,0:T(8,128)(2,1)S(1)}, u32[]{:S(2)}, u32[]{:S(2)}) collective-permute-start(bf16[40,4096]{1,0:T(8,128)(2,1)S(1)} %get-tuple-element.118), channel_id=1, source_target_pairs={{0,8},{8,0},{16,24},{24,16},{1,9},{9,1},{17,25},{25,17},{2,10},{10... | collective-permute-start | bytes 983048 | tf_op jit(solution)/shard_map/ppermute | solution.py:179
  51.2 18.8 %collective-permute-start.15 = (bf16[40,4096]{1,0:T(8,128)(2,1)S(1)}, bf16[40,4096]{1,0:T(8,128)(2,1)S(1)}, u32[]{:S(2)}, u32[]{:S(2)}) collective-permute-start(bf16[40,4096]{1,0:T(8,128)(2,1)S(1)} %get-tuple-element.125), channel_id=1, source_target_pairs={{0,8},{8,0},{16,24},{24,16},{1,9},{9,1},{17,25},{25,17},{2,10},{10... | collective-permute-start | bytes 983048 | tf_op jit(solution)/shard_map/ppermute | solution.py:179
  52.8 12.8 %collective-permute-start.11 = (bf16[64,2048]{1,0:T(8,128)(2,1)S(1)}, bf16[64,2048]{1,0:T(8,128)(2,1)S(1)}, u32[]{:S(2)}, u32[]{:S(2)}) collective-permute-start(bf16[64,2048]{1,0:T(8,128)(2,1)S(1)} %get-tuple-element.116), channel_id=1, source_target_pairs={{0,2},{1,3},{2,0},{3,1},{4,6},{5,7},{6,4},{7,5},{8,10},{9,11},{10,... | collective-permute-start | bytes 786440 | tf_op jit(solution)/shard_map/ppermute | solution.py:179
  58.3 11.6 %collective-permute-start.10 = (bf16[64,1024]{1,0:T(8,128)(2,1)S(1)}, bf16[64,1024]{1,0:T(8,128)(2,1)S(1)}, u32[]{:S(2)}, u32[]{:S(2)}) collective-permute-start(bf16[64,1024]{1,0:T(8,128)(2,1)S(1)} %get-tuple-element.114), channel_id=1, source_target_pairs={{0,4},{1,5},{2,6},{3,7},{4,0},{5,1},{6,2},{7,3},{8,12},{9,13},{10,... | collective-permute-start | bytes 393224 | tf_op jit(solution)/shard_map/ppermute | solution.py:179
  61.0 13.3 %collective-permute-start.14 = (bf16[40,4096]{1,0:T(8,128)(2,1)S(1)}, bf16[40,4096]{1,0:T(8,128)(2,1)S(1)}, u32[]{:S(2)}, u32[]{:S(2)}) collective-permute-start(bf16[40,4096]{1,0:T(8,128)(2,1)S(1)} %get-tuple-element.124), channel_id=1, source_target_pairs={{0,16},{8,24},{16,0},{24,8},{1,17},{9,25},{17,1},{25,9},{2,18},{10... | collective-permute-start | bytes 983048 | tf_op jit(solution)/shard_map/ppermute | solution.py:179
  64.1 16.5 %collective-permute-start.16 = (bf16[40,4096]{1,0:T(8,128)(2,1)S(1)}, bf16[40,4096]{1,0:T(8,128)(2,1)S(1)}, u32[]{:S(2)}, u32[]{:S(2)}) collective-permute-start(bf16[40,4096]{1,0:T(8,128)(2,1)S(1)} %get-tuple-element.132), channel_id=1, source_target_pairs={{0,16},{8,24},{16,0},{24,8},{1,17},{9,25},{17,1},{25,9},{2,18},{10... | collective-permute-start | bytes 983048 | tf_op jit(solution)/shard_map/ppermute | solution.py:179
  70.2 11.9 %collective-permute-start.17 = (bf16[40,4096]{1,0:T(8,128)(2,1)S(1)}, bf16[40,4096]{1,0:T(8,128)(2,1)S(1)}, u32[]{:S(2)}, u32[]{:S(2)}) collective-permute-start(bf16[40,4096]{1,0:T(8,128)(2,1)S(1)} %get-tuple-element.133), channel_id=1, source_target_pairs={{0,16},{8,24},{16,0},{24,8},{1,17},{9,25},{17,1},{25,9},{2,18},{10... | collective-permute-start | bytes 983048 | tf_op jit(solution)/shard_map/ppermute | solution.py:179
  71.7 8.1 %collective-permute-start.13 = (bf16[64,1024]{1,0:T(8,128)(2,1)S(1)}, bf16[64,1024]{1,0:T(8,128)(2,1)S(1)}, u32[]{:S(2)}, u32[]{:S(2)}) collective-permute-start(bf16[64,1024]{1,0:T(8,128)(2,1)S(1)} %get-tuple-element.122), channel_id=1, source_target_pairs={{0,4},{1,5},{2,6},{3,7},{4,0},{5,1},{6,2},{7,3},{8,12},{9,13},{10,... | collective-permute-start | bytes 393224 | tf_op jit(solution)/shard_map/ppermute | solution.py:179

commit v3 on v2

--- a/solution.py
+++ b/solution.py
@@ -44,6 +44,17 @@
 
 def is_odd():
     return lax.rem(lax.axis_index("section"), 2) == 1
+
+
+def packed(gate, up, down, low, high, both):
+    rows, half = gate.shape[0], low.shape[1]
+    shape = (2 * rows, rows)
+    place = lax.broadcasted_iota(jnp.int32, shape, 0) - lax.broadcasted_iota(jnp.int32, shape, 1)
+    top, bottom = ((place == shift).astype(F32).astype(BF) for shift in (0, rows))
+    for out, upper, lower, a, b in ((high, gate, up, half, half), (low, gate, up, 0, 0), (both, down, down, 0, half)):
+        for at in range(0, half, TILE):
+            value = dot(top, upper[:, a + at : a + at + TILE], NN) + dot(bottom, lower[:, b + at : b + at + TILE], NN)
+            out[:, at : at + TILE] = value.astype(BF)
 
 
 def project(x, low, high, both, hid_a, hid_b):
@@ -184,15 +195,6 @@
     return lax.ppermute(value, "section", [(source, (source + steps) % count) for source in range(count)])
 
 
-def packed_weights(gate, up, down):
-    half = gate.shape[1] // 2
-    low = jnp.concatenate([gate[:, :half], up[:, :half]], 0)
-    low, gate, up = lax.optimization_barrier((low, gate, up))
-    high = jnp.concatenate([gate[:, half:], up[:, half:]], 0)
-    high, down = lax.optimization_barrier((high, down))
-    return low, high, jnp.concatenate([down[:, :half], down[:, half:]], 0)
-
-
 def on_device(x, g, gate_weight, up_weight, down_weight):
     rows, wide = gate_weight.shape
     half, both_rows, tokens = wide // 2, 2 * rows, x.shape[0]
@@ -210,18 +212,18 @@
             return ring_passed(here, 1)
         return exchanged(step(picked, piece, [here, value]), "section", 1)
 
-    own = packed_weights(gate_weight, up_weight, down_weight)
+    own = step(packed, [piece] * 3, [gate_weight, up_weight, down_weight])
     first = [one_hop(value) for value in own]
     second = [None] * 3
     both_own, *hid_own = step(project, [small, small_bf, small_bf], [x, own[0], own[1]])
     pair_own = step(derive, small_bf, [g, own[2], both_own])
     grads_f32 = [((both_rows, half), F32)] * 3
     own_low, own_high, own_down = step(own_grads, grads_f32, [x, g, *hid_own, pair_own])
+    second[1] = relay(first[1], own[1])
     second[0] = relay(first[0], own[0])
-    second[1] = relay(first[1], own[1])
     both_first, *hid_first = step(project, [small, small_bf, small_bf], [x, first[0], first[1]])
     second[2] = relay(first[2], own[2])
-    pair_first = step(derive, small_bf, [g, first[2], both_first], also=[second[0]])
+    pair_first = step(derive, small_bf, [g, first[2], both_first], also=[second[1]])
     both_second, *hid_second = step(project, [small, small_bf, small_bf], [x, second[0], second[1]])
 
     def outward(value):
@@ -253,13 +255,13 @@
 
     width = wide // count
 
-    def next_half(keep, got, bit):
+    def next_half(keep, got, bit, also=()):
         cols = keep.shape[1] // 2
 
         def body(*refs):
             halved(bit, width, *refs)
 
-        send, keep = step(body, [((part, cols), BF), ((part, cols), F32)], [keep, got])
+        send, keep = step(body, [((part, cols), BF), ((part, cols), F32)], [keep, got], also)
         return exchanged(send, "tensor", bit), keep
 
     def back_down(gr, a, b, side, out):
@@ -286,7 +288,7 @@
     got_a, keep_a = next_half(keep_a, got_a, bit)
     last = step(back_pair(0), piece, [x, near, side_low])
     back_of_low = backward(last)
-    got_b, keep_b = next_half(keep_b, got_b, bit)
+    got_b, keep_b = next_half(keep_b, got_b, bit, [back_of_down])
     last = step(back_pair(half), piece, [x, near, side_high], also=[got_a])
     back_of_high = backward(last)
     bit *= 2

time: 83.6 us -> 76.6 us (0.916)
  waiting for transfers between devices: 42.3 us -> 28 us
  local copies, waits for them, and re-layouts: 2.16 us -> 6.88 us
  starting transfers between devices: 25 us -> 26.9 us
    ppermute x18, waiting for transfers between devices: 42.3 us -> 28 us  [exchanged(): lax.ppermute(value, axis, [(source, source ^ bit) for source in range(cou...]
    unnamed x6 -> x14, local copies, waits for them, and re-layouts: 0.02 us -> 6.88 us
    slice x7 -> x0, local copies, waits for them, and re-layouts: 2.14 us -> none  [the longest x2 2.1 us: packed_weights(): low = jnp.concatenate([gate[:, :half], up[:, :half]], 0)]
    ppermute x18, starting transfers between devices: 25 us -> 26.9 us  [exchanged(): lax.ppermute(value, axis, [(source, source ^ bit) for source in range(cou...]
    pallas_call x23 -> x24, Pallas kernels: 12.9 us -> 13.7 us  [__call__(): pl.pallas_call(kernel, out_shape=[jax.ShapeDtypeStruct(*s) for s in shape...]
  transfers between devices with their start and end apart: 18 -> 18, of which waited for: 11 -> 8; matrix products, arithmetic and copies ran while one was open for 0% -> 0% of each run, Pallas kernels for 12% -> 13%
where the time goes in v3:
time: 76.6 us; the launch traced here: 76.3 us
  waiting for transfers between devices  28 us (37%)
  starting transfers between devices  26.9 us (35%)
  Pallas kernels  13.7 us (18%)
  local copies, waits for them, and re-layouts  6.88 us (9%)
  between operations  0.83 us (1%)
    ppermute x18, waiting for transfers between devices, exchanged(): lax.ppermute(value, axis, [(source, source ^ bit) for source in range(cou...  28 us
    ppermute x18, starting transfers between devices, exchanged(): lax.ppermute(value, axis, [(source, source ^ bit) for source in range(cou...  26.9 us
    pallas_call x24, Pallas kernels, __call__(): pl.pallas_call(kernel, out_shape=[jax.ShapeDtypeStruct(*s) for s in shape...  13.7 us
    unnamed x14, local copies, waits for them, and re-layouts  6.88 us
  transfers between devices with their start and end apart: 18, of which 8 were waited for; matrix products, arithmetic and copies ran while one was open for 0% of the time, Pallas kernels for 13%

profile of v3, /device:TPU:0, one launch (start us, length us, event | category | flops | bytes accessed | tf_op | source)
XLA Modules:
  0.0 76.3 jit_solution(7092499677529345478)
XLA Ops:
  0.6 1.0 %copy-done.4 = bf16[20,8192]{1,0:T(8,128)(2,1)S(1)} copy-done((bf16[20,8192]{1,0:T(8,128)(2,1)S(1)}, bf16[20,8192]{1,0:T(8,128)(2,1)}, u32[]{:S(2)}) %copy-start.4) | copy-done | bytes 327704
  1.6 1.0 %copy-done.5 = bf16[20,8192]{1,0:T(8,128)(2,1)S(1)} copy-done((bf16[20,8192]{1,0:T(8,128)(2,1)S(1)}, bf16[20,8192]{1,0:T(8,128)(2,1)}, u32[]{:S(2)}) %copy-start.5) | copy-done | bytes 327704
  2.6 1.0 %copy-done.6 = bf16[20,8192]{1,0:T(8,128)(2,1)S(1)} copy-done((bf16[20,8192]{1,0:T(8,128)(2,1)S(1)}, bf16[20,8192]{1,0:T(8,128)(2,1)}, u32[]{:S(2)}) %copy-start.6) | copy-done | bytes 327704
  4.4 3.0 %collective-permute-start.1 = (bf16[40,4096]{1,0:T(8,128)(2,1)S(1)}, bf16[40,4096]{1,0:T(8,128)(2,1)S(1)}, u32[]{:S(2)}, u32[]{:S(2)}) collective-permute-start(bf16[40,4096]{1,0:T(8,128)(2,1)S(1)} %get-tuple-element.71.refs_2_.refs_1_), channel_id=1, source_target_pairs={{0,16},{8,24},{16,0},{24,8},{1,17},{9,25},{17,1},{25,9},{2,18},{10... | collective-permute-start | bytes 983048 | tf_op jit(solution)/shard_map/ppermute | solution.py:190
  7.5 1.9 %collective-permute-start.4 = (bf16[40,4096]{1,0:T(8,128)(2,1)S(1)}, bf16[40,4096]{1,0:T(8,128)(2,1)S(1)}, u32[]{:S(2)}, u32[]{:S(2)}) collective-permute-start(bf16[40,4096]{1,0:T(8,128)(2,1)S(1)} %get-tuple-element.75.refs_1_.refs_6_), channel_id=1, source_target_pairs={{0,16},{8,24},{16,0},{24,8},{1,17},{9,25},{17,1},{25,9},{2,18},{10... | collective-permute-start | bytes 983048 | tf_op jit(solution)/shard_map/ppermute | solution.py:190
  9.4 1.6 %copy-done = bf16[128,8192]{1,0:T(8,128)(2,1)S(1)} copy-done((bf16[128,8192]{1,0:T(8,128)(2,1)S(1)}, bf16[128,8192]{1,0:T(8,128)(2,1)}, u32[]{:S(2)}) %copy-start) | copy-done | bytes 2097176
  11.9 1.6 %copy-done.2 = bf16[128,8192]{1,0:T(8,128)(2,1)S(1)} copy-done((bf16[128,8192]{1,0:T(8,128)(2,1)S(1)}, bf16[128,8192]{1,0:T(8,128)(2,1)}, u32[]{:S(2)}) %copy-start.2) | copy-done | bytes 2097176
  13.5 0.9 %shard_map.86 = (bf16[40,128]{1,0:T(8,128)(2,1)S(1)}, f32[8,128]{1,0:T(8,128)S(1)}) custom-call(bf16[128,8192]{1,0:T(8,128)(2,1)S(1)} %copy-done.2, bf16[40,4096]{1,0:T(8,128)(2,1)S(1)} %get-tuple-element.75.refs_1_.refs_6_, f32[40,128]{1,0:T(8,128)S(1)} %get-tuple-element.76.refs_2_, f32[8,128]{1,0:T(8,128)S(1)} %get-tuple-element.77.refs_3_), custom_call_target="tpu_custom_call" | custom-call | flops 1 | bytes 1 | tf_op jit(solution)/shard_map/pallas_call | solution.py:34
  16.0 2.1 %collective-permute-start.3 = (bf16[40,4096]{1,0:T(8,128)(2,1)S(1)}, bf16[40,4096]{1,0:T(8,128)(2,1)S(1)}, u32[]{:S(2)}, u32[]{:S(2)}) collective-permute-start(bf16[40,4096]{1,0:T(8,128)(2,1)S(1)} %get-tuple-element.86), channel_id=1, source_target_pairs={{0,8},{8,0},{16,24},{24,16},{1,9},{9,1},{17,25},{25,17},{2,10},{10... | collective-permute-start | bytes 983048 | tf_op jit(solution)/shard_map/ppermute | solution.py:190
  18.1 4.9 %collective-permute-done.refs_0_.refs_1_ = bf16[40,4096]{1,0:T(8,128)(2,1)S(1)} collective-permute-done((bf16[40,4096]{1,0:T(8,128)(2,1)S(1)}, bf16[40,4096]{1,0:T(8,128)(2,1)S(1)}, u32[]{:S(2)}, u32[]{:S(2)}) %collective-permute-start) | collective-permute-done | bytes 327712 | tf_op jit(solution)/shard_map/ppermute | solution.py:190
  23.0 2.1 %collective-permute-start.2 = (bf16[40,4096]{1,0:T(8,128)(2,1)S(1)}, bf16[40,4096]{1,0:T(8,128)(2,1)S(1)}, u32[]{:S(2)}, u32[]{:S(2)}) collective-permute-start(bf16[40,4096]{1,0:T(8,128)(2,1)S(1)} %get-tuple-element.85), channel_id=1, source_target_pairs={{0,8},{8,0},{16,24},{24,16},{1,9},{9,1},{17,25},{25,17},{2,10},{10... | collective-permute-start | bytes 983048 | tf_op jit(solution)/shard_map/ppermute | solution.py:190
  25.9 3.2 %collective-permute-done.4.refs_0_.refs_1_.refs_7_ = bf16[40,4096]{1,0:T(8,128)(2,1)S(1)} collective-permute-done((bf16[40,4096]{1,0:T(8,128)(2,1)S(1)}, bf16[40,4096]{1,0:T(8,128)(2,1)S(1)}, u32[]{:S(2)}, u32[]{:S(2)}) %collective-permute-start.4) | collective-permute-done | bytes 327712 | tf_op jit(solution)/shard_map/ppermute | solution.py:190
  29.2 1.8 %collective-permute-start.5 = (bf16[40,4096]{1,0:T(8,128)(2,1)S(1)}, bf16[40,4096]{1,0:T(8,128)(2,1)S(1)}, u32[]{:S(2)}, u32[]{:S(2)}) collective-permute-start(bf16[40,4096]{1,0:T(8,128)(2,1)S(1)} %get-tuple-element.93), channel_id=1, source_target_pairs={{0,8},{8,0},{16,24},{24,16},{1,9},{9,1},{17,25},{25,17},{2,10},{10... | collective-permute-start | bytes 983048 | tf_op jit(solution)/shard_map/ppermute | solution.py:190
  31.0 0.8 %shard_map.92 = (bf16[40,128]{1,0:T(8,128)(2,1)S(1)}, f32[8,128]{1,0:T(8,128)S(1)}) custom-call(bf16[128,8192]{1,0:T(8,128)(2,1)S(1)} %copy-done.3, bf16[40,4096]{1,0:T(8,128)(2,1)S(1)} %collective-permute-done.4.refs_0_.refs_1_.refs_7_, f32[40,128]{1,0:T(8,128)S(1)} %get-tuple-element.87.refs_2_, ...), custom_call_target="tpu_custom_call" | custom-call | flops 1 | bytes 1 | tf_op jit(solution)/shard_map/pallas_call | solution.py:34
  33.1 5.4 %collective-permute-done.5.refs_8_.refs_1_ = bf16[40,4096]{1,0:T(8,128)(2,1)S(1)} collective-permute-done((bf16[40,4096]{1,0:T(8,128)(2,1)S(1)}, bf16[40,4096]{1,0:T(8,128)(2,1)S(1)}, u32[]{:S(2)}, u32[]{:S(2)}) %collective-permute-start.5) | collective-permute-done | bytes 327712 | tf_op jit(solution)/shard_map/ppermute | solution.py:190
  38.5 1.8 %shard_map.95 = (bf16[64,4096]{1,0:T(8,128)(2,1)S(1)}, f32[64,4096]{1,0:T(8,128)S(1)}, bf16[64,4096]{1,0:T(8,128)(2,1)S(1)}, f32[64,4096]{1,0:T(8,128)S(1)}, f32[8,128]{1,0:T(8,128)S(1)}) custom-call(bf16[40,128]{1,0:T(8,128)(2,1)S(1)} %get-tuple-element.73.refs_2_.refs_0_, bf16[40,128]{1,0:T(8,128)(2,1)S(1)} %get-tuple-element.74.refs_3_.refs_1_, ...), custom_call_target="tpu_custom_call" | custom-call | flops 1 | bytes 1 | tf_op jit(solution)/shard_map/pallas_call | solution.py:34
  40.9 1.5 %collective-permute-start.8 = (bf16[40,4096]{1,0:T(8,128)(2,1)S(1)}, bf16[40,4096]{1,0:T(8,128)(2,1)S(1)}, u32[]{:S(2)}, u32[]{:S(2)}) collective-permute-start(bf16[40,4096]{1,0:T(8,128)(2,1)S(1)} %get-tuple-element.105), channel_id=1, source_target_pairs={{0,8},{8,0},{16,24},{24,16},{1,9},{9,1},{17,25},{25,17},{2,10},{10... | collective-permute-start | bytes 983048 | tf_op jit(solution)/shard_map/ppermute | solution.py:190
  42.4 0.9 %shard_map.96 = (bf16[40,128]{1,0:T(8,128)(2,1)S(1)}, f32[8,128]{1,0:T(8,128)S(1)}) custom-call(bf16[128,8192]{1,0:T(8,128)(2,1)S(1)} %copy-done.3, bf16[40,4096]{1,0:T(8,128)(2,1)S(1)} %collective-permute-done.5.refs_8_.refs_1_, f32[40,128]{1,0:T(8,128)S(1)} %get-tuple-element.98.refs_2_, f32[8,128]{1,0:T(8,128)S(1)} %get-tuple-element.99.refs_3_), custom_call_target="tpu_custom_call" | custom-call | flops 1 | bytes 1 | tf_op jit(solution)/shard_map/pallas_call | solution.py:34
  43.8 1.6 %collective-permute-start.7 = (bf16[64,2048]{1,0:T(8,128)(2,1)S(1)}, bf16[64,2048]{1,0:T(8,128)(2,1)S(1)}, u32[]{:S(2)}, u32[]{:S(2)}) collective-permute-start(bf16[64,2048]{1,0:T(8,128)(2,1)S(1)} %get-tuple-element.104), channel_id=1, source_target_pairs={{0,2},{1,3},{2,0},{3,1},{4,6},{5,7},{6,4},{7,5},{8,10},{9,11},{10,... | collective-permute-start | bytes 786440 | tf_op jit(solution)/shard_map/ppermute | solution.py:190
  46.1 5.4 %collective-permute-done.8.refs_3_.refs_2_ = bf16[40,4096]{1,0:T(8,128)(2,1)S(1)} collective-permute-done((bf16[40,4096]{1,0:T(8,128)(2,1)S(1)}, bf16[40,4096]{1,0:T(8,128)(2,1)S(1)}, u32[]{:S(2)}, u32[]{:S(2)}) %collective-permute-start.8) | collective-permute-done | bytes 327712 | tf_op jit(solution)/shard_map/ppermute | solution.py:190
  51.9 1.1 %collective-permute-start.12 = (bf16[40,4096]{1,0:T(8,128)(2,1)S(1)}, bf16[40,4096]{1,0:T(8,128)(2,1)S(1)}, u32[]{:S(2)}, u32[]{:S(2)}) collective-permute-start(bf16[40,4096]{1,0:T(8,128)(2,1)S(1)} %get-tuple-element.115), channel_id=1, source_target_pairs={{0,16},{8,24},{16,0},{24,8},{1,17},{9,25},{17,1},{25,9},{2,18},{10... | collective-permute-start | bytes 983048 | tf_op jit(solution)/shard_map/ppermute | solution.py:190
  53.1 1.5 %collective-permute-start.15 = (bf16[40,4096]{1,0:T(8,128)(2,1)S(1)}, bf16[40,4096]{1,0:T(8,128)(2,1)S(1)}, u32[]{:S(2)}, u32[]{:S(2)}) collective-permute-start(bf16[40,4096]{1,0:T(8,128)(2,1)S(1)} %get-tuple-element.123), channel_id=1, source_target_pairs={{0,8},{8,0},{16,24},{24,16},{1,9},{9,1},{17,25},{25,17},{2,10},{10... | collective-permute-start | bytes 983048 | tf_op jit(solution)/shard_map/ppermute | solution.py:190
  54.5 1.6 %collective-permute-start.11 = (bf16[64,2048]{1,0:T(8,128)(2,1)S(1)}, bf16[64,2048]{1,0:T(8,128)(2,1)S(1)}, u32[]{:S(2)}, u32[]{:S(2)}) collective-permute-start(bf16[64,2048]{1,0:T(8,128)(2,1)S(1)} %get-tuple-element.114), channel_id=1, source_target_pairs={{0,2},{1,3},{2,0},{3,1},{4,6},{5,7},{6,4},{7,5},{8,10},{9,11},{10,... | collective-permute-start | bytes 786440 | tf_op jit(solution)/shard_map/ppermute | solution.py:190
  56.2 2.6 %collective-permute-start.10 = (bf16[64,1024]{1,0:T(8,128)(2,1)S(1)}, bf16[64,1024]{1,0:T(8,128)(2,1)S(1)}, u32[]{:S(2)}, u32[]{:S(2)}) collective-permute-start(bf16[64,1024]{1,0:T(8,128)(2,1)S(1)} %get-tuple-element.112), channel_id=1, source_target_pairs={{0,4},{1,5},{2,6},{3,7},{4,0},{5,1},{6,2},{7,3},{8,12},{9,13},{10,... | collective-permute-start | bytes 393224 | tf_op jit(solution)/shard_map/ppermute | solution.py:190
  59.1 1.0 %collective-permute-start.16 = (bf16[40,4096]{1,0:T(8,128)(2,1)S(1)}, bf16[40,4096]{1,0:T(8,128)(2,1)S(1)}, u32[]{:S(2)}, u32[]{:S(2)}) collective-permute-start(bf16[40,4096]{1,0:T(8,128)(2,1)S(1)} %get-tuple-element.130), channel_id=1, source_target_pairs={{0,16},{8,24},{16,0},{24,8},{1,17},{9,25},{17,1},{25,9},{2,18},{10... | collective-permute-start | bytes 983048 | tf_op jit(solution)/shard_map/ppermute | solution.py:190
  60.2 3.2 %collective-permute-done.11.refs_1_ = bf16[64,2048]{1,0:T(8,128)(2,1)S(1)} collective-permute-done((bf16[64,2048]{1,0:T(8,128)(2,1)S(1)}, bf16[64,2048]{1,0:T(8,128)(2,1)S(1)}, u32[]{:S(2)}, u32[]{:S(2)}) %collective-permute-start.11) | collective-permute-done | bytes 262176 | tf_op jit(solution)/shard_map/ppermute | solution.py:190
  63.4 1.2 %collective-permute-done.15.refs_2_.refs_5_ = bf16[40,4096]{1,0:T(8,128)(2,1)S(1)} collective-permute-done((bf16[40,4096]{1,0:T(8,128)(2,1)S(1)}, bf16[40,4096]{1,0:T(8,128)(2,1)S(1)}, u32[]{:S(2)}, u32[]{:S(2)}) %collective-permute-start.15) | collective-permute-done | bytes 327712 | tf_op jit(solution)/shard_map/ppermute | solution.py:190
  65.0 1.1 %collective-permute-start.17 = (bf16[40,4096]{1,0:T(8,128)(2,1)S(1)}, bf16[40,4096]{1,0:T(8,128)(2,1)S(1)}, u32[]{:S(2)}, u32[]{:S(2)}) collective-permute-start(bf16[40,4096]{1,0:T(8,128)(2,1)S(1)} %get-tuple-element.131), channel_id=1, source_target_pairs={{0,16},{8,24},{16,0},{24,8},{1,17},{9,25},{17,1},{25,9},{2,18},{10... | collective-permute-start | bytes 983048 | tf_op jit(solution)/shard_map/ppermute | solution.py:190
  66.1 2.6 %collective-permute-start.14 = (bf16[64,1024]{1,0:T(8,128)(2,1)S(1)}, bf16[64,1024]{1,0:T(8,128)(2,1)S(1)}, u32[]{:S(2)}, u32[]{:S(2)}) collective-permute-start(bf16[64,1024]{1,0:T(8,128)(2,1)S(1)} %get-tuple-element.121), channel_id=1, source_target_pairs={{0,4},{1,5},{2,6},{3,7},{4,0},{5,1},{6,2},{7,3},{8,12},{9,13},{10,... | collective-permute-start | bytes 393224 | tf_op jit(solution)/shard_map/ppermute | solution.py:190
  68.7 1.0 %shard_map.105 = (f32[20,8192]{1,0:T(8,128)}, f32[8,128]{1,0:T(8,128)S(1)}) custom-call(f32[40,4096]{1,0:T(8,128)S(1)} %get-tuple-element.122.refs_0_, bf16[40,4096]{1,0:T(8,128)(2,1)S(1)} %collective-permute-done.12.refs_2_.refs_1_, bf16[40,4096]{1,0:T(8,128)(2,1)S(1)} %collective-permute-done.8.refs_3_.refs_2_, f32[8,128]{1,0:T(8,128)S(1)} %get-tuple-element.125.refs_3_), custom_call_target="tpu_custom_call" | custom-call | flops 1 | bytes 1 | tf_op jit(solution)/shard_map/pallas_call | solution.py:34
  69.7 4.5 %collective-permute-done.14.refs_3_ = bf16[64,1024]{1,0:T(8,128)(2,1)S(1)} collective-permute-done((bf16[64,1024]{1,0:T(8,128)(2,1)S(1)}, bf16[64,1024]{1,0:T(8,128)(2,1)S(1)}, u32[]{:S(2)}, u32[]{:S(2)}) %collective-permute-start.14) | collective-permute-done | bytes 131104 | tf_op jit(solution)/shard_map/ppermute | solution.py:190
  74.9 1.3 %shard_map.107 = (f32[20,8192]{1,0:T(8,128)}, f32[20,8192]{1,0:T(8,128)}, f32[8,128]{1,0:T(8,128)}) custom-call(f32[40,4096]{1,0:T(8,128)S(1)} %get-tuple-element.128.refs_0_, f32[40,4096]{1,0:T(8,128)S(1)} %get-tuple-element.129.refs_1_, bf16[40,4096]{1,0:T(8,128)(2,1)S(1)} %collective-permute-done.16.refs_2_, ...), custom_call_target="tpu_custom_call" | custom-call | flops 1 | bytes 1 | tf_op jit(solution)/shard_map/pallas_call | solution.py:34
  (42 shorter events, 9.1 us)
Async XLA Ops:
  0.6 1.0 %copy-start.4 = (bf16[20,8192]{1,0:T(8,128)(2,1)S(1)}, bf16[20,8192]{1,0:T(8,128)(2,1)}, u32[]{:S(2)}) copy-start(bf16[20,8192]{1,0:T(8,128)(2,1)} %refs_0_.13) | copy-start | bytes 983044
  1.6 1.0 %copy-start.5 = (bf16[20,8192]{1,0:T(8,128)(2,1)S(1)}, bf16[20,8192]{1,0:T(8,128)(2,1)}, u32[]{:S(2)}) copy-start(bf16[20,8192]{1,0:T(8,128)(2,1)} %refs_1_.2) | copy-start | bytes 983044
  2.6 1.0 %copy-start.6 = (bf16[20,8192]{1,0:T(8,128)(2,1)S(1)}, bf16[20,8192]{1,0:T(8,128)(2,1)}, u32[]{:S(2)}) copy-start(bf16[20,8192]{1,0:T(8,128)(2,1)} %refs_2_.1) | copy-start | bytes 983044
  4.4 11.6 %collective-permute-start.1 = (bf16[40,4096]{1,0:T(8,128)(2,1)S(1)}, bf16[40,4096]{1,0:T(8,128)(2,1)S(1)}, u32[]{:S(2)}, u32[]{:S(2)}) collective-permute-start(bf16[40,4096]{1,0:T(8,128)(2,1)S(1)} %get-tuple-element.71.refs_2_.refs_1_), channel_id=1, source_target_pairs={{0,16},{8,24},{16,0},{24,8},{1,17},{9,25},{17,1},{25,9},{2,18},{10... | collective-permute-start | bytes 983048 | tf_op jit(solution)/shard_map/ppermute | solution.py:190
  7.4 15.6 %collective-permute-start = (bf16[40,4096]{1,0:T(8,128)(2,1)S(1)}, bf16[40,4096]{1,0:T(8,128)(2,1)S(1)}, u32[]{:S(2)}, u32[]{:S(2)}) collective-permute-start(bf16[40,4096]{1,0:T(8,128)(2,1)S(1)} %get-tuple-element.70.refs_1_), channel_id=1, source_target_pairs={{0,16},{8,24},{16,0},{24,8},{1,17},{9,25},{17,1},{25,9},{2,18},{10... | collective-permute-start | bytes 983048 | tf_op jit(solution)/shard_map/ppermute | solution.py:190
  7.5 21.7 %collective-permute-start.4 = (bf16[40,4096]{1,0:T(8,128)(2,1)S(1)}, bf16[40,4096]{1,0:T(8,128)(2,1)S(1)}, u32[]{:S(2)}, u32[]{:S(2)}) collective-permute-start(bf16[40,4096]{1,0:T(8,128)(2,1)S(1)} %get-tuple-element.75.refs_1_.refs_6_), channel_id=1, source_target_pairs={{0,16},{8,24},{16,0},{24,8},{1,17},{9,25},{17,1},{25,9},{2,18},{10... | collective-permute-start | bytes 983048 | tf_op jit(solution)/shard_map/ppermute | solution.py:190
  9.4 1.6 %copy-start = (bf16[128,8192]{1,0:T(8,128)(2,1)S(1)}, bf16[128,8192]{1,0:T(8,128)(2,1)}, u32[]{:S(2)}) copy-start(bf16[128,8192]{1,0:T(8,128)(2,1)} %refs_0_.25) | copy-start | bytes 6291460
  11.0 3.3 %copy-start.1 = (bf16[128,8192]{1,0:T(8,128)(2,1)S(1)}, bf16[128,8192]{1,0:T(8,128)(2,1)}, u32[]{:S(2)}) copy-start(bf16[128,8192]{1,0:T(8,128)(2,1)} %refs_0_.25) | copy-start | bytes 6291460
  11.9 1.6 %copy-start.2 = (bf16[128,8192]{1,0:T(8,128)(2,1)S(1)}, bf16[128,8192]{1,0:T(8,128)(2,1)}, u32[]{:S(2)}) copy-start(bf16[128,8192]{1,0:T(8,128)(2,1)} %refs_0_.23) | copy-start | bytes 6291460
  13.4 1.6 %copy-start.3 = (bf16[128,8192]{1,0:T(8,128)(2,1)S(1)}, bf16[128,8192]{1,0:T(8,128)(2,1)}, u32[]{:S(2)}) copy-start(bf16[128,8192]{1,0:T(8,128)(2,1)} %refs_0_.23) | copy-start | bytes 6291460
  16.0 15.0 %collective-permute-start.3 = (bf16[40,4096]{1,0:T(8,128)(2,1)S(1)}, bf16[40,4096]{1,0:T(8,128)(2,1)S(1)}, u32[]{:S(2)}, u32[]{:S(2)}) collective-permute-start(bf16[40,4096]{1,0:T(8,128)(2,1)S(1)} %get-tuple-element.86), channel_id=1, source_target_pairs={{0,8},{8,0},{16,24},{24,16},{1,9},{9,1},{17,25},{25,17},{2,10},{10... | collective-permute-start | bytes 983048 | tf_op jit(solution)/shard_map/ppermute | solution.py:190
  23.0 8.8 %collective-permute-start.2 = (bf16[40,4096]{1,0:T(8,128)(2,1)S(1)}, bf16[40,4096]{1,0:T(8,128)(2,1)S(1)}, u32[]{:S(2)}, u32[]{:S(2)}) collective-permute-start(bf16[40,4096]{1,0:T(8,128)(2,1)S(1)} %get-tuple-element.85), channel_id=1, source_target_pairs={{0,8},{8,0},{16,24},{24,16},{1,9},{9,1},{17,25},{25,17},{2,10},{10... | collective-permute-start | bytes 983048 | tf_op jit(solution)/shard_map/ppermute | solution.py:190
  29.2 9.3 %collective-permute-start.5 = (bf16[40,4096]{1,0:T(8,128)(2,1)S(1)}, bf16[40,4096]{1,0:T(8,128)(2,1)S(1)}, u32[]{:S(2)}, u32[]{:S(2)}) collective-permute-start(bf16[40,4096]{1,0:T(8,128)(2,1)S(1)} %get-tuple-element.93), channel_id=1, source_target_pairs={{0,8},{8,0},{16,24},{24,16},{1,9},{9,1},{17,25},{25,17},{2,10},{10... | collective-permute-start | bytes 983048 | tf_op jit(solution)/shard_map/ppermute | solution.py:190
  40.4 3.3 %collective-permute-start.6 = (bf16[64,4096]{1,0:T(8,128)(2,1)S(1)}, bf16[64,4096]{1,0:T(8,128)(2,1)S(1)}, u32[]{:S(2)}, u32[]{:S(2)}) collective-permute-start(bf16[64,4096]{1,0:T(8,128)(2,1)S(1)} %get-tuple-element.97), channel_id=1, source_target_pairs={{0,1},{1,0},{2,3},{3,2},{4,5},{5,4},{6,7},{7,6},{8,9},{9,8},{10,11... | collective-permute-start | bytes 1572872 | tf_op jit(solution)/shard_map/ppermute | solution.py:190
  40.4 5.6 %collective-permute-start.9 = (bf16[64,4096]{1,0:T(8,128)(2,1)S(1)}, bf16[64,4096]{1,0:T(8,128)(2,1)S(1)}, u32[]{:S(2)}, u32[]{:S(2)}) collective-permute-start(bf16[64,4096]{1,0:T(8,128)(2,1)S(1)} %get-tuple-element.107), channel_id=1, source_target_pairs={{0,1},{1,0},{2,3},{3,2},{4,5},{5,4},{6,7},{7,6},{8,9},{9,8},{10,11... | collective-permute-start | bytes 1572872 | tf_op jit(solution)/shard_map/ppermute | solution.py:190
  40.9 10.6 %collective-permute-start.8 = (bf16[40,4096]{1,0:T(8,128)(2,1)S(1)}, bf16[40,4096]{1,0:T(8,128)(2,1)S(1)}, u32[]{:S(2)}, u32[]{:S(2)}) collective-permute-start(bf16[40,4096]{1,0:T(8,128)(2,1)S(1)} %get-tuple-element.105), channel_id=1, source_target_pairs={{0,8},{8,0},{16,24},{24,16},{1,9},{9,1},{17,25},{25,17},{2,10},{10... | collective-permute-start | bytes 983048 | tf_op jit(solution)/shard_map/ppermute | solution.py:190
  43.8 12.3 %collective-permute-start.7 = (bf16[64,2048]{1,0:T(8,128)(2,1)S(1)}, bf16[64,2048]{1,0:T(8,128)(2,1)S(1)}, u32[]{:S(2)}, u32[]{:S(2)}) collective-permute-start(bf16[64,2048]{1,0:T(8,128)(2,1)S(1)} %get-tuple-element.104), channel_id=1, source_target_pairs={{0,2},{1,3},{2,0},{3,1},{4,6},{5,7},{6,4},{7,5},{8,10},{9,11},{10,... | collective-permute-start | bytes 786440 | tf_op jit(solution)/shard_map/ppermute | solution.py:190
  45.5 13.4 %collective-permute-start.13 = (bf16[40,4096]{1,0:T(8,128)(2,1)S(1)}, bf16[40,4096]{1,0:T(8,128)(2,1)S(1)}, u32[]{:S(2)}, u32[]{:S(2)}) collective-permute-start(bf16[40,4096]{1,0:T(8,128)(2,1)S(1)} %get-tuple-element.117), channel_id=1, source_target_pairs={{0,8},{8,0},{16,24},{24,16},{1,9},{9,1},{17,25},{25,17},{2,10},{10... | collective-permute-start | bytes 983048 | tf_op jit(solution)/shard_map/ppermute | solution.py:190
  51.9 11.4 %collective-permute-start.12 = (bf16[40,4096]{1,0:T(8,128)(2,1)S(1)}, bf16[40,4096]{1,0:T(8,128)(2,1)S(1)}, u32[]{:S(2)}, u32[]{:S(2)}) collective-permute-start(bf16[40,4096]{1,0:T(8,128)(2,1)S(1)} %get-tuple-element.115), channel_id=1, source_target_pairs={{0,16},{8,24},{16,0},{24,8},{1,17},{9,25},{17,1},{25,9},{2,18},{10... | collective-permute-start | bytes 983048 | tf_op jit(solution)/shard_map/ppermute | solution.py:190
  53.1 11.6 %collective-permute-start.15 = (bf16[40,4096]{1,0:T(8,128)(2,1)S(1)}, bf16[40,4096]{1,0:T(8,128)(2,1)S(1)}, u32[]{:S(2)}, u32[]{:S(2)}) collective-permute-start(bf16[40,4096]{1,0:T(8,128)(2,1)S(1)} %get-tuple-element.123), channel_id=1, source_target_pairs={{0,8},{8,0},{16,24},{24,16},{1,9},{9,1},{17,25},{25,17},{2,10},{10... | collective-permute-start | bytes 983048 | tf_op jit(solution)/shard_map/ppermute | solution.py:190
  54.5 8.8 %collective-permute-start.11 = (bf16[64,2048]{1,0:T(8,128)(2,1)S(1)}, bf16[64,2048]{1,0:T(8,128)(2,1)S(1)}, u32[]{:S(2)}, u32[]{:S(2)}) collective-permute-start(bf16[64,2048]{1,0:T(8,128)(2,1)S(1)} %get-tuple-element.114), channel_id=1, source_target_pairs={{0,2},{1,3},{2,0},{3,1},{4,6},{5,7},{6,4},{7,5},{8,10},{9,11},{10,... | collective-permute-start | bytes 786440 | tf_op jit(solution)/shard_map/ppermute | solution.py:190
  56.2 8.5 %collective-permute-start.10 = (bf16[64,1024]{1,0:T(8,128)(2,1)S(1)}, bf16[64,1024]{1,0:T(8,128)(2,1)S(1)}, u32[]{:S(2)}, u32[]{:S(2)}) collective-permute-start(bf16[64,1024]{1,0:T(8,128)(2,1)S(1)} %get-tuple-element.112), channel_id=1, source_target_pairs={{0,4},{1,5},{2,6},{3,7},{4,0},{5,1},{6,2},{7,3},{8,12},{9,13},{10,... | collective-permute-start | bytes 393224 | tf_op jit(solution)/shard_map/ppermute | solution.py:190
  59.1 15.8 %collective-permute-start.16 = (bf16[40,4096]{1,0:T(8,128)(2,1)S(1)}, bf16[40,4096]{1,0:T(8,128)(2,1)S(1)}, u32[]{:S(2)}, u32[]{:S(2)}) collective-permute-start(bf16[40,4096]{1,0:T(8,128)(2,1)S(1)} %get-tuple-element.130), channel_id=1, source_target_pairs={{0,16},{8,24},{16,0},{24,8},{1,17},{9,25},{17,1},{25,9},{2,18},{10... | collective-permute-start | bytes 983048 | tf_op jit(solution)/shard_map/ppermute | solution.py:190
  65.0 10.0 %collective-permute-start.17 = (bf16[40,4096]{1,0:T(8,128)(2,1)S(1)}, bf16[40,4096]{1,0:T(8,128)(2,1)S(1)}, u32[]{:S(2)}, u32[]{:S(2)}) collective-permute-start(bf16[40,4096]{1,0:T(8,128)(2,1)S(1)} %get-tuple-element.131), channel_id=1, source_target_pairs={{0,16},{8,24},{16,0},{24,8},{1,17},{9,25},{17,1},{25,9},{2,18},{10... | collective-permute-start | bytes 983048 | tf_op jit(solution)/shard_map/ppermute | solution.py:190
  66.1 8.1 %collective-permute-start.14 = (bf16[64,1024]{1,0:T(8,128)(2,1)S(1)}, bf16[64,1024]{1,0:T(8,128)(2,1)S(1)}, u32[]{:S(2)}, u32[]{:S(2)}) collective-permute-start(bf16[64,1024]{1,0:T(8,128)(2,1)S(1)} %get-tuple-element.121), channel_id=1, source_target_pairs={{0,4},{1,5},{2,6},{3,7},{4,0},{5,1},{6,2},{7,3},{8,12},{9,13},{10,... | collective-permute-start | bytes 393224 | tf_op jit(solution)/shard_map/ppermute | solution.py:190

commit v4 on v3

v4 whole, which is shorter than its diff:
```python
import jax
import jax.numpy as jnp
from jax import lax
from jax.experimental import pallas as pl
from jax.experimental.pallas import tpu as pltpu
from jax.sharding import PartitionSpec as P

BF = jnp.bfloat16
F32 = jnp.float32
NN = (((1,), (0,)), ((), ()))
NT = (((1,), (1,)), ((), ()))
TN = (((0,), (0,)), ((), ()))
TILE = 512
SWAP = 4


def dot(left, right, dims):
    return lax.dot_general(left, right, dims, preferred_element_type=F32)


class Steps:
    def __init__(self):
        self.mark = None

    def __call__(self, body, outs, ins, also=(), far=0, scratch=()):
        marks = [*also] if self.mark is None else [*also, self.mark]
        count = len(ins)
        ins = [pltpu.with_memory_space_constraint(v, pltpu.HBM) if k < far else v for k, v in enumerate(ins)]

        def kernel(*refs):
            last = count + len(marks) + len(shapes)
            body(*refs[:count], *refs[count + len(marks) : last - 1], *refs[last:])
            refs[last - 1][...] = jnp.zeros_like(refs[last - 1])

        single = isinstance(outs, tuple)
        shapes = ([outs] if single else list(outs)) + [((8, 128), F32)]
        *got, self.mark = pl.pallas_call(
            kernel,
            out_shape=[jax.ShapeDtypeStruct(*s) for s in shapes],
            in_specs=[pl.BlockSpec(memory_space=pltpu.HBM)] * far
            + [pl.BlockSpec(memory_space=pltpu.VMEM)] * (count + len(marks) - far),
            out_specs=[pl.BlockSpec(memory_space=pltpu.VMEM)] * len(shapes),
            scratch_shapes=list(scratch),
            compiler_params=pltpu.CompilerParams(vmem_limit_bytes=24 * 1024 * 1024),
            cost_estimate=pl.CostEstimate(flops=1, bytes_accessed=1, transcendentals=0),
        )(*ins, *marks)
        return got[0] if single else got


def is_odd():
    return lax.rem(lax.axis_index("section"), 2) == 1


def either(bit, run):
    for value in range(2):
        pl.when(bit == value)(lambda value=value: run(value))


def tensor_bit(bit):
    return lax.rem(lax.div(lax.axis_index("tensor"), bit), 2)


def is_odd():
    return lax.rem(lax.axis_index("section"), 2) == 1


def top_rows(like):
    return lax.broadcasted_iota(jnp.int32, like.shape, 0) < like.shape[0] // 2


def placed(rows):
    shape = (2 * rows, rows)
    place = lax.broadcasted_iota(jnp.int32, shape, 0) - lax.broadcasted_iota(jnp.int32, shape, 1)
    return [(place == shift).astype(F32).astype(BF) for shift in (0, rows)]


def stacked(out, upper, lower, upper_at=0, lower_at=0):
    top, bottom = placed(upper.shape[0])
    for at in range(0, out.shape[1], TILE):
        first, second = slice(upper_at + at, upper_at + at + TILE), slice(lower_at + at, lower_at + at + TILE)
        out[:, at : at + TILE] = (dot(top, upper[:, first], NN) + dot(bottom, lower[:, second], NN)).astype(BF)


def runs(width, wide):
    return [(SWAP * width * j, 2 * SWAP * width * j) for j in range(wide // (2 * SWAP * width))]


def packed(width, gate, up, down, high, low, keep, send, gate_here, up_here, down_here, sems):
    copies = [
        pltpu.make_async_copy(there, here, sems.at[k])
        for k, (there, here) in enumerate(((gate, gate_here), (up, up_here), (down, down_here)))
    ]
    for copy in copies:
        copy.start()
    half = high.shape[1]
    copies[0].wait()
    copies[1].wait()
    stacked(high, gate_here, up_here, half, half)
    stacked(low, gate_here, up_here)
    copies[2].wait()

    def run(mine):
        for near, there in runs(width, 2 * half):
            here = slice(near, near + SWAP * width)
            for out, which in ((keep, mine), (send, 1 - mine)):
                at = there + SWAP * width * which
                out[:, here] = down_here[:, at : at + SWAP * width]

    either(tensor_bit(SWAP), run)


def project_tiles(x, low, high):
    half = low.shape[1]
    tile = min(half, 1024)
    total = jnp.zeros((low.shape[0], x.shape[0]), F32)
    for at in range(0, half, tile):
        cut = slice(at, at + tile)
        total += dot(low[:, cut], x[:, cut], NT)
        total += dot(high[:, cut], x[:, half + at : half + at + tile], NT)
    return total


def project(x, low, high, both, hid_a, hid_b):
    rows = low.shape[0] // 2
    total = project_tiles(x, low, high)
    both[...] = total
    hidden = total * jax.nn.sigmoid(total) * pltpu.roll(total, rows, 0)
    hidden = jnp.where(top_rows(total), hidden, 0.0)
    hid_a[...] = hidden.astype(BF)
    hid_b[...] = pltpu.roll(hidden, rows, 0).astype(BF)


def project_first(x_there, g_there, low, high, x, g, both, hid_a, hid_b, sems):
    copies = [pltpu.make_async_copy(x_there, x, sems.at[0]), pltpu.make_async_copy(g_there, g, sems.at[1])]
    for copy in copies:
        copy.start()
    copies[0].wait()
    project(x, low, high, both, hid_a, hid_b)
    copies[1].wait()


def part_of(width, g, down, hid_b, part, out):
    rows, wide = down.shape[0] // 2, g.shape[1]
    tile = min(SWAP * width, 1024)

    def run(mine):
        total = jnp.zeros(part.shape, F32)
        for near, there in runs(width, wide):
            for at in range(0, SWAP * width, tile):
                far = there + SWAP * width * mine + at
                total += dot(down[:, near + at : near + at + tile], g[:, far : far + tile], NT)
        part[...] = total
        out[...] = jnp.where(top_rows(total), pltpu.roll(total, rows, 0), hid_b[...].astype(F32))

    either(tensor_bit(SWAP), run)


def finish(both, part, got, hid_a, pair, hid_pair):
    rows = both.shape[0] // 2
    gate, got = both[...], got[...]
    dhid = part[...] + got
    sig = jax.nn.sigmoid(gate)
    dgate = dhid * pltpu.roll(gate, rows, 0) * sig * (1.0 + gate * (1.0 - sig))
    dup = pltpu.roll(dhid * (gate * sig), rows, 0)
    first = top_rows(gate)
    pair[...] = jnp.where(first, dgate, dup).astype(BF)
    hid_pair[...] = jnp.where(first, hid_a[...].astype(F32), got).astype(BF)


def down_columns(g, hid_a, hid_b, at, half):
    cut = slice(at, at + TILE)
    return dot(hid_a[...], g[:, cut], NN) + dot(hid_b[...], g[:, half + at : half + at + TILE], NN)


def tiles(size):
    return [slice(at, min(at + TILE, size)) for at in range(0, size, TILE)]


def shifted(cut, offset):
    return slice(cut.start + offset, cut.stop + offset)


def own_grads(x, g, hid_a, hid_b, pair, low, high, down):
    half = down.shape[1]
    for out, offset in ((low, 0), (high, low.shape[1])):
        for cut in tiles(out.shape[1]):
            out[:, cut] = dot(pair[...], x[:, shifted(cut, offset)], NN)
    for at in range(0, half, TILE):
        down[:, at : at + TILE] = down_columns(g, hid_a, hid_b, at, half)


def sent_down(g, hid_a, hid_b, out):
    half = out.shape[1]
    for at in range(0, half, TILE):
        out[:, at : at + TILE] = down_columns(g, hid_a, hid_b, at, half).astype(BF)


def sent_pair(x, pair, low, high):
    for out, offset in ((low, 0), (high, low.shape[1])):
        for cut in tiles(out.shape[1]):
            out[:, cut] = dot(pair[...], x[:, shifted(cut, offset)], NN).astype(BF)


def kept(side, odd, four, wanted):
    value = side.astype(F32)
    return jnp.where(odd == wanted, value, 0.0) if four else value


def picked(here, piece, out):
    @pl.when(is_odd())
    def _():
        out[...] = here[...]

    @pl.when(jnp.logical_not(is_odd()))
    def _():
        out[...] = piece[...]


def output_sums(width, *refs):
    hids, downs, (send_a, send_b, keep) = refs[:3], refs[3:6], refs[6:]
    part = send_a.shape[0]
    tile = min(width, TILE)

    def run(mine):
        for block in range(keep.shape[1] // width):
            for which in range(2):
                for at in range(0, width, tile):
                    cols = slice((2 * block + which) * width + at, (2 * block + which) * width + at + tile)
                    here = slice(block * width + at, block * width + at + tile)
                    total = sum(dot(hid[...], down[:, cols], TN) for hid, down in zip(hids, downs))
                    if which == mine:
                        keep[:, here] = total
                    else:
                        send_a[:, here] = total[:part].astype(BF)
                        send_b[:, here] = total[part:].astype(BF)

    either(tensor_bit(1), run)


def halved(bit, width, keep, *refs):
    got, (send, left) = refs[:-2], refs[-2:]
    tile = min(width, TILE)
    part = keep.shape[0] // len(got)

    def run(mine):
        for block in range(left.shape[1] // width):
            for out, which in ((send, 1 - mine), (left, mine)):
                for at in range(0, width, tile):
                    cols = slice((2 * block + which) * width + at, (2 * block + which) * width + at + tile)
                    here = slice(block * width + at, block * width + at + tile)
                    for k, piece in enumerate(got):
                        rows = slice(k * part, (k + 1) * part)
                        out[rows, here] = (keep[rows, cols] + piece[:, cols].astype(F32)).astype(out.dtype)

    either(tensor_bit(bit), run)


def final_output(keep, *refs):
    got, out = refs[:-1], refs[-1]
    part = keep.shape[0] // len(got)
    for k, piece in enumerate(got):
        rows = slice(k * part, (k + 1) * part)
        out[rows, :] = (keep[rows, :] + piece[...].astype(F32)).astype(BF)


def exchanged(value, axis, bit):
    count = lax.axis_size(axis)
    return lax.ppermute(value, axis, [(source, source ^ bit) for source in range(count)])


def ring_passed(value, steps):
    count = lax.axis_size("section")
    return lax.ppermute(value, "section", [(source, (source + steps) % count) for source in range(count)])


def on_device(x, g, gate_weight, up_weight, down_weight):
    rows, wide = gate_weight.shape
    half, both_rows, tokens = wide // 2, 2 * rows, x.shape[0]
    count = lax.axis_size("tensor")
    assert count > SWAP and count & (count - 1) == 0
    width = wide // count
    four = lax.axis_size("section") == 4
    piece, narrow = ((both_rows, half), BF), ((rows, half), BF)
    small, small_bf = ((both_rows, tokens), F32), ((both_rows, tokens), BF)
    step = Steps()

    def with_width(body):
        def run(*refs):
            body(width, *refs)

        return run

    def one_hop(value):
        return exchanged(value, "section", 2) if four else ring_passed(value, 1)

    def relay(here, value):
        if not four:
            return ring_passed(here, 1)
        return exchanged(step(picked, piece, [here, value]), "section", 1)

    def outward(value):
        return exchanged(value, "section", 1) if four else ring_passed(value, -1)

    def backward(value):
        return exchanged(value, "section", 2) if four else ring_passed(value, -1)

    own, first, second = [None] * 3, [None] * 3, [None] * 3
    held = pltpu.VMEM((rows, wide), BF)
    own[1], own[0], down_keep, down_send = step(
        with_width(packed),
        [piece, piece, narrow, narrow],
        [gate_weight, up_weight, down_weight],
        far=3,
        scratch=[held, held, held, pltpu.SemaphoreType.DMA((3,))],
    )
    first[1] = one_hop(own[1])
    first[0] = one_hop(own[0])
    down_got = exchanged(down_send, "tensor", SWAP)
    x, g, both_own, *hid_own = step(
        project_first,
        [(x.shape, BF), (g.shape, BF), small, small_bf, small_bf],
        [x, g, own[0], own[1]],
        far=2,
        scratch=[pltpu.SemaphoreType.DMA((2,))],
    )
    second[1] = relay(first[1], own[1])

    def joined(keep, got, out):
        stacked(out, keep, got)

    own[2] = step(joined, piece, [down_keep, down_got])
    first[2] = one_hop(own[2])
    part_own, part_out = step(with_width(part_of), [small, small], [g, own[2], hid_own[1]])
    second[0] = relay(first[0], own[0])
    both_first, *hid_first = step(project, [small, small_bf, small_bf], [x, first[0], first[1]], also=[second[1]])
    second[2] = relay(first[2], own[2])

    def part_two(gr, down, hid_b, earlier, part, out):
        out[:both_rows, :] = earlier[...]
        part_of(width, gr, down, hid_b, part, out.at[both_rows:, :])

    part_first, part_out = step(
        part_two, [small, ((2 * both_rows, tokens), F32)], [g, first[2], hid_first[1], part_out]
    )
    part_got = exchanged(part_out, "tensor", SWAP)
    both_second, *hid_second = step(project, [small, small_bf, small_bf], [x, second[0], second[1]])
    side_down = outward(step(sent_down, piece, [g, *hid_second]))

    def finish_two(both_a, part_a, hid_a, both_b, part_b, hid_b, got, pair_a, out_a, pair_b, out_b):
        finish(both_a, part_a, got.at[:both_rows, :], hid_a, pair_a, out_a)
        finish(both_b, part_b, got.at[both_rows:, :], hid_b, pair_b, out_b)

    pair_own, wide_own, pair_first, wide_first = step(
        finish_two, [small_bf] * 4, [both_own, part_own, hid_own[0], both_first, part_first, hid_first[0], part_got]
    )
    low_columns = half + 128
    low_shape, high_shape = (both_rows, low_columns), (both_rows, wide - low_columns)
    grads_f32 = [(low_shape, F32), (high_shape, F32), ((both_rows, half), F32)]
    own_low, own_high, own_down = step(own_grads, grads_f32, [x, g, *hid_own, pair_own])
    part_second, part_out = step(with_width(part_of), [small, small], [g, second[2], hid_second[1]])
    part_got = exchanged(part_out, "tensor", SWAP)
    pair_second, wide_second = step(finish, [small_bf] * 2, [both_second, part_second, part_got, hid_second[0]])
    low, high = step(sent_pair, [(low_shape, BF), (high_shape, BF)], [x, pair_second])
    side_low, side_high = outward(low), outward(high)

    def back_down(gr, a, b, side, out):
        odd = is_odd()
        for at in range(0, half, TILE):
            value = down_columns(gr, a, b, at, half) + kept(side[:, at : at + TILE], odd, four, True)
            out[:, at : at + TILE] = value.astype(BF)

    def back_pair(offset):
        def body(xr, pair, side, out):
            odd = is_odd()
            for cut in tiles(out.shape[1]):
                value = dot(pair[...], xr[:, shifted(cut, offset)], NN)
                out[:, cut] = (value + kept(side[:, cut], odd, four, True)).astype(BF)

        return body

    quarter = wide // 4
    send_a, send_b, keep = step(
        with_width(output_sums),
        [((tokens // 2, quarter), BF), ((tokens // 2, quarter), BF), ((tokens, quarter), F32)],
        [wide_own, wide_first, wide_second, own[2], first[2], second[2]],
    )
    back_of_down = backward(step(back_down, piece, [g, *hid_first, side_down]))
    got = [exchanged(send_a, "tensor", 1), exchanged(send_b, "tensor", 1)]

    def next_half(keep, got, bit):
        cols = keep.shape[1] // 2

        def body(*refs):
            halved(bit, width, *refs)

        send, keep = step(body, [((tokens, cols), BF), ((tokens, cols), F32)], [keep, *got])
        return keep, [exchanged(send, "tensor", bit)]

    keep, got = next_half(keep, got, 2)
    back_of_low = backward(step(back_pair(0), (low_shape, BF), [x, pair_first, side_low]))
    back_of_high = backward(step(back_pair(low_columns), (high_shape, BF), [x, pair_first, side_high], also=[back_of_down]))
    bit = 2 * SWAP
    while bit < count:
        keep, got = next_half(keep, got, bit)
        bit *= 2

    def finished(own_ref, back, side, odd, cut):
        value = own_ref[:, cut] + back[:, cut].astype(F32)
        return value + kept(side[:, cut], odd, four, False) if four else value

    def final_down(own_ref, back, side, out):
        odd = is_odd()
        for at in range(0, half, TILE):
            cut = slice(at, at + TILE)
            value = finished(own_ref, back, side, odd, cut)
            out[:, cut] = value[:rows]
            out[:, half + at : half + at + TILE] = value[rows:]

    def final_pair(low_ref, high_ref, low_back, high_back, low_side, high_side, out_gate, out_up):
        odd = is_odd()
        for offset, refs in ((0, (low_ref, low_back, low_side)), (low_columns, (high_ref, high_back, high_side))):
            for cut in tiles(refs[0].shape[1]):
                value = finished(*refs, odd, cut)
                out_gate[:, shifted(cut, offset)] = value[:rows]
                out_up[:, shifted(cut, offset)] = value[rows:]

    whole = ((rows, wide), F32)
    grad_down = step(final_down, whole, [own_down, back_of_down, side_down])
    output = step(final_output, ((tokens, width), BF), [keep, *got])
    grad_gate, grad_up = step(
        final_pair, [whole, whole], [own_low, own_high, back_of_low, back_of_high, side_low, side_high]
    )
    return (output, grad_gate, grad_up, grad_down)


def solution(mesh):
    placed = (
        P("section", None),
        P("section", None),
        P(("section", "tensor"), None),
        P(("section", "tensor"), None),
        P(("section", "tensor"), None),
    )
    return jax.shard_map(
        on_device,
        mesh=mesh,
        in_specs=placed,
        out_specs=(
            P("section", "tensor"),
            P(("section", "tensor"), None),
            P(("section", "tensor"), None),
            P(("section", "tensor"), None),
        ),
        check_vma=False,
    )
```

time: 76.6 us -> 69.6 us (0.909)
  local copies, waits for them, and re-layouts: 6.88 us -> 0 us
  waiting for transfers between devices: 28 us -> 24.8 us
  starting transfers between devices: 26.9 us -> 29.4 us
  Pallas kernels: 13.7 us -> 14.5 us
    unnamed x14 -> x0, local copies, waits for them, and re-layouts: 6.88 us -> none
    ppermute x18, waiting for transfers between devices: 28 us -> 24.8 us  [exchanged(): lax.ppermute(value, axis, [(source, source ^ bit) for source in range(cou...]
    ppermute x18, starting transfers between devices: 26.9 us -> 29.4 us  [exchanged(): lax.ppermute(value, axis, [(source, source ^ bit) for source in range(cou...]
    pallas_call x24, Pallas kernels: 13.7 us -> 14.5 us  [__call__(): pl.pallas_call(kernel, out_shape=[jax.ShapeDtypeStruct(*s) for s in shape...]
  transfers between devices with their start and end apart: 18 -> 18, of which waited for: 8 -> 13; matrix products, arithmetic and copies ran while one was open for 0% -> 0% of each run, Pallas kernels for 13% -> 16%
where the time goes in v4:
time: 69.6 us; the launch traced here: 69.5 us
  starting transfers between devices  29.4 us (42%)
  waiting for transfers between devices  24.8 us (36%)
  Pallas kernels  14.5 us (21%)
  between operations  0.79 us (1%)
    ppermute x18, starting transfers between devices, exchanged(): lax.ppermute(value, axis, [(source, source ^ bit) for source in range(cou...  29.4 us
    ppermute x18, waiting for transfers between devices, exchanged(): lax.ppermute(value, axis, [(source, source ^ bit) for source in range(cou...  24.8 us
    pallas_call x24, Pallas kernels, __call__(): pl.pallas_call(kernel, out_shape=[jax.ShapeDtypeStruct(*s) for s in shape...  14.5 us
  transfers between devices with their start and end apart: 18, of which 13 were waited for; matrix products, arithmetic and copies ran while one was open for 0% of the time, Pallas kernels for 16%

profile of v4, /device:TPU:0, one launch (start us, length us, event | category | flops | bytes accessed | tf_op | source)
XLA Modules:
  0.0 69.5 jit_solution(12485060654869055463)
XLA Ops:
  0.6 1.7 %shard_map.84 = (bf16[40,4096]{1,0:T(8,128)(2,1)S(1)}, bf16[40,4096]{1,0:T(8,128)(2,1)S(1)}, bf16[20,4096]{1,0:T(8,128)(2,1)S(1)}, bf16[20,4096]{1,0:T(8,128)(2,1)S(1)}, f32[8,128]{1,0:T(8,128)S(1)}) custom-call(bf16[20,8192]{1,0:T(8,128)(2,1)} %refs_0_.2, bf16[20,8192]{1,0:T(8,128)(2,1)} %refs_1_.2, bf16[20,8192]{1,0:T(8,128)(2,1)} %refs_2_.1), custom_call_target="tpu_custom_call" | custom-call | flops 1 | bytes 1 | tf_op jit(solution)/shard_map/pallas_call | solution.py:37
  2.4 3.0 %collective-permute-start.1 = (bf16[40,4096]{1,0:T(8,128)(2,1)S(1)}, bf16[40,4096]{1,0:T(8,128)(2,1)S(1)}, u32[]{:S(2)}, u32[]{:S(2)}) collective-permute-start(bf16[40,4096]{1,0:T(8,128)(2,1)S(1)} %get-tuple-element.77.refs_3_.refs_1_), channel_id=1, source_target_pairs={{0,16},{8,24},{16,0},{24,8},{1,17},{9,25},{17,1},{25,9},{2,18},{10... | collective-permute-start | bytes 983048 | tf_op jit(solution)/shard_map/ppermute | solution.py:268
  5.5 3.0 %collective-permute-start = (bf16[20,4096]{1,0:T(8,128)(2,1)S(1)}, bf16[20,4096]{1,0:T(8,128)(2,1)S(1)}, u32[]{:S(2)}, u32[]{:S(2)}) collective-permute-start(bf16[20,4096]{1,0:T(8,128)(2,1)S(1)} %get-tuple-element.82), channel_id=1, source_target_pairs={{0,4},{1,5},{2,6},{3,7},{4,0},{5,1},{6,2},{7,3},{8,12},{9,13},{10,... | collective-permute-start | bytes 491528 | tf_op jit(solution)/shard_map/ppermute | solution.py:268
  8.5 2.4 %shard_map.85 = (bf16[128,8192]{1,0:T(8,128)(2,1)S(1)}, bf16[128,8192]{1,0:T(8,128)(2,1)S(1)}, f32[40,128]{1,0:T(8,128)S(1)}, bf16[40,128]{1,0:T(8,128)(2,1)S(1)...) custom-call(bf16[128,8192]{1,0:T(8,128)(2,1)} %refs_0_.3, bf16[128,8192]{1,0:T(8,128)(2,1)} %refs_1_.3, ...), custom_call_target="tpu_custom_call" | custom-call | flops 1 | bytes 1 | tf_op jit(solution)/shard_map/pallas_call | solution.py:37
  11.0 3.0 %collective-permute-done.1.refs_0_.refs_2_ = bf16[40,4096]{1,0:T(8,128)(2,1)S(1)} collective-permute-done((bf16[40,4096]{1,0:T(8,128)(2,1)S(1)}, bf16[40,4096]{1,0:T(8,128)(2,1)S(1)}, u32[]{:S(2)}, u32[]{:S(2)}) %collective-permute-start.1) | collective-permute-done | bytes 327712 | tf_op jit(solution)/shard_map/ppermute | solution.py:268
  14.0 2.1 %collective-permute-start.3 = (bf16[40,4096]{1,0:T(8,128)(2,1)S(1)}, bf16[40,4096]{1,0:T(8,128)(2,1)S(1)}, u32[]{:S(2)}, u32[]{:S(2)}) collective-permute-start(bf16[40,4096]{1,0:T(8,128)(2,1)S(1)} %get-tuple-element.91), channel_id=1, source_target_pairs={{0,8},{8,0},{16,24},{24,16},{1,9},{9,1},{17,25},{25,17},{2,10},{10... | collective-permute-start | bytes 983048 | tf_op jit(solution)/shard_map/ppermute | solution.py:268
  16.1 1.0 %collective-permute-done.refs_1_ = bf16[20,4096]{1,0:T(8,128)(2,1)S(1)} collective-permute-done((bf16[20,4096]{1,0:T(8,128)(2,1)S(1)}, bf16[20,4096]{1,0:T(8,128)(2,1)S(1)}, u32[]{:S(2)}, u32[]{:S(2)}) %collective-permute-start) | collective-permute-done | bytes 163872 | tf_op jit(solution)/shard_map/ppermute | solution.py:268
  17.4 1.6 %collective-permute-start.4 = (bf16[40,4096]{1,0:T(8,128)(2,1)S(1)}, bf16[40,4096]{1,0:T(8,128)(2,1)S(1)}, u32[]{:S(2)}, u32[]{:S(2)}) collective-permute-start(bf16[40,4096]{1,0:T(8,128)(2,1)S(1)} %get-tuple-element.85.refs_1_.refs_3_), channel_id=1, source_target_pairs={{0,16},{8,24},{16,0},{24,8},{1,17},{9,25},{17,1},{25,9},{2,18},{10... | collective-permute-start | bytes 983048 | tf_op jit(solution)/shard_map/ppermute | solution.py:268
  19.5 1.5 %collective-permute-done.2.refs_0_.refs_1_ = bf16[40,4096]{1,0:T(8,128)(2,1)S(1)} collective-permute-done((bf16[40,4096]{1,0:T(8,128)(2,1)S(1)}, bf16[40,4096]{1,0:T(8,128)(2,1)S(1)}, u32[]{:S(2)}, u32[]{:S(2)}) %collective-permute-start.2) | collective-permute-done | bytes 327712 | tf_op jit(solution)/shard_map/ppermute | solution.py:268
  21.0 2.1 %collective-permute-start.6 = (bf16[40,4096]{1,0:T(8,128)(2,1)S(1)}, bf16[40,4096]{1,0:T(8,128)(2,1)S(1)}, u32[]{:S(2)}, u32[]{:S(2)}) collective-permute-start(bf16[40,4096]{1,0:T(8,128)(2,1)S(1)} %get-tuple-element.102), channel_id=1, source_target_pairs={{0,8},{8,0},{16,24},{24,16},{1,9},{9,1},{17,25},{25,17},{2,10},{10... | collective-permute-start | bytes 983048 | tf_op jit(solution)/shard_map/ppermute | solution.py:268
  23.1 0.8 %shard_map.90 = (f32[40,128]{1,0:T(8,128)S(1)}, bf16[40,128]{1,0:T(8,128)(2,1)S(1)}, bf16[40,128]{1,0:T(8,128)(2,1)S(1)}, f32[8,128]{1,0:T(8,128)S(1)}) custom-call(bf16[128,8192]{1,0:T(8,128)(2,1)S(1)} %get-tuple-element.90.refs_0_, bf16[40,4096]{1,0:T(8,128)(2,1)S(1)} %collective-permute-done.2.refs_0_.refs_1_, ...), custom_call_target="tpu_custom_call" | custom-call | flops 1 | bytes 1 | tf_op jit(solution)/shard_map/pallas_call | solution.py:37
  23.9 3.2 %collective-permute-done.4.refs_0_.refs_1_.refs_4_ = bf16[40,4096]{1,0:T(8,128)(2,1)S(1)} collective-permute-done((bf16[40,4096]{1,0:T(8,128)(2,1)S(1)}, bf16[40,4096]{1,0:T(8,128)(2,1)S(1)}, u32[]{:S(2)}, u32[]{:S(2)}) %collective-permute-start.4) | collective-permute-done | bytes 327712 | tf_op jit(solution)/shard_map/ppermute | solution.py:268
  27.2 1.8 %collective-permute-start.7 = (bf16[40,4096]{1,0:T(8,128)(2,1)S(1)}, bf16[40,4096]{1,0:T(8,128)(2,1)S(1)}, u32[]{:S(2)}, u32[]{:S(2)}) collective-permute-start(bf16[40,4096]{1,0:T(8,128)(2,1)S(1)} %get-tuple-element.111), channel_id=1, source_target_pairs={{0,8},{8,0},{16,24},{24,16},{1,9},{9,1},{17,25},{25,17},{2,10},{10... | collective-permute-start | bytes 983048 | tf_op jit(solution)/shard_map/ppermute | solution.py:268
  29.5 0.8 %shard_map.93 = (f32[40,128]{1,0:T(8,128)S(1)}, bf16[40,128]{1,0:T(8,128)(2,1)S(1)}, bf16[40,128]{1,0:T(8,128)(2,1)S(1)}, f32[8,128]{1,0:T(8,128)S(1)}) custom-call(bf16[128,8192]{1,0:T(8,128)(2,1)S(1)} %get-tuple-element.90.refs_0_, bf16[40,4096]{1,0:T(8,128)(2,1)S(1)} %collective-permute-done.6.refs_1_, ...), custom_call_target="tpu_custom_call" | custom-call | flops 1 | bytes 1 | tf_op jit(solution)/shard_map/pallas_call | solution.py:37
  30.7 1.1 %collective-permute-start.11 = (bf16[40,4096]{1,0:T(8,128)(2,1)S(1)}, bf16[40,4096]{1,0:T(8,128)(2,1)S(1)}, u32[]{:S(2)}, u32[]{:S(2)}) collective-permute-start(bf16[40,4096]{1,0:T(8,128)(2,1)S(1)} %get-tuple-element.125), channel_id=1, source_target_pairs={{0,8},{8,0},{16,24},{24,16},{1,9},{9,1},{17,25},{25,17},{2,10},{10... | collective-permute-start | bytes 983048 | tf_op jit(solution)/shard_map/ppermute | solution.py:268
  31.8 2.6 %collective-permute-start.5 = (f32[80,128]{1,0:T(8,128)S(1)}, f32[80,128]{1,0:T(8,128)S(1)}, u32[]{:S(2)}, u32[]{:S(2)}) collective-permute-start(f32[80,128]{1,0:T(8,128)S(1)} %get-tuple-element.101), channel_id=1, source_target_pairs={{0,4},{1,5},{2,6},{3,7},{4,0},{5,1},{6,2},{7,3},{8,12},{9,13},{10,... | collective-permute-start | bytes 122888 | tf_op jit(solution)/shard_map/ppermute | solution.py:268
  34.4 2.3 %collective-permute-done.5.refs_6_ = f32[80,128]{1,0:T(8,128)S(1)} collective-permute-done((f32[80,128]{1,0:T(8,128)S(1)}, f32[80,128]{1,0:T(8,128)S(1)}, u32[]{:S(2)}, u32[]{:S(2)}) %collective-permute-start.5) | collective-permute-done | bytes 40992 | tf_op jit(solution)/shard_map/ppermute | solution.py:268
  38.4 2.9 %collective-permute-start.8 = (f32[40,128]{1,0:T(8,128)S(1)}, f32[40,128]{1,0:T(8,128)S(1)}, u32[]{:S(2)}, u32[]{:S(2)}) collective-permute-start(f32[40,128]{1,0:T(8,128)S(1)} %get-tuple-element.116), channel_id=1, source_target_pairs={{0,4},{1,5},{2,6},{3,7},{4,0},{5,1},{6,2},{7,3},{8,12},{9,13},{10,... | collective-permute-start | bytes 61448 | tf_op jit(solution)/shard_map/ppermute | solution.py:268
  41.2 1.9 %collective-permute-done.8.refs_2_ = f32[40,128]{1,0:T(8,128)S(1)} collective-permute-done((f32[40,128]{1,0:T(8,128)S(1)}, f32[40,128]{1,0:T(8,128)S(1)}, u32[]{:S(2)}, u32[]{:S(2)}) %collective-permute-start.8) | collective-permute-done | bytes 20512 | tf_op jit(solution)/shard_map/ppermute | solution.py:268
  43.6 1.8 %collective-permute-start.15 = (bf16[40,4224]{1,0:T(8,128)(2,1)S(1)}, bf16[40,4224]{1,0:T(8,128)(2,1)S(1)}, u32[]{:S(2)}, u32[]{:S(2)}) collective-permute-start(bf16[40,4224]{1,0:T(8,128)(2,1)S(1)} %get-tuple-element.134), channel_id=1, source_target_pairs={{0,8},{8,0},{16,24},{24,16},{1,9},{9,1},{17,25},{25,17},{2,10},{10... | collective-permute-start | bytes 1013768 | tf_op jit(solution)/shard_map/ppermute | solution.py:268
  45.4 1.0 %shard_map.100 = (bf16[64,2048]{1,0:T(8,128)(2,1)S(1)}, bf16[64,2048]{1,0:T(8,128)(2,1)S(1)}, f32[128,2048]{1,0:T(8,128)S(1)}, f32[8,128]{1,0:T(8,128)S(1)}) custom-call(bf16[40,128]{1,0:T(8,128)(2,1)S(1)} %get-tuple-element.108.refs_0_, bf16[40,128]{1,0:T(8,128)(2,1)S(1)} %get-tuple-element.109.refs_1_, bf16[40,128]{1,0:T(8,128)(2,1)S(1)} %get-tuple-element.118.refs_2_, ...), custom_call_target="tpu_custom_call" | custom-call | flops 1 | bytes 1 | tf_op jit(solution)/shard_map/pallas_call | solution.py:37
  46.8 1.6 %collective-permute-start.13 = (bf16[40,4096]{1,0:T(8,128)(2,1)S(1)}, bf16[40,4096]{1,0:T(8,128)(2,1)S(1)}, u32[]{:S(2)}, u32[]{:S(2)}) collective-permute-start(bf16[40,4096]{1,0:T(8,128)(2,1)S(1)} %get-tuple-element.131), channel_id=1, source_target_pairs={{0,16},{8,24},{16,0},{24,8},{1,17},{9,25},{17,1},{25,9},{2,18},{10... | collective-permute-start | bytes 983048 | tf_op jit(solution)/shard_map/ppermute | solution.py:268
  49.4 1.0 %collective-permute-done.9.refs_1_ = bf16[64,2048]{1,0:T(8,128)(2,1)S(1)} collective-permute-done((bf16[64,2048]{1,0:T(8,128)(2,1)S(1)}, bf16[64,2048]{1,0:T(8,128)(2,1)S(1)}, u32[]{:S(2)}, u32[]{:S(2)}) %collective-permute-start.9) | collective-permute-done | bytes 262176 | tf_op jit(solution)/shard_map/ppermute | solution.py:268
  51.0 2.9 %collective-permute-done.15.refs_2_.refs_4_ = bf16[40,4224]{1,0:T(8,128)(2,1)S(1)} collective-permute-done((bf16[40,4224]{1,0:T(8,128)(2,1)S(1)}, bf16[40,4224]{1,0:T(8,128)(2,1)S(1)}, u32[]{:S(2)}, u32[]{:S(2)}) %collective-permute-start.15) | collective-permute-done | bytes 337952 | tf_op jit(solution)/shard_map/ppermute | solution.py:268
  54.1 1.5 %collective-permute-start.16 = (bf16[40,4224]{1,0:T(8,128)(2,1)S(1)}, bf16[40,4224]{1,0:T(8,128)(2,1)S(1)}, u32[]{:S(2)}, u32[]{:S(2)}) collective-permute-start(bf16[40,4224]{1,0:T(8,128)(2,1)S(1)} %get-tuple-element.142), channel_id=1, source_target_pairs={{0,16},{8,24},{16,0},{24,8},{1,17},{9,25},{17,1},{25,9},{2,18},{10... | collective-permute-start | bytes 1013768 | tf_op jit(solution)/shard_map/ppermute | solution.py:268
  55.6 1.6 %collective-permute-done.14.refs_2_.refs_5_ = bf16[40,3968]{1,0:T(8,128)(2,1)S(1)} collective-permute-done((bf16[40,3968]{1,0:T(8,128)(2,1)S(1)}, bf16[40,3968]{1,0:T(8,128)(2,1)S(1)}, u32[]{:S(2)}, u32[]{:S(2)}) %collective-permute-start.14) | collective-permute-done | bytes 317472 | tf_op jit(solution)/shard_map/ppermute | solution.py:268
  57.5 1.5 %collective-permute-start.17 = (bf16[40,3968]{1,0:T(8,128)(2,1)S(1)}, bf16[40,3968]{1,0:T(8,128)(2,1)S(1)}, u32[]{:S(2)}, u32[]{:S(2)}) collective-permute-start(bf16[40,3968]{1,0:T(8,128)(2,1)S(1)} %get-tuple-element.143), channel_id=1, source_target_pairs={{0,16},{8,24},{16,0},{24,8},{1,17},{9,25},{17,1},{25,9},{2,18},{10... | collective-permute-start | bytes 952328 | tf_op jit(solution)/shard_map/ppermute | solution.py:268
  59.0 1.7 %collective-permute-start.12 = (bf16[128,1024]{1,0:T(8,128)(2,1)S(1)}, bf16[128,1024]{1,0:T(8,128)(2,1)S(1)}, u32[]{:S(2)}, u32[]{:S(2)}) collective-permute-start(bf16[128,1024]{1,0:T(8,128)(2,1)S(1)} %get-tuple-element.129), channel_id=1, source_target_pairs={{0,2},{1,3},{2,0},{3,1},{4,6},{5,7},{6,4},{7,5},{8,10},{9,11},{10,... | collective-permute-start | bytes 786440 | tf_op jit(solution)/shard_map/ppermute | solution.py:268
  60.7 1.0 %shard_map.105 = (f32[20,8192]{1,0:T(8,128)}, f32[8,128]{1,0:T(8,128)S(1)}) custom-call(f32[40,4096]{1,0:T(8,128)S(1)} %get-tuple-element.130.refs_0_, bf16[40,4096]{1,0:T(8,128)(2,1)S(1)} %collective-permute-done.13.refs_3_.refs_1_, bf16[40,4096]{1,0:T(8,128)(2,1)S(1)} %collective-permute-done.11.refs_3_.refs_2_, f32[8,128]{1,0:T(8,128)S(1)} %get-tuple-element.137.refs_3_), custom_call_target="tpu_custom_call" | custom-call | flops 1 | bytes 1 | tf_op jit(solution)/shard_map/pallas_call | solution.py:37
  61.7 3.7 %collective-permute-done.12.refs_1_ = bf16[128,1024]{1,0:T(8,128)(2,1)S(1)} collective-permute-done((bf16[128,1024]{1,0:T(8,128)(2,1)S(1)}, bf16[128,1024]{1,0:T(8,128)(2,1)S(1)}, u32[]{:S(2)}, u32[]{:S(2)}) %collective-permute-start.12) | collective-permute-done | bytes 262176 | tf_op jit(solution)/shard_map/ppermute | solution.py:268
  66.1 2.0 %collective-permute-done.17.refs_3_ = bf16[40,3968]{1,0:T(8,128)(2,1)S(1)} collective-permute-done((bf16[40,3968]{1,0:T(8,128)(2,1)S(1)}, bf16[40,3968]{1,0:T(8,128)(2,1)S(1)}, u32[]{:S(2)}, u32[]{:S(2)}) %collective-permute-start.17) | collective-permute-done | bytes 317472 | tf_op jit(solution)/shard_map/ppermute | solution.py:268
  68.1 1.4 %shard_map.107 = (f32[20,8192]{1,0:T(8,128)}, f32[20,8192]{1,0:T(8,128)}, f32[8,128]{1,0:T(8,128)}) custom-call(f32[40,4224]{1,0:T(8,128)S(1)} %get-tuple-element.140.refs_0_, f32[40,3968]{1,0:T(8,128)S(1)} %get-tuple-element.141.refs_1_, bf16[40,4224]{1,0:T(8,128)(2,1)S(1)} %collective-permute-done.16.refs_2_, ...), custom_call_target="tpu_custom_call" | custom-call | flops 1 | bytes 1 | tf_op jit(solution)/shard_map/pallas_call | solution.py:37
  (28 shorter events, 7.2 us)
Async XLA Ops:
  2.4 11.6 %collective-permute-start.1 = (bf16[40,4096]{1,0:T(8,128)(2,1)S(1)}, bf16[40,4096]{1,0:T(8,128)(2,1)S(1)}, u32[]{:S(2)}, u32[]{:S(2)}) collective-permute-start(bf16[40,4096]{1,0:T(8,128)(2,1)S(1)} %get-tuple-element.77.refs_3_.refs_1_), channel_id=1, source_target_pairs={{0,16},{8,24},{16,0},{24,8},{1,17},{9,25},{17,1},{25,9},{2,18},{10... | collective-permute-start | bytes 983048 | tf_op jit(solution)/shard_map/ppermute | solution.py:268
  5.4 15.6 %collective-permute-start.2 = (bf16[40,4096]{1,0:T(8,128)(2,1)S(1)}, bf16[40,4096]{1,0:T(8,128)(2,1)S(1)}, u32[]{:S(2)}, u32[]{:S(2)}) collective-permute-start(bf16[40,4096]{1,0:T(8,128)(2,1)S(1)} %get-tuple-element.76.refs_2_.refs_1_), channel_id=1, source_target_pairs={{0,16},{8,24},{16,0},{24,8},{1,17},{9,25},{17,1},{25,9},{2,18},{10... | collective-permute-start | bytes 983048 | tf_op jit(solution)/shard_map/ppermute | solution.py:268
  5.5 11.6 %collective-permute-start = (bf16[20,4096]{1,0:T(8,128)(2,1)S(1)}, bf16[20,4096]{1,0:T(8,128)(2,1)S(1)}, u32[]{:S(2)}, u32[]{:S(2)}) collective-permute-start(bf16[20,4096]{1,0:T(8,128)(2,1)S(1)} %get-tuple-element.82), channel_id=1, source_target_pairs={{0,4},{1,5},{2,6},{3,7},{4,0},{5,1},{6,2},{7,3},{8,12},{9,13},{10,... | collective-permute-start | bytes 491528 | tf_op jit(solution)/shard_map/ppermute | solution.py:268
  14.0 9.1 %collective-permute-start.3 = (bf16[40,4096]{1,0:T(8,128)(2,1)S(1)}, bf16[40,4096]{1,0:T(8,128)(2,1)S(1)}, u32[]{:S(2)}, u32[]{:S(2)}) collective-permute-start(bf16[40,4096]{1,0:T(8,128)(2,1)S(1)} %get-tuple-element.91), channel_id=1, source_target_pairs={{0,8},{8,0},{16,24},{24,16},{1,9},{9,1},{17,25},{25,17},{2,10},{10... | collective-permute-start | bytes 983048 | tf_op jit(solution)/shard_map/ppermute | solution.py:268
  17.4 9.8 %collective-permute-start.4 = (bf16[40,4096]{1,0:T(8,128)(2,1)S(1)}, bf16[40,4096]{1,0:T(8,128)(2,1)S(1)}, u32[]{:S(2)}, u32[]{:S(2)}) collective-permute-start(bf16[40,4096]{1,0:T(8,128)(2,1)S(1)} %get-tuple-element.85.refs_1_.refs_3_), channel_id=1, source_target_pairs={{0,16},{8,24},{16,0},{24,8},{1,17},{9,25},{17,1},{25,9},{2,18},{10... | collective-permute-start | bytes 983048 | tf_op jit(solution)/shard_map/ppermute | solution.py:268
  21.0 8.5 %collective-permute-start.6 = (bf16[40,4096]{1,0:T(8,128)(2,1)S(1)}, bf16[40,4096]{1,0:T(8,128)(2,1)S(1)}, u32[]{:S(2)}, u32[]{:S(2)}) collective-permute-start(bf16[40,4096]{1,0:T(8,128)(2,1)S(1)} %get-tuple-element.102), channel_id=1, source_target_pairs={{0,8},{8,0},{16,24},{24,16},{1,9},{9,1},{17,25},{25,17},{2,10},{10... | collective-permute-start | bytes 983048 | tf_op jit(solution)/shard_map/ppermute | solution.py:268
  27.2 10.7 %collective-permute-start.7 = (bf16[40,4096]{1,0:T(8,128)(2,1)S(1)}, bf16[40,4096]{1,0:T(8,128)(2,1)S(1)}, u32[]{:S(2)}, u32[]{:S(2)}) collective-permute-start(bf16[40,4096]{1,0:T(8,128)(2,1)S(1)} %get-tuple-element.111), channel_id=1, source_target_pairs={{0,8},{8,0},{16,24},{24,16},{1,9},{9,1},{17,25},{25,17},{2,10},{10... | collective-permute-start | bytes 983048 | tf_op jit(solution)/shard_map/ppermute | solution.py:268
  30.7 15.7 %collective-permute-start.11 = (bf16[40,4096]{1,0:T(8,128)(2,1)S(1)}, bf16[40,4096]{1,0:T(8,128)(2,1)S(1)}, u32[]{:S(2)}, u32[]{:S(2)}) collective-permute-start(bf16[40,4096]{1,0:T(8,128)(2,1)S(1)} %get-tuple-element.125), channel_id=1, source_target_pairs={{0,8},{8,0},{16,24},{24,16},{1,9},{9,1},{17,25},{25,17},{2,10},{10... | collective-permute-start | bytes 983048 | tf_op jit(solution)/shard_map/ppermute | solution.py:268
  31.8 4.9 %collective-permute-start.5 = (f32[80,128]{1,0:T(8,128)S(1)}, f32[80,128]{1,0:T(8,128)S(1)}, u32[]{:S(2)}, u32[]{:S(2)}) collective-permute-start(f32[80,128]{1,0:T(8,128)S(1)} %get-tuple-element.101), channel_id=1, source_target_pairs={{0,4},{1,5},{2,6},{3,7},{4,0},{5,1},{6,2},{7,3},{8,12},{9,13},{10,... | collective-permute-start | bytes 122888 | tf_op jit(solution)/shard_map/ppermute | solution.py:268
  38.4 4.7 %collective-permute-start.8 = (f32[40,128]{1,0:T(8,128)S(1)}, f32[40,128]{1,0:T(8,128)S(1)}, u32[]{:S(2)}, u32[]{:S(2)}) collective-permute-start(f32[40,128]{1,0:T(8,128)S(1)} %get-tuple-element.116), channel_id=1, source_target_pairs={{0,4},{1,5},{2,6},{3,7},{4,0},{5,1},{6,2},{7,3},{8,12},{9,13},{10,... | collective-permute-start | bytes 61448 | tf_op jit(solution)/shard_map/ppermute | solution.py:268
  43.6 10.2 %collective-permute-start.15 = (bf16[40,4224]{1,0:T(8,128)(2,1)S(1)}, bf16[40,4224]{1,0:T(8,128)(2,1)S(1)}, u32[]{:S(2)}, u32[]{:S(2)}) collective-permute-start(bf16[40,4224]{1,0:T(8,128)(2,1)S(1)} %get-tuple-element.134), channel_id=1, source_target_pairs={{0,8},{8,0},{16,24},{24,16},{1,9},{9,1},{17,25},{25,17},{2,10},{10... | collective-permute-start | bytes 1013768 | tf_op jit(solution)/shard_map/ppermute | solution.py:268
  46.8 10.4 %collective-permute-start.13 = (bf16[40,4096]{1,0:T(8,128)(2,1)S(1)}, bf16[40,4096]{1,0:T(8,128)(2,1)S(1)}, u32[]{:S(2)}, u32[]{:S(2)}) collective-permute-start(bf16[40,4096]{1,0:T(8,128)(2,1)S(1)} %get-tuple-element.131), channel_id=1, source_target_pairs={{0,16},{8,24},{16,0},{24,8},{1,17},{9,25},{17,1},{25,9},{2,18},{10... | collective-permute-start | bytes 983048 | tf_op jit(solution)/shard_map/ppermute | solution.py:268
  48.4 8.8 %collective-permute-start.14 = (bf16[40,3968]{1,0:T(8,128)(2,1)S(1)}, bf16[40,3968]{1,0:T(8,128)(2,1)S(1)}, u32[]{:S(2)}, u32[]{:S(2)}) collective-permute-start(bf16[40,3968]{1,0:T(8,128)(2,1)S(1)} %get-tuple-element.133), channel_id=1, source_target_pairs={{0,8},{8,0},{16,24},{24,16},{1,9},{9,1},{17,25},{25,17},{2,10},{10... | collective-permute-start | bytes 952328 | tf_op jit(solution)/shard_map/ppermute | solution.py:268
  48.9 1.5 %collective-permute-start.9 = (bf16[64,2048]{1,0:T(8,128)(2,1)S(1)}, bf16[64,2048]{1,0:T(8,128)(2,1)S(1)}, u32[]{:S(2)}, u32[]{:S(2)}) collective-permute-start(bf16[64,2048]{1,0:T(8,128)(2,1)S(1)} %get-tuple-element.123), channel_id=1, source_target_pairs={{0,1},{1,0},{2,3},{3,2},{4,5},{5,4},{6,7},{7,6},{8,9},{9,8},{10,11... | collective-permute-start | bytes 786440 | tf_op jit(solution)/shard_map/ppermute | solution.py:268
  48.9 1.9 %collective-permute-start.10 = (bf16[64,2048]{1,0:T(8,128)(2,1)S(1)}, bf16[64,2048]{1,0:T(8,128)(2,1)S(1)}, u32[]{:S(2)}, u32[]{:S(2)}) collective-permute-start(bf16[64,2048]{1,0:T(8,128)(2,1)S(1)} %get-tuple-element.124), channel_id=1, source_target_pairs={{0,1},{1,0},{2,3},{3,2},{4,5},{5,4},{6,7},{7,6},{8,9},{9,8},{10,11... | collective-permute-start | bytes 786440 | tf_op jit(solution)/shard_map/ppermute | solution.py:268
  54.1 14.0 %collective-permute-start.16 = (bf16[40,4224]{1,0:T(8,128)(2,1)S(1)}, bf16[40,4224]{1,0:T(8,128)(2,1)S(1)}, u32[]{:S(2)}, u32[]{:S(2)}) collective-permute-start(bf16[40,4224]{1,0:T(8,128)(2,1)S(1)} %get-tuple-element.142), channel_id=1, source_target_pairs={{0,16},{8,24},{16,0},{24,8},{1,17},{9,25},{17,1},{25,9},{2,18},{10... | collective-permute-start | bytes 1013768 | tf_op jit(solution)/shard_map/ppermute | solution.py:268
  57.5 10.6 %collective-permute-start.17 = (bf16[40,3968]{1,0:T(8,128)(2,1)S(1)}, bf16[40,3968]{1,0:T(8,128)(2,1)S(1)}, u32[]{:S(2)}, u32[]{:S(2)}) collective-permute-start(bf16[40,3968]{1,0:T(8,128)(2,1)S(1)} %get-tuple-element.143), channel_id=1, source_target_pairs={{0,16},{8,24},{16,0},{24,8},{1,17},{9,25},{17,1},{25,9},{2,18},{10... | collective-permute-start | bytes 952328 | tf_op jit(solution)/shard_map/ppermute | solution.py:268
  59.0 6.4 %collective-permute-start.12 = (bf16[128,1024]{1,0:T(8,128)(2,1)S(1)}, bf16[128,1024]{1,0:T(8,128)(2,1)S(1)}, u32[]{:S(2)}, u32[]{:S(2)}) collective-permute-start(bf16[128,1024]{1,0:T(8,128)(2,1)S(1)} %get-tuple-element.129), channel_id=1, source_target_pairs={{0,2},{1,3},{2,0},{3,1},{4,6},{5,7},{6,4},{7,5},{8,10},{9,11},{10,... | collective-permute-start | bytes 786440 | tf_op jit(solution)/shard_map/ppermute | solution.py:268

commit v5 on v4

--- a/solution.py
+++ b/solution.py
@@ -11,7 +11,8 @@
 NT = (((1,), (1,)), ((), ()))
 TN = (((0,), (0,)), ((), ()))
 TILE = 512
-SWAP = 4
+SWAP = 1
+BITS = (2, 4)
 
 
 def dot(left, right, dims):
@@ -85,7 +86,7 @@
     return [(SWAP * width * j, 2 * SWAP * width * j) for j in range(wide // (2 * SWAP * width))]
 
 
-def packed(width, gate, up, down, high, low, keep, send, gate_here, up_here, down_here, sems):
+def packed(gate, up, down, high, low, both, gate_here, up_here, down_here, sems):
     copies = [
         pltpu.make_async_copy(there, here, sems.at[k])
         for k, (there, here) in enumerate(((gate, gate_here), (up, up_here), (down, down_here)))
@@ -98,15 +99,7 @@
     stacked(high, gate_here, up_here, half, half)
     stacked(low, gate_here, up_here)
     copies[2].wait()
-
-    def run(mine):
-        for near, there in runs(width, 2 * half):
-            here = slice(near, near + SWAP * width)
-            for out, which in ((keep, mine), (send, 1 - mine)):
-                at = there + SWAP * width * which
-                out[:, here] = down_here[:, at : at + SWAP * width]
-
-    either(tensor_bit(SWAP), run)
+    stacked(both, down_here, down_here, 0, half)
 
 
 def project_tiles(x, low, high):
@@ -139,32 +132,45 @@
     copies[1].wait()
 
 
-def part_of(width, g, down, hid_b, part, out):
-    rows, wide = down.shape[0] // 2, g.shape[1]
-    tile = min(SWAP * width, 1024)
+def joined(width, ours, theirs, out):
+    rows, half = ours.shape[0] // 2, ours.shape[1]
+    shape = (2 * rows, 2 * rows)
+    to, from_ = lax.broadcasted_iota(jnp.int32, shape, 0), lax.broadcasted_iota(jnp.int32, shape, 1)
+
+    def moved(first_from, first_to):
+        wanted = (to - first_to == from_ - first_from) & (to >= first_to) & (to < first_to + rows)
+        return wanted.astype(F32).astype(BF)
+
+    places = [(moved(start, 0), moved(start, rows)) for start in (0, rows)]
+    tile = min(SWAP * width, TILE)
 
     def run(mine):
-        total = jnp.zeros(part.shape, F32)
-        for near, there in runs(width, wide):
+        for near, there in runs(width, 2 * half):
             for at in range(0, SWAP * width, tile):
-                far = there + SWAP * width * mine + at
-                total += dot(down[:, near + at : near + at + tile], g[:, far : far + tile], NT)
-        part[...] = total
-        out[...] = jnp.where(top_rows(total), pltpu.roll(total, rows, 0), hid_b[...].astype(F32))
+                column = there + SWAP * width * mine + at
+                cut = slice(column % half, column % half + tile)
+                above, below = places[column // half]
+                value = dot(above, ours[:, cut], NN) + dot(below, theirs[:, cut], NN)
+                out[:, near + at : near + at + tile] = value.astype(BF)
 
     either(tensor_bit(SWAP), run)
 
 
-def finish(both, part, got, hid_a, pair, hid_pair):
-    rows = both.shape[0] // 2
-    gate, got = both[...], got[...]
-    dhid = part[...] + got
+def derive(g, down, both, pair):
+    rows, half = down.shape[0] // 2, down.shape[1]
+    tile = min(half, 1024)
+    low = jnp.zeros(both.shape, F32)
+    high = jnp.zeros(both.shape, F32)
+    for at in range(0, half, tile):
+        cut = slice(at, at + tile)
+        low += dot(down[:, cut], g[:, cut], NT)
+        high += dot(down[:, cut], g[:, half + at : half + at + tile], NT)
+    dhid = low + pltpu.roll(high, rows, 0)
+    gate = both[...]
     sig = jax.nn.sigmoid(gate)
     dgate = dhid * pltpu.roll(gate, rows, 0) * sig * (1.0 + gate * (1.0 - sig))
     dup = pltpu.roll(dhid * (gate * sig), rows, 0)
-    first = top_rows(gate)
-    pair[...] = jnp.where(first, dgate, dup).astype(BF)
-    hid_pair[...] = jnp.where(first, hid_a[...].astype(F32), got).astype(BF)
+    pair[...] = jnp.where(top_rows(gate), dgate, dup).astype(BF)
 
 
 def down_columns(g, hid_a, hid_b, at, half):
@@ -217,8 +223,7 @@
 
 
 def output_sums(width, *refs):
-    hids, downs, (send_a, send_b, keep) = refs[:3], refs[3:6], refs[6:]
-    part = send_a.shape[0]
+    hids, downs, (send, keep) = refs[:3], refs[3:6], refs[6:]
     tile = min(width, TILE)
 
     def run(mine):
@@ -227,40 +232,32 @@
                 for at in range(0, width, tile):
                     cols = slice((2 * block + which) * width + at, (2 * block + which) * width + at + tile)
                     here = slice(block * width + at, block * width + at + tile)
-                    total = sum(dot(hid[...], down[:, cols], TN) for hid, down in zip(hids, downs))
+                    total = sum(dot(hid, down[:, cols], TN) for hid, down in zip(hids, downs))
                     if which == mine:
                         keep[:, here] = total
                     else:
-                        send_a[:, here] = total[:part].astype(BF)
-                        send_b[:, here] = total[part:].astype(BF)
-
-    either(tensor_bit(1), run)
-
-
-def halved(bit, width, keep, *refs):
-    got, (send, left) = refs[:-2], refs[-2:]
+                        send[:, here] = total.astype(BF)
+
+    either(tensor_bit(BITS[0]), run)
+
+
+def halved(bit, width, keep, got, send, left):
     tile = min(width, TILE)
-    part = keep.shape[0] // len(got)
 
     def run(mine):
         for block in range(left.shape[1] // width):
             for out, which in ((send, 1 - mine), (left, mine)):
                 for at in range(0, width, tile):
                     cols = slice((2 * block + which) * width + at, (2 * block + which) * width + at + tile)
-                    here = slice(block * width + at, block * width + at + tile)
-                    for k, piece in enumerate(got):
-                        rows = slice(k * part, (k + 1) * part)
-                        out[rows, here] = (keep[rows, cols] + piece[:, cols].astype(F32)).astype(out.dtype)
+                    value = keep[:, cols] + got[:, cols].astype(F32)
+                    out[:, block * width + at : block * width + at + tile] = value.astype(out.dtype)
 
     either(tensor_bit(bit), run)
 
 
-def final_output(keep, *refs):
-    got, out = refs[:-1], refs[-1]
-    part = keep.shape[0] // len(got)
-    for k, piece in enumerate(got):
-        rows = slice(k * part, (k + 1) * part)
-        out[rows, :] = (keep[rows, :] + piece[...].astype(F32)).astype(BF)
+def final_output(keep, got, out, end):
+    out[...] = (keep[...] + got[...].astype(F32)).astype(BF)
+    end[...] = jnp.zeros_like(end)
 
 
 def exchanged(value, axis, bit):
@@ -277,10 +274,10 @@
     rows, wide = gate_weight.shape
     half, both_rows, tokens = wide // 2, 2 * rows, x.shape[0]
     count = lax.axis_size("tensor")
-    assert count > SWAP and count & (count - 1) == 0
+    assert count > BITS[1] and count & (count - 1) == 0
     width = wide // count
     four = lax.axis_size("section") == 4
-    piece, narrow = ((both_rows, half), BF), ((rows, half), BF)
+    piece = ((both_rows, half), BF)
     small, small_bf = ((both_rows, tokens), F32), ((both_rows, tokens), BF)
     step = Steps()
 
@@ -293,10 +290,10 @@
     def one_hop(value):
         return exchanged(value, "section", 2) if four else ring_passed(value, 1)
 
-    def relay(here, value):
+    def relay(here, value, also=()):
         if not four:
             return ring_passed(here, 1)
-        return exchanged(step(picked, piece, [here, value]), "section", 1)
+        return exchanged(step(picked, piece, [here, value], also), "section", 1)
 
     def outward(value):
         return exchanged(value, "section", 1) if four else ring_passed(value, -1)
@@ -306,16 +303,17 @@
 
     own, first, second = [None] * 3, [None] * 3, [None] * 3
     held = pltpu.VMEM((rows, wide), BF)
-    own[1], own[0], down_keep, down_send = step(
-        with_width(packed),
-        [piece, piece, narrow, narrow],
+    own[1], own[0], own[2] = step(
+        packed,
+        [piece, piece, piece],
         [gate_weight, up_weight, down_weight],
         far=3,
         scratch=[held, held, held, pltpu.SemaphoreType.DMA((3,))],
     )
     first[1] = one_hop(own[1])
     first[0] = one_hop(own[0])
-    down_got = exchanged(down_send, "tensor", SWAP)
+    first[2] = one_hop(own[2])
+    theirs = [exchanged(own[2], "tensor", SWAP), None, None]
     x, g, both_own, *hid_own = step(
         project_first,
         [(x.shape, BF), (g.shape, BF), small, small_bf, small_bf],
@@ -323,45 +321,38 @@
         far=2,
         scratch=[pltpu.SemaphoreType.DMA((2,))],
     )
-    second[1] = relay(first[1], own[1])
-
-    def joined(keep, got, out):
-        stacked(out, keep, got)
-
-    own[2] = step(joined, piece, [down_keep, down_got])
-    first[2] = one_hop(own[2])
-    part_own, part_out = step(with_width(part_of), [small, small], [g, own[2], hid_own[1]])
-    second[0] = relay(first[0], own[0])
-    both_first, *hid_first = step(project, [small, small_bf, small_bf], [x, first[0], first[1]], also=[second[1]])
-    second[2] = relay(first[2], own[2])
-
-    def part_two(gr, down, hid_b, earlier, part, out):
-        out[:both_rows, :] = earlier[...]
-        part_of(width, gr, down, hid_b, part, out.at[both_rows:, :])
-
-    part_first, part_out = step(
-        part_two, [small, ((2 * both_rows, tokens), F32)], [g, first[2], hid_first[1], part_out]
-    )
-    part_got = exchanged(part_out, "tensor", SWAP)
-    both_second, *hid_second = step(project, [small, small_bf, small_bf], [x, second[0], second[1]])
-    side_down = outward(step(sent_down, piece, [g, *hid_second]))
-
-    def finish_two(both_a, part_a, hid_a, both_b, part_b, hid_b, got, pair_a, out_a, pair_b, out_b):
-        finish(both_a, part_a, got.at[:both_rows, :], hid_a, pair_a, out_a)
-        finish(both_b, part_b, got.at[both_rows:, :], hid_b, pair_b, out_b)
-
-    pair_own, wide_own, pair_first, wide_first = step(
-        finish_two, [small_bf] * 4, [both_own, part_own, hid_own[0], both_first, part_first, hid_first[0], part_got]
-    )
+    pair_own = step(derive, small_bf, [g, own[2], both_own])
     low_columns = half + 128
     low_shape, high_shape = (both_rows, low_columns), (both_rows, wide - low_columns)
     grads_f32 = [(low_shape, F32), (high_shape, F32), ((both_rows, half), F32)]
     own_low, own_high, own_down = step(own_grads, grads_f32, [x, g, *hid_own, pair_own])
-    part_second, part_out = step(with_width(part_of), [small, small], [g, second[2], hid_second[1]])
-    part_got = exchanged(part_out, "tensor", SWAP)
-    pair_second, wide_second = step(finish, [small_bf] * 2, [both_second, part_second, part_got, hid_second[0]])
+    second[1] = relay(first[1], own[1])
+
+    second[0] = relay(first[0], own[0])
+    second[2] = ring_passed(own[2] if four else first[2], 1)
+    also = [second[1], second[2]] if four else [second[1]]
+    both_first, *hid_first = step(project, [small, small_bf, small_bf], [x, first[0], first[1]], also=also)
+    join = with_width(joined)
+    wide_own = step(join, piece, [own[2], theirs[0]])
+    theirs[2] = exchanged(second[2], "tensor", SWAP)
+    wide_second = step(join, piece, [second[2], theirs[2]])
+    pair_first = step(derive, small_bf, [g, first[2], both_first])
+    both_second, *hid_second = step(project, [small, small_bf, small_bf], [x, second[0], second[1]])
+    held_down, both_second = lax.optimization_barrier((first[2], both_second))
+    theirs[1] = exchanged(held_down, "tensor", SWAP)
+    side_down = outward(step(sent_down, piece, [g, *hid_second]))
+
+
+    def hids_out(a, b, c, out):
+        for k, hid in enumerate((a, b, c)):
+            out[k * both_rows : (k + 1) * both_rows, :] = hid[...].astype(F32)
+
+    hids = step(hids_out, ((3 * both_rows, tokens), F32), [hid_own[1], hid_first[1], hid_second[1]])
+    hids_got = exchanged(hids, "tensor", SWAP)
+    pair_second = step(derive, small_bf, [g, second[2], both_second])
     low, high = step(sent_pair, [(low_shape, BF), (high_shape, BF)], [x, pair_second])
     side_low, side_high = outward(low), outward(high)
+    wide_first = step(join, piece, [first[2], theirs[1]])
 
     def back_down(gr, a, b, side, out):
         odd = is_odd()
@@ -379,13 +370,22 @@
         return body
 
     quarter = wide // 4
-    send_a, send_b, keep = step(
-        with_width(output_sums),
-        [((tokens // 2, quarter), BF), ((tokens // 2, quarter), BF), ((tokens, quarter), F32)],
-        [wide_own, wide_first, wide_second, own[2], first[2], second[2]],
-    )
+
+    def sums(*refs):
+        ours, theirs, downs = refs[:3], refs[3], refs[4:7]
+        hids = [
+            (ours[k][...].astype(F32) + theirs[k * both_rows : (k + 1) * both_rows, :]).astype(BF) for k in range(3)
+        ]
+        output_sums(width, *hids, *downs, *refs[7:])
+
+    send, keep = step(
+        sums,
+        [((tokens, quarter), BF), ((tokens, quarter), F32)],
+        [hid_own[0], hid_first[0], hid_second[0], hids_got, wide_own, wide_first, wide_second],
+    )
+    got = exchanged(send, "tensor", BITS[0])
     back_of_down = backward(step(back_down, piece, [g, *hid_first, side_down]))
-    got = [exchanged(send_a, "tensor", 1), exchanged(send_b, "tensor", 1)]
+    back_of_low = backward(step(back_pair(0), (low_shape, BF), [x, pair_first, side_low]))
 
     def next_half(keep, got, bit):
         cols = keep.shape[1] // 2
@@ -393,13 +393,12 @@
         def body(*refs):
             halved(bit, width, *refs)
 
-        send, keep = step(body, [((tokens, cols), BF), ((tokens, cols), F32)], [keep, *got])
-        return keep, [exchanged(send, "tensor", bit)]
-
-    keep, got = next_half(keep, got, 2)
-    back_of_low = backward(step(back_pair(0), (low_shape, BF), [x, pair_first, side_low]))
+        send, keep = step(body, [((tokens, cols), BF), ((tokens, cols), F32)], [keep, got])
+        return keep, exchanged(send, "tensor", bit)
+
+    keep, got = next_half(keep, got, BITS[1])
     back_of_high = backward(step(back_pair(low_columns), (high_shape, BF), [x, pair_first, side_high], also=[back_of_down]))
-    bit = 2 * SWAP
+    bit = 2 * BITS[1]
     while bit < count:
         keep, got = next_half(keep, got, bit)
         bit *= 2
@@ -426,9 +425,13 @@
 
     whole = ((rows, wide), F32)
     grad_down = step(final_down, whole, [own_down, back_of_down, side_down])
-    output = step(final_output, ((tokens, width), BF), [keep, *got])
+    output, end = step(final_output, [((tokens, width), BF), ((128, 128), F32)], [keep, got])
+    end = exchanged(end, "tensor", SWAP)
     grad_gate, grad_up = step(
-        final_pair, [whole, whole], [own_low, own_high, back_of_low, back_of_high, side_low, side_high]
+        final_pair,
+        [whole, whole],
+        [own_low, own_high, back_of_low, back_of_high, side_low, side_high],
+        also=[end],
     )
     return (output, grad_gate, grad_up, grad_down)
 

time: 69.6 us -> 74.9 us (1.076)
  waiting for transfers between devices: 24.8 us -> 38.1 us
  starting transfers between devices: 29.4 us -> 19.2 us
  Pallas kernels: 14.5 us -> 16.6 us
    ppermute x18, waiting for transfers between devices: 24.8 us -> 38.1 us  [exchanged(): lax.ppermute(value, axis, [(source, source ^ bit) for source in range(cou...]
    ppermute x18, starting transfers between devices: 29.4 us -> 17.7 us  [exchanged(): lax.ppermute(value, axis, [(source, source ^ bit) for source in range(cou...]
    pallas_call x24, Pallas kernels: 14.5 us -> 16.6 us  [__call__(): pl.pallas_call(kernel, out_shape=[jax.ShapeDtypeStruct(*s) for s in shape...]
    ppermute x0 -> x1, starting transfers between devices: none -> 1.49 us  [ring_passed(): lax.ppermute(value, 'section', [(source, (source + steps) % count) for so...]
  transfers between devices with their start and end apart: 18 -> 19, of which waited for: 13 -> 10; matrix products, arithmetic and copies ran while one was open for 0% -> 0% of each run, Pallas kernels for 16% -> 17%
where the time goes in v5:
time: 74.9 us; the launch traced here: 74.8 us
  waiting for transfers between devices  38.1 us (51%)
  starting transfers between devices  19.2 us (26%)
  Pallas kernels  16.6 us (22%)
  between operations  0.85 us (1%)
    ppermute x18, waiting for transfers between devices, exchanged(): lax.ppermute(value, axis, [(source, source ^ bit) for source in range(cou...  38.1 us
    ppermute x18, starting transfers between devices, exchanged(): lax.ppermute(value, axis, [(source, source ^ bit) for source in range(cou...  17.7 us
    pallas_call x24, Pallas kernels, __call__(): pl.pallas_call(kernel, out_shape=[jax.ShapeDtypeStruct(*s) for s in shape...  16.6 us
  transfers between devices with their start and end apart: 19, of which 10 were waited for; matrix products, arithmetic and copies ran while one was open for 0% of the time, Pallas kernels for 17%

profile of v5, /device:TPU:0, one launch (start us, length us, event | category | flops | bytes accessed | tf_op | source)
XLA Modules:
  0.0 74.8 jit_solution(1707431570526976133)
XLA Ops:
  0.6 2.0 %shard_map.84 = (bf16[40,4096]{1,0:T(8,128)(2,1)S(1)}, bf16[40,4096]{1,0:T(8,128)(2,1)S(1)}, bf16[40,4096]{1,0:T(8,128)(2,1)S(1)}, f32[8,128]{1,0:T(8,128)S(1)}) custom-call(bf16[20,8192]{1,0:T(8,128)(2,1)} %refs_0_.2, bf16[20,8192]{1,0:T(8,128)(2,1)} %refs_1_.2, bf16[20,8192]{1,0:T(8,128)(2,1)} %refs_2_.1), custom_call_target="tpu_custom_call" | custom-call | flops 1 | bytes 1 | tf_op jit(solution)/shard_map/pallas_call | solution.py:38
  2.7 3.0 %collective-permute-start.1 = (bf16[40,4096]{1,0:T(8,128)(2,1)S(1)}, bf16[40,4096]{1,0:T(8,128)(2,1)S(1)}, u32[]{:S(2)}, u32[]{:S(2)}) collective-permute-start(bf16[40,4096]{1,0:T(8,128)(2,1)S(1)} %get-tuple-element.71.refs_3_.refs_1_), channel_id=1, source_target_pairs={{0,16},{8,24},{16,0},{24,8},{1,17},{9,25},{17,1},{25,9},{2,18},{10... | collective-permute-start | bytes 983048 | tf_op jit(solution)/shard_map/ppermute | solution.py:265
  5.7 1.5 %collective-permute-start.3 = (bf16[40,4096]{1,0:T(8,128)(2,1)S(1)}, bf16[40,4096]{1,0:T(8,128)(2,1)S(1)}, u32[]{:S(2)}, u32[]{:S(2)}) collective-permute-start(bf16[40,4096]{1,0:T(8,128)(2,1)S(1)} %get-tuple-element.77.refs_1_.refs_0_), channel_id=1, source_target_pairs={{0,8},{8,16},{16,24},{24,0},{1,9},{9,17},{17,25},{25,1},{2,10},{10... | collective-permute-start | bytes 983048 | tf_op jit(solution)/shard_map/ppermute | solution.py:270
  7.2 0.5 collective-permute-start
  7.7 2.4 %shard_map.85 = (bf16[128,8192]{1,0:T(8,128)(2,1)S(1)}, bf16[128,8192]{1,0:T(8,128)(2,1)S(1)}, f32[40,128]{1,0:T(8,128)S(1)}, bf16[40,128]{1,0:T(8,128)(2,1)S(1)...) custom-call(bf16[128,8192]{1,0:T(8,128)(2,1)} %refs_0_.3, bf16[128,8192]{1,0:T(8,128)(2,1)} %refs_1_.3, ...), custom_call_target="tpu_custom_call" | custom-call | flops 1 | bytes 1 | tf_op jit(solution)/shard_map/pallas_call | solution.py:38
  10.2 0.8 %shard_map.86 = (bf16[40,128]{1,0:T(8,128)(2,1)S(1)}, f32[8,128]{1,0:T(8,128)S(1)}) custom-call(bf16[128,8192]{1,0:T(8,128)(2,1)S(1)} %get-tuple-element.75.refs_0_.refs_1_, bf16[40,4096]{1,0:T(8,128)(2,1)S(1)} %get-tuple-element.77.refs_1_.refs_0_, f32[40,128]{1,0:T(8,128)S(1)} %get-tuple-element.78.refs_2_, f32[8,128]{1,0:T(8,128)S(1)} %get-tuple-element.79.refs_3_), custom_call_target="tpu_custom_call" | custom-call | flops 1 | bytes 1 | tf_op jit(solution)/shard_map/pallas_call | solution.py:38
  11.0 0.7 shard_map.87
  11.7 9.6 %collective-permute-done.1.refs_0_.refs_2_ = bf16[40,4096]{1,0:T(8,128)(2,1)S(1)} collective-permute-done((bf16[40,4096]{1,0:T(8,128)(2,1)S(1)}, bf16[40,4096]{1,0:T(8,128)(2,1)S(1)}, u32[]{:S(2)}, u32[]{:S(2)}) %collective-permute-start.1) | collective-permute-done | bytes 327712 | tf_op jit(solution)/shard_map/ppermute | solution.py:265
  22.0 2.0 %collective-permute-start.5 = (bf16[40,4096]{1,0:T(8,128)(2,1)S(1)}, bf16[40,4096]{1,0:T(8,128)(2,1)S(1)}, u32[]{:S(2)}, u32[]{:S(2)}) collective-permute-start(bf16[40,4096]{1,0:T(8,128)(2,1)S(1)} %get-tuple-element.77.refs_1_.refs_0_), channel_id=1, source_target_pairs={{0,16},{8,24},{16,0},{24,8},{1,17},{9,25},{17,1},{25,9},{2,18},{10... | collective-permute-start | bytes 983048 | tf_op jit(solution)/shard_map/ppermute | solution.py:265
  23.9 4.3 %collective-permute-done.refs_0_.refs_1_ = bf16[40,4096]{1,0:T(8,128)(2,1)S(1)} collective-permute-done((bf16[40,4096]{1,0:T(8,128)(2,1)S(1)}, bf16[40,4096]{1,0:T(8,128)(2,1)S(1)}, u32[]{:S(2)}, u32[]{:S(2)}) %collective-permute-start) | collective-permute-done | bytes 327712 | tf_op jit(solution)/shard_map/ppermute | solution.py:265
  28.4 1.0 %collective-permute-done.2.refs_3_.refs_2_ = bf16[40,4096]{1,0:T(8,128)(2,1)S(1)} collective-permute-done((bf16[40,4096]{1,0:T(8,128)(2,1)S(1)}, bf16[40,4096]{1,0:T(8,128)(2,1)S(1)}, u32[]{:S(2)}, u32[]{:S(2)}) %collective-permute-start.2) | collective-permute-done | bytes 327712 | tf_op jit(solution)/shard_map/ppermute | solution.py:265
  29.4 0.8 %shard_map.90 = (f32[40,128]{1,0:T(8,128)S(1)}, bf16[40,128]{1,0:T(8,128)(2,1)S(1)}, bf16[40,128]{1,0:T(8,128)(2,1)S(1)}, f32[8,128]{1,0:T(8,128)S(1)}) custom-call(bf16[128,8192]{1,0:T(8,128)(2,1)S(1)} %get-tuple-element.74.refs_0_, bf16[40,4096]{1,0:T(8,128)(2,1)S(1)} %collective-permute-done.refs_0_.refs_1_, ...), custom_call_target="tpu_custom_call" | custom-call | flops 1 | bytes 1 | tf_op jit(solution)/shard_map/pallas_call | solution.py:38
  31.0 3.5 %collective-permute-done.5.refs_1_.refs_0_ = bf16[40,4096]{1,0:T(8,128)(2,1)S(1)} collective-permute-done((bf16[40,4096]{1,0:T(8,128)(2,1)S(1)}, bf16[40,4096]{1,0:T(8,128)(2,1)S(1)}, u32[]{:S(2)}, u32[]{:S(2)}) %collective-permute-start.5) | collective-permute-done | bytes 327712 | tf_op jit(solution)/shard_map/ppermute | solution.py:265
  34.5 0.8 %shard_map.93 = (bf16[40,128]{1,0:T(8,128)(2,1)S(1)}, f32[8,128]{1,0:T(8,128)S(1)}) custom-call(bf16[128,8192]{1,0:T(8,128)(2,1)S(1)} %get-tuple-element.75.refs_0_.refs_1_, bf16[40,4096]{1,0:T(8,128)(2,1)S(1)} %collective-permute-done.5.refs_1_.refs_0_, f32[40,128]{1,0:T(8,128)S(1)} %get-tuple-element.88.refs_2_, f32[8,128]{1,0:T(8,128)S(1)} %get-tuple-element.91.refs_3_), custom_call_target="tpu_custom_call" | custom-call | flops 1 | bytes 1 | tf_op jit(solution)/shard_map/pallas_call | solution.py:38
  35.3 1.1 %collective-permute-done.4.refs_1_ = bf16[40,4096]{1,0:T(8,128)(2,1)S(1)} collective-permute-done((bf16[40,4096]{1,0:T(8,128)(2,1)S(1)}, bf16[40,4096]{1,0:T(8,128)(2,1)S(1)}, u32[]{:S(2)}, u32[]{:S(2)}) %collective-permute-start.4) | collective-permute-done | bytes 327712 | tf_op jit(solution)/shard_map/ppermute | solution.py:265
  36.5 0.8 %shard_map.94 = (f32[40,128]{1,0:T(8,128)S(1)}, bf16[40,128]{1,0:T(8,128)(2,1)S(1)}, bf16[40,128]{1,0:T(8,128)(2,1)S(1)}, f32[8,128]{1,0:T(8,128)S(1)}) custom-call(bf16[128,8192]{1,0:T(8,128)(2,1)S(1)} %get-tuple-element.74.refs_0_, bf16[40,4096]{1,0:T(8,128)(2,1)S(1)} %collective-permute-done.4.refs_1_, ...), custom_call_target="tpu_custom_call" | custom-call | flops 1 | bytes 1 | tf_op jit(solution)/shard_map/pallas_call | solution.py:38
  38.4 0.8 %shard_map.97 = (bf16[40,128]{1,0:T(8,128)(2,1)S(1)}, f32[8,128]{1,0:T(8,128)S(1)}) custom-call(bf16[128,8192]{1,0:T(8,128)(2,1)S(1)} %get-tuple-element.75.refs_0_.refs_1_, bf16[40,4096]{1,0:T(8,128)(2,1)S(1)} %collective-permute-done.3.refs_4_.refs_0_.refs_1_, f32[40,128]{1,0:T(8,128)S(1)} %get-tuple-element.102.refs_2_, ...), custom_call_target="tpu_custom_call" | custom-call | flops 1 | bytes 1 | tf_op jit(solution)/shard_map/pallas_call | solution.py:38
  40.1 1.0 %shard_map.100 = (bf16[128,2048]{1,0:T(8,128)(2,1)S(1)}, f32[128,2048]{1,0:T(8,128)S(1)}, f32[8,128]{1,0:T(8,128)S(1)}) custom-call(bf16[40,128]{1,0:T(8,128)(2,1)S(1)} %get-tuple-element.73.refs_2_.refs_0_, bf16[40,128]{1,0:T(8,128)(2,1)S(1)} %get-tuple-element.86.refs_1_, bf16[40,128]{1,0:T(8,128)(2,1)S(1)} %get-tuple-element.93.refs_1_.refs_2_, ...), custom_call_target="tpu_custom_call" | custom-call | flops 1 | bytes 1 | tf_op jit(solution)/shard_map/pallas_call | solution.py:38
  41.1 1.5 %collective-permute-start.10 = (bf16[128,2048]{1,0:T(8,128)(2,1)S(1)}, bf16[128,2048]{1,0:T(8,128)(2,1)S(1)}, u32[]{:S(2)}, u32[]{:S(2)}) collective-permute-start(bf16[128,2048]{1,0:T(8,128)(2,1)S(1)} %get-tuple-element.111), channel_id=1, source_target_pairs={{0,2},{1,3},{2,0},{3,1},{4,6},{5,7},{6,4},{7,5},{8,10},{9,11},{10,... | collective-permute-start | bytes 1572872 | tf_op jit(solution)/shard_map/ppermute | solution.py:265
  42.7 1.7 %collective-permute-start.11 = (bf16[40,4224]{1,0:T(8,128)(2,1)S(1)}, bf16[40,4224]{1,0:T(8,128)(2,1)S(1)}, u32[]{:S(2)}, u32[]{:S(2)}) collective-permute-start(bf16[40,4224]{1,0:T(8,128)(2,1)S(1)} %get-tuple-element.113), channel_id=1, source_target_pairs={{0,8},{8,0},{16,24},{24,16},{1,9},{9,1},{17,25},{25,17},{2,10},{10... | collective-permute-start | bytes 1013768 | tf_op jit(solution)/shard_map/ppermute | solution.py:265
  44.3 4.0 %collective-permute-done.12.refs_3_.refs_2_ = bf16[40,4096]{1,0:T(8,128)(2,1)S(1)} collective-permute-done((bf16[40,4096]{1,0:T(8,128)(2,1)S(1)}, bf16[40,4096]{1,0:T(8,128)(2,1)S(1)}, u32[]{:S(2)}, u32[]{:S(2)}) %collective-permute-start.12) | collective-permute-done | bytes 327712 | tf_op jit(solution)/shard_map/ppermute | solution.py:265
  48.8 1.6 %collective-permute-start.14 = (bf16[40,4096]{1,0:T(8,128)(2,1)S(1)}, bf16[40,4096]{1,0:T(8,128)(2,1)S(1)}, u32[]{:S(2)}, u32[]{:S(2)}) collective-permute-start(bf16[40,4096]{1,0:T(8,128)(2,1)S(1)} %get-tuple-element.121), channel_id=1, source_target_pairs={{0,16},{8,24},{16,0},{24,8},{1,17},{9,25},{17,1},{25,9},{2,18},{10... | collective-permute-start | bytes 983048 | tf_op jit(solution)/shard_map/ppermute | solution.py:265
  50.6 5.0 %collective-permute-done.11.refs_2_.refs_4_ = bf16[40,4224]{1,0:T(8,128)(2,1)S(1)} collective-permute-done((bf16[40,4224]{1,0:T(8,128)(2,1)S(1)}, bf16[40,4224]{1,0:T(8,128)(2,1)S(1)}, u32[]{:S(2)}, u32[]{:S(2)}) %collective-permute-start.11) | collective-permute-done | bytes 337952 | tf_op jit(solution)/shard_map/ppermute | solution.py:265
  55.9 1.6 %collective-permute-start.16 = (bf16[40,4224]{1,0:T(8,128)(2,1)S(1)}, bf16[40,4224]{1,0:T(8,128)(2,1)S(1)}, u32[]{:S(2)}, u32[]{:S(2)}) collective-permute-start(bf16[40,4224]{1,0:T(8,128)(2,1)S(1)} %get-tuple-element.129), channel_id=1, source_target_pairs={{0,16},{8,24},{16,0},{24,8},{1,17},{9,25},{17,1},{25,9},{2,18},{10... | collective-permute-start | bytes 1013768 | tf_op jit(solution)/shard_map/ppermute | solution.py:265
  57.6 2.6 %collective-permute-start.13 = (bf16[128,1024]{1,0:T(8,128)(2,1)S(1)}, bf16[128,1024]{1,0:T(8,128)(2,1)S(1)}, u32[]{:S(2)}, u32[]{:S(2)}) collective-permute-start(bf16[128,1024]{1,0:T(8,128)(2,1)S(1)} %get-tuple-element.119), channel_id=1, source_target_pairs={{0,4},{1,5},{2,6},{3,7},{4,0},{5,1},{6,2},{7,3},{8,12},{9,13},{10,... | collective-permute-start | bytes 786440 | tf_op jit(solution)/shard_map/ppermute | solution.py:265
  60.2 1.8 %collective-permute-done.15.refs_2_.refs_5_ = bf16[40,3968]{1,0:T(8,128)(2,1)S(1)} collective-permute-done((bf16[40,3968]{1,0:T(8,128)(2,1)S(1)}, bf16[40,3968]{1,0:T(8,128)(2,1)S(1)}, u32[]{:S(2)}, u32[]{:S(2)}) %collective-permute-start.15) | collective-permute-done | bytes 317472 | tf_op jit(solution)/shard_map/ppermute | solution.py:265
  62.3 1.6 %collective-permute-start.17 = (bf16[40,3968]{1,0:T(8,128)(2,1)S(1)}, bf16[40,3968]{1,0:T(8,128)(2,1)S(1)}, u32[]{:S(2)}, u32[]{:S(2)}) collective-permute-start(bf16[40,3968]{1,0:T(8,128)(2,1)S(1)} %get-tuple-element.130), channel_id=1, source_target_pairs={{0,16},{8,24},{16,0},{24,8},{1,17},{9,25},{17,1},{25,9},{2,18},{10... | collective-permute-start | bytes 952328 | tf_op jit(solution)/shard_map/ppermute | solution.py:265
  63.9 1.0 %shard_map.105 = (f32[20,8192]{1,0:T(8,128)}, f32[8,128]{1,0:T(8,128)S(1)}) custom-call(f32[40,4096]{1,0:T(8,128)S(1)} %get-tuple-element.120.refs_0_, bf16[40,4096]{1,0:T(8,128)(2,1)S(1)} %collective-permute-done.14.refs_3_.refs_1_, bf16[40,4096]{1,0:T(8,128)(2,1)S(1)} %collective-permute-done.12.refs_3_.refs_2_, f32[8,128]{1,0:T(8,128)S(1)} %get-tuple-element.124.refs_3_), custom_call_target="tpu_custom_call" | custom-call | flops 1 | bytes 1 | tf_op jit(solution)/shard_map/pallas_call | solution.py:38
  64.9 6.5 %collective-permute-done.13.refs_1_ = bf16[128,1024]{1,0:T(8,128)(2,1)S(1)} collective-permute-done((bf16[128,1024]{1,0:T(8,128)(2,1)S(1)}, bf16[128,1024]{1,0:T(8,128)(2,1)S(1)}, u32[]{:S(2)}, u32[]{:S(2)}) %collective-permute-start.13) | collective-permute-done | bytes 262176 | tf_op jit(solution)/shard_map/ppermute | solution.py:265
  71.4 0.7 %shard_map.106 = (bf16[128,1024]{1,0:T(8,128)(2,1)}, f32[128,128]{1,0:T(8,128)S(1)}, f32[8,128]{1,0:T(8,128)S(1)}) custom-call(f32[128,1024]{1,0:T(8,128)S(1)} %get-tuple-element.118.refs_0_, bf16[128,1024]{1,0:T(8,128)(2,1)S(1)} %collective-permute-done.13.refs_1_, f32[8,128]{1,0:T(8,128)S(1)} %get-tuple-element.125.refs_2_), custom_call_target="tpu_custom_call" | custom-call | flops 1 | bytes 1 | tf_op jit(solution)/shard_map/pallas_call | solution.py:38
  72.2 1.2 %collective-permute-done.18.refs_6_ = f32[128,128]{1,0:T(8,128)S(1)} collective-permute-done((f32[128,128]{1,0:T(8,128)S(1)}, f32[128,128]{1,0:T(8,128)S(1)}, u32[]{:S(2)}, u32[]{:S(2)}) %collective-permute-start.18) | collective-permute-done | bytes 65568 | tf_op jit(solution)/shard_map/ppermute | solution.py:265
  73.4 1.4 %shard_map.107 = (f32[20,8192]{1,0:T(8,128)}, f32[20,8192]{1,0:T(8,128)}, f32[8,128]{1,0:T(8,128)}) custom-call(f32[40,4224]{1,0:T(8,128)S(1)} %get-tuple-element.127.refs_0_, f32[40,3968]{1,0:T(8,128)S(1)} %get-tuple-element.128.refs_1_, bf16[40,4224]{1,0:T(8,128)(2,1)S(1)} %collective-permute-done.16.refs_2_, ...), custom_call_target="tpu_custom_call" | custom-call | flops 1 | bytes 1 | tf_op jit(solution)/shard_map/pallas_call | solution.py:38
  (30 shorter events, 4.8 us)
Async XLA Ops:
  2.7 18.6 %collective-permute-start.1 = (bf16[40,4096]{1,0:T(8,128)(2,1)S(1)}, bf16[40,4096]{1,0:T(8,128)(2,1)S(1)}, u32[]{:S(2)}, u32[]{:S(2)}) collective-permute-start(bf16[40,4096]{1,0:T(8,128)(2,1)S(1)} %get-tuple-element.71.refs_3_.refs_1_), channel_id=1, source_target_pairs={{0,16},{8,24},{16,0},{24,8},{1,17},{9,25},{17,1},{25,9},{2,18},{10... | collective-permute-start | bytes 983048 | tf_op jit(solution)/shard_map/ppermute | solution.py:265
  5.7 15.8 %collective-permute-start.3 = (bf16[40,4096]{1,0:T(8,128)(2,1)S(1)}, bf16[40,4096]{1,0:T(8,128)(2,1)S(1)}, u32[]{:S(2)}, u32[]{:S(2)}) collective-permute-start(bf16[40,4096]{1,0:T(8,128)(2,1)S(1)} %get-tuple-element.77.refs_1_.refs_0_), channel_id=1, source_target_pairs={{0,8},{8,16},{16,24},{24,0},{1,9},{9,17},{17,25},{25,1},{2,10},{10... | collective-permute-start | bytes 983048 | tf_op jit(solution)/shard_map/ppermute | solution.py:270
  7.2 21.1 %collective-permute-start = (bf16[40,4096]{1,0:T(8,128)(2,1)S(1)}, bf16[40,4096]{1,0:T(8,128)(2,1)S(1)}, u32[]{:S(2)}, u32[]{:S(2)}) collective-permute-start(bf16[40,4096]{1,0:T(8,128)(2,1)S(1)} %get-tuple-element.70.refs_2_.refs_1_), channel_id=1, source_target_pairs={{0,16},{8,24},{16,0},{24,8},{1,17},{9,25},{17,1},{25,9},{2,18},{10... | collective-permute-start | bytes 983048 | tf_op jit(solution)/shard_map/ppermute | solution.py:265
  21.3 8.1 %collective-permute-start.2 = (bf16[40,4096]{1,0:T(8,128)(2,1)S(1)}, bf16[40,4096]{1,0:T(8,128)(2,1)S(1)}, u32[]{:S(2)}, u32[]{:S(2)}) collective-permute-start(bf16[40,4096]{1,0:T(8,128)(2,1)S(1)} %get-tuple-element.83), channel_id=1, source_target_pairs={{0,8},{8,0},{16,24},{24,16},{1,9},{9,1},{17,25},{25,17},{2,10},{10... | collective-permute-start | bytes 983048 | tf_op jit(solution)/shard_map/ppermute | solution.py:265
  21.4 8.9 %collective-permute-start.7 = (bf16[40,4096]{1,0:T(8,128)(2,1)S(1)}, bf16[40,4096]{1,0:T(8,128)(2,1)S(1)}, u32[]{:S(2)}, u32[]{:S(2)}) collective-permute-start(bf16[40,4096]{1,0:T(8,128)(2,1)S(1)} %get-tuple-element.77.refs_1_.refs_0_), channel_id=1, source_target_pairs={{0,1},{1,0},{2,3},{3,2},{4,5},{5,4},{6,7},{7,6},{8,9},{9,8},{10,11... | collective-permute-start | bytes 983048 | tf_op jit(solution)/shard_map/ppermute | solution.py:265
  21.5 9.2 %collective-permute-start.6 = (bf16[40,4096]{1,0:T(8,128)(2,1)S(1)}, bf16[40,4096]{1,0:T(8,128)(2,1)S(1)}, u32[]{:S(2)}, u32[]{:S(2)}) collective-permute-start(bf16[40,4096]{1,0:T(8,128)(2,1)S(1)} %collective-permute-done.3.refs_4_.refs_0_.refs_1_), channel_id=1, source_target_pairs={{0,1},{1,0},{2,3},{3,2},{4,5},{5,4},{6,7},{7,6},{8,9},{9,8},{10,11... | collective-permute-start | bytes 983048 | tf_op jit(solution)/shard_map/ppermute | solution.py:265
  22.0 12.5 %collective-permute-start.5 = (bf16[40,4096]{1,0:T(8,128)(2,1)S(1)}, bf16[40,4096]{1,0:T(8,128)(2,1)S(1)}, u32[]{:S(2)}, u32[]{:S(2)}) collective-permute-start(bf16[40,4096]{1,0:T(8,128)(2,1)S(1)} %get-tuple-element.77.refs_1_.refs_0_), channel_id=1, source_target_pairs={{0,16},{8,24},{16,0},{24,8},{1,17},{9,25},{17,1},{25,9},{2,18},{10... | collective-permute-start | bytes 983048 | tf_op jit(solution)/shard_map/ppermute | solution.py:265
  28.3 8.1 %collective-permute-start.4 = (bf16[40,4096]{1,0:T(8,128)(2,1)S(1)}, bf16[40,4096]{1,0:T(8,128)(2,1)S(1)}, u32[]{:S(2)}, u32[]{:S(2)}) collective-permute-start(bf16[40,4096]{1,0:T(8,128)(2,1)S(1)} %get-tuple-element.87), channel_id=1, source_target_pairs={{0,8},{8,0},{16,24},{24,16},{1,9},{9,1},{17,25},{25,17},{2,10},{10... | collective-permute-start | bytes 983048 | tf_op jit(solution)/shard_map/ppermute | solution.py:265
  37.3 2.4 %collective-permute-start.9 = (bf16[40,4096]{1,0:T(8,128)(2,1)S(1)}, bf16[40,4096]{1,0:T(8,128)(2,1)S(1)}, u32[]{:S(2)}, u32[]{:S(2)}) collective-permute-start(bf16[40,4096]{1,0:T(8,128)(2,1)S(1)} %collective-permute-done.5.refs_1_.refs_0_), channel_id=1, source_target_pairs={{0,1},{1,0},{2,3},{3,2},{4,5},{5,4},{6,7},{7,6},{8,9},{9,8},{10,11... | collective-permute-start | bytes 983048 | tf_op jit(solution)/shard_map/ppermute | solution.py:265
  37.8 10.6 %collective-permute-start.12 = (bf16[40,4096]{1,0:T(8,128)(2,1)S(1)}, bf16[40,4096]{1,0:T(8,128)(2,1)S(1)}, u32[]{:S(2)}, u32[]{:S(2)}) collective-permute-start(bf16[40,4096]{1,0:T(8,128)(2,1)S(1)} %get-tuple-element.114), channel_id=1, source_target_pairs={{0,8},{8,0},{16,24},{24,16},{1,9},{9,1},{17,25},{25,17},{2,10},{10... | collective-permute-start | bytes 983048 | tf_op jit(solution)/shard_map/ppermute | solution.py:265
  38.1 2.0 %collective-permute-start.8 = (f32[120,128]{1,0:T(8,128)S(1)}, f32[120,128]{1,0:T(8,128)S(1)}, u32[]{:S(2)}, u32[]{:S(2)}) collective-permute-start(f32[120,128]{1,0:T(8,128)S(1)} %get-tuple-element.98), channel_id=1, source_target_pairs={{0,1},{1,0},{2,3},{3,2},{4,5},{5,4},{6,7},{7,6},{8,9},{9,8},{10,11... | collective-permute-start | bytes 184328 | tf_op jit(solution)/shard_map/ppermute | solution.py:265
  41.1 16.3 %collective-permute-start.10 = (bf16[128,2048]{1,0:T(8,128)(2,1)S(1)}, bf16[128,2048]{1,0:T(8,128)(2,1)S(1)}, u32[]{:S(2)}, u32[]{:S(2)}) collective-permute-start(bf16[128,2048]{1,0:T(8,128)(2,1)S(1)} %get-tuple-element.111), channel_id=1, source_target_pairs={{0,2},{1,3},{2,0},{3,1},{4,6},{5,7},{6,4},{7,5},{8,10},{9,11},{10,... | collective-permute-start | bytes 1572872 | tf_op jit(solution)/shard_map/ppermute | solution.py:265
  42.7 12.9 %collective-permute-start.11 = (bf16[40,4224]{1,0:T(8,128)(2,1)S(1)}, bf16[40,4224]{1,0:T(8,128)(2,1)S(1)}, u32[]{:S(2)}, u32[]{:S(2)}) collective-permute-start(bf16[40,4224]{1,0:T(8,128)(2,1)S(1)} %get-tuple-element.113), channel_id=1, source_target_pairs={{0,8},{8,0},{16,24},{24,16},{1,9},{9,1},{17,25},{25,17},{2,10},{10... | collective-permute-start | bytes 1013768 | tf_op jit(solution)/shard_map/ppermute | solution.py:265
  48.8 13.2 %collective-permute-start.14 = (bf16[40,4096]{1,0:T(8,128)(2,1)S(1)}, bf16[40,4096]{1,0:T(8,128)(2,1)S(1)}, u32[]{:S(2)}, u32[]{:S(2)}) collective-permute-start(bf16[40,4096]{1,0:T(8,128)(2,1)S(1)} %get-tuple-element.121), channel_id=1, source_target_pairs={{0,16},{8,24},{16,0},{24,8},{1,17},{9,25},{17,1},{25,9},{2,18},{10... | collective-permute-start | bytes 983048 | tf_op jit(solution)/shard_map/ppermute | solution.py:265
  50.3 11.7 %collective-permute-start.15 = (bf16[40,3968]{1,0:T(8,128)(2,1)S(1)}, bf16[40,3968]{1,0:T(8,128)(2,1)S(1)}, u32[]{:S(2)}, u32[]{:S(2)}) collective-permute-start(bf16[40,3968]{1,0:T(8,128)(2,1)S(1)} %get-tuple-element.122), channel_id=1, source_target_pairs={{0,8},{8,0},{16,24},{24,16},{1,9},{9,1},{17,25},{25,17},{2,10},{10... | collective-permute-start | bytes 952328 | tf_op jit(solution)/shard_map/ppermute | solution.py:265
  55.9 16.3 %collective-permute-start.16 = (bf16[40,4224]{1,0:T(8,128)(2,1)S(1)}, bf16[40,4224]{1,0:T(8,128)(2,1)S(1)}, u32[]{:S(2)}, u32[]{:S(2)}) collective-permute-start(bf16[40,4224]{1,0:T(8,128)(2,1)S(1)} %get-tuple-element.129), channel_id=1, source_target_pairs={{0,16},{8,24},{16,0},{24,8},{1,17},{9,25},{17,1},{25,9},{2,18},{10... | collective-permute-start | bytes 1013768 | tf_op jit(solution)/shard_map/ppermute | solution.py:265
  57.6 13.8 %collective-permute-start.13 = (bf16[128,1024]{1,0:T(8,128)(2,1)S(1)}, bf16[128,1024]{1,0:T(8,128)(2,1)S(1)}, u32[]{:S(2)}, u32[]{:S(2)}) collective-permute-start(bf16[128,1024]{1,0:T(8,128)(2,1)S(1)} %get-tuple-element.119), channel_id=1, source_target_pairs={{0,4},{1,5},{2,6},{3,7},{4,0},{5,1},{6,2},{7,3},{8,12},{9,13},{10,... | collective-permute-start | bytes 786440 | tf_op jit(solution)/shard_map/ppermute | solution.py:265
  62.3 9.9 %collective-permute-start.17 = (bf16[40,3968]{1,0:T(8,128)(2,1)S(1)}, bf16[40,3968]{1,0:T(8,128)(2,1)S(1)}, u32[]{:S(2)}, u32[]{:S(2)}) collective-permute-start(bf16[40,3968]{1,0:T(8,128)(2,1)S(1)} %get-tuple-element.130), channel_id=1, source_target_pairs={{0,16},{8,24},{16,0},{24,8},{1,17},{9,25},{17,1},{25,9},{2,18},{10... | collective-permute-start | bytes 952328 | tf_op jit(solution)/shard_map/ppermute | solution.py:265
  72.2 1.3 %collective-permute-start.18 = (f32[128,128]{1,0:T(8,128)S(1)}, f32[128,128]{1,0:T(8,128)S(1)}, u32[]{:S(2)}, u32[]{:S(2)}) collective-permute-start(f32[128,128]{1,0:T(8,128)S(1)} %get-tuple-element.131), channel_id=1, source_target_pairs={{0,1},{1,0},{2,3},{3,2},{4,5},{5,4},{6,7},{7,6},{8,9},{9,8},{10,11... | collective-permute-start | bytes 196616 | tf_op jit(solution)/shard_map/ppermute | solution.py:265

commit v6 on v4

--- a/solution.py
+++ b/solution.py
@@ -11,7 +11,8 @@
 NT = (((1,), (1,)), ((), ()))
 TN = (((0,), (0,)), ((), ()))
 TILE = 512
-SWAP = 4
+SWAP = 1
+BITS = (2, 4)
 
 
 def dot(left, right, dims):
@@ -139,8 +140,8 @@
     copies[1].wait()
 
 
-def part_of(width, g, down, hid_b, part, out):
-    rows, wide = down.shape[0] // 2, g.shape[1]
+def shares(width, g, down, part):
+    wide = g.shape[1]
     tile = min(SWAP * width, 1024)
 
     def run(mine):
@@ -150,9 +151,13 @@
                 far = there + SWAP * width * mine + at
                 total += dot(down[:, near + at : near + at + tile], g[:, far : far + tile], NT)
         part[...] = total
-        out[...] = jnp.where(top_rows(total), pltpu.roll(total, rows, 0), hid_b[...].astype(F32))
 
     either(tensor_bit(SWAP), run)
+
+
+def sent_share(part, hid_b):
+    share = part[...]
+    return jnp.where(top_rows(share), pltpu.roll(share, share.shape[0] // 2, 0), hid_b[...].astype(F32))
 
 
 def finish(both, part, got, hid_a, pair, hid_pair):
@@ -217,8 +222,7 @@
 
 
 def output_sums(width, *refs):
-    hids, downs, (send_a, send_b, keep) = refs[:3], refs[3:6], refs[6:]
-    part = send_a.shape[0]
+    hids, downs, (send, keep) = refs[:3], refs[3:6], refs[6:]
     tile = min(width, TILE)
 
     def run(mine):
@@ -231,36 +235,28 @@
                     if which == mine:
                         keep[:, here] = total
                     else:
-                        send_a[:, here] = total[:part].astype(BF)
-                        send_b[:, here] = total[part:].astype(BF)
-
-    either(tensor_bit(1), run)
-
-
-def halved(bit, width, keep, *refs):
-    got, (send, left) = refs[:-2], refs[-2:]
+                        send[:, here] = total.astype(BF)
+
+    either(tensor_bit(BITS[0]), run)
+
+
+def halved(bit, width, keep, got, send, left):
     tile = min(width, TILE)
-    part = keep.shape[0] // len(got)
 
     def run(mine):
         for block in range(left.shape[1] // width):
             for out, which in ((send, 1 - mine), (left, mine)):
                 for at in range(0, width, tile):
                     cols = slice((2 * block + which) * width + at, (2 * block + which) * width + at + tile)
-                    here = slice(block * width + at, block * width + at + tile)
-                    for k, piece in enumerate(got):
-                        rows = slice(k * part, (k + 1) * part)
-                        out[rows, here] = (keep[rows, cols] + piece[:, cols].astype(F32)).astype(out.dtype)
+                    value = keep[:, cols] + got[:, cols].astype(F32)
+                    out[:, block * width + at : block * width + at + tile] = value.astype(out.dtype)
 
     either(tensor_bit(bit), run)
 
 
-def final_output(keep, *refs):
-    got, out = refs[:-1], refs[-1]
-    part = keep.shape[0] // len(got)
-    for k, piece in enumerate(got):
-        rows = slice(k * part, (k + 1) * part)
-        out[rows, :] = (keep[rows, :] + piece[...].astype(F32)).astype(BF)
+def final_output(keep, got, out, end):
+    out[...] = (keep[...] + got[...].astype(F32)).astype(BF)
+    end[...] = jnp.zeros_like(end)
 
 
 def exchanged(value, axis, bit):
@@ -277,7 +273,7 @@
     rows, wide = gate_weight.shape
     half, both_rows, tokens = wide // 2, 2 * rows, x.shape[0]
     count = lax.axis_size("tensor")
-    assert count > SWAP and count & (count - 1) == 0
+    assert count > BITS[1] and count & (count - 1) == 0
     width = wide // count
     four = lax.axis_size("section") == 4
     piece, narrow = ((both_rows, half), BF), ((rows, half), BF)
@@ -314,8 +310,17 @@
         scratch=[held, held, held, pltpu.SemaphoreType.DMA((3,))],
     )
     first[1] = one_hop(own[1])
+    down_got = exchanged(down_send, "tensor", SWAP)
     first[0] = one_hop(own[0])
-    down_got = exchanged(down_send, "tensor", SWAP)
+
+    def joined(keep, got, out):
+        stacked(out, keep, got)
+
+    own[2] = step(joined, piece, [down_keep, down_got])
+    if four:
+        crossed = exchanged(own[2], "section", 1)
+        onward = lax.ppermute(crossed, "section", [(source, source ^ 2) for source in (0, 2)])
+    first[2] = one_hop(own[2])
     x, g, both_own, *hid_own = step(
         project_first,
         [(x.shape, BF), (g.shape, BF), small, small_bf, small_bf],
@@ -323,45 +328,50 @@
         far=2,
         scratch=[pltpu.SemaphoreType.DMA((2,))],
     )
+    share = with_width(shares)
+    share_own = step(share, small, [g, own[2]])
     second[1] = relay(first[1], own[1])
-
-    def joined(keep, got, out):
-        stacked(out, keep, got)
-
-    own[2] = step(joined, piece, [down_keep, down_got])
-    first[2] = one_hop(own[2])
-    part_own, part_out = step(with_width(part_of), [small, small], [g, own[2], hid_own[1]])
     second[0] = relay(first[0], own[0])
     both_first, *hid_first = step(project, [small, small_bf, small_bf], [x, first[0], first[1]], also=[second[1]])
-    second[2] = relay(first[2], own[2])
-
-    def part_two(gr, down, hid_b, earlier, part, out):
-        out[:both_rows, :] = earlier[...]
-        part_of(width, gr, down, hid_b, part, out.at[both_rows:, :])
-
-    part_first, part_out = step(
-        part_two, [small, ((2 * both_rows, tokens), F32)], [g, first[2], hid_first[1], part_out]
-    )
-    part_got = exchanged(part_out, "tensor", SWAP)
+    second[2] = step(picked, piece, [crossed, onward]) if four else ring_passed(first[2], 1)
+    share_second = step(share, small, [g, second[2]])
     both_second, *hid_second = step(project, [small, small_bf, small_bf], [x, second[0], second[1]])
+
+    def two_sent(share_a, hid_a, share_b, hid_b, out):
+        out[:both_rows, :] = sent_share(share_a, hid_a)
+        out[both_rows:, :] = sent_share(share_b, hid_b)
+
+    sent = step(two_sent, ((2 * both_rows, tokens), F32), [share_own, hid_own[1], share_second, hid_second[1]])
+    got_two = exchanged(sent, "tensor", SWAP)
     side_down = outward(step(sent_down, piece, [g, *hid_second]))
 
     def finish_two(both_a, part_a, hid_a, both_b, part_b, hid_b, got, pair_a, out_a, pair_b, out_b):
         finish(both_a, part_a, got.at[:both_rows, :], hid_a, pair_a, out_a)
         finish(both_b, part_b, got.at[both_rows:, :], hid_b, pair_b, out_b)
 
-    pair_own, wide_own, pair_first, wide_first = step(
-        finish_two, [small_bf] * 4, [both_own, part_own, hid_own[0], both_first, part_first, hid_first[0], part_got]
+    pair_own, wide_own, pair_second, wide_second = step(
+        finish_two, [small_bf] * 4, [both_own, share_own, hid_own[0], both_second, share_second, hid_second[0], got_two]
     )
     low_columns = half + 128
     low_shape, high_shape = (both_rows, low_columns), (both_rows, wide - low_columns)
-    grads_f32 = [(low_shape, F32), (high_shape, F32), ((both_rows, half), F32)]
-    own_low, own_high, own_down = step(own_grads, grads_f32, [x, g, *hid_own, pair_own])
-    part_second, part_out = step(with_width(part_of), [small, small], [g, second[2], hid_second[1]])
-    part_got = exchanged(part_out, "tensor", SWAP)
-    pair_second, wide_second = step(finish, [small_bf] * 2, [both_second, part_second, part_got, hid_second[0]])
     low, high = step(sent_pair, [(low_shape, BF), (high_shape, BF)], [x, pair_second])
     side_low, side_high = outward(low), outward(high)
+
+    def one_sent(gr, down, hid, part, out):
+        shares(width, gr, down, part)
+        out[...] = sent_share(part, hid)
+
+    share_first, sent = step(one_sent, [small, small], [g, first[2], hid_first[1]])
+    got_one = exchanged(sent, "tensor", SWAP)
+    grads_f32 = [(low_shape, F32), (high_shape, F32), ((both_rows, half), F32)]
+    pair_first, wide_first = step(finish, [small_bf] * 2, [both_first, share_first, got_one, hid_first[0]])
+    quarter = wide // 4
+    send, keep = step(
+        with_width(output_sums),
+        [((tokens, quarter), BF), ((tokens, quarter), F32)],
+        [wide_own, wide_first, wide_second, own[2], first[2], second[2]],
+    )
+    got = exchanged(send, "tensor", BITS[0])
 
     def back_down(gr, a, b, side, out):
         odd = is_odd()
@@ -378,14 +388,9 @@
 
         return body
 
-    quarter = wide // 4
-    send_a, send_b, keep = step(
-        with_width(output_sums),
-        [((tokens // 2, quarter), BF), ((tokens // 2, quarter), BF), ((tokens, quarter), F32)],
-        [wide_own, wide_first, wide_second, own[2], first[2], second[2]],
-    )
     back_of_down = backward(step(back_down, piece, [g, *hid_first, side_down]))
-    got = [exchanged(send_a, "tensor", 1), exchanged(send_b, "tensor", 1)]
+    own_low, own_high, own_down = step(own_grads, grads_f32, [x, g, *hid_own, pair_own])
+    back_of_low = backward(step(back_pair(0), (low_shape, BF), [x, pair_first, side_low]))
 
     def next_half(keep, got, bit):
         cols = keep.shape[1] // 2
@@ -393,13 +398,12 @@
         def body(*refs):
             halved(bit, width, *refs)
 
-        send, keep = step(body, [((tokens, cols), BF), ((tokens, cols), F32)], [keep, *got])
-        return keep, [exchanged(send, "tensor", bit)]
-
-    keep, got = next_half(keep, got, 2)
-    back_of_low = backward(step(back_pair(0), (low_shape, BF), [x, pair_first, side_low]))
+        send, keep = step(body, [((tokens, cols), BF), ((tokens, cols), F32)], [keep, got])
+        return keep, exchanged(send, "tensor", bit)
+
+    keep, got = next_half(keep, got, BITS[1])
     back_of_high = backward(step(back_pair(low_columns), (high_shape, BF), [x, pair_first, side_high], also=[back_of_down]))
-    bit = 2 * SWAP
+    bit = 2 * BITS[1]
     while bit < count:
         keep, got = next_half(keep, got, bit)
         bit *= 2
@@ -426,9 +430,13 @@
 
     whole = ((rows, wide), F32)
     grad_down = step(final_down, whole, [own_down, back_of_down, side_down])
-    output = step(final_output, ((tokens, width), BF), [keep, *got])
+    output, end = step(final_output, [((tokens, width), BF), ((128, 128), F32)], [keep, got])
+    end = exchanged(end, "tensor", SWAP)
     grad_gate, grad_up = step(
-        final_pair, [whole, whole], [own_low, own_high, back_of_low, back_of_high, side_low, side_high]
+        final_pair,
+        [whole, whole],
+        [own_low, own_high, back_of_low, back_of_high, side_low, side_high],
+        also=[end],
     )
     return (output, grad_gate, grad_up, grad_down)
 

time: 69.6 us -> 69.7 us (level)
  starting transfers between devices: 29.4 us -> 27.5 us
  waiting for transfers between devices: 24.8 us -> 26.6 us
    ppermute x18, starting transfers between devices: 29.4 us -> 24.1 us  [exchanged(): lax.ppermute(value, axis, [(source, source ^ bit) for source in range(cou...]
    ppermute x0 -> x1, waiting for transfers between devices: none -> 3.6 us  [on_device(): lax.ppermute(crossed, 'section', [(source, source ^ 2) for source in (0,...]
    ppermute x0 -> x1, starting transfers between devices: none -> 3.41 us  [on_device(): lax.ppermute(crossed, 'section', [(source, source ^ 2) for source in (0,...]
    ppermute x18, waiting for transfers between devices: 24.8 us -> 23 us  [exchanged(): lax.ppermute(value, axis, [(source, source ^ bit) for source in range(cou...]
    pallas_call x24 -> x25, Pallas kernels: 14.5 us -> 14.6 us  [__call__(): pl.pallas_call(kernel, out_shape=[jax.ShapeDtypeStruct(*s) for s in shape...]
  transfers between devices with their start and end apart: 18 -> 19, of which waited for: 13 -> 11; matrix products, arithmetic and copies ran while one was open for 0% -> 0% of each run, Pallas kernels for 16% -> 17%
where the time goes in v6:
time: 69.7 us; the launch traced here: 69.5 us
  starting transfers between devices  27.5 us (39%)
  waiting for transfers between devices  26.6 us (38%)
  Pallas kernels  14.6 us (21%)
  between operations  0.8 us (1%)
    ppermute x18, starting transfers between devices, exchanged(): lax.ppermute(value, axis, [(source, source ^ bit) for source in range(cou...  24.1 us
    ppermute x18, waiting for transfers between devices, exchanged(): lax.ppermute(value, axis, [(source, source ^ bit) for source in range(cou...  23 us
    pallas_call x25, Pallas kernels, __call__(): pl.pallas_call(kernel, out_shape=[jax.ShapeDtypeStruct(*s) for s in shape...  14.6 us
    ppermute x1, waiting for transfers between devices, on_device(): lax.ppermute(crossed, 'section', [(source, source ^ 2) for source in (0,...  3.6 us
    ppermute x1, starting transfers between devices, on_device(): lax.ppermute(crossed, 'section', [(source, source ^ 2) for source in (0,...  3.41 us
  transfers between devices with their start and end apart: 19, of which 11 were waited for; matrix products, arithmetic and copies ran while one was open for 0% of the time, Pallas kernels for 17%

profile of v6, /device:TPU:0, one launch (start us, length us, event | category | flops | bytes accessed | tf_op | source)
XLA Modules:
  0.0 69.5 jit_solution(1775485862282665930)
XLA Ops:
  0.6 1.7 %shard_map.84 = (bf16[40,4096]{1,0:T(8,128)(2,1)S(1)}, bf16[40,4096]{1,0:T(8,128)(2,1)S(1)}, bf16[20,4096]{1,0:T(8,128)(2,1)S(1)}, bf16[20,4096]{1,0:T(8,128)(2,1)S(1)}, f32[8,128]{1,0:T(8,128)S(1)}) custom-call(bf16[20,8192]{1,0:T(8,128)(2,1)} %refs_0_.2, bf16[20,8192]{1,0:T(8,128)(2,1)} %refs_1_.2, bf16[20,8192]{1,0:T(8,128)(2,1)} %refs_2_.1), custom_call_target="tpu_custom_call" | custom-call | flops 1 | bytes 1 | tf_op jit(solution)/shard_map/pallas_call | solution.py:38
  2.9 2.6 %collective-permute-start.2 = (bf16[40,4096]{1,0:T(8,128)(2,1)S(1)}, bf16[40,4096]{1,0:T(8,128)(2,1)S(1)}, u32[]{:S(2)}, u32[]{:S(2)}) collective-permute-start(bf16[40,4096]{1,0:T(8,128)(2,1)S(1)} %get-tuple-element.77.refs_3_.refs_1_), channel_id=1, source_target_pairs={{0,16},{8,24},{16,0},{24,8},{1,17},{9,25},{17,1},{25,9},{2,18},{10... | collective-permute-start | bytes 983048 | tf_op jit(solution)/shard_map/ppermute | solution.py:264
  5.8 1.6 %collective-permute-start.5 = (bf16[40,4096]{1,0:T(8,128)(2,1)S(1)}, bf16[40,4096]{1,0:T(8,128)(2,1)S(1)}, u32[]{:S(2)}, u32[]{:S(2)}) collective-permute-start(bf16[40,4096]{1,0:T(8,128)(2,1)S(1)} %get-tuple-element.84.refs_1_.refs_3_), channel_id=1, source_target_pairs={{0,8},{8,0},{16,24},{24,16},{1,9},{9,1},{17,25},{25,17},{2,10},{10... | collective-permute-start | bytes 983048 | tf_op jit(solution)/shard_map/ppermute | solution.py:264
  7.4 1.4 %collective-permute-start.1 = (bf16[40,4096]{1,0:T(8,128)(2,1)S(1)}, bf16[40,4096]{1,0:T(8,128)(2,1)S(1)}, u32[]{:S(2)}, u32[]{:S(2)}) collective-permute-start(bf16[40,4096]{1,0:T(8,128)(2,1)S(1)} %get-tuple-element.76.refs_2_.refs_1_), channel_id=1, source_target_pairs={{0,16},{8,24},{16,0},{24,8},{1,17},{9,25},{17,1},{25,9},{2,18},{10... | collective-permute-start | bytes 983048 | tf_op jit(solution)/shard_map/ppermute | solution.py:264
  8.7 2.5 %shard_map.86 = (bf16[128,8192]{1,0:T(8,128)(2,1)S(1)}, bf16[128,8192]{1,0:T(8,128)(2,1)S(1)}, f32[40,128]{1,0:T(8,128)S(1)}, bf16[40,128]{1,0:T(8,128)(2,1)S(1)...) custom-call(bf16[128,8192]{1,0:T(8,128)(2,1)} %refs_0_.3, bf16[128,8192]{1,0:T(8,128)(2,1)} %refs_1_.3, ...), custom_call_target="tpu_custom_call" | custom-call | flops 1 | bytes 1 | tf_op jit(solution)/shard_map/pallas_call | solution.py:38
  11.7 2.3 %collective-permute-done.2.refs_0_.refs_2_ = bf16[40,4096]{1,0:T(8,128)(2,1)S(1)} collective-permute-done((bf16[40,4096]{1,0:T(8,128)(2,1)S(1)}, bf16[40,4096]{1,0:T(8,128)(2,1)S(1)}, u32[]{:S(2)}, u32[]{:S(2)}) %collective-permute-start.2) | collective-permute-done | bytes 327712 | tf_op jit(solution)/shard_map/ppermute | solution.py:264
  14.1 2.0 %collective-permute-start.4 = (bf16[40,4096]{1,0:T(8,128)(2,1)S(1)}, bf16[40,4096]{1,0:T(8,128)(2,1)S(1)}, u32[]{:S(2)}, u32[]{:S(2)}) collective-permute-start(bf16[40,4096]{1,0:T(8,128)(2,1)S(1)} %get-tuple-element.92), channel_id=1, source_target_pairs={{0,8},{8,0},{16,24},{24,16},{1,9},{9,1},{17,25},{25,17},{2,10},{10... | collective-permute-start | bytes 983048 | tf_op jit(solution)/shard_map/ppermute | solution.py:264
  16.1 3.4 %collective-permute-start.6 = (bf16[40,4096]{1,0:T(8,128)(2,1)S(1)}, bf16[40,4096]{1,0:T(8,128)(2,1)S(1)}, u32[]{:S(2)}, u32[]{:S(2)}) collective-permute-start(bf16[40,4096]{1,0:T(8,128)(2,1)S(1)} %collective-permute-done.5.refs_0_), channel_id=1, source_target_pairs={{0,16},{16,0},{1,17},{17,1},{2,18},{18,2},{3,19},{19,3},{4,20},{20... | collective-permute-start | bytes 983048 | tf_op jit(solution)/shard_map/ppermute | solution.py:322
  19.5 1.6 %collective-permute-done.1.refs_0_.refs_1_ = bf16[40,4096]{1,0:T(8,128)(2,1)S(1)} collective-permute-done((bf16[40,4096]{1,0:T(8,128)(2,1)S(1)}, bf16[40,4096]{1,0:T(8,128)(2,1)S(1)}, u32[]{:S(2)}, u32[]{:S(2)}) %collective-permute-start.1) | collective-permute-done | bytes 327712 | tf_op jit(solution)/shard_map/ppermute | solution.py:264
  21.1 1.5 %collective-permute-start.3 = (bf16[40,4096]{1,0:T(8,128)(2,1)S(1)}, bf16[40,4096]{1,0:T(8,128)(2,1)S(1)}, u32[]{:S(2)}, u32[]{:S(2)}) collective-permute-start(bf16[40,4096]{1,0:T(8,128)(2,1)S(1)} %get-tuple-element.91), channel_id=1, source_target_pairs={{0,8},{8,0},{16,24},{24,16},{1,9},{9,1},{17,25},{25,17},{2,10},{10... | collective-permute-start | bytes 983048 | tf_op jit(solution)/shard_map/ppermute | solution.py:264
  22.6 1.5 %collective-permute-start.8 = (bf16[40,4096]{1,0:T(8,128)(2,1)S(1)}, bf16[40,4096]{1,0:T(8,128)(2,1)S(1)}, u32[]{:S(2)}, u32[]{:S(2)}) collective-permute-start(bf16[40,4096]{1,0:T(8,128)(2,1)S(1)} %get-tuple-element.84.refs_1_.refs_3_), channel_id=1, source_target_pairs={{0,16},{8,24},{16,0},{24,8},{1,17},{9,25},{17,1},{25,9},{2,18},{10... | collective-permute-start | bytes 983048 | tf_op jit(solution)/shard_map/ppermute | solution.py:264
  24.1 0.8 %shard_map.90 = (f32[40,128]{1,0:T(8,128)S(1)}, bf16[40,128]{1,0:T(8,128)(2,1)S(1)}, bf16[40,128]{1,0:T(8,128)(2,1)S(1)}, f32[8,128]{1,0:T(8,128)S(1)}) custom-call(bf16[128,8192]{1,0:T(8,128)(2,1)S(1)} %get-tuple-element.88.refs_0_, bf16[40,4096]{1,0:T(8,128)(2,1)S(1)} %collective-permute-done.1.refs_0_.refs_1_, ...), custom_call_target="tpu_custom_call" | custom-call | flops 1 | bytes 1 | tf_op jit(solution)/shard_map/pallas_call | solution.py:38
  25.0 3.6 %collective-permute-done.6.refs_1_ = bf16[40,4096]{1,0:T(8,128)(2,1)S(1)} collective-permute-done((bf16[40,4096]{1,0:T(8,128)(2,1)S(1)}, bf16[40,4096]{1,0:T(8,128)(2,1)S(1)}, u32[]{:S(2)}, u32[]{:S(2)}) %collective-permute-start.6) | collective-permute-done | bytes 327712 | tf_op jit(solution)/shard_map/ppermute | solution.py:322
  29.1 1.3 %collective-permute-done.3.refs_1_ = bf16[40,4096]{1,0:T(8,128)(2,1)S(1)} collective-permute-done((bf16[40,4096]{1,0:T(8,128)(2,1)S(1)}, bf16[40,4096]{1,0:T(8,128)(2,1)S(1)}, u32[]{:S(2)}, u32[]{:S(2)}) %collective-permute-start.3) | collective-permute-done | bytes 327712 | tf_op jit(solution)/shard_map/ppermute | solution.py:264
  30.4 0.8 %shard_map.93 = (f32[40,128]{1,0:T(8,128)S(1)}, bf16[40,128]{1,0:T(8,128)(2,1)S(1)}, bf16[40,128]{1,0:T(8,128)(2,1)S(1)}, f32[8,128]{1,0:T(8,128)S(1)}) custom-call(bf16[128,8192]{1,0:T(8,128)(2,1)S(1)} %get-tuple-element.88.refs_0_, bf16[40,4096]{1,0:T(8,128)(2,1)S(1)} %collective-permute-done.3.refs_1_, ...), custom_call_target="tpu_custom_call" | custom-call | flops 1 | bytes 1 | tf_op jit(solution)/shard_map/pallas_call | solution.py:38
  31.6 1.6 %collective-permute-start.12 = (bf16[40,4096]{1,0:T(8,128)(2,1)S(1)}, bf16[40,4096]{1,0:T(8,128)(2,1)S(1)}, u32[]{:S(2)}, u32[]{:S(2)}) collective-permute-start(bf16[40,4096]{1,0:T(8,128)(2,1)S(1)} %get-tuple-element.125), channel_id=1, source_target_pairs={{0,8},{8,0},{16,24},{24,16},{1,9},{9,1},{17,25},{25,17},{2,10},{10... | collective-permute-start | bytes 983048 | tf_op jit(solution)/shard_map/ppermute | solution.py:264
  33.2 1.2 %collective-permute-done.7.refs_6_ = f32[80,128]{1,0:T(8,128)S(1)} collective-permute-done((f32[80,128]{1,0:T(8,128)S(1)}, f32[80,128]{1,0:T(8,128)S(1)}, u32[]{:S(2)}, u32[]{:S(2)}) %collective-permute-start.7) | collective-permute-done | bytes 40992 | tf_op jit(solution)/shard_map/ppermute | solution.py:264
  35.7 1.0 %collective-permute-done.9.refs_2_ = f32[40,128]{1,0:T(8,128)S(1)} collective-permute-done((f32[40,128]{1,0:T(8,128)S(1)}, f32[40,128]{1,0:T(8,128)S(1)}, u32[]{:S(2)}, u32[]{:S(2)}) %collective-permute-start.9) | collective-permute-done | bytes 20512 | tf_op jit(solution)/shard_map/ppermute | solution.py:264
  36.7 1.0 %shard_map.100 = (bf16[128,2048]{1,0:T(8,128)(2,1)S(1)}, f32[128,2048]{1,0:T(8,128)S(1)}, f32[8,128]{1,0:T(8,128)S(1)}) custom-call(bf16[40,128]{1,0:T(8,128)(2,1)S(1)} %get-tuple-element.107.refs_0_, bf16[40,128]{1,0:T(8,128)(2,1)S(1)} %get-tuple-element.117.refs_1_, bf16[40,128]{1,0:T(8,128)(2,1)S(1)} %get-tuple-element.118.refs_2_, ...), custom_call_target="tpu_custom_call" | custom-call | flops 1 | bytes 1 | tf_op jit(solution)/shard_map/pallas_call | solution.py:38
  37.7 1.8 %collective-permute-start.10 = (bf16[128,2048]{1,0:T(8,128)(2,1)S(1)}, bf16[128,2048]{1,0:T(8,128)(2,1)S(1)}, u32[]{:S(2)}, u32[]{:S(2)}) collective-permute-start(bf16[128,2048]{1,0:T(8,128)(2,1)S(1)} %get-tuple-element.121), channel_id=1, source_target_pairs={{0,2},{1,3},{2,0},{3,1},{4,6},{5,7},{6,4},{7,5},{8,10},{9,11},{10,... | collective-permute-start | bytes 1572872 | tf_op jit(solution)/shard_map/ppermute | solution.py:264
  40.4 1.5 %collective-permute-start.14 = (bf16[40,4096]{1,0:T(8,128)(2,1)S(1)}, bf16[40,4096]{1,0:T(8,128)(2,1)S(1)}, u32[]{:S(2)}, u32[]{:S(2)}) collective-permute-start(bf16[40,4096]{1,0:T(8,128)(2,1)S(1)} %get-tuple-element.133), channel_id=1, source_target_pairs={{0,16},{8,24},{16,0},{24,8},{1,17},{9,25},{17,1},{25,9},{2,18},{10... | collective-permute-start | bytes 983048 | tf_op jit(solution)/shard_map/ppermute | solution.py:264
  41.9 1.7 %collective-permute-start.15 = (bf16[40,3968]{1,0:T(8,128)(2,1)S(1)}, bf16[40,3968]{1,0:T(8,128)(2,1)S(1)}, u32[]{:S(2)}, u32[]{:S(2)}) collective-permute-start(bf16[40,3968]{1,0:T(8,128)(2,1)S(1)} %get-tuple-element.134), channel_id=1, source_target_pairs={{0,8},{8,0},{16,24},{24,16},{1,9},{9,1},{17,25},{25,17},{2,10},{10... | collective-permute-start | bytes 952328 | tf_op jit(solution)/shard_map/ppermute | solution.py:264
  44.3 6.0 %collective-permute-done.11.refs_2_.refs_4_ = bf16[40,4224]{1,0:T(8,128)(2,1)S(1)} collective-permute-done((bf16[40,4224]{1,0:T(8,128)(2,1)S(1)}, bf16[40,4224]{1,0:T(8,128)(2,1)S(1)}, u32[]{:S(2)}, u32[]{:S(2)}) %collective-permute-start.11) | collective-permute-done | bytes 337952 | tf_op jit(solution)/shard_map/ppermute | solution.py:264
  50.6 1.6 %collective-permute-start.16 = (bf16[40,4224]{1,0:T(8,128)(2,1)S(1)}, bf16[40,4224]{1,0:T(8,128)(2,1)S(1)}, u32[]{:S(2)}, u32[]{:S(2)}) collective-permute-start(bf16[40,4224]{1,0:T(8,128)(2,1)S(1)} %get-tuple-element.141), channel_id=1, source_target_pairs={{0,16},{8,24},{16,0},{24,8},{1,17},{9,25},{17,1},{25,9},{2,18},{10... | collective-permute-start | bytes 1013768 | tf_op jit(solution)/shard_map/ppermute | solution.py:264
  52.3 2.7 %collective-permute-start.13 = (bf16[128,1024]{1,0:T(8,128)(2,1)S(1)}, bf16[128,1024]{1,0:T(8,128)(2,1)S(1)}, u32[]{:S(2)}, u32[]{:S(2)}) collective-permute-start(bf16[128,1024]{1,0:T(8,128)(2,1)S(1)} %get-tuple-element.131), channel_id=1, source_target_pairs={{0,4},{1,5},{2,6},{3,7},{4,0},{5,1},{6,2},{7,3},{8,12},{9,13},{10,... | collective-permute-start | bytes 786440 | tf_op jit(solution)/shard_map/ppermute | solution.py:264
  55.0 1.1 %collective-permute-done.15.refs_2_.refs_5_ = bf16[40,3968]{1,0:T(8,128)(2,1)S(1)} collective-permute-done((bf16[40,3968]{1,0:T(8,128)(2,1)S(1)}, bf16[40,3968]{1,0:T(8,128)(2,1)S(1)}, u32[]{:S(2)}, u32[]{:S(2)}) %collective-permute-start.15) | collective-permute-done | bytes 317472 | tf_op jit(solution)/shard_map/ppermute | solution.py:264
  56.4 1.6 %collective-permute-start.17 = (bf16[40,3968]{1,0:T(8,128)(2,1)S(1)}, bf16[40,3968]{1,0:T(8,128)(2,1)S(1)}, u32[]{:S(2)}, u32[]{:S(2)}) collective-permute-start(bf16[40,3968]{1,0:T(8,128)(2,1)S(1)} %get-tuple-element.142), channel_id=1, source_target_pairs={{0,16},{8,24},{16,0},{24,8},{1,17},{9,25},{17,1},{25,9},{2,18},{10... | collective-permute-start | bytes 952328 | tf_op jit(solution)/shard_map/ppermute | solution.py:264
  57.9 1.0 %shard_map.106 = (f32[20,8192]{1,0:T(8,128)}, f32[8,128]{1,0:T(8,128)S(1)}) custom-call(f32[40,4096]{1,0:T(8,128)S(1)} %get-tuple-element.132.refs_0_, bf16[40,4096]{1,0:T(8,128)(2,1)S(1)} %collective-permute-done.14.refs_3_.refs_1_, bf16[40,4096]{1,0:T(8,128)(2,1)S(1)} %collective-permute-done.12.refs_3_.refs_2_, f32[8,128]{1,0:T(8,128)S(1)} %get-tuple-element.136.refs_3_), custom_call_target="tpu_custom_call" | custom-call | flops 1 | bytes 1 | tf_op jit(solution)/shard_map/pallas_call | solution.py:38
  59.0 7.2 %collective-permute-done.13.refs_1_ = bf16[128,1024]{1,0:T(8,128)(2,1)S(1)} collective-permute-done((bf16[128,1024]{1,0:T(8,128)(2,1)S(1)}, bf16[128,1024]{1,0:T(8,128)(2,1)S(1)}, u32[]{:S(2)}, u32[]{:S(2)}) %collective-permute-start.13) | collective-permute-done | bytes 262176 | tf_op jit(solution)/shard_map/ppermute | solution.py:264
  66.1 0.8 %shard_map.107 = (bf16[128,1024]{1,0:T(8,128)(2,1)}, f32[128,128]{1,0:T(8,128)S(1)}, f32[8,128]{1,0:T(8,128)S(1)}) custom-call(f32[128,1024]{1,0:T(8,128)S(1)} %get-tuple-element.130.refs_0_, bf16[128,1024]{1,0:T(8,128)(2,1)S(1)} %collective-permute-done.13.refs_1_, f32[8,128]{1,0:T(8,128)S(1)} %get-tuple-element.137.refs_2_), custom_call_target="tpu_custom_call" | custom-call | flops 1 | bytes 1 | tf_op jit(solution)/shard_map/pallas_call | solution.py:38
  66.9 1.2 %collective-permute-done.18.refs_6_ = f32[128,128]{1,0:T(8,128)S(1)} collective-permute-done((f32[128,128]{1,0:T(8,128)S(1)}, f32[128,128]{1,0:T(8,128)S(1)}, u32[]{:S(2)}, u32[]{:S(2)}) %collective-permute-start.18) | collective-permute-done | bytes 65568 | tf_op jit(solution)/shard_map/ppermute | solution.py:264
  68.2 1.4 %shard_map.108 = (f32[20,8192]{1,0:T(8,128)}, f32[20,8192]{1,0:T(8,128)}, f32[8,128]{1,0:T(8,128)}) custom-call(f32[40,4224]{1,0:T(8,128)S(1)} %get-tuple-element.139.refs_0_, f32[40,3968]{1,0:T(8,128)S(1)} %get-tuple-element.140.refs_1_, bf16[40,4224]{1,0:T(8,128)(2,1)S(1)} %collective-permute-done.16.refs_2_, ...), custom_call_target="tpu_custom_call" | custom-call | flops 1 | bytes 1 | tf_op jit(solution)/shard_map/pallas_call | solution.py:38
  (31 shorter events, 5.8 us)
Async XLA Ops:
  2.4 3.1 %collective-permute-start = (bf16[20,4096]{1,0:T(8,128)(2,1)S(1)}, bf16[20,4096]{1,0:T(8,128)(2,1)S(1)}, u32[]{:S(2)}, u32[]{:S(2)}) collective-permute-start(bf16[20,4096]{1,0:T(8,128)(2,1)S(1)} %get-tuple-element.79), channel_id=1, source_target_pairs={{0,1},{1,0},{2,3},{3,2},{4,5},{5,4},{6,7},{7,6},{8,9},{9,8},{10,11... | collective-permute-start | bytes 491528 | tf_op jit(solution)/shard_map/ppermute | solution.py:264
  2.9 11.2 %collective-permute-start.2 = (bf16[40,4096]{1,0:T(8,128)(2,1)S(1)}, bf16[40,4096]{1,0:T(8,128)(2,1)S(1)}, u32[]{:S(2)}, u32[]{:S(2)}) collective-permute-start(bf16[40,4096]{1,0:T(8,128)(2,1)S(1)} %get-tuple-element.77.refs_3_.refs_1_), channel_id=1, source_target_pairs={{0,16},{8,24},{16,0},{24,8},{1,17},{9,25},{17,1},{25,9},{2,18},{10... | collective-permute-start | bytes 983048 | tf_op jit(solution)/shard_map/ppermute | solution.py:264
  5.8 10.2 %collective-permute-start.5 = (bf16[40,4096]{1,0:T(8,128)(2,1)S(1)}, bf16[40,4096]{1,0:T(8,128)(2,1)S(1)}, u32[]{:S(2)}, u32[]{:S(2)}) collective-permute-start(bf16[40,4096]{1,0:T(8,128)(2,1)S(1)} %get-tuple-element.84.refs_1_.refs_3_), channel_id=1, source_target_pairs={{0,8},{8,0},{16,24},{24,16},{1,9},{9,1},{17,25},{25,17},{2,10},{10... | collective-permute-start | bytes 983048 | tf_op jit(solution)/shard_map/ppermute | solution.py:264
  7.4 13.7 %collective-permute-start.1 = (bf16[40,4096]{1,0:T(8,128)(2,1)S(1)}, bf16[40,4096]{1,0:T(8,128)(2,1)S(1)}, u32[]{:S(2)}, u32[]{:S(2)}) collective-permute-start(bf16[40,4096]{1,0:T(8,128)(2,1)S(1)} %get-tuple-element.76.refs_2_.refs_1_), channel_id=1, source_target_pairs={{0,16},{8,24},{16,0},{24,8},{1,17},{9,25},{17,1},{25,9},{2,18},{10... | collective-permute-start | bytes 983048 | tf_op jit(solution)/shard_map/ppermute | solution.py:264
  14.1 10.1 %collective-permute-start.4 = (bf16[40,4096]{1,0:T(8,128)(2,1)S(1)}, bf16[40,4096]{1,0:T(8,128)(2,1)S(1)}, u32[]{:S(2)}, u32[]{:S(2)}) collective-permute-start(bf16[40,4096]{1,0:T(8,128)(2,1)S(1)} %get-tuple-element.92), channel_id=1, source_target_pairs={{0,8},{8,0},{16,24},{24,16},{1,9},{9,1},{17,25},{25,17},{2,10},{10... | collective-permute-start | bytes 983048 | tf_op jit(solution)/shard_map/ppermute | solution.py:264
  16.1 12.5 %collective-permute-start.6 = (bf16[40,4096]{1,0:T(8,128)(2,1)S(1)}, bf16[40,4096]{1,0:T(8,128)(2,1)S(1)}, u32[]{:S(2)}, u32[]{:S(2)}) collective-permute-start(bf16[40,4096]{1,0:T(8,128)(2,1)S(1)} %collective-permute-done.5.refs_0_), channel_id=1, source_target_pairs={{0,16},{16,0},{1,17},{17,1},{2,18},{18,2},{3,19},{19,3},{4,20},{20... | collective-permute-start | bytes 983048 | tf_op jit(solution)/shard_map/ppermute | solution.py:322
  21.1 9.3 %collective-permute-start.3 = (bf16[40,4096]{1,0:T(8,128)(2,1)S(1)}, bf16[40,4096]{1,0:T(8,128)(2,1)S(1)}, u32[]{:S(2)}, u32[]{:S(2)}) collective-permute-start(bf16[40,4096]{1,0:T(8,128)(2,1)S(1)} %get-tuple-element.91), channel_id=1, source_target_pairs={{0,8},{8,0},{16,24},{24,16},{1,9},{9,1},{17,25},{25,17},{2,10},{10... | collective-permute-start | bytes 983048 | tf_op jit(solution)/shard_map/ppermute | solution.py:264
  22.6 12.3 %collective-permute-start.8 = (bf16[40,4096]{1,0:T(8,128)(2,1)S(1)}, bf16[40,4096]{1,0:T(8,128)(2,1)S(1)}, u32[]{:S(2)}, u32[]{:S(2)}) collective-permute-start(bf16[40,4096]{1,0:T(8,128)(2,1)S(1)} %get-tuple-element.84.refs_1_.refs_3_), channel_id=1, source_target_pairs={{0,16},{8,24},{16,0},{24,8},{1,17},{9,25},{17,1},{25,9},{2,18},{10... | collective-permute-start | bytes 983048 | tf_op jit(solution)/shard_map/ppermute | solution.py:264
  31.6 8.4 %collective-permute-start.12 = (bf16[40,4096]{1,0:T(8,128)(2,1)S(1)}, bf16[40,4096]{1,0:T(8,128)(2,1)S(1)}, u32[]{:S(2)}, u32[]{:S(2)}) collective-permute-start(bf16[40,4096]{1,0:T(8,128)(2,1)S(1)} %get-tuple-element.125), channel_id=1, source_target_pairs={{0,8},{8,0},{16,24},{24,16},{1,9},{9,1},{17,25},{25,17},{2,10},{10... | collective-permute-start | bytes 983048 | tf_op jit(solution)/shard_map/ppermute | solution.py:264
  33.2 1.2 %collective-permute-start.7 = (f32[80,128]{1,0:T(8,128)S(1)}, f32[80,128]{1,0:T(8,128)S(1)}, u32[]{:S(2)}, u32[]{:S(2)}) collective-permute-start(f32[80,128]{1,0:T(8,128)S(1)} %get-tuple-element.104), channel_id=1, source_target_pairs={{0,1},{1,0},{2,3},{3,2},{4,5},{5,4},{6,7},{7,6},{8,9},{9,8},{10,11... | collective-permute-start | bytes 122888 | tf_op jit(solution)/shard_map/ppermute | solution.py:264
  35.4 1.3 %collective-permute-start.9 = (f32[40,128]{1,0:T(8,128)S(1)}, f32[40,128]{1,0:T(8,128)S(1)}, u32[]{:S(2)}, u32[]{:S(2)}) collective-permute-start(f32[40,128]{1,0:T(8,128)S(1)} %get-tuple-element.114), channel_id=1, source_target_pairs={{0,1},{1,0},{2,3},{3,2},{4,5},{5,4},{6,7},{7,6},{8,9},{9,8},{10,11... | collective-permute-start | bytes 61448 | tf_op jit(solution)/shard_map/ppermute | solution.py:264
  37.7 14.5 %collective-permute-start.10 = (bf16[128,2048]{1,0:T(8,128)(2,1)S(1)}, bf16[128,2048]{1,0:T(8,128)(2,1)S(1)}, u32[]{:S(2)}, u32[]{:S(2)}) collective-permute-start(bf16[128,2048]{1,0:T(8,128)(2,1)S(1)} %get-tuple-element.121), channel_id=1, source_target_pairs={{0,2},{1,3},{2,0},{3,1},{4,6},{5,7},{6,4},{7,5},{8,10},{9,11},{10,... | collective-permute-start | bytes 1572872 | tf_op jit(solution)/shard_map/ppermute | solution.py:264
  39.5 10.8 %collective-permute-start.11 = (bf16[40,4224]{1,0:T(8,128)(2,1)S(1)}, bf16[40,4224]{1,0:T(8,128)(2,1)S(1)}, u32[]{:S(2)}, u32[]{:S(2)}) collective-permute-start(bf16[40,4224]{1,0:T(8,128)(2,1)S(1)} %get-tuple-element.123), channel_id=1, source_target_pairs={{0,8},{8,0},{16,24},{24,16},{1,9},{9,1},{17,25},{25,17},{2,10},{10... | collective-permute-start | bytes 1013768 | tf_op jit(solution)/shard_map/ppermute | solution.py:264
  40.4 15.6 %collective-permute-start.14 = (bf16[40,4096]{1,0:T(8,128)(2,1)S(1)}, bf16[40,4096]{1,0:T(8,128)(2,1)S(1)}, u32[]{:S(2)}, u32[]{:S(2)}) collective-permute-start(bf16[40,4096]{1,0:T(8,128)(2,1)S(1)} %get-tuple-element.133), channel_id=1, source_target_pairs={{0,16},{8,24},{16,0},{24,8},{1,17},{9,25},{17,1},{25,9},{2,18},{10... | collective-permute-start | bytes 983048 | tf_op jit(solution)/shard_map/ppermute | solution.py:264
  41.9 14.1 %collective-permute-start.15 = (bf16[40,3968]{1,0:T(8,128)(2,1)S(1)}, bf16[40,3968]{1,0:T(8,128)(2,1)S(1)}, u32[]{:S(2)}, u32[]{:S(2)}) collective-permute-start(bf16[40,3968]{1,0:T(8,128)(2,1)S(1)} %get-tuple-element.134), channel_id=1, source_target_pairs={{0,8},{8,0},{16,24},{24,16},{1,9},{9,1},{17,25},{25,17},{2,10},{10... | collective-permute-start | bytes 952328 | tf_op jit(solution)/shard_map/ppermute | solution.py:264
  50.6 16.3 %collective-permute-start.16 = (bf16[40,4224]{1,0:T(8,128)(2,1)S(1)}, bf16[40,4224]{1,0:T(8,128)(2,1)S(1)}, u32[]{:S(2)}, u32[]{:S(2)}) collective-permute-start(bf16[40,4224]{1,0:T(8,128)(2,1)S(1)} %get-tuple-element.141), channel_id=1, source_target_pairs={{0,16},{8,24},{16,0},{24,8},{1,17},{9,25},{17,1},{25,9},{2,18},{10... | collective-permute-start | bytes 1013768 | tf_op jit(solution)/shard_map/ppermute | solution.py:264
  52.3 13.8 %collective-permute-start.13 = (bf16[128,1024]{1,0:T(8,128)(2,1)S(1)}, bf16[128,1024]{1,0:T(8,128)(2,1)S(1)}, u32[]{:S(2)}, u32[]{:S(2)}) collective-permute-start(bf16[128,1024]{1,0:T(8,128)(2,1)S(1)} %get-tuple-element.131), channel_id=1, source_target_pairs={{0,4},{1,5},{2,6},{3,7},{4,0},{5,1},{6,2},{7,3},{8,12},{9,13},{10,... | collective-permute-start | bytes 786440 | tf_op jit(solution)/shard_map/ppermute | solution.py:264
  56.4 11.8 %collective-permute-start.17 = (bf16[40,3968]{1,0:T(8,128)(2,1)S(1)}, bf16[40,3968]{1,0:T(8,128)(2,1)S(1)}, u32[]{:S(2)}, u32[]{:S(2)}) collective-permute-start(bf16[40,3968]{1,0:T(8,128)(2,1)S(1)} %get-tuple-element.142), channel_id=1, source_target_pairs={{0,16},{8,24},{16,0},{24,8},{1,17},{9,25},{17,1},{25,9},{2,18},{10... | collective-permute-start | bytes 952328 | tf_op jit(solution)/shard_map/ppermute | solution.py:264
  66.9 1.3 %collective-permute-start.18 = (f32[128,128]{1,0:T(8,128)S(1)}, f32[128,128]{1,0:T(8,128)S(1)}, u32[]{:S(2)}, u32[]{:S(2)}) collective-permute-start(f32[128,128]{1,0:T(8,128)S(1)} %get-tuple-element.143), channel_id=1, source_target_pairs={{0,1},{1,0},{2,3},{3,2},{4,5},{5,4},{6,7},{7,6},{8,9},{9,8},{10,11... | collective-permute-start | bytes 196616 | tf_op jit(solution)/shard_map/ppermute | solution.py:264

commit v7 on v6

--- a/solution.py
+++ b/solution.py
@@ -12,7 +12,8 @@
 TN = (((0,), (0,)), ((), ()))
 TILE = 512
 SWAP = 1
-BITS = (2, 4)
+SECOND = 2
+BITS = (4,)
 
 
 def dot(left, right, dims):
@@ -48,10 +49,6 @@
         return got[0] if single else got
 
 
-def is_odd():
-    return lax.rem(lax.axis_index("section"), 2) == 1
-
-
 def either(bit, run):
     for value in range(2):
         pl.when(bit == value)(lambda value=value: run(value))
@@ -59,6 +56,10 @@
 
 def tensor_bit(bit):
     return lax.rem(lax.div(lax.axis_index("tensor"), bit), 2)
+
+
+def both_bits(run):
+    either(tensor_bit(SECOND), lambda here: either(tensor_bit(BITS[0]), lambda mine: run(here, mine)))
 
 
 def is_odd():
@@ -221,23 +222,35 @@
         out[...] = piece[...]
 
 
+def other_columns(width, down, out, at):
+    def run(mine):
+        for k in range(down.shape[1] // (2 * width)):
+            column = (2 * k + 1 - mine) * width
+            out[:, at + k * width : at + (k + 1) * width] = down[:, column : column + width]
+
+    either(tensor_bit(SECOND), run)
+
+
 def output_sums(width, *refs):
-    hids, downs, (send, keep) = refs[:3], refs[3:6], refs[6:]
+    hids, downs, (two, last, send, keep) = refs[:3], refs[3:6], refs[6:]
+    tokens, quarter = send.shape[0], downs[0].shape[1] // 2
+    gots = ((two, 0), (two, quarter), (last, 0))
     tile = min(width, TILE)
 
-    def run(mine):
-        for block in range(keep.shape[1] // width):
-            for which in range(2):
-                for at in range(0, width, tile):
-                    cols = slice((2 * block + which) * width + at, (2 * block + which) * width + at + tile)
-                    here = slice(block * width + at, block * width + at + tile)
-                    total = sum(dot(hid[...], down[:, cols], TN) for hid, down in zip(hids, downs))
-                    if which == mine:
-                        keep[:, here] = total
-                    else:
-                        send[:, here] = total.astype(BF)
-
-    either(tensor_bit(BITS[0]), run)
+    def run(here, mine):
+        for block in range(2 * keep.shape[1] // width):
+            out = keep if block % 2 == mine else send
+            for at in range(0, width, tile):
+                near, far = (2 * block + here) * width + at, block * width + at
+                total = 0.0
+                for k, (hid, down, (got, offset)) in enumerate(zip(hids, downs, gots)):
+                    total += dot(hid[...], down[:, near : near + tile], TN)
+                    other = last[:, quarter + k * tokens : quarter + (k + 1) * tokens]
+                    total += dot(other, got[:, offset + far : offset + far + tile], TN)
+                column = block // 2 * width + at
+                out[:, column : column + tile] = total.astype(out.dtype)
+
+    both_bits(run)
 
 
 def halved(bit, width, keep, got, send, left):
@@ -273,7 +286,7 @@
     rows, wide = gate_weight.shape
     half, both_rows, tokens = wide // 2, 2 * rows, x.shape[0]
     count = lax.axis_size("tensor")
-    assert count > BITS[1] and count & (count - 1) == 0
+    assert count > BITS[0] and count & (count - 1) == 0
     width = wide // count
     four = lax.axis_size("section") == 4
     piece, narrow = ((both_rows, half), BF), ((rows, half), BF)
@@ -335,6 +348,12 @@
     both_first, *hid_first = step(project, [small, small_bf, small_bf], [x, first[0], first[1]], also=[second[1]])
     second[2] = step(picked, piece, [crossed, onward]) if four else ring_passed(first[2], 1)
     share_second = step(share, small, [g, second[2]])
+
+    def two_other(down_a, down_b, out):
+        other_columns(width, down_a, out, 0)
+        other_columns(width, down_b, out, half // 2)
+
+    two_theirs = exchanged(step(two_other, piece, [own[2], second[2]]), "tensor", SECOND)
     both_second, *hid_second = step(project, [small, small_bf, small_bf], [x, second[0], second[1]])
 
     def two_sent(share_a, hid_a, share_b, hid_b, out):
@@ -361,18 +380,22 @@
         shares(width, gr, down, part)
         out[...] = sent_share(part, hid)
 
-    share_first, sent = step(one_sent, [small, small], [g, first[2], hid_first[1]])
+    share_first, sent = step(one_sent, [small, small], [g, first[2], hid_first[1]], also=[two_theirs])
     got_one = exchanged(sent, "tensor", SWAP)
     grads_f32 = [(low_shape, F32), (high_shape, F32), ((both_rows, half), F32)]
-    pair_first, wide_first = step(finish, [small_bf] * 2, [both_first, share_first, got_one, hid_first[0]])
-    quarter = wide // 4
-    send, keep = step(
-        with_width(output_sums),
-        [((tokens, quarter), BF), ((tokens, quarter), F32)],
-        [wide_own, wide_first, wide_second, own[2], first[2], second[2]],
-    )
-    got = exchanged(send, "tensor", BITS[0])
-
+
+    def finish_last(both, share, got, hid, wide_a, wide_b, down, pair, wide_out, out):
+        finish(both, share, got, hid, pair, wide_out)
+        other_columns(width, down, out, 0)
+        for k, ref in enumerate((wide_a, wide_b, wide_out)):
+            out[:, half // 2 + k * tokens : half // 2 + (k + 1) * tokens] = ref[...]
+
+    pair_first, wide_first, sent = step(
+        finish_last,
+        [small_bf, small_bf, ((both_rows, half // 2 + 3 * tokens), BF)],
+        [both_first, share_first, got_one, hid_first[0], wide_own, wide_second, first[2]],
+    )
+    last_theirs = exchanged(sent, "tensor", SECOND)
     def back_down(gr, a, b, side, out):
         odd = is_odd()
         for at in range(0, half, TILE):
@@ -391,6 +414,12 @@
     back_of_down = backward(step(back_down, piece, [g, *hid_first, side_down]))
     own_low, own_high, own_down = step(own_grads, grads_f32, [x, g, *hid_own, pair_own])
     back_of_low = backward(step(back_pair(0), (low_shape, BF), [x, pair_first, side_low]))
+    send, keep = step(
+        with_width(output_sums),
+        [((tokens, wide // 8), BF), ((tokens, wide // 8), F32)],
+        [wide_own, wide_second, wide_first, own[2], second[2], first[2], two_theirs, last_theirs],
+    )
+    got = exchanged(send, "tensor", BITS[0])
 
     def next_half(keep, got, bit):
         cols = keep.shape[1] // 2
@@ -401,9 +430,8 @@
         send, keep = step(body, [((tokens, cols), BF), ((tokens, cols), F32)], [keep, got])
         return keep, exchanged(send, "tensor", bit)
 
-    keep, got = next_half(keep, got, BITS[1])
     back_of_high = backward(step(back_pair(low_columns), (high_shape, BF), [x, pair_first, side_high], also=[back_of_down]))
-    bit = 2 * BITS[1]
+    bit = 2 * BITS[0]
     while bit < count:
         keep, got = next_half(keep, got, bit)
         bit *= 2

time: 69.7 us -> 67.2 us (0.964)
  waiting for transfers between devices: 26.6 us -> 23.4 us
  starting transfers between devices: 27.5 us -> 28.3 us
    ppermute x18 -> x19, waiting for transfers between devices: 23 us -> 19.8 us  [exchanged(): lax.ppermute(value, axis, [(source, source ^ bit) for source in range(cou...]
    ppermute x18 -> x19, starting transfers between devices: 24.1 us -> 24.9 us  [exchanged(): lax.ppermute(value, axis, [(source, source ^ bit) for source in range(cou...]
  transfers between devices with their start and end apart: 19 -> 20, of which waited for: 11 -> 10; matrix products, arithmetic and copies ran while one was open for 0% -> 0% of each run, Pallas kernels for 17% -> 17%
where the time goes in v7:
time: 67.2 us; the launch traced here: 67 us
  starting transfers between devices  28.3 us (42%)
  waiting for transfers between devices  23.4 us (35%)
  Pallas kernels  14.5 us (22%)
  between operations  0.81 us (1%)
    ppermute x19, starting transfers between devices, exchanged(): lax.ppermute(value, axis, [(source, source ^ bit) for source in range(cou...  24.9 us
    ppermute x19, waiting for transfers between devices, exchanged(): lax.ppermute(value, axis, [(source, source ^ bit) for source in range(cou...  19.8 us
    pallas_call x25, Pallas kernels, __call__(): pl.pallas_call(kernel, out_shape=[jax.ShapeDtypeStruct(*s) for s in shape...  14.5 us
    ppermute x1, waiting for transfers between devices, on_device(): lax.ppermute(crossed, 'section', [(source, source ^ 2) for source in (0,...  3.6 us
    ppermute x1, starting transfers between devices, on_device(): lax.ppermute(crossed, 'section', [(source, source ^ 2) for source in (0,...  3.41 us
  transfers between devices with their start and end apart: 20, of which 10 were waited for; matrix products, arithmetic and copies ran while one was open for 0% of the time, Pallas kernels for 17%

profile of v7, /device:TPU:0, one launch (start us, length us, event | category | flops | bytes accessed | tf_op | source)
XLA Modules:
  0.0 67.0 jit_solution(8519878940228303722)
XLA Ops:
  0.6 1.7 %shard_map.84 = (bf16[40,4096]{1,0:T(8,128)(2,1)S(1)}, bf16[40,4096]{1,0:T(8,128)(2,1)S(1)}, bf16[20,4096]{1,0:T(8,128)(2,1)S(1)}, bf16[20,4096]{1,0:T(8,128)(2,1)S(1)}, f32[8,128]{1,0:T(8,128)S(1)}) custom-call(bf16[20,8192]{1,0:T(8,128)(2,1)} %refs_0_.2, bf16[20,8192]{1,0:T(8,128)(2,1)} %refs_1_.2, bf16[20,8192]{1,0:T(8,128)(2,1)} %refs_2_.1), custom_call_target="tpu_custom_call" | custom-call | flops 1 | bytes 1 | tf_op jit(solution)/shard_map/pallas_call | solution.py:39
  2.9 2.6 %collective-permute-start.2 = (bf16[40,4096]{1,0:T(8,128)(2,1)S(1)}, bf16[40,4096]{1,0:T(8,128)(2,1)S(1)}, u32[]{:S(2)}, u32[]{:S(2)}) collective-permute-start(bf16[40,4096]{1,0:T(8,128)(2,1)S(1)} %get-tuple-element.77.refs_3_.refs_1_), channel_id=1, source_target_pairs={{0,16},{8,24},{16,0},{24,8},{1,17},{9,25},{17,1},{25,9},{2,18},{10... | collective-permute-start | bytes 983048 | tf_op jit(solution)/shard_map/ppermute | solution.py:277
  5.8 1.6 %collective-permute-start.5 = (bf16[40,4096]{1,0:T(8,128)(2,1)S(1)}, bf16[40,4096]{1,0:T(8,128)(2,1)S(1)}, u32[]{:S(2)}, u32[]{:S(2)}) collective-permute-start(bf16[40,4096]{1,0:T(8,128)(2,1)S(1)} %get-tuple-element.84.refs_1_.refs_0_.refs_3_), channel_id=1, source_target_pairs={{0,8},{8,0},{16,24},{24,16},{1,9},{9,1},{17,25},{25,17},{2,10},{10... | collective-permute-start | bytes 983048 | tf_op jit(solution)/shard_map/ppermute | solution.py:277
  7.4 1.4 %collective-permute-start.1 = (bf16[40,4096]{1,0:T(8,128)(2,1)S(1)}, bf16[40,4096]{1,0:T(8,128)(2,1)S(1)}, u32[]{:S(2)}, u32[]{:S(2)}) collective-permute-start(bf16[40,4096]{1,0:T(8,128)(2,1)S(1)} %get-tuple-element.76.refs_2_.refs_1_), channel_id=1, source_target_pairs={{0,16},{8,24},{16,0},{24,8},{1,17},{9,25},{17,1},{25,9},{2,18},{10... | collective-permute-start | bytes 983048 | tf_op jit(solution)/shard_map/ppermute | solution.py:277
  8.7 2.4 %shard_map.86 = (bf16[128,8192]{1,0:T(8,128)(2,1)S(1)}, bf16[128,8192]{1,0:T(8,128)(2,1)S(1)}, f32[40,128]{1,0:T(8,128)S(1)}, bf16[40,128]{1,0:T(8,128)(2,1)S(1)...) custom-call(bf16[128,8192]{1,0:T(8,128)(2,1)} %refs_0_.3, bf16[128,8192]{1,0:T(8,128)(2,1)} %refs_1_.3, ...), custom_call_target="tpu_custom_call" | custom-call | flops 1 | bytes 1 | tf_op jit(solution)/shard_map/pallas_call | solution.py:39
  11.7 2.4 %collective-permute-done.2.refs_0_.refs_2_ = bf16[40,4096]{1,0:T(8,128)(2,1)S(1)} collective-permute-done((bf16[40,4096]{1,0:T(8,128)(2,1)S(1)}, bf16[40,4096]{1,0:T(8,128)(2,1)S(1)}, u32[]{:S(2)}, u32[]{:S(2)}) %collective-permute-start.2) | collective-permute-done | bytes 327712 | tf_op jit(solution)/shard_map/ppermute | solution.py:277
  14.1 2.0 %collective-permute-start.4 = (bf16[40,4096]{1,0:T(8,128)(2,1)S(1)}, bf16[40,4096]{1,0:T(8,128)(2,1)S(1)}, u32[]{:S(2)}, u32[]{:S(2)}) collective-permute-start(bf16[40,4096]{1,0:T(8,128)(2,1)S(1)} %get-tuple-element.92), channel_id=1, source_target_pairs={{0,8},{8,0},{16,24},{24,16},{1,9},{9,1},{17,25},{25,17},{2,10},{10... | collective-permute-start | bytes 983048 | tf_op jit(solution)/shard_map/ppermute | solution.py:277
  16.1 3.4 %collective-permute-start.6 = (bf16[40,4096]{1,0:T(8,128)(2,1)S(1)}, bf16[40,4096]{1,0:T(8,128)(2,1)S(1)}, u32[]{:S(2)}, u32[]{:S(2)}) collective-permute-start(bf16[40,4096]{1,0:T(8,128)(2,1)S(1)} %collective-permute-done.5.refs_0_), channel_id=1, source_target_pairs={{0,16},{16,0},{1,17},{17,1},{2,18},{18,2},{3,19},{19,3},{4,20},{20... | collective-permute-start | bytes 983048 | tf_op jit(solution)/shard_map/ppermute | solution.py:335
  19.5 1.6 %collective-permute-done.1.refs_0_.refs_1_ = bf16[40,4096]{1,0:T(8,128)(2,1)S(1)} collective-permute-done((bf16[40,4096]{1,0:T(8,128)(2,1)S(1)}, bf16[40,4096]{1,0:T(8,128)(2,1)S(1)}, u32[]{:S(2)}, u32[]{:S(2)}) %collective-permute-start.1) | collective-permute-done | bytes 327712 | tf_op jit(solution)/shard_map/ppermute | solution.py:277
  21.1 1.5 %collective-permute-start.3 = (bf16[40,4096]{1,0:T(8,128)(2,1)S(1)}, bf16[40,4096]{1,0:T(8,128)(2,1)S(1)}, u32[]{:S(2)}, u32[]{:S(2)}) collective-permute-start(bf16[40,4096]{1,0:T(8,128)(2,1)S(1)} %get-tuple-element.91), channel_id=1, source_target_pairs={{0,8},{8,0},{16,24},{24,16},{1,9},{9,1},{17,25},{25,17},{2,10},{10... | collective-permute-start | bytes 983048 | tf_op jit(solution)/shard_map/ppermute | solution.py:277
  22.6 1.5 %collective-permute-start.8 = (bf16[40,4096]{1,0:T(8,128)(2,1)S(1)}, bf16[40,4096]{1,0:T(8,128)(2,1)S(1)}, u32[]{:S(2)}, u32[]{:S(2)}) collective-permute-start(bf16[40,4096]{1,0:T(8,128)(2,1)S(1)} %get-tuple-element.84.refs_1_.refs_0_.refs_3_), channel_id=1, source_target_pairs={{0,16},{8,24},{16,0},{24,8},{1,17},{9,25},{17,1},{25,9},{2,18},{10... | collective-permute-start | bytes 983048 | tf_op jit(solution)/shard_map/ppermute | solution.py:277
  24.1 0.8 %shard_map.90 = (f32[40,128]{1,0:T(8,128)S(1)}, bf16[40,128]{1,0:T(8,128)(2,1)S(1)}, bf16[40,128]{1,0:T(8,128)(2,1)S(1)}, f32[8,128]{1,0:T(8,128)S(1)}) custom-call(bf16[128,8192]{1,0:T(8,128)(2,1)S(1)} %get-tuple-element.88.refs_0_, bf16[40,4096]{1,0:T(8,128)(2,1)S(1)} %collective-permute-done.1.refs_0_.refs_1_, ...), custom_call_target="tpu_custom_call" | custom-call | flops 1 | bytes 1 | tf_op jit(solution)/shard_map/pallas_call | solution.py:39
  25.0 3.6 %collective-permute-done.6.refs_1_ = bf16[40,4096]{1,0:T(8,128)(2,1)S(1)} collective-permute-done((bf16[40,4096]{1,0:T(8,128)(2,1)S(1)}, bf16[40,4096]{1,0:T(8,128)(2,1)S(1)}, u32[]{:S(2)}, u32[]{:S(2)}) %collective-permute-start.6) | collective-permute-done | bytes 327712 | tf_op jit(solution)/shard_map/ppermute | solution.py:335
  29.2 1.6 %collective-permute-start.9 = (bf16[40,4096]{1,0:T(8,128)(2,1)S(1)}, bf16[40,4096]{1,0:T(8,128)(2,1)S(1)}, u32[]{:S(2)}, u32[]{:S(2)}) collective-permute-start(bf16[40,4096]{1,0:T(8,128)(2,1)S(1)} %get-tuple-element.112), channel_id=1, source_target_pairs={{0,2},{1,3},{2,0},{3,1},{4,6},{5,7},{6,4},{7,5},{8,10},{9,11},{10,... | collective-permute-start | bytes 983048 | tf_op jit(solution)/shard_map/ppermute | solution.py:277
  30.8 0.8 %shard_map.94 = (f32[40,128]{1,0:T(8,128)S(1)}, bf16[40,128]{1,0:T(8,128)(2,1)S(1)}, bf16[40,128]{1,0:T(8,128)(2,1)S(1)}, f32[8,128]{1,0:T(8,128)S(1)}) custom-call(bf16[128,8192]{1,0:T(8,128)(2,1)S(1)} %get-tuple-element.88.refs_0_, bf16[40,4096]{1,0:T(8,128)(2,1)S(1)} %collective-permute-done.3.refs_1_, ...), custom_call_target="tpu_custom_call" | custom-call | flops 1 | bytes 1 | tf_op jit(solution)/shard_map/pallas_call | solution.py:39
  32.1 1.2 %collective-permute-start.13 = (bf16[40,4096]{1,0:T(8,128)(2,1)S(1)}, bf16[40,4096]{1,0:T(8,128)(2,1)S(1)}, u32[]{:S(2)}, u32[]{:S(2)}) collective-permute-start(bf16[40,4096]{1,0:T(8,128)(2,1)S(1)} %get-tuple-element.125), channel_id=1, source_target_pairs={{0,8},{8,0},{16,24},{24,16},{1,9},{9,1},{17,25},{25,17},{2,10},{10... | collective-permute-start | bytes 983048 | tf_op jit(solution)/shard_map/ppermute | solution.py:277
  33.2 1.2 %collective-permute-done.7.refs_6_ = f32[80,128]{1,0:T(8,128)S(1)} collective-permute-done((f32[80,128]{1,0:T(8,128)S(1)}, f32[80,128]{1,0:T(8,128)S(1)}, u32[]{:S(2)}, u32[]{:S(2)}) %collective-permute-start.7) | collective-permute-done | bytes 40992 | tf_op jit(solution)/shard_map/ppermute | solution.py:277
  34.9 1.0 %collective-permute-start.12 = (bf16[40,4224]{1,0:T(8,128)(2,1)S(1)}, bf16[40,4224]{1,0:T(8,128)(2,1)S(1)}, u32[]{:S(2)}, u32[]{:S(2)}) collective-permute-start(bf16[40,4224]{1,0:T(8,128)(2,1)S(1)} %get-tuple-element.123), channel_id=1, source_target_pairs={{0,8},{8,0},{16,24},{24,16},{1,9},{9,1},{17,25},{25,17},{2,10},{10... | collective-permute-start | bytes 1013768 | tf_op jit(solution)/shard_map/ppermute | solution.py:277
  35.9 1.8 %collective-permute-done.9.refs_3_.refs_6_ = bf16[40,4096]{1,0:T(8,128)(2,1)S(1)} collective-permute-done((bf16[40,4096]{1,0:T(8,128)(2,1)S(1)}, bf16[40,4096]{1,0:T(8,128)(2,1)S(1)}, u32[]{:S(2)}, u32[]{:S(2)}) %collective-permute-start.9) | collective-permute-done | bytes 327712 | tf_op jit(solution)/shard_map/ppermute | solution.py:277
  38.3 1.2 %collective-permute-done.10.refs_2_ = f32[40,128]{1,0:T(8,128)S(1)} collective-permute-done((f32[40,128]{1,0:T(8,128)S(1)}, f32[40,128]{1,0:T(8,128)S(1)}, u32[]{:S(2)}, u32[]{:S(2)}) %collective-permute-start.10) | collective-permute-done | bytes 20512 | tf_op jit(solution)/shard_map/ppermute | solution.py:277
  39.5 3.3 %collective-permute-done.13.refs_3_.refs_2_ = bf16[40,4096]{1,0:T(8,128)(2,1)S(1)} collective-permute-done((bf16[40,4096]{1,0:T(8,128)(2,1)S(1)}, bf16[40,4096]{1,0:T(8,128)(2,1)S(1)}, u32[]{:S(2)}, u32[]{:S(2)}) %collective-permute-start.13) | collective-permute-done | bytes 327712 | tf_op jit(solution)/shard_map/ppermute | solution.py:277
  43.2 1.6 %collective-permute-start.15 = (bf16[40,4096]{1,0:T(8,128)(2,1)S(1)}, bf16[40,4096]{1,0:T(8,128)(2,1)S(1)}, u32[]{:S(2)}, u32[]{:S(2)}) collective-permute-start(bf16[40,4096]{1,0:T(8,128)(2,1)S(1)} %get-tuple-element.133), channel_id=1, source_target_pairs={{0,16},{8,24},{16,0},{24,8},{1,17},{9,25},{17,1},{25,9},{2,18},{10... | collective-permute-start | bytes 983048 | tf_op jit(solution)/shard_map/ppermute | solution.py:277
  44.8 1.1 %collective-permute-start.16 = (bf16[40,3968]{1,0:T(8,128)(2,1)S(1)}, bf16[40,3968]{1,0:T(8,128)(2,1)S(1)}, u32[]{:S(2)}, u32[]{:S(2)}) collective-permute-start(bf16[40,3968]{1,0:T(8,128)(2,1)S(1)} %get-tuple-element.134), channel_id=1, source_target_pairs={{0,8},{8,0},{16,24},{24,16},{1,9},{9,1},{17,25},{25,17},{2,10},{10... | collective-permute-start | bytes 952328 | tf_op jit(solution)/shard_map/ppermute | solution.py:277
  45.9 1.6 %collective-permute-start.11 = (bf16[40,2432]{1,0:T(8,128)(2,1)S(1)}, bf16[40,2432]{1,0:T(8,128)(2,1)S(1)}, u32[]{:S(2)}, u32[]{:S(2)}) collective-permute-start(bf16[40,2432]{1,0:T(8,128)(2,1)S(1)} %get-tuple-element.121), channel_id=1, source_target_pairs={{0,2},{1,3},{2,0},{3,1},{4,6},{5,7},{6,4},{7,5},{8,10},{9,11},{10,... | collective-permute-start | bytes 583688 | tf_op jit(solution)/shard_map/ppermute | solution.py:277
  48.2 1.8 %collective-permute-done.12.refs_2_.refs_4_ = bf16[40,4224]{1,0:T(8,128)(2,1)S(1)} collective-permute-done((bf16[40,4224]{1,0:T(8,128)(2,1)S(1)}, bf16[40,4224]{1,0:T(8,128)(2,1)S(1)}, u32[]{:S(2)}, u32[]{:S(2)}) %collective-permute-start.12) | collective-permute-done | bytes 337952 | tf_op jit(solution)/shard_map/ppermute | solution.py:277
  50.3 1.6 %collective-permute-start.17 = (bf16[40,4224]{1,0:T(8,128)(2,1)S(1)}, bf16[40,4224]{1,0:T(8,128)(2,1)S(1)}, u32[]{:S(2)}, u32[]{:S(2)}) collective-permute-start(bf16[40,4224]{1,0:T(8,128)(2,1)S(1)} %get-tuple-element.141), channel_id=1, source_target_pairs={{0,16},{8,24},{16,0},{24,8},{1,17},{9,25},{17,1},{25,9},{2,18},{10... | collective-permute-start | bytes 1013768 | tf_op jit(solution)/shard_map/ppermute | solution.py:277
  51.9 1.0 %shard_map.104 = (bf16[128,1024]{1,0:T(8,128)(2,1)S(1)}, f32[128,1024]{1,0:T(8,128)S(1)}, f32[8,128]{1,0:T(8,128)S(1)}) custom-call(bf16[40,128]{1,0:T(8,128)(2,1)S(1)} %get-tuple-element.108.refs_4_.refs_0_, bf16[40,128]{1,0:T(8,128)(2,1)S(1)} %get-tuple-element.109.refs_5_.refs_1_, bf16[40,128]{1,0:T(8,128)(2,1)S(1)} %get-tuple-element.120.refs_2_, ...), custom_call_target="tpu_custom_call" | custom-call | flops 1 | bytes 1 | tf_op jit(solution)/shard_map/pallas_call | solution.py:39
  52.9 3.5 %collective-permute-start.14 = (bf16[128,1024]{1,0:T(8,128)(2,1)S(1)}, bf16[128,1024]{1,0:T(8,128)(2,1)S(1)}, u32[]{:S(2)}, u32[]{:S(2)}) collective-permute-start(bf16[128,1024]{1,0:T(8,128)(2,1)S(1)} %get-tuple-element.131), channel_id=1, source_target_pairs={{0,4},{1,5},{2,6},{3,7},{4,0},{5,1},{6,2},{7,3},{8,12},{9,13},{10,... | collective-permute-start | bytes 786440 | tf_op jit(solution)/shard_map/ppermute | solution.py:277
  57.3 1.0 %shard_map.106 = (f32[20,8192]{1,0:T(8,128)}, f32[8,128]{1,0:T(8,128)S(1)}) custom-call(f32[40,4096]{1,0:T(8,128)S(1)} %get-tuple-element.132.refs_0_, bf16[40,4096]{1,0:T(8,128)(2,1)S(1)} %collective-permute-done.15.refs_3_.refs_1_, bf16[40,4096]{1,0:T(8,128)(2,1)S(1)} %collective-permute-done.13.refs_3_.refs_2_, f32[8,128]{1,0:T(8,128)S(1)} %get-tuple-element.136.refs_3_), custom_call_target="tpu_custom_call" | custom-call | flops 1 | bytes 1 | tf_op jit(solution)/shard_map/pallas_call | solution.py:39
  58.4 5.3 %collective-permute-done.14.refs_1_ = bf16[128,1024]{1,0:T(8,128)(2,1)S(1)} collective-permute-done((bf16[128,1024]{1,0:T(8,128)(2,1)S(1)}, bf16[128,1024]{1,0:T(8,128)(2,1)S(1)}, u32[]{:S(2)}, u32[]{:S(2)}) %collective-permute-start.14) | collective-permute-done | bytes 262176 | tf_op jit(solution)/shard_map/ppermute | solution.py:277
  64.4 1.2 %collective-permute-done.19.refs_6_ = f32[128,128]{1,0:T(8,128)S(1)} collective-permute-done((f32[128,128]{1,0:T(8,128)S(1)}, f32[128,128]{1,0:T(8,128)S(1)}, u32[]{:S(2)}, u32[]{:S(2)}) %collective-permute-start.19) | collective-permute-done | bytes 65568 | tf_op jit(solution)/shard_map/ppermute | solution.py:277
  65.7 1.4 %shard_map.108 = (f32[20,8192]{1,0:T(8,128)}, f32[20,8192]{1,0:T(8,128)}, f32[8,128]{1,0:T(8,128)}) custom-call(f32[40,4224]{1,0:T(8,128)S(1)} %get-tuple-element.139.refs_0_, f32[40,3968]{1,0:T(8,128)S(1)} %get-tuple-element.140.refs_1_, bf16[40,4224]{1,0:T(8,128)(2,1)S(1)} %collective-permute-done.17.refs_2_, ...), custom_call_target="tpu_custom_call" | custom-call | flops 1 | bytes 1 | tf_op jit(solution)/shard_map/pallas_call | solution.py:39
  (33 shorter events, 6.4 us)
Async XLA Ops:
  2.4 3.1 %collective-permute-start = (bf16[20,4096]{1,0:T(8,128)(2,1)S(1)}, bf16[20,4096]{1,0:T(8,128)(2,1)S(1)}, u32[]{:S(2)}, u32[]{:S(2)}) collective-permute-start(bf16[20,4096]{1,0:T(8,128)(2,1)S(1)} %get-tuple-element.79), channel_id=1, source_target_pairs={{0,1},{1,0},{2,3},{3,2},{4,5},{5,4},{6,7},{7,6},{8,9},{9,8},{10,11... | collective-permute-start | bytes 491528 | tf_op jit(solution)/shard_map/ppermute | solution.py:277
  2.9 11.2 %collective-permute-start.2 = (bf16[40,4096]{1,0:T(8,128)(2,1)S(1)}, bf16[40,4096]{1,0:T(8,128)(2,1)S(1)}, u32[]{:S(2)}, u32[]{:S(2)}) collective-permute-start(bf16[40,4096]{1,0:T(8,128)(2,1)S(1)} %get-tuple-element.77.refs_3_.refs_1_), channel_id=1, source_target_pairs={{0,16},{8,24},{16,0},{24,8},{1,17},{9,25},{17,1},{25,9},{2,18},{10... | collective-permute-start | bytes 983048 | tf_op jit(solution)/shard_map/ppermute | solution.py:277
  5.8 10.2 %collective-permute-start.5 = (bf16[40,4096]{1,0:T(8,128)(2,1)S(1)}, bf16[40,4096]{1,0:T(8,128)(2,1)S(1)}, u32[]{:S(2)}, u32[]{:S(2)}) collective-permute-start(bf16[40,4096]{1,0:T(8,128)(2,1)S(1)} %get-tuple-element.84.refs_1_.refs_0_.refs_3_), channel_id=1, source_target_pairs={{0,8},{8,0},{16,24},{24,16},{1,9},{9,1},{17,25},{25,17},{2,10},{10... | collective-permute-start | bytes 983048 | tf_op jit(solution)/shard_map/ppermute | solution.py:277
  7.4 13.7 %collective-permute-start.1 = (bf16[40,4096]{1,0:T(8,128)(2,1)S(1)}, bf16[40,4096]{1,0:T(8,128)(2,1)S(1)}, u32[]{:S(2)}, u32[]{:S(2)}) collective-permute-start(bf16[40,4096]{1,0:T(8,128)(2,1)S(1)} %get-tuple-element.76.refs_2_.refs_1_), channel_id=1, source_target_pairs={{0,16},{8,24},{16,0},{24,8},{1,17},{9,25},{17,1},{25,9},{2,18},{10... | collective-permute-start | bytes 983048 | tf_op jit(solution)/shard_map/ppermute | solution.py:277
  14.1 10.1 %collective-permute-start.4 = (bf16[40,4096]{1,0:T(8,128)(2,1)S(1)}, bf16[40,4096]{1,0:T(8,128)(2,1)S(1)}, u32[]{:S(2)}, u32[]{:S(2)}) collective-permute-start(bf16[40,4096]{1,0:T(8,128)(2,1)S(1)} %get-tuple-element.92), channel_id=1, source_target_pairs={{0,8},{8,0},{16,24},{24,16},{1,9},{9,1},{17,25},{25,17},{2,10},{10... | collective-permute-start | bytes 983048 | tf_op jit(solution)/shard_map/ppermute | solution.py:277
  16.1 12.5 %collective-permute-start.6 = (bf16[40,4096]{1,0:T(8,128)(2,1)S(1)}, bf16[40,4096]{1,0:T(8,128)(2,1)S(1)}, u32[]{:S(2)}, u32[]{:S(2)}) collective-permute-start(bf16[40,4096]{1,0:T(8,128)(2,1)S(1)} %collective-permute-done.5.refs_0_), channel_id=1, source_target_pairs={{0,16},{16,0},{1,17},{17,1},{2,18},{18,2},{3,19},{19,3},{4,20},{20... | collective-permute-start | bytes 983048 | tf_op jit(solution)/shard_map/ppermute | solution.py:335
  21.1 9.7 %collective-permute-start.3 = (bf16[40,4096]{1,0:T(8,128)(2,1)S(1)}, bf16[40,4096]{1,0:T(8,128)(2,1)S(1)}, u32[]{:S(2)}, u32[]{:S(2)}) collective-permute-start(bf16[40,4096]{1,0:T(8,128)(2,1)S(1)} %get-tuple-element.91), channel_id=1, source_target_pairs={{0,8},{8,0},{16,24},{24,16},{1,9},{9,1},{17,25},{25,17},{2,10},{10... | collective-permute-start | bytes 983048 | tf_op jit(solution)/shard_map/ppermute | solution.py:277
  22.6 13.3 %collective-permute-start.8 = (bf16[40,4096]{1,0:T(8,128)(2,1)S(1)}, bf16[40,4096]{1,0:T(8,128)(2,1)S(1)}, u32[]{:S(2)}, u32[]{:S(2)}) collective-permute-start(bf16[40,4096]{1,0:T(8,128)(2,1)S(1)} %get-tuple-element.84.refs_1_.refs_0_.refs_3_), channel_id=1, source_target_pairs={{0,16},{8,24},{16,0},{24,8},{1,17},{9,25},{17,1},{25,9},{2,18},{10... | collective-permute-start | bytes 983048 | tf_op jit(solution)/shard_map/ppermute | solution.py:277
  29.2 8.6 %collective-permute-start.9 = (bf16[40,4096]{1,0:T(8,128)(2,1)S(1)}, bf16[40,4096]{1,0:T(8,128)(2,1)S(1)}, u32[]{:S(2)}, u32[]{:S(2)}) collective-permute-start(bf16[40,4096]{1,0:T(8,128)(2,1)S(1)} %get-tuple-element.112), channel_id=1, source_target_pairs={{0,2},{1,3},{2,0},{3,1},{4,6},{5,7},{6,4},{7,5},{8,10},{9,11},{10,... | collective-permute-start | bytes 983048 | tf_op jit(solution)/shard_map/ppermute | solution.py:277
  32.1 10.7 %collective-permute-start.13 = (bf16[40,4096]{1,0:T(8,128)(2,1)S(1)}, bf16[40,4096]{1,0:T(8,128)(2,1)S(1)}, u32[]{:S(2)}, u32[]{:S(2)}) collective-permute-start(bf16[40,4096]{1,0:T(8,128)(2,1)S(1)} %get-tuple-element.125), channel_id=1, source_target_pairs={{0,8},{8,0},{16,24},{24,16},{1,9},{9,1},{17,25},{25,17},{2,10},{10... | collective-permute-start | bytes 983048 | tf_op jit(solution)/shard_map/ppermute | solution.py:277
  33.2 1.2 %collective-permute-start.7 = (f32[80,128]{1,0:T(8,128)S(1)}, f32[80,128]{1,0:T(8,128)S(1)}, u32[]{:S(2)}, u32[]{:S(2)}) collective-permute-start(f32[80,128]{1,0:T(8,128)S(1)} %get-tuple-element.105), channel_id=1, source_target_pairs={{0,1},{1,0},{2,3},{3,2},{4,5},{5,4},{6,7},{7,6},{8,9},{9,8},{10,11... | collective-permute-start | bytes 122888 | tf_op jit(solution)/shard_map/ppermute | solution.py:277
  34.9 15.1 %collective-permute-start.12 = (bf16[40,4224]{1,0:T(8,128)(2,1)S(1)}, bf16[40,4224]{1,0:T(8,128)(2,1)S(1)}, u32[]{:S(2)}, u32[]{:S(2)}) collective-permute-start(bf16[40,4224]{1,0:T(8,128)(2,1)S(1)} %get-tuple-element.123), channel_id=1, source_target_pairs={{0,8},{8,0},{16,24},{24,16},{1,9},{9,1},{17,25},{25,17},{2,10},{10... | collective-permute-start | bytes 1013768 | tf_op jit(solution)/shard_map/ppermute | solution.py:277
  38.2 1.3 %collective-permute-start.10 = (f32[40,128]{1,0:T(8,128)S(1)}, f32[40,128]{1,0:T(8,128)S(1)}, u32[]{:S(2)}, u32[]{:S(2)}) collective-permute-start(f32[40,128]{1,0:T(8,128)S(1)} %get-tuple-element.117), channel_id=1, source_target_pairs={{0,1},{1,0},{2,3},{3,2},{4,5},{5,4},{6,7},{7,6},{8,9},{9,8},{10,11... | collective-permute-start | bytes 61448 | tf_op jit(solution)/shard_map/ppermute | solution.py:277
  43.2 13.3 %collective-permute-start.15 = (bf16[40,4096]{1,0:T(8,128)(2,1)S(1)}, bf16[40,4096]{1,0:T(8,128)(2,1)S(1)}, u32[]{:S(2)}, u32[]{:S(2)}) collective-permute-start(bf16[40,4096]{1,0:T(8,128)(2,1)S(1)} %get-tuple-element.133), channel_id=1, source_target_pairs={{0,16},{8,24},{16,0},{24,8},{1,17},{9,25},{17,1},{25,9},{2,18},{10... | collective-permute-start | bytes 983048 | tf_op jit(solution)/shard_map/ppermute | solution.py:277
  44.8 11.7 %collective-permute-start.16 = (bf16[40,3968]{1,0:T(8,128)(2,1)S(1)}, bf16[40,3968]{1,0:T(8,128)(2,1)S(1)}, u32[]{:S(2)}, u32[]{:S(2)}) collective-permute-start(bf16[40,3968]{1,0:T(8,128)(2,1)S(1)} %get-tuple-element.134), channel_id=1, source_target_pairs={{0,8},{8,0},{16,24},{24,16},{1,9},{9,1},{17,25},{25,17},{2,10},{10... | collective-permute-start | bytes 952328 | tf_op jit(solution)/shard_map/ppermute | solution.py:277
  45.9 6.0 %collective-permute-start.11 = (bf16[40,2432]{1,0:T(8,128)(2,1)S(1)}, bf16[40,2432]{1,0:T(8,128)(2,1)S(1)}, u32[]{:S(2)}, u32[]{:S(2)}) collective-permute-start(bf16[40,2432]{1,0:T(8,128)(2,1)S(1)} %get-tuple-element.121), channel_id=1, source_target_pairs={{0,2},{1,3},{2,0},{3,1},{4,6},{5,7},{6,4},{7,5},{8,10},{9,11},{10,... | collective-permute-start | bytes 583688 | tf_op jit(solution)/shard_map/ppermute | solution.py:277
  50.3 14.1 %collective-permute-start.17 = (bf16[40,4224]{1,0:T(8,128)(2,1)S(1)}, bf16[40,4224]{1,0:T(8,128)(2,1)S(1)}, u32[]{:S(2)}, u32[]{:S(2)}) collective-permute-start(bf16[40,4224]{1,0:T(8,128)(2,1)S(1)} %get-tuple-element.141), channel_id=1, source_target_pairs={{0,16},{8,24},{16,0},{24,8},{1,17},{9,25},{17,1},{25,9},{2,18},{10... | collective-permute-start | bytes 1013768 | tf_op jit(solution)/shard_map/ppermute | solution.py:277
  52.9 10.7 %collective-permute-start.14 = (bf16[128,1024]{1,0:T(8,128)(2,1)S(1)}, bf16[128,1024]{1,0:T(8,128)(2,1)S(1)}, u32[]{:S(2)}, u32[]{:S(2)}) collective-permute-start(bf16[128,1024]{1,0:T(8,128)(2,1)S(1)} %get-tuple-element.131), channel_id=1, source_target_pairs={{0,4},{1,5},{2,6},{3,7},{4,0},{5,1},{6,2},{7,3},{8,12},{9,13},{10,... | collective-permute-start | bytes 786440 | tf_op jit(solution)/shard_map/ppermute | solution.py:277
  56.8 8.9 %collective-permute-start.18 = (bf16[40,3968]{1,0:T(8,128)(2,1)S(1)}, bf16[40,3968]{1,0:T(8,128)(2,1)S(1)}, u32[]{:S(2)}, u32[]{:S(2)}) collective-permute-start(bf16[40,3968]{1,0:T(8,128)(2,1)S(1)} %get-tuple-element.142), channel_id=1, source_target_pairs={{0,16},{8,24},{16,0},{24,8},{1,17},{9,25},{17,1},{25,9},{2,18},{10... | collective-permute-start | bytes 952328 | tf_op jit(solution)/shard_map/ppermute | solution.py:277
  64.4 1.3 %collective-permute-start.19 = (f32[128,128]{1,0:T(8,128)S(1)}, f32[128,128]{1,0:T(8,128)S(1)}, u32[]{:S(2)}, u32[]{:S(2)}) collective-permute-start(f32[128,128]{1,0:T(8,128)S(1)} %get-tuple-element.143), channel_id=1, source_target_pairs={{0,1},{1,0},{2,3},{3,2},{4,5},{5,4},{6,7},{7,6},{8,9},{9,8},{10,11... | collective-permute-start | bytes 196616 | tf_op jit(solution)/shard_map/ppermute | solution.py:277

commit v8 on v7

--- a/solution.py
+++ b/solution.py
@@ -70,6 +70,18 @@
     return lax.broadcasted_iota(jnp.int32, like.shape, 0) < like.shape[0] // 2
 
 
+def tiles(size, step=TILE):
+    return [slice(at, min(at + step, size)) for at in range(0, size, step)]
+
+
+def shifted(cut, offset):
+    return slice(cut.start + offset, cut.stop + offset)
+
+
+def starts_of(sizes):
+    return [sum(sizes[:k]) for k in range(len(sizes))]
+
+
 def placed(rows):
     shape = (2 * rows, rows)
     place = lax.broadcasted_iota(jnp.int32, shape, 0) - lax.broadcasted_iota(jnp.int32, shape, 1)
@@ -78,27 +90,30 @@
 
 def stacked(out, upper, lower, upper_at=0, lower_at=0):
     top, bottom = placed(upper.shape[0])
-    for at in range(0, out.shape[1], TILE):
-        first, second = slice(upper_at + at, upper_at + at + TILE), slice(lower_at + at, lower_at + at + TILE)
-        out[:, at : at + TILE] = (dot(top, upper[:, first], NN) + dot(bottom, lower[:, second], NN)).astype(BF)
+    for cut in tiles(out.shape[1]):
+        first, second = shifted(cut, upper_at), shifted(cut, lower_at)
+        out[:, cut] = (dot(top, upper[:, first], NN) + dot(bottom, lower[:, second], NN)).astype(BF)
 
 
 def runs(width, wide):
     return [(SWAP * width * j, 2 * SWAP * width * j) for j in range(wide // (2 * SWAP * width))]
 
 
-def packed(width, gate, up, down, high, low, keep, send, gate_here, up_here, down_here, sems):
+def packed(width, gate, up, down, *refs):
+    *pieces, keep, send, gate_here, up_here, down_here, sems = refs
     copies = [
         pltpu.make_async_copy(there, here, sems.at[k])
         for k, (there, here) in enumerate(((gate, gate_here), (up, up_here), (down, down_here)))
     ]
     for copy in copies:
         copy.start()
-    half = high.shape[1]
+    half = down.shape[1] // 2
     copies[0].wait()
     copies[1].wait()
-    stacked(high, gate_here, up_here, half, half)
-    stacked(low, gate_here, up_here)
+    at = 0
+    for piece in pieces:
+        stacked(piece, gate_here, up_here, at, at)
+        at += piece.shape[1]
     copies[2].wait()
 
     def run(mine):
@@ -111,20 +126,15 @@
     either(tensor_bit(SWAP), run)
 
 
-def project_tiles(x, low, high):
-    half = low.shape[1]
-    tile = min(half, 1024)
-    total = jnp.zeros((low.shape[0], x.shape[0]), F32)
-    for at in range(0, half, tile):
-        cut = slice(at, at + tile)
-        total += dot(low[:, cut], x[:, cut], NT)
-        total += dot(high[:, cut], x[:, half + at : half + at + tile], NT)
-    return total
-
-
-def project(x, low, high, both, hid_a, hid_b):
-    rows = low.shape[0] // 2
-    total = project_tiles(x, low, high)
+def project(x, *refs):
+    pieces, (both, hid_a, hid_b) = refs[:-3], refs[-3:]
+    rows = both.shape[0] // 2
+    total = jnp.zeros(both.shape, F32)
+    at = 0
+    for piece in pieces:
+        for cut in tiles(piece.shape[1], 1024):
+            total += dot(piece[:, cut], x[:, shifted(cut, at)], NT)
+        at += piece.shape[1]
     both[...] = total
     hidden = total * jax.nn.sigmoid(total) * pltpu.roll(total, rows, 0)
     hidden = jnp.where(top_rows(total), hidden, 0.0)
@@ -132,12 +142,13 @@
     hid_b[...] = pltpu.roll(hidden, rows, 0).astype(BF)
 
 
-def project_first(x_there, g_there, low, high, x, g, both, hid_a, hid_b, sems):
+def project_first(x_there, g_there, *refs):
+    *pieces, x, g, both, hid_a, hid_b, sems = refs
     copies = [pltpu.make_async_copy(x_there, x, sems.at[0]), pltpu.make_async_copy(g_there, g, sems.at[1])]
     for copy in copies:
         copy.start()
     copies[0].wait()
-    project(x, low, high, both, hid_a, hid_b)
+    project(x, *pieces, both, hid_a, hid_b)
     copies[1].wait()
 
 
@@ -178,19 +189,18 @@
     return dot(hid_a[...], g[:, cut], NN) + dot(hid_b[...], g[:, half + at : half + at + TILE], NN)
 
 
-def tiles(size):
-    return [slice(at, min(at + TILE, size)) for at in range(0, size, TILE)]
-
-
-def shifted(cut, offset):
-    return slice(cut.start + offset, cut.stop + offset)
-
-
-def own_grads(x, g, hid_a, hid_b, pair, low, high, down):
+def pair_columns(x, pair, outs):
+    at = 0
+    for out in outs:
+        for cut in tiles(out.shape[1]):
+            out[:, cut] = dot(pair[...], x[:, shifted(cut, at)], NN).astype(out.dtype)
+        at += out.shape[1]
+
+
+def own_grads(x, g, hid_a, hid_b, pair, *refs):
+    *outs, down = refs
     half = down.shape[1]
-    for out, offset in ((low, 0), (high, low.shape[1])):
-        for cut in tiles(out.shape[1]):
-            out[:, cut] = dot(pair[...], x[:, shifted(cut, offset)], NN)
+    pair_columns(x, pair, outs)
     for at in range(0, half, TILE):
         down[:, at : at + TILE] = down_columns(g, hid_a, hid_b, at, half)
 
@@ -201,10 +211,8 @@
         out[:, at : at + TILE] = down_columns(g, hid_a, hid_b, at, half).astype(BF)
 
 
-def sent_pair(x, pair, low, high):
-    for out, offset in ((low, 0), (high, low.shape[1])):
-        for cut in tiles(out.shape[1]):
-            out[:, cut] = dot(pair[...], x[:, shifted(cut, offset)], NN).astype(BF)
+def sent_pair(x, pair, *outs):
+    pair_columns(x, pair, outs)
 
 
 def kept(side, odd, four, wanted):
@@ -267,9 +275,8 @@
     either(tensor_bit(bit), run)
 
 
-def final_output(keep, got, out, end):
+def final_output(keep, got, out):
     out[...] = (keep[...] + got[...].astype(F32)).astype(BF)
-    end[...] = jnp.zeros_like(end)
 
 
 def exchanged(value, axis, bit):
@@ -305,7 +312,7 @@
     def relay(here, value):
         if not four:
             return ring_passed(here, 1)
-        return exchanged(step(picked, piece, [here, value]), "section", 1)
+        return exchanged(step(picked, (value.shape, BF), [here, value]), "section", 1)
 
     def outward(value):
         return exchanged(value, "section", 1) if four else ring_passed(value, -1)
@@ -313,48 +320,47 @@
     def backward(value):
         return exchanged(value, "section", 2) if four else ring_passed(value, -1)
 
-    own, first, second = [None] * 3, [None] * 3, [None] * 3
+    third = wide // 128 // 3 * 128
     held = pltpu.VMEM((rows, wide), BF)
-    own[1], own[0], down_keep, down_send = step(
+    *own, down_keep, down_send = step(
         with_width(packed),
-        [piece, piece, narrow, narrow],
+        [((both_rows, size), BF) for size in (half, half)] + [narrow, narrow],
         [gate_weight, up_weight, down_weight],
         far=3,
         scratch=[held, held, held, pltpu.SemaphoreType.DMA((3,))],
     )
-    first[1] = one_hop(own[1])
+    first = [one_hop(own[0])]
     down_got = exchanged(down_send, "tensor", SWAP)
-    first[0] = one_hop(own[0])
+    first += [one_hop(value) for value in own[1:]]
 
     def joined(keep, got, out):
         stacked(out, keep, got)
 
-    own[2] = step(joined, piece, [down_keep, down_got])
+    down_own = step(joined, piece, [down_keep, down_got])
     if four:
-        crossed = exchanged(own[2], "section", 1)
+        crossed = exchanged(down_own, "section", 1)
         onward = lax.ppermute(crossed, "section", [(source, source ^ 2) for source in (0, 2)])
-    first[2] = one_hop(own[2])
+    down_first = one_hop(down_own)
     x, g, both_own, *hid_own = step(
         project_first,
         [(x.shape, BF), (g.shape, BF), small, small_bf, small_bf],
-        [x, g, own[0], own[1]],
+        [x, g, *own],
         far=2,
         scratch=[pltpu.SemaphoreType.DMA((2,))],
     )
     share = with_width(shares)
-    share_own = step(share, small, [g, own[2]])
-    second[1] = relay(first[1], own[1])
-    second[0] = relay(first[0], own[0])
-    both_first, *hid_first = step(project, [small, small_bf, small_bf], [x, first[0], first[1]], also=[second[1]])
-    second[2] = step(picked, piece, [crossed, onward]) if four else ring_passed(first[2], 1)
-    share_second = step(share, small, [g, second[2]])
+    share_own = step(share, small, [g, down_own])
+    second = [relay(here, value) for here, value in zip(first, own)]
+    both_first, *hid_first = step(project, [small, small_bf, small_bf], [x, *first], also=[second[0]])
+    down_second = step(picked, piece, [crossed, onward]) if four else ring_passed(down_first, 1)
+    share_second = step(share, small, [g, down_second])
 
     def two_other(down_a, down_b, out):
         other_columns(width, down_a, out, 0)
         other_columns(width, down_b, out, half // 2)
 
-    two_theirs = exchanged(step(two_other, piece, [own[2], second[2]]), "tensor", SECOND)
-    both_second, *hid_second = step(project, [small, small_bf, small_bf], [x, second[0], second[1]])
+    two_theirs = exchanged(step(two_other, piece, [down_own, down_second]), "tensor", SECOND)
+    both_second, *hid_second = step(project, [small, small_bf, small_bf], [x, *second])
 
     def two_sent(share_a, hid_a, share_b, hid_b, out):
         out[:both_rows, :] = sent_share(share_a, hid_a)
@@ -371,18 +377,16 @@
     pair_own, wide_own, pair_second, wide_second = step(
         finish_two, [small_bf] * 4, [both_own, share_own, hid_own[0], both_second, share_second, hid_second[0], got_two]
     )
-    low_columns = half + 128
-    low_shape, high_shape = (both_rows, low_columns), (both_rows, wide - low_columns)
-    low, high = step(sent_pair, [(low_shape, BF), (high_shape, BF)], [x, pair_second])
-    side_low, side_high = outward(low), outward(high)
+    sizes = (third + 256, third, wide - 2 * third - 256)
+    shapes = [(both_rows, size) for size in sizes]
+    sides = [outward(value) for value in step(sent_pair, [(shape, BF) for shape in shapes], [x, pair_second])]
 
     def one_sent(gr, down, hid, part, out):
         shares(width, gr, down, part)
         out[...] = sent_share(part, hid)
 
-    share_first, sent = step(one_sent, [small, small], [g, first[2], hid_first[1]], also=[two_theirs])
+    share_first, sent = step(one_sent, [small, small], [g, down_first, hid_first[1]], also=[two_theirs])
     got_one = exchanged(sent, "tensor", SWAP)
-    grads_f32 = [(low_shape, F32), (high_shape, F32), ((both_rows, half), F32)]
 
     def finish_last(both, share, got, hid, wide_a, wide_b, down, pair, wide_out, out):
         finish(both, share, got, hid, pair, wide_out)
@@ -393,9 +397,10 @@
     pair_first, wide_first, sent = step(
         finish_last,
         [small_bf, small_bf, ((both_rows, half // 2 + 3 * tokens), BF)],
-        [both_first, share_first, got_one, hid_first[0], wide_own, wide_second, first[2]],
+        [both_first, share_first, got_one, hid_first[0], wide_own, wide_second, down_first],
     )
     last_theirs = exchanged(sent, "tensor", SECOND)
+
     def back_down(gr, a, b, side, out):
         odd = is_odd()
         for at in range(0, half, TILE):
@@ -412,14 +417,25 @@
         return body
 
     back_of_down = backward(step(back_down, piece, [g, *hid_first, side_down]))
-    own_low, own_high, own_down = step(own_grads, grads_f32, [x, g, *hid_own, pair_own])
-    back_of_low = backward(step(back_pair(0), (low_shape, BF), [x, pair_first, side_low]))
+    own_sums = step(
+        own_grads,
+        [(shape, F32) for shape in shapes] + [((both_rows, half), F32)],
+        [x, g, *hid_own, pair_own],
+
+    )
+
     send, keep = step(
         with_width(output_sums),
         [((tokens, wide // 8), BF), ((tokens, wide // 8), F32)],
-        [wide_own, wide_second, wide_first, own[2], second[2], first[2], two_theirs, last_theirs],
+        [wide_own, wide_second, wide_first, down_own, down_second, down_first, two_theirs, last_theirs],
     )
     got = exchanged(send, "tensor", BITS[0])
+
+    def back_piece(k, also=()):
+        body = back_pair(starts_of(sizes)[k])
+        return backward(step(body, (shapes[k], BF), [x, pair_first, sides[k]], also=also))
+
+    backs = [back_piece(0)]
 
     def next_half(keep, got, bit):
         cols = keep.shape[1] // 2
@@ -430,7 +446,7 @@
         send, keep = step(body, [((tokens, cols), BF), ((tokens, cols), F32)], [keep, got])
         return keep, exchanged(send, "tensor", bit)
 
-    back_of_high = backward(step(back_pair(low_columns), (high_shape, BF), [x, pair_first, side_high], also=[back_of_down]))
+    backs += [back_piece(1), back_piece(2)]
     bit = 2 * BITS[0]
     while bit < count:
         keep, got = next_half(keep, got, bit)
@@ -448,23 +464,21 @@
             out[:, cut] = value[:rows]
             out[:, half + at : half + at + TILE] = value[rows:]
 
-    def final_pair(low_ref, high_ref, low_back, high_back, low_side, high_side, out_gate, out_up):
-        odd = is_odd()
-        for offset, refs in ((0, (low_ref, low_back, low_side)), (low_columns, (high_ref, high_back, high_side))):
-            for cut in tiles(refs[0].shape[1]):
-                value = finished(*refs, odd, cut)
+    def final_pair(*refs):
+        odd, (out_gate, out_up) = is_odd(), refs[9:]
+        for k, offset in enumerate(starts_of(sizes)):
+            for cut in tiles(sizes[k]):
+                value = finished(*refs[k:9:3], odd, cut)
                 out_gate[:, shifted(cut, offset)] = value[:rows]
                 out_up[:, shifted(cut, offset)] = value[rows:]
 
     whole = ((rows, wide), F32)
-    grad_down = step(final_down, whole, [own_down, back_of_down, side_down])
-    output, end = step(final_output, [((tokens, width), BF), ((128, 128), F32)], [keep, got])
-    end = exchanged(end, "tensor", SWAP)
+    grad_down = step(final_down, whole, [own_sums[3], back_of_down, side_down])
+    output = step(final_output, ((tokens, width), BF), [keep, got])
     grad_gate, grad_up = step(
         final_pair,
         [whole, whole],
-        [own_low, own_high, back_of_low, back_of_high, side_low, side_high],
-        also=[end],
+        [*own_sums[:3], *backs, *sides],
     )
     return (output, grad_gate, grad_up, grad_down)
 

time: 67.2 us -> 68.4 us (1.018)
  starting transfers between devices: 28.3 us -> 30.1 us
  waiting for transfers between devices: 23.4 us -> 22.7 us
    ppermute x19 -> x20, starting transfers between devices: 24.9 us -> 26.6 us  [exchanged(): lax.ppermute(value, axis, [(source, source ^ bit) for source in range(cou...]
    ppermute x19 -> x20, waiting for transfers between devices: 19.8 us -> 19.1 us  [exchanged(): lax.ppermute(value, axis, [(source, source ^ bit) for source in range(cou...]
    pallas_call x25 -> x26, Pallas kernels: 14.5 us -> 14.6 us  [__call__(): pl.pallas_call(kernel, out_shape=[jax.ShapeDtypeStruct(*s) for s in shape...]
  transfers between devices with their start and end apart: 20 -> 21, of which waited for: 10 -> 10; matrix products, arithmetic and copies ran while one was open for 0% -> 0% of each run, Pallas kernels for 17% -> 17%
where the time goes in v8:
time: 68.4 us; the launch traced here: 68.2 us
  starting transfers between devices  30.1 us (44%)
  waiting for transfers between devices  22.7 us (33%)
  Pallas kernels  14.6 us (21%)
  between operations  0.83 us (1%)
    ppermute x20, starting transfers between devices, exchanged(): lax.ppermute(value, axis, [(source, source ^ bit) for source in range(cou...  26.6 us
    ppermute x20, waiting for transfers between devices, exchanged(): lax.ppermute(value, axis, [(source, source ^ bit) for source in range(cou...  19.1 us
    pallas_call x26, Pallas kernels, __call__(): pl.pallas_call(kernel, out_shape=[jax.ShapeDtypeStruct(*s) for s in shape...  14.6 us
    ppermute x1, waiting for transfers between devices, on_device(): lax.ppermute(crossed, 'section', [(source, source ^ 2) for source in (0,...  3.6 us
    ppermute x1, starting transfers between devices, on_device(): lax.ppermute(crossed, 'section', [(source, source ^ 2) for source in (0,...  3.41 us
  transfers between devices with their start and end apart: 21, of which 10 were waited for; matrix products, arithmetic and copies ran while one was open for 0% of the time, Pallas kernels for 17%

profile of v8, /device:TPU:0, one launch (start us, length us, event | category | flops | bytes accessed | tf_op | source)
XLA Modules:
  0.0 68.2 jit_solution(3309519178196155758)
XLA Ops:
  0.6 1.7 %shard_map.84 = (bf16[40,4096]{1,0:T(8,128)(2,1)S(1)}, bf16[40,4096]{1,0:T(8,128)(2,1)S(1)}, bf16[20,4096]{1,0:T(8,128)(2,1)S(1)}, bf16[20,4096]{1,0:T(8,128)(2,1)S(1)}, f32[8,128]{1,0:T(8,128)S(1)}) custom-call(bf16[20,8192]{1,0:T(8,128)(2,1)} %refs_0_.2, bf16[20,8192]{1,0:T(8,128)(2,1)} %refs_1_.2, bf16[20,8192]{1,0:T(8,128)(2,1)} %refs_2_.1), custom_call_target="tpu_custom_call" | custom-call | flops 1 | bytes 1 | tf_op jit(solution)/shard_map/pallas_call | solution.py:39
  2.9 2.6 %collective-permute-start.1 = (bf16[40,4096]{1,0:T(8,128)(2,1)S(1)}, bf16[40,4096]{1,0:T(8,128)(2,1)S(1)}, u32[]{:S(2)}, u32[]{:S(2)}) collective-permute-start(bf16[40,4096]{1,0:T(8,128)(2,1)S(1)} %get-tuple-element.79.refs_2_.refs_1_), channel_id=1, source_target_pairs={{0,16},{8,24},{16,0},{24,8},{1,17},{9,25},{17,1},{25,9},{2,18},{10... | collective-permute-start | bytes 983048 | tf_op jit(solution)/shard_map/ppermute | solution.py:284
  5.8 1.6 %collective-permute-start.5 = (bf16[40,4096]{1,0:T(8,128)(2,1)S(1)}, bf16[40,4096]{1,0:T(8,128)(2,1)S(1)}, u32[]{:S(2)}, u32[]{:S(2)}) collective-permute-start(bf16[40,4096]{1,0:T(8,128)(2,1)S(1)} %get-tuple-element.87.refs_1_.refs_0_.refs_3_), channel_id=1, source_target_pairs={{0,8},{8,0},{16,24},{24,16},{1,9},{9,1},{17,25},{25,17},{2,10},{10... | collective-permute-start | bytes 983048 | tf_op jit(solution)/shard_map/ppermute | solution.py:284
  7.4 1.4 %collective-permute-start.3 = (bf16[40,4096]{1,0:T(8,128)(2,1)S(1)}, bf16[40,4096]{1,0:T(8,128)(2,1)S(1)}, u32[]{:S(2)}, u32[]{:S(2)}) collective-permute-start(bf16[40,4096]{1,0:T(8,128)(2,1)S(1)} %get-tuple-element.80.refs_3_.refs_1_), channel_id=1, source_target_pairs={{0,16},{8,24},{16,0},{24,8},{1,17},{9,25},{17,1},{25,9},{2,18},{10... | collective-permute-start | bytes 983048 | tf_op jit(solution)/shard_map/ppermute | solution.py:284
  8.7 2.4 %shard_map.86 = (bf16[128,8192]{1,0:T(8,128)(2,1)S(1)}, bf16[128,8192]{1,0:T(8,128)(2,1)S(1)}, f32[40,128]{1,0:T(8,128)S(1)}, bf16[40,128]{1,0:T(8,128)(2,1)S(1)...) custom-call(bf16[128,8192]{1,0:T(8,128)(2,1)} %refs_0_.3, bf16[128,8192]{1,0:T(8,128)(2,1)} %refs_1_.3, ...), custom_call_target="tpu_custom_call" | custom-call | flops 1 | bytes 1 | tf_op jit(solution)/shard_map/pallas_call | solution.py:39
  11.7 2.4 %collective-permute-done.1.refs_0_.refs_1_ = bf16[40,4096]{1,0:T(8,128)(2,1)S(1)} collective-permute-done((bf16[40,4096]{1,0:T(8,128)(2,1)S(1)}, bf16[40,4096]{1,0:T(8,128)(2,1)S(1)}, u32[]{:S(2)}, u32[]{:S(2)}) %collective-permute-start.1) | collective-permute-done | bytes 327712 | tf_op jit(solution)/shard_map/ppermute | solution.py:284
  14.1 2.0 %collective-permute-start.2 = (bf16[40,4096]{1,0:T(8,128)(2,1)S(1)}, bf16[40,4096]{1,0:T(8,128)(2,1)S(1)}, u32[]{:S(2)}, u32[]{:S(2)}) collective-permute-start(bf16[40,4096]{1,0:T(8,128)(2,1)S(1)} %get-tuple-element.93), channel_id=1, source_target_pairs={{0,8},{8,0},{16,24},{24,16},{1,9},{9,1},{17,25},{25,17},{2,10},{10... | collective-permute-start | bytes 983048 | tf_op jit(solution)/shard_map/ppermute | solution.py:284
  16.1 3.4 %collective-permute-start.6 = (bf16[40,4096]{1,0:T(8,128)(2,1)S(1)}, bf16[40,4096]{1,0:T(8,128)(2,1)S(1)}, u32[]{:S(2)}, u32[]{:S(2)}) collective-permute-start(bf16[40,4096]{1,0:T(8,128)(2,1)S(1)} %collective-permute-done.5.refs_0_), channel_id=1, source_target_pairs={{0,16},{16,0},{1,17},{17,1},{2,18},{18,2},{3,19},{19,3},{4,20},{20... | collective-permute-start | bytes 983048 | tf_op jit(solution)/shard_map/ppermute | solution.py:342
  19.5 1.6 %collective-permute-done.3.refs_0_.refs_2_ = bf16[40,4096]{1,0:T(8,128)(2,1)S(1)} collective-permute-done((bf16[40,4096]{1,0:T(8,128)(2,1)S(1)}, bf16[40,4096]{1,0:T(8,128)(2,1)S(1)}, u32[]{:S(2)}, u32[]{:S(2)}) %collective-permute-start.3) | collective-permute-done | bytes 327712 | tf_op jit(solution)/shard_map/ppermute | solution.py:284
  21.1 1.5 %collective-permute-start.4 = (bf16[40,4096]{1,0:T(8,128)(2,1)S(1)}, bf16[40,4096]{1,0:T(8,128)(2,1)S(1)}, u32[]{:S(2)}, u32[]{:S(2)}) collective-permute-start(bf16[40,4096]{1,0:T(8,128)(2,1)S(1)} %get-tuple-element.95), channel_id=1, source_target_pairs={{0,8},{8,0},{16,24},{24,16},{1,9},{9,1},{17,25},{25,17},{2,10},{10... | collective-permute-start | bytes 983048 | tf_op jit(solution)/shard_map/ppermute | solution.py:284
  22.6 1.5 %collective-permute-start.8 = (bf16[40,4096]{1,0:T(8,128)(2,1)S(1)}, bf16[40,4096]{1,0:T(8,128)(2,1)S(1)}, u32[]{:S(2)}, u32[]{:S(2)}) collective-permute-start(bf16[40,4096]{1,0:T(8,128)(2,1)S(1)} %get-tuple-element.87.refs_1_.refs_0_.refs_3_), channel_id=1, source_target_pairs={{0,16},{8,24},{16,0},{24,8},{1,17},{9,25},{17,1},{25,9},{2,18},{10... | collective-permute-start | bytes 983048 | tf_op jit(solution)/shard_map/ppermute | solution.py:284
  25.0 3.6 %collective-permute-done.6.refs_1_ = bf16[40,4096]{1,0:T(8,128)(2,1)S(1)} collective-permute-done((bf16[40,4096]{1,0:T(8,128)(2,1)S(1)}, bf16[40,4096]{1,0:T(8,128)(2,1)S(1)}, u32[]{:S(2)}, u32[]{:S(2)}) %collective-permute-start.6) | collective-permute-done | bytes 327712 | tf_op jit(solution)/shard_map/ppermute | solution.py:342
  29.2 1.6 %collective-permute-start.9 = (bf16[40,4096]{1,0:T(8,128)(2,1)S(1)}, bf16[40,4096]{1,0:T(8,128)(2,1)S(1)}, u32[]{:S(2)}, u32[]{:S(2)}) collective-permute-start(bf16[40,4096]{1,0:T(8,128)(2,1)S(1)} %get-tuple-element.115), channel_id=1, source_target_pairs={{0,2},{1,3},{2,0},{3,1},{4,6},{5,7},{6,4},{7,5},{8,10},{9,11},{10,... | collective-permute-start | bytes 983048 | tf_op jit(solution)/shard_map/ppermute | solution.py:284
  30.8 0.8 %shard_map.94 = (f32[40,128]{1,0:T(8,128)S(1)}, bf16[40,128]{1,0:T(8,128)(2,1)S(1)}, bf16[40,128]{1,0:T(8,128)(2,1)S(1)}, f32[8,128]{1,0:T(8,128)S(1)}) custom-call(bf16[128,8192]{1,0:T(8,128)(2,1)S(1)} %get-tuple-element.91.refs_0_, bf16[40,4096]{1,0:T(8,128)(2,1)S(1)} %collective-permute-done.2.refs_3_.refs_1_, ...), custom_call_target="tpu_custom_call" | custom-call | flops 1 | bytes 1 | tf_op jit(solution)/shard_map/pallas_call | solution.py:39
  32.1 1.2 %collective-permute-start.12 = (bf16[40,4096]{1,0:T(8,128)(2,1)S(1)}, bf16[40,4096]{1,0:T(8,128)(2,1)S(1)}, u32[]{:S(2)}, u32[]{:S(2)}) collective-permute-start(bf16[40,4096]{1,0:T(8,128)(2,1)S(1)} %get-tuple-element.126), channel_id=1, source_target_pairs={{0,8},{8,0},{16,24},{24,16},{1,9},{9,1},{17,25},{25,17},{2,10},{10... | collective-permute-start | bytes 983048 | tf_op jit(solution)/shard_map/ppermute | solution.py:284
  33.2 1.2 %collective-permute-done.7.refs_6_ = f32[80,128]{1,0:T(8,128)S(1)} collective-permute-done((f32[80,128]{1,0:T(8,128)S(1)}, f32[80,128]{1,0:T(8,128)S(1)}, u32[]{:S(2)}, u32[]{:S(2)}) %collective-permute-start.7) | collective-permute-done | bytes 40992 | tf_op jit(solution)/shard_map/ppermute | solution.py:284
  34.9 2.8 %collective-permute-done.9.refs_3_.refs_6_ = bf16[40,4096]{1,0:T(8,128)(2,1)S(1)} collective-permute-done((bf16[40,4096]{1,0:T(8,128)(2,1)S(1)}, bf16[40,4096]{1,0:T(8,128)(2,1)S(1)}, u32[]{:S(2)}, u32[]{:S(2)}) %collective-permute-start.9) | collective-permute-done | bytes 327712 | tf_op jit(solution)/shard_map/ppermute | solution.py:284
  38.4 1.1 %collective-permute-done.10.refs_2_ = f32[40,128]{1,0:T(8,128)S(1)} collective-permute-done((f32[40,128]{1,0:T(8,128)S(1)}, f32[40,128]{1,0:T(8,128)S(1)}, u32[]{:S(2)}, u32[]{:S(2)}) %collective-permute-start.10) | collective-permute-done | bytes 20512 | tf_op jit(solution)/shard_map/ppermute | solution.py:284
  39.5 1.8 %collective-permute-start.11 = (bf16[40,2432]{1,0:T(8,128)(2,1)S(1)}, bf16[40,2432]{1,0:T(8,128)(2,1)S(1)}, u32[]{:S(2)}, u32[]{:S(2)}) collective-permute-start(bf16[40,2432]{1,0:T(8,128)(2,1)S(1)} %get-tuple-element.124), channel_id=1, source_target_pairs={{0,2},{1,3},{2,0},{3,1},{4,6},{5,7},{6,4},{7,5},{8,10},{9,11},{10,... | collective-permute-start | bytes 583688 | tf_op jit(solution)/shard_map/ppermute | solution.py:284
  41.3 0.9 %collective-permute-start.16 = (bf16[40,2688]{1,0:T(8,128)(2,1)S(1)}, bf16[40,2688]{1,0:T(8,128)(2,1)S(1)}, u32[]{:S(2)}, u32[]{:S(2)}) collective-permute-start(bf16[40,2688]{1,0:T(8,128)(2,1)S(1)} %get-tuple-element.136), channel_id=1, source_target_pairs={{0,8},{8,0},{16,24},{24,16},{1,9},{9,1},{17,25},{25,17},{2,10},{10... | collective-permute-start | bytes 645128 | tf_op jit(solution)/shard_map/ppermute | solution.py:284
  42.2 1.1 %collective-permute-start.15 = (bf16[40,2560]{1,0:T(8,128)(2,1)S(1)}, bf16[40,2560]{1,0:T(8,128)(2,1)S(1)}, u32[]{:S(2)}, u32[]{:S(2)}) collective-permute-start(bf16[40,2560]{1,0:T(8,128)(2,1)S(1)} %get-tuple-element.135), channel_id=1, source_target_pairs={{0,8},{8,0},{16,24},{24,16},{1,9},{9,1},{17,25},{25,17},{2,10},{10... | collective-permute-start | bytes 614408 | tf_op jit(solution)/shard_map/ppermute | solution.py:284
  43.8 1.6 %collective-permute-start.14 = (bf16[40,4096]{1,0:T(8,128)(2,1)S(1)}, bf16[40,4096]{1,0:T(8,128)(2,1)S(1)}, u32[]{:S(2)}, u32[]{:S(2)}) collective-permute-start(bf16[40,4096]{1,0:T(8,128)(2,1)S(1)} %get-tuple-element.133), channel_id=1, source_target_pairs={{0,16},{8,24},{16,0},{24,8},{1,17},{9,25},{17,1},{25,9},{2,18},{10... | collective-permute-start | bytes 983048 | tf_op jit(solution)/shard_map/ppermute | solution.py:284
  46.5 1.0 %shard_map.103 = (bf16[128,1024]{1,0:T(8,128)(2,1)S(1)}, f32[128,1024]{1,0:T(8,128)S(1)}, f32[8,128]{1,0:T(8,128)S(1)}) custom-call(bf16[40,128]{1,0:T(8,128)(2,1)S(1)} %get-tuple-element.111.refs_4_.refs_0_, bf16[40,128]{1,0:T(8,128)(2,1)S(1)} %get-tuple-element.112.refs_5_.refs_1_, bf16[40,128]{1,0:T(8,128)(2,1)S(1)} %get-tuple-element.123.refs_2_, ...), custom_call_target="tpu_custom_call" | custom-call | flops 1 | bytes 1 | tf_op jit(solution)/shard_map/pallas_call | solution.py:39
  47.5 2.8 %collective-permute-start.13 = (bf16[128,1024]{1,0:T(8,128)(2,1)S(1)}, bf16[128,1024]{1,0:T(8,128)(2,1)S(1)}, u32[]{:S(2)}, u32[]{:S(2)}) collective-permute-start(bf16[128,1024]{1,0:T(8,128)(2,1)S(1)} %get-tuple-element.131), channel_id=1, source_target_pairs={{0,4},{1,5},{2,6},{3,7},{4,0},{5,1},{6,2},{7,3},{8,12},{9,13},{10,... | collective-permute-start | bytes 786440 | tf_op jit(solution)/shard_map/ppermute | solution.py:284
  50.6 1.6 %collective-permute-start.18 = (bf16[40,2944]{1,0:T(8,128)(2,1)S(1)}, bf16[40,2944]{1,0:T(8,128)(2,1)S(1)}, u32[]{:S(2)}, u32[]{:S(2)}) collective-permute-start(bf16[40,2944]{1,0:T(8,128)(2,1)S(1)} %get-tuple-element.147), channel_id=1, source_target_pairs={{0,16},{8,24},{16,0},{24,8},{1,17},{9,25},{17,1},{25,9},{2,18},{10... | collective-permute-start | bytes 706568 | tf_op jit(solution)/shard_map/ppermute | solution.py:284
  52.4 1.1 %collective-permute-start.19 = (bf16[40,2688]{1,0:T(8,128)(2,1)S(1)}, bf16[40,2688]{1,0:T(8,128)(2,1)S(1)}, u32[]{:S(2)}, u32[]{:S(2)}) collective-permute-start(bf16[40,2688]{1,0:T(8,128)(2,1)S(1)} %get-tuple-element.148), channel_id=1, source_target_pairs={{0,16},{8,24},{16,0},{24,8},{1,17},{9,25},{17,1},{25,9},{2,18},{10... | collective-permute-start | bytes 645128 | tf_op jit(solution)/shard_map/ppermute | solution.py:284
  53.5 1.9 %collective-permute-done.15.refs_2_.refs_8_ = bf16[40,2560]{1,0:T(8,128)(2,1)S(1)} collective-permute-done((bf16[40,2560]{1,0:T(8,128)(2,1)S(1)}, bf16[40,2560]{1,0:T(8,128)(2,1)S(1)}, u32[]{:S(2)}, u32[]{:S(2)}) %collective-permute-start.15) | collective-permute-done | bytes 204832 | tf_op jit(solution)/shard_map/ppermute | solution.py:284
  55.7 1.8 %collective-permute-start.20 = (bf16[40,2560]{1,0:T(8,128)(2,1)S(1)}, bf16[40,2560]{1,0:T(8,128)(2,1)S(1)}, u32[]{:S(2)}, u32[]{:S(2)}) collective-permute-start(bf16[40,2560]{1,0:T(8,128)(2,1)S(1)} %get-tuple-element.149), channel_id=1, source_target_pairs={{0,16},{8,24},{16,0},{24,8},{1,17},{9,25},{17,1},{25,9},{2,18},{10... | collective-permute-start | bytes 614408 | tf_op jit(solution)/shard_map/ppermute | solution.py:284
  57.4 1.0 %shard_map.107 = (f32[20,8192]{1,0:T(8,128)}, f32[8,128]{1,0:T(8,128)S(1)}) custom-call(f32[40,4096]{1,0:T(8,128)S(1)} %get-tuple-element.132.refs_0_, bf16[40,4096]{1,0:T(8,128)(2,1)S(1)} %collective-permute-done.14.refs_1_, bf16[40,4096]{1,0:T(8,128)(2,1)S(1)} %collective-permute-done.12.refs_3_.refs_2_, f32[8,128]{1,0:T(8,128)S(1)} %get-tuple-element.141.refs_3_), custom_call_target="tpu_custom_call" | custom-call | flops 1 | bytes 1 | tf_op jit(solution)/shard_map/pallas_call | solution.py:39
  58.5 3.3 %collective-permute-done.13.refs_1_ = bf16[128,1024]{1,0:T(8,128)(2,1)S(1)} collective-permute-done((bf16[128,1024]{1,0:T(8,128)(2,1)S(1)}, bf16[128,1024]{1,0:T(8,128)(2,1)S(1)}, u32[]{:S(2)}, u32[]{:S(2)}) %collective-permute-start.13) | collective-permute-done | bytes 262176 | tf_op jit(solution)/shard_map/ppermute | solution.py:284
  62.5 4.3 %collective-permute-done.20.refs_5_ = bf16[40,2560]{1,0:T(8,128)(2,1)S(1)} collective-permute-done((bf16[40,2560]{1,0:T(8,128)(2,1)S(1)}, bf16[40,2560]{1,0:T(8,128)(2,1)S(1)}, u32[]{:S(2)}, u32[]{:S(2)}) %collective-permute-start.20) | collective-permute-done | bytes 204832 | tf_op jit(solution)/shard_map/ppermute | solution.py:284
  66.8 1.4 %shard_map.109 = (f32[20,8192]{1,0:T(8,128)}, f32[20,8192]{1,0:T(8,128)}, f32[8,128]{1,0:T(8,128)}) custom-call(f32[40,2944]{1,0:T(8,128)S(1)} %get-tuple-element.144.refs_0_, f32[40,2688]{1,0:T(8,128)S(1)} %get-tuple-element.145.refs_1_, f32[40,2560]{1,0:T(8,128)S(1)} %get-tuple-element.146.refs_2_, bf16[40,2944]{1,0:T(8,128)(2,1)S(1)} %collective-permute-done.18.refs_3_, ...), custom_call_target="tpu_custom_call" | custom-call | flops 1 | bytes 1 | tf_op jit(solution)/shard_map/pallas_call | solution.py:39
  (36 shorter events, 7.3 us)
Async XLA Ops:
  2.4 3.1 %collective-permute-start = (bf16[20,4096]{1,0:T(8,128)(2,1)S(1)}, bf16[20,4096]{1,0:T(8,128)(2,1)S(1)}, u32[]{:S(2)}, u32[]{:S(2)}) collective-permute-start(bf16[20,4096]{1,0:T(8,128)(2,1)S(1)} %get-tuple-element.82), channel_id=1, source_target_pairs={{0,1},{1,0},{2,3},{3,2},{4,5},{5,4},{6,7},{7,6},{8,9},{9,8},{10,11... | collective-permute-start | bytes 491528 | tf_op jit(solution)/shard_map/ppermute | solution.py:284
  2.9 11.2 %collective-permute-start.1 = (bf16[40,4096]{1,0:T(8,128)(2,1)S(1)}, bf16[40,4096]{1,0:T(8,128)(2,1)S(1)}, u32[]{:S(2)}, u32[]{:S(2)}) collective-permute-start(bf16[40,4096]{1,0:T(8,128)(2,1)S(1)} %get-tuple-element.79.refs_2_.refs_1_), channel_id=1, source_target_pairs={{0,16},{8,24},{16,0},{24,8},{1,17},{9,25},{17,1},{25,9},{2,18},{10... | collective-permute-start | bytes 983048 | tf_op jit(solution)/shard_map/ppermute | solution.py:284
  5.8 10.2 %collective-permute-start.5 = (bf16[40,4096]{1,0:T(8,128)(2,1)S(1)}, bf16[40,4096]{1,0:T(8,128)(2,1)S(1)}, u32[]{:S(2)}, u32[]{:S(2)}) collective-permute-start(bf16[40,4096]{1,0:T(8,128)(2,1)S(1)} %get-tuple-element.87.refs_1_.refs_0_.refs_3_), channel_id=1, source_target_pairs={{0,8},{8,0},{16,24},{24,16},{1,9},{9,1},{17,25},{25,17},{2,10},{10... | collective-permute-start | bytes 983048 | tf_op jit(solution)/shard_map/ppermute | solution.py:284
  7.4 13.7 %collective-permute-start.3 = (bf16[40,4096]{1,0:T(8,128)(2,1)S(1)}, bf16[40,4096]{1,0:T(8,128)(2,1)S(1)}, u32[]{:S(2)}, u32[]{:S(2)}) collective-permute-start(bf16[40,4096]{1,0:T(8,128)(2,1)S(1)} %get-tuple-element.80.refs_3_.refs_1_), channel_id=1, source_target_pairs={{0,16},{8,24},{16,0},{24,8},{1,17},{9,25},{17,1},{25,9},{2,18},{10... | collective-permute-start | bytes 983048 | tf_op jit(solution)/shard_map/ppermute | solution.py:284
  14.1 10.1 %collective-permute-start.2 = (bf16[40,4096]{1,0:T(8,128)(2,1)S(1)}, bf16[40,4096]{1,0:T(8,128)(2,1)S(1)}, u32[]{:S(2)}, u32[]{:S(2)}) collective-permute-start(bf16[40,4096]{1,0:T(8,128)(2,1)S(1)} %get-tuple-element.93), channel_id=1, source_target_pairs={{0,8},{8,0},{16,24},{24,16},{1,9},{9,1},{17,25},{25,17},{2,10},{10... | collective-permute-start | bytes 983048 | tf_op jit(solution)/shard_map/ppermute | solution.py:284
  16.1 12.5 %collective-permute-start.6 = (bf16[40,4096]{1,0:T(8,128)(2,1)S(1)}, bf16[40,4096]{1,0:T(8,128)(2,1)S(1)}, u32[]{:S(2)}, u32[]{:S(2)}) collective-permute-start(bf16[40,4096]{1,0:T(8,128)(2,1)S(1)} %collective-permute-done.5.refs_0_), channel_id=1, source_target_pairs={{0,16},{16,0},{1,17},{17,1},{2,18},{18,2},{3,19},{19,3},{4,20},{20... | collective-permute-start | bytes 983048 | tf_op jit(solution)/shard_map/ppermute | solution.py:342
  21.1 9.7 %collective-permute-start.4 = (bf16[40,4096]{1,0:T(8,128)(2,1)S(1)}, bf16[40,4096]{1,0:T(8,128)(2,1)S(1)}, u32[]{:S(2)}, u32[]{:S(2)}) collective-permute-start(bf16[40,4096]{1,0:T(8,128)(2,1)S(1)} %get-tuple-element.95), channel_id=1, source_target_pairs={{0,8},{8,0},{16,24},{24,16},{1,9},{9,1},{17,25},{25,17},{2,10},{10... | collective-permute-start | bytes 983048 | tf_op jit(solution)/shard_map/ppermute | solution.py:284
  22.6 12.3 %collective-permute-start.8 = (bf16[40,4096]{1,0:T(8,128)(2,1)S(1)}, bf16[40,4096]{1,0:T(8,128)(2,1)S(1)}, u32[]{:S(2)}, u32[]{:S(2)}) collective-permute-start(bf16[40,4096]{1,0:T(8,128)(2,1)S(1)} %get-tuple-element.87.refs_1_.refs_0_.refs_3_), channel_id=1, source_target_pairs={{0,16},{8,24},{16,0},{24,8},{1,17},{9,25},{17,1},{25,9},{2,18},{10... | collective-permute-start | bytes 983048 | tf_op jit(solution)/shard_map/ppermute | solution.py:284
  29.2 8.6 %collective-permute-start.9 = (bf16[40,4096]{1,0:T(8,128)(2,1)S(1)}, bf16[40,4096]{1,0:T(8,128)(2,1)S(1)}, u32[]{:S(2)}, u32[]{:S(2)}) collective-permute-start(bf16[40,4096]{1,0:T(8,128)(2,1)S(1)} %get-tuple-element.115), channel_id=1, source_target_pairs={{0,2},{1,3},{2,0},{3,1},{4,6},{5,7},{6,4},{7,5},{8,10},{9,11},{10,... | collective-permute-start | bytes 983048 | tf_op jit(solution)/shard_map/ppermute | solution.py:284
  32.1 11.3 %collective-permute-start.12 = (bf16[40,4096]{1,0:T(8,128)(2,1)S(1)}, bf16[40,4096]{1,0:T(8,128)(2,1)S(1)}, u32[]{:S(2)}, u32[]{:S(2)}) collective-permute-start(bf16[40,4096]{1,0:T(8,128)(2,1)S(1)} %get-tuple-element.126), channel_id=1, source_target_pairs={{0,8},{8,0},{16,24},{24,16},{1,9},{9,1},{17,25},{25,17},{2,10},{10... | collective-permute-start | bytes 983048 | tf_op jit(solution)/shard_map/ppermute | solution.py:284
  33.2 1.2 %collective-permute-start.7 = (f32[80,128]{1,0:T(8,128)S(1)}, f32[80,128]{1,0:T(8,128)S(1)}, u32[]{:S(2)}, u32[]{:S(2)}) collective-permute-start(f32[80,128]{1,0:T(8,128)S(1)} %get-tuple-element.108), channel_id=1, source_target_pairs={{0,1},{1,0},{2,3},{3,2},{4,5},{5,4},{6,7},{7,6},{8,9},{9,8},{10,11... | collective-permute-start | bytes 122888 | tf_op jit(solution)/shard_map/ppermute | solution.py:284
  38.2 1.3 %collective-permute-start.10 = (f32[40,128]{1,0:T(8,128)S(1)}, f32[40,128]{1,0:T(8,128)S(1)}, u32[]{:S(2)}, u32[]{:S(2)}) collective-permute-start(f32[40,128]{1,0:T(8,128)S(1)} %get-tuple-element.120), channel_id=1, source_target_pairs={{0,1},{1,0},{2,3},{3,2},{4,5},{5,4},{6,7},{7,6},{8,9},{9,8},{10,11... | collective-permute-start | bytes 61448 | tf_op jit(solution)/shard_map/ppermute | solution.py:284
  38.3 12.1 %collective-permute-start.17 = (bf16[40,2944]{1,0:T(8,128)(2,1)S(1)}, bf16[40,2944]{1,0:T(8,128)(2,1)S(1)}, u32[]{:S(2)}, u32[]{:S(2)}) collective-permute-start(bf16[40,2944]{1,0:T(8,128)(2,1)S(1)} %get-tuple-element.137), channel_id=1, source_target_pairs={{0,8},{8,0},{16,24},{24,16},{1,9},{9,1},{17,25},{25,17},{2,10},{10... | collective-permute-start | bytes 706568 | tf_op jit(solution)/shard_map/ppermute | solution.py:284
  39.5 7.0 %collective-permute-start.11 = (bf16[40,2432]{1,0:T(8,128)(2,1)S(1)}, bf16[40,2432]{1,0:T(8,128)(2,1)S(1)}, u32[]{:S(2)}, u32[]{:S(2)}) collective-permute-start(bf16[40,2432]{1,0:T(8,128)(2,1)S(1)} %get-tuple-element.124), channel_id=1, source_target_pairs={{0,2},{1,3},{2,0},{3,1},{4,6},{5,7},{6,4},{7,5},{8,10},{9,11},{10,... | collective-permute-start | bytes 583688 | tf_op jit(solution)/shard_map/ppermute | solution.py:284
  41.3 10.9 %collective-permute-start.16 = (bf16[40,2688]{1,0:T(8,128)(2,1)S(1)}, bf16[40,2688]{1,0:T(8,128)(2,1)S(1)}, u32[]{:S(2)}, u32[]{:S(2)}) collective-permute-start(bf16[40,2688]{1,0:T(8,128)(2,1)S(1)} %get-tuple-element.136), channel_id=1, source_target_pairs={{0,8},{8,0},{16,24},{24,16},{1,9},{9,1},{17,25},{25,17},{2,10},{10... | collective-permute-start | bytes 645128 | tf_op jit(solution)/shard_map/ppermute | solution.py:284
  42.2 13.2 %collective-permute-start.15 = (bf16[40,2560]{1,0:T(8,128)(2,1)S(1)}, bf16[40,2560]{1,0:T(8,128)(2,1)S(1)}, u32[]{:S(2)}, u32[]{:S(2)}) collective-permute-start(bf16[40,2560]{1,0:T(8,128)(2,1)S(1)} %get-tuple-element.135), channel_id=1, source_target_pairs={{0,8},{8,0},{16,24},{24,16},{1,9},{9,1},{17,25},{25,17},{2,10},{10... | collective-permute-start | bytes 614408 | tf_op jit(solution)/shard_map/ppermute | solution.py:284
  43.8 13.7 %collective-permute-start.14 = (bf16[40,4096]{1,0:T(8,128)(2,1)S(1)}, bf16[40,4096]{1,0:T(8,128)(2,1)S(1)}, u32[]{:S(2)}, u32[]{:S(2)}) collective-permute-start(bf16[40,4096]{1,0:T(8,128)(2,1)S(1)} %get-tuple-element.133), channel_id=1, source_target_pairs={{0,16},{8,24},{16,0},{24,8},{1,17},{9,25},{17,1},{25,9},{2,18},{10... | collective-permute-start | bytes 983048 | tf_op jit(solution)/shard_map/ppermute | solution.py:284
  47.5 14.2 %collective-permute-start.13 = (bf16[128,1024]{1,0:T(8,128)(2,1)S(1)}, bf16[128,1024]{1,0:T(8,128)(2,1)S(1)}, u32[]{:S(2)}, u32[]{:S(2)}) collective-permute-start(bf16[128,1024]{1,0:T(8,128)(2,1)S(1)} %get-tuple-element.131), channel_id=1, source_target_pairs={{0,4},{1,5},{2,6},{3,7},{4,0},{5,1},{6,2},{7,3},{8,12},{9,13},{10,... | collective-permute-start | bytes 786440 | tf_op jit(solution)/shard_map/ppermute | solution.py:284
  50.6 16.2 %collective-permute-start.18 = (bf16[40,2944]{1,0:T(8,128)(2,1)S(1)}, bf16[40,2944]{1,0:T(8,128)(2,1)S(1)}, u32[]{:S(2)}, u32[]{:S(2)}) collective-permute-start(bf16[40,2944]{1,0:T(8,128)(2,1)S(1)} %get-tuple-element.147), channel_id=1, source_target_pairs={{0,16},{8,24},{16,0},{24,8},{1,17},{9,25},{17,1},{25,9},{2,18},{10... | collective-permute-start | bytes 706568 | tf_op jit(solution)/shard_map/ppermute | solution.py:284
  52.4 14.4 %collective-permute-start.19 = (bf16[40,2688]{1,0:T(8,128)(2,1)S(1)}, bf16[40,2688]{1,0:T(8,128)(2,1)S(1)}, u32[]{:S(2)}, u32[]{:S(2)}) collective-permute-start(bf16[40,2688]{1,0:T(8,128)(2,1)S(1)} %get-tuple-element.148), channel_id=1, source_target_pairs={{0,16},{8,24},{16,0},{24,8},{1,17},{9,25},{17,1},{25,9},{2,18},{10... | collective-permute-start | bytes 645128 | tf_op jit(solution)/shard_map/ppermute | solution.py:284
  55.7 11.1 %collective-permute-start.20 = (bf16[40,2560]{1,0:T(8,128)(2,1)S(1)}, bf16[40,2560]{1,0:T(8,128)(2,1)S(1)}, u32[]{:S(2)}, u32[]{:S(2)}) collective-permute-start(bf16[40,2560]{1,0:T(8,128)(2,1)S(1)} %get-tuple-element.149), channel_id=1, source_target_pairs={{0,16},{8,24},{16,0},{24,8},{1,17},{9,25},{17,1},{25,9},{2,18},{10... | collective-permute-start | bytes 614408 | tf_op jit(solution)/shard_map/ppermute | solution.py:284

commit v9 on v7

--- a/solution.py
+++ b/solution.py
@@ -24,7 +24,7 @@
     def __init__(self):
         self.mark = None
 
-    def __call__(self, body, outs, ins, also=(), far=0, scratch=()):
+    def __call__(self, body, outs, ins, also=(), far=0, scratch=(), far_outs=0, in_place=False):
         marks = [*also] if self.mark is None else [*also, self.mark]
         count = len(ins)
         ins = [pltpu.with_memory_space_constraint(v, pltpu.HBM) if k < far else v for k, v in enumerate(ins)]
@@ -41,7 +41,9 @@
             out_shape=[jax.ShapeDtypeStruct(*s) for s in shapes],
             in_specs=[pl.BlockSpec(memory_space=pltpu.HBM)] * far
             + [pl.BlockSpec(memory_space=pltpu.VMEM)] * (count + len(marks) - far),
-            out_specs=[pl.BlockSpec(memory_space=pltpu.VMEM)] * len(shapes),
+            out_specs=[pl.BlockSpec(memory_space=pltpu.HBM)] * far_outs
+            + [pl.BlockSpec(memory_space=pltpu.VMEM)] * (len(shapes) - far_outs),
+            input_output_aliases={k: k for k in range(far_outs)} if in_place else {},
             scratch_shapes=list(scratch),
             compiler_params=pltpu.CompilerParams(vmem_limit_bytes=24 * 1024 * 1024),
             cost_estimate=pl.CostEstimate(flops=1, bytes_accessed=1, transcendentals=0),
@@ -123,8 +125,18 @@
 
 
 def project(x, low, high, both, hid_a, hid_b):
-    rows = low.shape[0] // 2
-    total = project_tiles(x, low, high)
+    finish_projection(project_tiles(x, low, high), both, hid_a, hid_b)
+
+
+def project_half(x, low, at, out):
+    total = jnp.zeros(out.shape, F32)
+    for cut in tiles(low.shape[1], 1024):
+        total += dot(low[:, cut], x[:, shifted(cut, at)], NT)
+    out[...] = total
+
+
+def finish_projection(total, both, hid_a, hid_b):
+    rows = total.shape[0] // 2
     both[...] = total
     hidden = total * jax.nn.sigmoid(total) * pltpu.roll(total, rows, 0)
     hidden = jnp.where(top_rows(total), hidden, 0.0)
@@ -178,8 +190,8 @@
     return dot(hid_a[...], g[:, cut], NN) + dot(hid_b[...], g[:, half + at : half + at + TILE], NN)
 
 
-def tiles(size):
-    return [slice(at, min(at + TILE, size)) for at in range(0, size, TILE)]
+def tiles(size, step=TILE):
+    return [slice(at, min(at + step, size)) for at in range(0, size, step)]
 
 
 def shifted(cut, offset):
@@ -354,7 +366,13 @@
         other_columns(width, down_b, out, half // 2)
 
     two_theirs = exchanged(step(two_other, piece, [own[2], second[2]]), "tensor", SECOND)
-    both_second, *hid_second = step(project, [small, small_bf, small_bf], [x, second[0], second[1]])
+    both_high = step(lambda xr, high, out: project_half(xr, high, half, out), small, [x, second[1]])
+
+    def project_rest(xr, low, high_part, both, hid_a, hid_b):
+        project_half(xr, low, 0, both)
+        finish_projection(both[...] + high_part[...], both, hid_a, hid_b)
+
+    both_second, *hid_second = step(project_rest, [small, small_bf, small_bf], [x, second[0], both_high])
 
     def two_sent(share_a, hid_a, share_b, hid_b, out):
         out[:both_rows, :] = sent_share(share_a, hid_a)
@@ -448,23 +466,51 @@
             out[:, cut] = value[:rows]
             out[:, half + at : half + at + TILE] = value[rows:]
 
-    def final_pair(low_ref, high_ref, low_back, high_back, low_side, high_side, out_gate, out_up):
-        odd = is_odd()
-        for offset, refs in ((0, (low_ref, low_back, low_side)), (low_columns, (high_ref, high_back, high_side))):
-            for cut in tiles(refs[0].shape[1]):
-                value = finished(*refs, odd, cut)
-                out_gate[:, shifted(cut, offset)] = value[:rows]
-                out_up[:, shifted(cut, offset)] = value[rows:]
+    def final_piece(offset, columns):
+        def body(own_ref, back, side, out_gate, out_up, gate_here, up_here, sems):
+            odd = is_odd()
+            for cut in tiles(columns):
+                value = finished(own_ref, back, side, odd, cut)
+                gate_here[:, cut] = value[:rows]
+                up_here[:, cut] = value[rows:]
+            copies = [
+                pltpu.make_async_copy(here, out.at[:, pl.ds(offset, columns)], sems.at[k])
+                for k, (here, out) in enumerate(((gate_here, out_gate), (up_here, out_up)))
+            ]
+            for copy in copies:
+                copy.start()
+            for copy in copies:
+                copy.wait()
+
+        return body
+
+    def final_last(gate_there, up_there, *refs):
+        final_piece(low_columns, wide - low_columns)(*refs)
+
+    def kept_columns(columns):
+        held = pltpu.VMEM((rows, columns), F32)
+        return [held, held, pltpu.SemaphoreType.DMA((2,))]
 
     whole = ((rows, wide), F32)
     grad_down = step(final_down, whole, [own_down, back_of_down, side_down])
+    part_gate, part_up = step(
+        final_piece(0, low_columns),
+        [whole, whole],
+        [own_low, back_of_low, side_low],
+        far_outs=2,
+        scratch=kept_columns(low_columns),
+    )
     output, end = step(final_output, [((tokens, width), BF), ((128, 128), F32)], [keep, got])
     end = exchanged(end, "tensor", SWAP)
     grad_gate, grad_up = step(
-        final_pair,
+        final_last,
         [whole, whole],
-        [own_low, own_high, back_of_low, back_of_high, side_low, side_high],
+        [part_gate, part_up, own_high, back_of_high, side_high],
         also=[end],
+        far=2,
+        far_outs=2,
+        in_place=True,
+        scratch=kept_columns(wide - low_columns),
     )
     return (output, grad_gate, grad_up, grad_down)
 

time: 67.2 us -> 67 us (level)
  Pallas kernels: 14.5 us -> 15.8 us
  starting transfers between devices: 28.3 us -> 27.4 us
    pallas_call x25 -> x27, Pallas kernels: 14.5 us -> 15.8 us  [__call__(): pl.pallas_call(kernel, out_shape=[jax.ShapeDtypeStruct(*s) for s in shape...]
    ppermute x19, starting transfers between devices: 24.9 us -> 23.9 us  [exchanged(): lax.ppermute(value, axis, [(source, source ^ bit) for source in range(cou...]
  transfers between devices with their start and end apart: 20 -> 20, of which waited for: 10 -> 11; matrix products, arithmetic and copies ran while one was open for 0% -> 0% of each run, Pallas kernels for 17% -> 19%
where the time goes in v9:
time: 67 us; the launch traced here: 66.9 us
  starting transfers between devices  27.4 us (41%)
  waiting for transfers between devices  22.9 us (34%)
  Pallas kernels  15.8 us (24%)
  between operations  0.83 us (1%)
    ppermute x19, starting transfers between devices, exchanged(): lax.ppermute(value, axis, [(source, source ^ bit) for source in range(cou...  23.9 us
    ppermute x19, waiting for transfers between devices, exchanged(): lax.ppermute(value, axis, [(source, source ^ bit) for source in range(cou...  19.3 us
    pallas_call x27, Pallas kernels, __call__(): pl.pallas_call(kernel, out_shape=[jax.ShapeDtypeStruct(*s) for s in shape...  15.8 us
    ppermute x1, waiting for transfers between devices, on_device(): lax.ppermute(crossed, 'section', [(source, source ^ 2) for source in (0,...  3.6 us
    ppermute x1, starting transfers between devices, on_device(): lax.ppermute(crossed, 'section', [(source, source ^ 2) for source in (0,...  3.41 us
  transfers between devices with their start and end apart: 20, of which 11 were waited for; matrix products, arithmetic and copies ran while one was open for 0% of the time, Pallas kernels for 19%

profile of v9, /device:TPU:0, one launch (start us, length us, event | category | flops | bytes accessed | tf_op | source)
XLA Modules:
  0.0 66.9 jit_solution(16933081104605751953)
XLA Ops:
  0.6 1.7 %shard_map.84 = (bf16[40,4096]{1,0:T(8,128)(2,1)S(1)}, bf16[40,4096]{1,0:T(8,128)(2,1)S(1)}, bf16[20,4096]{1,0:T(8,128)(2,1)S(1)}, bf16[20,4096]{1,0:T(8,128)(2,1)S(1)}, f32[8,128]{1,0:T(8,128)S(1)}) custom-call(bf16[20,8192]{1,0:T(8,128)(2,1)} %refs_0_.2, bf16[20,8192]{1,0:T(8,128)(2,1)} %refs_1_.2, bf16[20,8192]{1,0:T(8,128)(2,1)} %refs_2_.1), custom_call_target="tpu_custom_call" | custom-call | flops 1 | bytes 1 | tf_op jit(solution)/shard_map/pallas_call | solution.py:39
  2.9 2.6 %collective-permute-start.2 = (bf16[40,4096]{1,0:T(8,128)(2,1)S(1)}, bf16[40,4096]{1,0:T(8,128)(2,1)S(1)}, u32[]{:S(2)}, u32[]{:S(2)}) collective-permute-start(bf16[40,4096]{1,0:T(8,128)(2,1)S(1)} %get-tuple-element.82.refs_3_.refs_1_), channel_id=1, source_target_pairs={{0,16},{8,24},{16,0},{24,8},{1,17},{9,25},{17,1},{25,9},{2,18},{10... | collective-permute-start | bytes 983048 | tf_op jit(solution)/shard_map/ppermute | solution.py:289
  5.8 1.6 %collective-permute-start.5 = (bf16[40,4096]{1,0:T(8,128)(2,1)S(1)}, bf16[40,4096]{1,0:T(8,128)(2,1)S(1)}, u32[]{:S(2)}, u32[]{:S(2)}) collective-permute-start(bf16[40,4096]{1,0:T(8,128)(2,1)S(1)} %get-tuple-element.89.refs_1_.refs_0_.refs_3_), channel_id=1, source_target_pairs={{0,8},{8,0},{16,24},{24,16},{1,9},{9,1},{17,25},{25,17},{2,10},{10... | collective-permute-start | bytes 983048 | tf_op jit(solution)/shard_map/ppermute | solution.py:289
  7.4 1.4 %collective-permute-start.1 = (bf16[40,4096]{1,0:T(8,128)(2,1)S(1)}, bf16[40,4096]{1,0:T(8,128)(2,1)S(1)}, u32[]{:S(2)}, u32[]{:S(2)}) collective-permute-start(bf16[40,4096]{1,0:T(8,128)(2,1)S(1)} %get-tuple-element.81.refs_2_.refs_1_), channel_id=1, source_target_pairs={{0,16},{8,24},{16,0},{24,8},{1,17},{9,25},{17,1},{25,9},{2,18},{10... | collective-permute-start | bytes 983048 | tf_op jit(solution)/shard_map/ppermute | solution.py:289
  8.7 2.4 %shard_map.86 = (bf16[128,8192]{1,0:T(8,128)(2,1)S(1)}, bf16[128,8192]{1,0:T(8,128)(2,1)S(1)}, f32[40,128]{1,0:T(8,128)S(1)}, bf16[40,128]{1,0:T(8,128)(2,1)S(1)...) custom-call(bf16[128,8192]{1,0:T(8,128)(2,1)} %refs_0_.3, bf16[128,8192]{1,0:T(8,128)(2,1)} %refs_1_.3, ...), custom_call_target="tpu_custom_call" | custom-call | flops 1 | bytes 1 | tf_op jit(solution)/shard_map/pallas_call | solution.py:39
  11.7 2.4 %collective-permute-done.2.refs_0_.refs_2_ = bf16[40,4096]{1,0:T(8,128)(2,1)S(1)} collective-permute-done((bf16[40,4096]{1,0:T(8,128)(2,1)S(1)}, bf16[40,4096]{1,0:T(8,128)(2,1)S(1)}, u32[]{:S(2)}, u32[]{:S(2)}) %collective-permute-start.2) | collective-permute-done | bytes 327712 | tf_op jit(solution)/shard_map/ppermute | solution.py:289
  14.1 2.0 %collective-permute-start.4 = (bf16[40,4096]{1,0:T(8,128)(2,1)S(1)}, bf16[40,4096]{1,0:T(8,128)(2,1)S(1)}, u32[]{:S(2)}, u32[]{:S(2)}) collective-permute-start(bf16[40,4096]{1,0:T(8,128)(2,1)S(1)} %get-tuple-element.97), channel_id=1, source_target_pairs={{0,8},{8,0},{16,24},{24,16},{1,9},{9,1},{17,25},{25,17},{2,10},{10... | collective-permute-start | bytes 983048 | tf_op jit(solution)/shard_map/ppermute | solution.py:289
  16.1 3.4 %collective-permute-start.6 = (bf16[40,4096]{1,0:T(8,128)(2,1)S(1)}, bf16[40,4096]{1,0:T(8,128)(2,1)S(1)}, u32[]{:S(2)}, u32[]{:S(2)}) collective-permute-start(bf16[40,4096]{1,0:T(8,128)(2,1)S(1)} %collective-permute-done.5.refs_0_), channel_id=1, source_target_pairs={{0,16},{16,0},{1,17},{17,1},{2,18},{18,2},{3,19},{19,3},{4,20},{20... | collective-permute-start | bytes 983048 | tf_op jit(solution)/shard_map/ppermute | solution.py:347
  19.5 1.6 %collective-permute-done.1.refs_0_.refs_1_ = bf16[40,4096]{1,0:T(8,128)(2,1)S(1)} collective-permute-done((bf16[40,4096]{1,0:T(8,128)(2,1)S(1)}, bf16[40,4096]{1,0:T(8,128)(2,1)S(1)}, u32[]{:S(2)}, u32[]{:S(2)}) %collective-permute-start.1) | collective-permute-done | bytes 327712 | tf_op jit(solution)/shard_map/ppermute | solution.py:289
  21.1 1.5 %collective-permute-start.3 = (bf16[40,4096]{1,0:T(8,128)(2,1)S(1)}, bf16[40,4096]{1,0:T(8,128)(2,1)S(1)}, u32[]{:S(2)}, u32[]{:S(2)}) collective-permute-start(bf16[40,4096]{1,0:T(8,128)(2,1)S(1)} %get-tuple-element.96), channel_id=1, source_target_pairs={{0,8},{8,0},{16,24},{24,16},{1,9},{9,1},{17,25},{25,17},{2,10},{10... | collective-permute-start | bytes 983048 | tf_op jit(solution)/shard_map/ppermute | solution.py:289
  22.6 1.5 %collective-permute-start.8 = (bf16[40,4096]{1,0:T(8,128)(2,1)S(1)}, bf16[40,4096]{1,0:T(8,128)(2,1)S(1)}, u32[]{:S(2)}, u32[]{:S(2)}) collective-permute-start(bf16[40,4096]{1,0:T(8,128)(2,1)S(1)} %get-tuple-element.89.refs_1_.refs_0_.refs_3_), channel_id=1, source_target_pairs={{0,16},{8,24},{16,0},{24,8},{1,17},{9,25},{17,1},{25,9},{2,18},{10... | collective-permute-start | bytes 983048 | tf_op jit(solution)/shard_map/ppermute | solution.py:289
  24.1 0.8 %shard_map.90 = (f32[40,128]{1,0:T(8,128)S(1)}, bf16[40,128]{1,0:T(8,128)(2,1)S(1)}, bf16[40,128]{1,0:T(8,128)(2,1)S(1)}, f32[8,128]{1,0:T(8,128)S(1)}) custom-call(bf16[128,8192]{1,0:T(8,128)(2,1)S(1)} %get-tuple-element.93.refs_0_, bf16[40,4096]{1,0:T(8,128)(2,1)S(1)} %collective-permute-done.1.refs_0_.refs_1_, ...), custom_call_target="tpu_custom_call" | custom-call | flops 1 | bytes 1 | tf_op jit(solution)/shard_map/pallas_call | solution.py:39
  25.0 3.6 %collective-permute-done.6.refs_1_ = bf16[40,4096]{1,0:T(8,128)(2,1)S(1)} collective-permute-done((bf16[40,4096]{1,0:T(8,128)(2,1)S(1)}, bf16[40,4096]{1,0:T(8,128)(2,1)S(1)}, u32[]{:S(2)}, u32[]{:S(2)}) %collective-permute-start.6) | collective-permute-done | bytes 327712 | tf_op jit(solution)/shard_map/ppermute | solution.py:347
  29.2 1.6 %collective-permute-start.9 = (bf16[40,4096]{1,0:T(8,128)(2,1)S(1)}, bf16[40,4096]{1,0:T(8,128)(2,1)S(1)}, u32[]{:S(2)}, u32[]{:S(2)}) collective-permute-start(bf16[40,4096]{1,0:T(8,128)(2,1)S(1)} %get-tuple-element.119), channel_id=1, source_target_pairs={{0,2},{1,3},{2,0},{3,1},{4,6},{5,7},{6,4},{7,5},{8,10},{9,11},{10,... | collective-permute-start | bytes 983048 | tf_op jit(solution)/shard_map/ppermute | solution.py:289
  32.9 1.2 %collective-permute-done.7.refs_6_ = f32[80,128]{1,0:T(8,128)S(1)} collective-permute-done((f32[80,128]{1,0:T(8,128)S(1)}, f32[80,128]{1,0:T(8,128)S(1)}, u32[]{:S(2)}, u32[]{:S(2)}) %collective-permute-start.7) | collective-permute-done | bytes 40992 | tf_op jit(solution)/shard_map/ppermute | solution.py:289
  34.6 1.5 %collective-permute-start.12 = (bf16[40,4224]{1,0:T(8,128)(2,1)S(1)}, bf16[40,4224]{1,0:T(8,128)(2,1)S(1)}, u32[]{:S(2)}, u32[]{:S(2)}) collective-permute-start(bf16[40,4224]{1,0:T(8,128)(2,1)S(1)} %get-tuple-element.130), channel_id=1, source_target_pairs={{0,8},{8,0},{16,24},{24,16},{1,9},{9,1},{17,25},{25,17},{2,10},{10... | collective-permute-start | bytes 1013768 | tf_op jit(solution)/shard_map/ppermute | solution.py:289
  36.0 1.7 %collective-permute-done.9.refs_3_.refs_6_ = bf16[40,4096]{1,0:T(8,128)(2,1)S(1)} collective-permute-done((bf16[40,4096]{1,0:T(8,128)(2,1)S(1)}, bf16[40,4096]{1,0:T(8,128)(2,1)S(1)}, u32[]{:S(2)}, u32[]{:S(2)}) %collective-permute-start.9) | collective-permute-done | bytes 327712 | tf_op jit(solution)/shard_map/ppermute | solution.py:289
  38.3 1.2 %collective-permute-done.10.refs_2_ = f32[40,128]{1,0:T(8,128)S(1)} collective-permute-done((f32[40,128]{1,0:T(8,128)S(1)}, f32[40,128]{1,0:T(8,128)S(1)}, u32[]{:S(2)}, u32[]{:S(2)}) %collective-permute-start.10) | collective-permute-done | bytes 20512 | tf_op jit(solution)/shard_map/ppermute | solution.py:289
  39.5 3.4 %collective-permute-done.13.refs_3_.refs_2_ = bf16[40,4096]{1,0:T(8,128)(2,1)S(1)} collective-permute-done((bf16[40,4096]{1,0:T(8,128)(2,1)S(1)}, bf16[40,4096]{1,0:T(8,128)(2,1)S(1)}, u32[]{:S(2)}, u32[]{:S(2)}) %collective-permute-start.13) | collective-permute-done | bytes 327712 | tf_op jit(solution)/shard_map/ppermute | solution.py:289
  43.3 1.6 %collective-permute-start.16 = (bf16[40,4096]{1,0:T(8,128)(2,1)S(1)}, bf16[40,4096]{1,0:T(8,128)(2,1)S(1)}, u32[]{:S(2)}, u32[]{:S(2)}) collective-permute-start(bf16[40,4096]{1,0:T(8,128)(2,1)S(1)} %get-tuple-element.142), channel_id=1, source_target_pairs={{0,16},{8,24},{16,0},{24,8},{1,17},{9,25},{17,1},{25,9},{2,18},{10... | collective-permute-start | bytes 983048 | tf_op jit(solution)/shard_map/ppermute | solution.py:289
  45.5 1.6 %collective-permute-start.11 = (bf16[40,2432]{1,0:T(8,128)(2,1)S(1)}, bf16[40,2432]{1,0:T(8,128)(2,1)S(1)}, u32[]{:S(2)}, u32[]{:S(2)}) collective-permute-start(bf16[40,2432]{1,0:T(8,128)(2,1)S(1)} %get-tuple-element.128), channel_id=1, source_target_pairs={{0,2},{1,3},{2,0},{3,1},{4,6},{5,7},{6,4},{7,5},{8,10},{9,11},{10,... | collective-permute-start | bytes 583688 | tf_op jit(solution)/shard_map/ppermute | solution.py:289
  47.8 2.3 %collective-permute-done.12.refs_2_ = bf16[40,4224]{1,0:T(8,128)(2,1)S(1)} collective-permute-done((bf16[40,4224]{1,0:T(8,128)(2,1)S(1)}, bf16[40,4224]{1,0:T(8,128)(2,1)S(1)}, u32[]{:S(2)}, u32[]{:S(2)}) %collective-permute-start.12) | collective-permute-done | bytes 337952 | tf_op jit(solution)/shard_map/ppermute | solution.py:289
  50.4 1.6 %collective-permute-start.15 = (bf16[40,4224]{1,0:T(8,128)(2,1)S(1)}, bf16[40,4224]{1,0:T(8,128)(2,1)S(1)}, u32[]{:S(2)}, u32[]{:S(2)}) collective-permute-start(bf16[40,4224]{1,0:T(8,128)(2,1)S(1)} %get-tuple-element.140), channel_id=1, source_target_pairs={{0,16},{8,24},{16,0},{24,8},{1,17},{9,25},{17,1},{25,9},{2,18},{10... | collective-permute-start | bytes 1013768 | tf_op jit(solution)/shard_map/ppermute | solution.py:289
  52.0 1.0 %shard_map.105 = (bf16[128,1024]{1,0:T(8,128)(2,1)S(1)}, f32[128,1024]{1,0:T(8,128)S(1)}, f32[8,128]{1,0:T(8,128)S(1)}) custom-call(bf16[40,128]{1,0:T(8,128)(2,1)S(1)} %get-tuple-element.115.refs_4_.refs_0_, bf16[40,128]{1,0:T(8,128)(2,1)S(1)} %get-tuple-element.116.refs_5_.refs_1_, bf16[40,128]{1,0:T(8,128)(2,1)S(1)} %get-tuple-element.127.refs_2_, ...), custom_call_target="tpu_custom_call" | custom-call | flops 1 | bytes 1 | tf_op jit(solution)/shard_map/pallas_call | solution.py:39
  53.1 3.0 %collective-permute-start.14 = (bf16[128,1024]{1,0:T(8,128)(2,1)S(1)}, bf16[128,1024]{1,0:T(8,128)(2,1)S(1)}, u32[]{:S(2)}, u32[]{:S(2)}) collective-permute-start(bf16[128,1024]{1,0:T(8,128)(2,1)S(1)} %get-tuple-element.138), channel_id=1, source_target_pairs={{0,4},{1,5},{2,6},{3,7},{4,0},{5,1},{6,2},{7,3},{8,12},{9,13},{10,... | collective-permute-start | bytes 786440 | tf_op jit(solution)/shard_map/ppermute | solution.py:289
  57.0 1.0 %shard_map.107 = (f32[20,8192]{1,0:T(8,128)}, f32[8,128]{1,0:T(8,128)S(1)}) custom-call(f32[40,4096]{1,0:T(8,128)S(1)} %get-tuple-element.141.refs_0_, bf16[40,4096]{1,0:T(8,128)(2,1)S(1)} %collective-permute-done.16.refs_3_.refs_1_, bf16[40,4096]{1,0:T(8,128)(2,1)S(1)} %collective-permute-done.13.refs_3_.refs_2_, f32[8,128]{1,0:T(8,128)S(1)} %get-tuple-element.145.refs_3_), custom_call_target="tpu_custom_call" | custom-call | flops 1 | bytes 1 | tf_op jit(solution)/shard_map/pallas_call | solution.py:39
  58.0 1.9 %collective-permute-done.15.refs_1_ = bf16[40,4224]{1,0:T(8,128)(2,1)S(1)} collective-permute-done((bf16[40,4224]{1,0:T(8,128)(2,1)S(1)}, bf16[40,4224]{1,0:T(8,128)(2,1)S(1)}, u32[]{:S(2)}, u32[]{:S(2)}) %collective-permute-start.15) | collective-permute-done | bytes 337952 | tf_op jit(solution)/shard_map/ppermute | solution.py:289
  59.9 1.0 %shard_map.108 = (f32[20,8192]{1,0:T(8,128)}, f32[20,8192]{1,0:T(8,128)}, f32[8,128]{1,0:T(8,128)S(1)}) custom-call(f32[40,4224]{1,0:T(8,128)S(1)} %get-tuple-element.139.refs_0_, bf16[40,4224]{1,0:T(8,128)(2,1)S(1)} %collective-permute-done.15.refs_1_, bf16[40,4224]{1,0:T(8,128)(2,1)S(1)} %collective-permute-done.12.refs_2_, ...), custom_call_target="tpu_custom_call" | custom-call | flops 1 | bytes 1 | tf_op jit(solution)/shard_map/pallas_call | solution.py:39
  60.9 2.4 %collective-permute-done.14.refs_1_ = bf16[128,1024]{1,0:T(8,128)(2,1)S(1)} collective-permute-done((bf16[128,1024]{1,0:T(8,128)(2,1)S(1)}, bf16[128,1024]{1,0:T(8,128)(2,1)S(1)}, u32[]{:S(2)}, u32[]{:S(2)}) %collective-permute-start.14) | collective-permute-done | bytes 262176 | tf_op jit(solution)/shard_map/ppermute | solution.py:289
  63.3 0.8 %shard_map.109 = (bf16[128,1024]{1,0:T(8,128)(2,1)}, f32[128,128]{1,0:T(8,128)S(1)}, f32[8,128]{1,0:T(8,128)S(1)}) custom-call(f32[128,1024]{1,0:T(8,128)S(1)} %get-tuple-element.137.refs_0_, bf16[128,1024]{1,0:T(8,128)(2,1)S(1)} %collective-permute-done.14.refs_1_, f32[8,128]{1,0:T(8,128)S(1)} %get-tuple-element.147.refs_2_), custom_call_target="tpu_custom_call" | custom-call | flops 1 | bytes 1 | tf_op jit(solution)/shard_map/pallas_call | solution.py:39
  64.0 1.3 %collective-permute-done.19.refs_5_ = f32[128,128]{1,0:T(8,128)S(1)} collective-permute-done((f32[128,128]{1,0:T(8,128)S(1)}, f32[128,128]{1,0:T(8,128)S(1)}, u32[]{:S(2)}, u32[]{:S(2)}) %collective-permute-start.19) | collective-permute-done | bytes 65568 | tf_op jit(solution)/shard_map/ppermute | solution.py:289
  65.3 1.6 %shard_map.110 = (f32[20,8192]{1,0:T(8,128)}, f32[20,8192]{1,0:T(8,128)}, f32[8,128]{1,0:T(8,128)}) custom-call(f32[20,8192]{1,0:T(8,128)} %get-tuple-element.149.refs_0_, f32[20,8192]{1,0:T(8,128)} %get-tuple-element.150.refs_1_, f32[40,3968]{1,0:T(8,128)S(1)} %get-tuple-element.151.refs_2_, ...), custom_call_target="tpu_custom_call", output_to_operand_aliasing={{0}: (0, {}), {1}: (1, {})} | custom-call | flops 1 | bytes 1 | tf_op jit(solution)/shard_map/pallas_call | solution.py:39
  (35 shorter events, 7.9 us)
Async XLA Ops:
  2.4 3.1 %collective-permute-start = (bf16[20,4096]{1,0:T(8,128)(2,1)S(1)}, bf16[20,4096]{1,0:T(8,128)(2,1)S(1)}, u32[]{:S(2)}, u32[]{:S(2)}) collective-permute-start(bf16[20,4096]{1,0:T(8,128)(2,1)S(1)} %get-tuple-element.84), channel_id=1, source_target_pairs={{0,1},{1,0},{2,3},{3,2},{4,5},{5,4},{6,7},{7,6},{8,9},{9,8},{10,11... | collective-permute-start | bytes 491528 | tf_op jit(solution)/shard_map/ppermute | solution.py:289
  2.9 11.2 %collective-permute-start.2 = (bf16[40,4096]{1,0:T(8,128)(2,1)S(1)}, bf16[40,4096]{1,0:T(8,128)(2,1)S(1)}, u32[]{:S(2)}, u32[]{:S(2)}) collective-permute-start(bf16[40,4096]{1,0:T(8,128)(2,1)S(1)} %get-tuple-element.82.refs_3_.refs_1_), channel_id=1, source_target_pairs={{0,16},{8,24},{16,0},{24,8},{1,17},{9,25},{17,1},{25,9},{2,18},{10... | collective-permute-start | bytes 983048 | tf_op jit(solution)/shard_map/ppermute | solution.py:289
  5.8 10.2 %collective-permute-start.5 = (bf16[40,4096]{1,0:T(8,128)(2,1)S(1)}, bf16[40,4096]{1,0:T(8,128)(2,1)S(1)}, u32[]{:S(2)}, u32[]{:S(2)}) collective-permute-start(bf16[40,4096]{1,0:T(8,128)(2,1)S(1)} %get-tuple-element.89.refs_1_.refs_0_.refs_3_), channel_id=1, source_target_pairs={{0,8},{8,0},{16,24},{24,16},{1,9},{9,1},{17,25},{25,17},{2,10},{10... | collective-permute-start | bytes 983048 | tf_op jit(solution)/shard_map/ppermute | solution.py:289
  7.4 13.7 %collective-permute-start.1 = (bf16[40,4096]{1,0:T(8,128)(2,1)S(1)}, bf16[40,4096]{1,0:T(8,128)(2,1)S(1)}, u32[]{:S(2)}, u32[]{:S(2)}) collective-permute-start(bf16[40,4096]{1,0:T(8,128)(2,1)S(1)} %get-tuple-element.81.refs_2_.refs_1_), channel_id=1, source_target_pairs={{0,16},{8,24},{16,0},{24,8},{1,17},{9,25},{17,1},{25,9},{2,18},{10... | collective-permute-start | bytes 983048 | tf_op jit(solution)/shard_map/ppermute | solution.py:289
  14.1 10.1 %collective-permute-start.4 = (bf16[40,4096]{1,0:T(8,128)(2,1)S(1)}, bf16[40,4096]{1,0:T(8,128)(2,1)S(1)}, u32[]{:S(2)}, u32[]{:S(2)}) collective-permute-start(bf16[40,4096]{1,0:T(8,128)(2,1)S(1)} %get-tuple-element.97), channel_id=1, source_target_pairs={{0,8},{8,0},{16,24},{24,16},{1,9},{9,1},{17,25},{25,17},{2,10},{10... | collective-permute-start | bytes 983048 | tf_op jit(solution)/shard_map/ppermute | solution.py:289
  16.1 12.5 %collective-permute-start.6 = (bf16[40,4096]{1,0:T(8,128)(2,1)S(1)}, bf16[40,4096]{1,0:T(8,128)(2,1)S(1)}, u32[]{:S(2)}, u32[]{:S(2)}) collective-permute-start(bf16[40,4096]{1,0:T(8,128)(2,1)S(1)} %collective-permute-done.5.refs_0_), channel_id=1, source_target_pairs={{0,16},{16,0},{1,17},{17,1},{2,18},{18,2},{3,19},{19,3},{4,20},{20... | collective-permute-start | bytes 983048 | tf_op jit(solution)/shard_map/ppermute | solution.py:347
  21.1 10.2 %collective-permute-start.3 = (bf16[40,4096]{1,0:T(8,128)(2,1)S(1)}, bf16[40,4096]{1,0:T(8,128)(2,1)S(1)}, u32[]{:S(2)}, u32[]{:S(2)}) collective-permute-start(bf16[40,4096]{1,0:T(8,128)(2,1)S(1)} %get-tuple-element.96), channel_id=1, source_target_pairs={{0,8},{8,0},{16,24},{24,16},{1,9},{9,1},{17,25},{25,17},{2,10},{10... | collective-permute-start | bytes 983048 | tf_op jit(solution)/shard_map/ppermute | solution.py:289
  22.6 13.4 %collective-permute-start.8 = (bf16[40,4096]{1,0:T(8,128)(2,1)S(1)}, bf16[40,4096]{1,0:T(8,128)(2,1)S(1)}, u32[]{:S(2)}, u32[]{:S(2)}) collective-permute-start(bf16[40,4096]{1,0:T(8,128)(2,1)S(1)} %get-tuple-element.89.refs_1_.refs_0_.refs_3_), channel_id=1, source_target_pairs={{0,16},{8,24},{16,0},{24,8},{1,17},{9,25},{17,1},{25,9},{2,18},{10... | collective-permute-start | bytes 983048 | tf_op jit(solution)/shard_map/ppermute | solution.py:289
  29.2 8.6 %collective-permute-start.9 = (bf16[40,4096]{1,0:T(8,128)(2,1)S(1)}, bf16[40,4096]{1,0:T(8,128)(2,1)S(1)}, u32[]{:S(2)}, u32[]{:S(2)}) collective-permute-start(bf16[40,4096]{1,0:T(8,128)(2,1)S(1)} %get-tuple-element.119), channel_id=1, source_target_pairs={{0,2},{1,3},{2,0},{3,1},{4,6},{5,7},{6,4},{7,5},{8,10},{9,11},{10,... | collective-permute-start | bytes 983048 | tf_op jit(solution)/shard_map/ppermute | solution.py:289
  32.2 10.7 %collective-permute-start.13 = (bf16[40,4096]{1,0:T(8,128)(2,1)S(1)}, bf16[40,4096]{1,0:T(8,128)(2,1)S(1)}, u32[]{:S(2)}, u32[]{:S(2)}) collective-permute-start(bf16[40,4096]{1,0:T(8,128)(2,1)S(1)} %get-tuple-element.132), channel_id=1, source_target_pairs={{0,8},{8,0},{16,24},{24,16},{1,9},{9,1},{17,25},{25,17},{2,10},{10... | collective-permute-start | bytes 983048 | tf_op jit(solution)/shard_map/ppermute | solution.py:289
  32.9 1.2 %collective-permute-start.7 = (f32[80,128]{1,0:T(8,128)S(1)}, f32[80,128]{1,0:T(8,128)S(1)}, u32[]{:S(2)}, u32[]{:S(2)}) collective-permute-start(f32[80,128]{1,0:T(8,128)S(1)} %get-tuple-element.112), channel_id=1, source_target_pairs={{0,1},{1,0},{2,3},{3,2},{4,5},{5,4},{6,7},{7,6},{8,9},{9,8},{10,11... | collective-permute-start | bytes 122888 | tf_op jit(solution)/shard_map/ppermute | solution.py:289
  34.6 15.6 %collective-permute-start.12 = (bf16[40,4224]{1,0:T(8,128)(2,1)S(1)}, bf16[40,4224]{1,0:T(8,128)(2,1)S(1)}, u32[]{:S(2)}, u32[]{:S(2)}) collective-permute-start(bf16[40,4224]{1,0:T(8,128)(2,1)S(1)} %get-tuple-element.130), channel_id=1, source_target_pairs={{0,8},{8,0},{16,24},{24,16},{1,9},{9,1},{17,25},{25,17},{2,10},{10... | collective-permute-start | bytes 1013768 | tf_op jit(solution)/shard_map/ppermute | solution.py:289
  38.2 1.3 %collective-permute-start.10 = (f32[40,128]{1,0:T(8,128)S(1)}, f32[40,128]{1,0:T(8,128)S(1)}, u32[]{:S(2)}, u32[]{:S(2)}) collective-permute-start(f32[40,128]{1,0:T(8,128)S(1)} %get-tuple-element.124), channel_id=1, source_target_pairs={{0,1},{1,0},{2,3},{3,2},{4,5},{5,4},{6,7},{7,6},{8,9},{9,8},{10,11... | collective-permute-start | bytes 61448 | tf_op jit(solution)/shard_map/ppermute | solution.py:289
  43.3 12.8 %collective-permute-start.16 = (bf16[40,4096]{1,0:T(8,128)(2,1)S(1)}, bf16[40,4096]{1,0:T(8,128)(2,1)S(1)}, u32[]{:S(2)}, u32[]{:S(2)}) collective-permute-start(bf16[40,4096]{1,0:T(8,128)(2,1)S(1)} %get-tuple-element.142), channel_id=1, source_target_pairs={{0,16},{8,24},{16,0},{24,8},{1,17},{9,25},{17,1},{25,9},{2,18},{10... | collective-permute-start | bytes 983048 | tf_op jit(solution)/shard_map/ppermute | solution.py:289
  44.9 11.2 %collective-permute-start.17 = (bf16[40,3968]{1,0:T(8,128)(2,1)S(1)}, bf16[40,3968]{1,0:T(8,128)(2,1)S(1)}, u32[]{:S(2)}, u32[]{:S(2)}) collective-permute-start(bf16[40,3968]{1,0:T(8,128)(2,1)S(1)} %get-tuple-element.143), channel_id=1, source_target_pairs={{0,8},{8,0},{16,24},{24,16},{1,9},{9,1},{17,25},{25,17},{2,10},{10... | collective-permute-start | bytes 952328 | tf_op jit(solution)/shard_map/ppermute | solution.py:289
  45.5 6.5 %collective-permute-start.11 = (bf16[40,2432]{1,0:T(8,128)(2,1)S(1)}, bf16[40,2432]{1,0:T(8,128)(2,1)S(1)}, u32[]{:S(2)}, u32[]{:S(2)}) collective-permute-start(bf16[40,2432]{1,0:T(8,128)(2,1)S(1)} %get-tuple-element.128), channel_id=1, source_target_pairs={{0,2},{1,3},{2,0},{3,1},{4,6},{5,7},{6,4},{7,5},{8,10},{9,11},{10,... | collective-permute-start | bytes 583688 | tf_op jit(solution)/shard_map/ppermute | solution.py:289
  50.4 9.4 %collective-permute-start.15 = (bf16[40,4224]{1,0:T(8,128)(2,1)S(1)}, bf16[40,4224]{1,0:T(8,128)(2,1)S(1)}, u32[]{:S(2)}, u32[]{:S(2)}) collective-permute-start(bf16[40,4224]{1,0:T(8,128)(2,1)S(1)} %get-tuple-element.140), channel_id=1, source_target_pairs={{0,16},{8,24},{16,0},{24,8},{1,17},{9,25},{17,1},{25,9},{2,18},{10... | collective-permute-start | bytes 1013768 | tf_op jit(solution)/shard_map/ppermute | solution.py:289
  53.1 10.2 %collective-permute-start.14 = (bf16[128,1024]{1,0:T(8,128)(2,1)S(1)}, bf16[128,1024]{1,0:T(8,128)(2,1)S(1)}, u32[]{:S(2)}, u32[]{:S(2)}) collective-permute-start(bf16[128,1024]{1,0:T(8,128)(2,1)S(1)} %get-tuple-element.138), channel_id=1, source_target_pairs={{0,4},{1,5},{2,6},{3,7},{4,0},{5,1},{6,2},{7,3},{8,12},{9,13},{10,... | collective-permute-start | bytes 786440 | tf_op jit(solution)/shard_map/ppermute | solution.py:289
  56.4 8.9 %collective-permute-start.18 = (bf16[40,3968]{1,0:T(8,128)(2,1)S(1)}, bf16[40,3968]{1,0:T(8,128)(2,1)S(1)}, u32[]{:S(2)}, u32[]{:S(2)}) collective-permute-start(bf16[40,3968]{1,0:T(8,128)(2,1)S(1)} %get-tuple-element.152), channel_id=1, source_target_pairs={{0,16},{8,24},{16,0},{24,8},{1,17},{9,25},{17,1},{25,9},{2,18},{10... | collective-permute-start | bytes 952328 | tf_op jit(solution)/shard_map/ppermute | solution.py:289
  64.0 1.3 %collective-permute-start.19 = (f32[128,128]{1,0:T(8,128)S(1)}, f32[128,128]{1,0:T(8,128)S(1)}, u32[]{:S(2)}, u32[]{:S(2)}) collective-permute-start(f32[128,128]{1,0:T(8,128)S(1)} %get-tuple-element.153), channel_id=1, source_target_pairs={{0,1},{1,0},{2,3},{3,2},{4,5},{5,4},{6,7},{7,6},{8,9},{9,8},{10,11... | collective-permute-start | bytes 196616 | tf_op jit(solution)/shard_map/ppermute | solution.py:289

commit v10 on v7

--- a/solution.py
+++ b/solution.py
@@ -48,6 +48,10 @@
         )(*ins, *marks)
         return got[0] if single else got
 
+    def hold(self, value):
+        value, self.mark = lax.optimization_barrier((value, self.mark))
+        return value
+
 
 def either(bit, run):
     for value in range(2):
@@ -324,7 +328,6 @@
     )
     first[1] = one_hop(own[1])
     down_got = exchanged(down_send, "tensor", SWAP)
-    first[0] = one_hop(own[0])
 
     def joined(keep, got, out):
         stacked(out, keep, got)
@@ -341,6 +344,7 @@
         far=2,
         scratch=[pltpu.SemaphoreType.DMA((2,))],
     )
+    first[0] = one_hop(step.hold(own[0]))
     share = with_width(shares)
     share_own = step(share, small, [g, own[2]])
     second[1] = relay(first[1], own[1])
@@ -374,7 +378,6 @@
     low_columns = half + 128
     low_shape, high_shape = (both_rows, low_columns), (both_rows, wide - low_columns)
     low, high = step(sent_pair, [(low_shape, BF), (high_shape, BF)], [x, pair_second])
-    side_low, side_high = outward(low), outward(high)
 
     def one_sent(gr, down, hid, part, out):
         shares(width, gr, down, part)
@@ -382,6 +385,7 @@
 
     share_first, sent = step(one_sent, [small, small], [g, first[2], hid_first[1]], also=[two_theirs])
     got_one = exchanged(sent, "tensor", SWAP)
+    side_low = outward(step.hold(low))
     grads_f32 = [(low_shape, F32), (high_shape, F32), ((both_rows, half), F32)]
 
     def finish_last(both, share, got, hid, wide_a, wide_b, down, pair, wide_out, out):
@@ -413,6 +417,7 @@
 
     back_of_down = backward(step(back_down, piece, [g, *hid_first, side_down]))
     own_low, own_high, own_down = step(own_grads, grads_f32, [x, g, *hid_own, pair_own])
+    side_high = outward(step.hold(high))
     back_of_low = backward(step(back_pair(0), (low_shape, BF), [x, pair_first, side_low]))
     send, keep = step(
         with_width(output_sums),

time: 67.2 us -> 68.3 us (1.016)
  waiting for transfers between devices: 23.4 us -> 25.8 us
  starting transfers between devices: 28.3 us -> 27 us
    ppermute x19, waiting for transfers between devices: 19.8 us -> 22.2 us  [exchanged(): lax.ppermute(value, axis, [(source, source ^ bit) for source in range(cou...]
    ppermute x19, starting transfers between devices: 24.9 us -> 23.6 us  [exchanged(): lax.ppermute(value, axis, [(source, source ^ bit) for source in range(cou...]
  transfers between devices with their start and end apart: 20 -> 20, of which waited for: 10 -> 11; matrix products, arithmetic and copies ran while one was open for 0% -> 0% of each run, Pallas kernels for 17% -> 17%
where the time goes in v10:
time: 68.3 us; the launch traced here: 68.1 us
  starting transfers between devices  27 us (40%)
  waiting for transfers between devices  25.8 us (38%)
  Pallas kernels  14.5 us (21%)
  between operations  0.82 us (1%)
    ppermute x19, starting transfers between devices, exchanged(): lax.ppermute(value, axis, [(source, source ^ bit) for source in range(cou...  23.6 us
    ppermute x19, waiting for transfers between devices, exchanged(): lax.ppermute(value, axis, [(source, source ^ bit) for source in range(cou...  22.2 us
    pallas_call x25, Pallas kernels, __call__(): pl.pallas_call(kernel, out_shape=[jax.ShapeDtypeStruct(*s) for s in shape...  14.5 us
    ppermute x1, waiting for transfers between devices, on_device(): lax.ppermute(crossed, 'section', [(source, source ^ 2) for source in (0,...  3.6 us
    ppermute x1, starting transfers between devices, on_device(): lax.ppermute(crossed, 'section', [(source, source ^ 2) for source in (0,...  3.41 us
  transfers between devices with their start and end apart: 20, of which 11 were waited for; matrix products, arithmetic and copies ran while one was open for 0% of the time, Pallas kernels for 17%

profile of v10, /device:TPU:0, one launch (start us, length us, event | category | flops | bytes accessed | tf_op | source)
XLA Modules:
  0.0 68.1 jit_solution(12179106158660421764)
XLA Ops:
  0.6 1.7 %shard_map.84 = (bf16[40,4096]{1,0:T(8,128)(2,1)S(1)}, bf16[40,4096]{1,0:T(8,128)(2,1)S(1)}, bf16[20,4096]{1,0:T(8,128)(2,1)S(1)}, bf16[20,4096]{1,0:T(8,128)(2,1)S(1)}, f32[8,128]{1,0:T(8,128)S(1)}) custom-call(bf16[20,8192]{1,0:T(8,128)(2,1)} %refs_0_.2, bf16[20,8192]{1,0:T(8,128)(2,1)} %refs_1_.2, bf16[20,8192]{1,0:T(8,128)(2,1)} %refs_2_.1), custom_call_target="tpu_custom_call" | custom-call | flops 1 | bytes 1 | tf_op jit(solution)/shard_map/pallas_call | solution.py:39
  2.9 2.6 %collective-permute-start.2 = (bf16[40,4096]{1,0:T(8,128)(2,1)S(1)}, bf16[40,4096]{1,0:T(8,128)(2,1)S(1)}, u32[]{:S(2)}, u32[]{:S(2)}) collective-permute-start(bf16[40,4096]{1,0:T(8,128)(2,1)S(1)} %get-tuple-element.83.refs_3_.refs_1_), channel_id=1, source_target_pairs={{0,16},{8,24},{16,0},{24,8},{1,17},{9,25},{17,1},{25,9},{2,18},{10... | collective-permute-start | bytes 983048 | tf_op jit(solution)/shard_map/ppermute | solution.py:281
  5.8 1.6 %collective-permute-start.5 = (bf16[40,4096]{1,0:T(8,128)(2,1)S(1)}, bf16[40,4096]{1,0:T(8,128)(2,1)S(1)}, u32[]{:S(2)}, u32[]{:S(2)}) collective-permute-start(bf16[40,4096]{1,0:T(8,128)(2,1)S(1)} %get-tuple-element.90.refs_1_.refs_0_.refs_3_), channel_id=1, source_target_pairs={{0,8},{8,0},{16,24},{24,16},{1,9},{9,1},{17,25},{25,17},{2,10},{10... | collective-permute-start | bytes 983048 | tf_op jit(solution)/shard_map/ppermute | solution.py:281
  7.4 2.4 %shard_map.86 = (bf16[128,8192]{1,0:T(8,128)(2,1)S(1)}, bf16[128,8192]{1,0:T(8,128)(2,1)S(1)}, f32[40,128]{1,0:T(8,128)S(1)}, bf16[40,128]{1,0:T(8,128)(2,1)S(1)...) custom-call(bf16[128,8192]{1,0:T(8,128)(2,1)} %refs_0_.3, bf16[128,8192]{1,0:T(8,128)(2,1)} %refs_1_.3, ...), custom_call_target="tpu_custom_call" | custom-call | flops 1 | bytes 1 | tf_op jit(solution)/shard_map/pallas_call | solution.py:39
  9.8 1.4 %collective-permute-start.1 = (bf16[40,4096]{1,0:T(8,128)(2,1)S(1)}, bf16[40,4096]{1,0:T(8,128)(2,1)S(1)}, u32[]{:S(2)}, u32[]{:S(2)}) collective-permute-start(bf16[40,4096]{1,0:T(8,128)(2,1)S(1)} %get-tuple-element.96.refs_2_.refs_1_), channel_id=1, source_target_pairs={{0,16},{8,24},{16,0},{24,8},{1,17},{9,25},{17,1},{25,9},{2,18},{10... | collective-permute-start | bytes 983048 | tf_op jit(solution)/shard_map/ppermute | solution.py:281
  11.7 2.3 %collective-permute-done.2.refs_0_.refs_2_ = bf16[40,4096]{1,0:T(8,128)(2,1)S(1)} collective-permute-done((bf16[40,4096]{1,0:T(8,128)(2,1)S(1)}, bf16[40,4096]{1,0:T(8,128)(2,1)S(1)}, u32[]{:S(2)}, u32[]{:S(2)}) %collective-permute-start.2) | collective-permute-done | bytes 327712 | tf_op jit(solution)/shard_map/ppermute | solution.py:281
  14.1 2.0 %collective-permute-start.4 = (bf16[40,4096]{1,0:T(8,128)(2,1)S(1)}, bf16[40,4096]{1,0:T(8,128)(2,1)S(1)}, u32[]{:S(2)}, u32[]{:S(2)}) collective-permute-start(bf16[40,4096]{1,0:T(8,128)(2,1)S(1)} %get-tuple-element.100), channel_id=1, source_target_pairs={{0,8},{8,0},{16,24},{24,16},{1,9},{9,1},{17,25},{25,17},{2,10},{10... | collective-permute-start | bytes 983048 | tf_op jit(solution)/shard_map/ppermute | solution.py:281
  16.1 3.4 %collective-permute-start.6 = (bf16[40,4096]{1,0:T(8,128)(2,1)S(1)}, bf16[40,4096]{1,0:T(8,128)(2,1)S(1)}, u32[]{:S(2)}, u32[]{:S(2)}) collective-permute-start(bf16[40,4096]{1,0:T(8,128)(2,1)S(1)} %collective-permute-done.5.refs_0_), channel_id=1, source_target_pairs={{0,16},{16,0},{1,17},{17,1},{2,18},{18,2},{3,19},{19,3},{4,20},{20... | collective-permute-start | bytes 983048 | tf_op jit(solution)/shard_map/ppermute | solution.py:338
  19.5 1.6 %collective-permute-done.1.refs_0_.refs_1_ = bf16[40,4096]{1,0:T(8,128)(2,1)S(1)} collective-permute-done((bf16[40,4096]{1,0:T(8,128)(2,1)S(1)}, bf16[40,4096]{1,0:T(8,128)(2,1)S(1)}, u32[]{:S(2)}, u32[]{:S(2)}) %collective-permute-start.1) | collective-permute-done | bytes 327712 | tf_op jit(solution)/shard_map/ppermute | solution.py:281
  21.1 1.5 %collective-permute-start.3 = (bf16[40,4096]{1,0:T(8,128)(2,1)S(1)}, bf16[40,4096]{1,0:T(8,128)(2,1)S(1)}, u32[]{:S(2)}, u32[]{:S(2)}) collective-permute-start(bf16[40,4096]{1,0:T(8,128)(2,1)S(1)} %get-tuple-element.99), channel_id=1, source_target_pairs={{0,8},{8,0},{16,24},{24,16},{1,9},{9,1},{17,25},{25,17},{2,10},{10... | collective-permute-start | bytes 983048 | tf_op jit(solution)/shard_map/ppermute | solution.py:281
  22.6 1.5 %collective-permute-start.8 = (bf16[40,4096]{1,0:T(8,128)(2,1)S(1)}, bf16[40,4096]{1,0:T(8,128)(2,1)S(1)}, u32[]{:S(2)}, u32[]{:S(2)}) collective-permute-start(bf16[40,4096]{1,0:T(8,128)(2,1)S(1)} %get-tuple-element.90.refs_1_.refs_0_.refs_3_), channel_id=1, source_target_pairs={{0,16},{8,24},{16,0},{24,8},{1,17},{9,25},{17,1},{25,9},{2,18},{10... | collective-permute-start | bytes 983048 | tf_op jit(solution)/shard_map/ppermute | solution.py:281
  24.1 0.8 %shard_map.90 = (f32[40,128]{1,0:T(8,128)S(1)}, bf16[40,128]{1,0:T(8,128)(2,1)S(1)}, bf16[40,128]{1,0:T(8,128)(2,1)S(1)}, f32[8,128]{1,0:T(8,128)S(1)}) custom-call(bf16[128,8192]{1,0:T(8,128)(2,1)S(1)} %get-tuple-element.95.refs_0_, bf16[40,4096]{1,0:T(8,128)(2,1)S(1)} %collective-permute-done.1.refs_0_.refs_1_, ...), custom_call_target="tpu_custom_call" | custom-call | flops 1 | bytes 1 | tf_op jit(solution)/shard_map/pallas_call | solution.py:39
  25.0 3.6 %collective-permute-done.6.refs_1_ = bf16[40,4096]{1,0:T(8,128)(2,1)S(1)} collective-permute-done((bf16[40,4096]{1,0:T(8,128)(2,1)S(1)}, bf16[40,4096]{1,0:T(8,128)(2,1)S(1)}, u32[]{:S(2)}, u32[]{:S(2)}) %collective-permute-start.6) | collective-permute-done | bytes 327712 | tf_op jit(solution)/shard_map/ppermute | solution.py:338
  29.2 1.6 %collective-permute-start.9 = (bf16[40,4096]{1,0:T(8,128)(2,1)S(1)}, bf16[40,4096]{1,0:T(8,128)(2,1)S(1)}, u32[]{:S(2)}, u32[]{:S(2)}) collective-permute-start(bf16[40,4096]{1,0:T(8,128)(2,1)S(1)} %get-tuple-element.120), channel_id=1, source_target_pairs={{0,2},{1,3},{2,0},{3,1},{4,6},{5,7},{6,4},{7,5},{8,10},{9,11},{10,... | collective-permute-start | bytes 983048 | tf_op jit(solution)/shard_map/ppermute | solution.py:281
  30.8 0.8 %shard_map.94 = (f32[40,128]{1,0:T(8,128)S(1)}, bf16[40,128]{1,0:T(8,128)(2,1)S(1)}, bf16[40,128]{1,0:T(8,128)(2,1)S(1)}, f32[8,128]{1,0:T(8,128)S(1)}) custom-call(bf16[128,8192]{1,0:T(8,128)(2,1)S(1)} %get-tuple-element.95.refs_0_, bf16[40,4096]{1,0:T(8,128)(2,1)S(1)} %collective-permute-done.3.refs_1_, ...), custom_call_target="tpu_custom_call" | custom-call | flops 1 | bytes 1 | tf_op jit(solution)/shard_map/pallas_call | solution.py:39
  32.1 1.2 %collective-permute-start.13 = (bf16[40,4096]{1,0:T(8,128)(2,1)S(1)}, bf16[40,4096]{1,0:T(8,128)(2,1)S(1)}, u32[]{:S(2)}, u32[]{:S(2)}) collective-permute-start(bf16[40,4096]{1,0:T(8,128)(2,1)S(1)} %get-tuple-element.136), channel_id=1, source_target_pairs={{0,8},{8,0},{16,24},{24,16},{1,9},{9,1},{17,25},{25,17},{2,10},{10... | collective-permute-start | bytes 983048 | tf_op jit(solution)/shard_map/ppermute | solution.py:281
  33.2 1.2 %collective-permute-done.7.refs_6_ = f32[80,128]{1,0:T(8,128)S(1)} collective-permute-done((f32[80,128]{1,0:T(8,128)S(1)}, f32[80,128]{1,0:T(8,128)S(1)}, u32[]{:S(2)}, u32[]{:S(2)}) %collective-permute-start.7) | collective-permute-done | bytes 40992 | tf_op jit(solution)/shard_map/ppermute | solution.py:281
  34.9 2.8 %collective-permute-done.9.refs_3_.refs_6_ = bf16[40,4096]{1,0:T(8,128)(2,1)S(1)} collective-permute-done((bf16[40,4096]{1,0:T(8,128)(2,1)S(1)}, bf16[40,4096]{1,0:T(8,128)(2,1)S(1)}, u32[]{:S(2)}, u32[]{:S(2)}) %collective-permute-start.9) | collective-permute-done | bytes 327712 | tf_op jit(solution)/shard_map/ppermute | solution.py:281
  38.4 1.2 %collective-permute-done.10.refs_2_ = f32[40,128]{1,0:T(8,128)S(1)} collective-permute-done((f32[40,128]{1,0:T(8,128)S(1)}, f32[40,128]{1,0:T(8,128)S(1)}, u32[]{:S(2)}, u32[]{:S(2)}) %collective-permute-start.10) | collective-permute-done | bytes 20512 | tf_op jit(solution)/shard_map/ppermute | solution.py:281
  39.6 2.6 %collective-permute-done.13.refs_3_.refs_2_ = bf16[40,4096]{1,0:T(8,128)(2,1)S(1)} collective-permute-done((bf16[40,4096]{1,0:T(8,128)(2,1)S(1)}, bf16[40,4096]{1,0:T(8,128)(2,1)S(1)}, u32[]{:S(2)}, u32[]{:S(2)}) %collective-permute-start.13) | collective-permute-done | bytes 327712 | tf_op jit(solution)/shard_map/ppermute | solution.py:281
  42.6 1.3 %collective-permute-start.15 = (bf16[40,4096]{1,0:T(8,128)(2,1)S(1)}, bf16[40,4096]{1,0:T(8,128)(2,1)S(1)}, u32[]{:S(2)}, u32[]{:S(2)}) collective-permute-start(bf16[40,4096]{1,0:T(8,128)(2,1)S(1)} %get-tuple-element.145), channel_id=1, source_target_pairs={{0,16},{8,24},{16,0},{24,8},{1,17},{9,25},{17,1},{25,9},{2,18},{10... | collective-permute-start | bytes 983048 | tf_op jit(solution)/shard_map/ppermute | solution.py:281
  44.5 1.9 %collective-permute-start.16 = (bf16[40,3968]{1,0:T(8,128)(2,1)S(1)}, bf16[40,3968]{1,0:T(8,128)(2,1)S(1)}, u32[]{:S(2)}, u32[]{:S(2)}) collective-permute-start(bf16[40,3968]{1,0:T(8,128)(2,1)S(1)} %get-tuple-element.146), channel_id=1, source_target_pairs={{0,8},{8,0},{16,24},{24,16},{1,9},{9,1},{17,25},{25,17},{2,10},{10... | collective-permute-start | bytes 952328 | tf_op jit(solution)/shard_map/ppermute | solution.py:281
  46.5 1.6 %collective-permute-start.11 = (bf16[40,2432]{1,0:T(8,128)(2,1)S(1)}, bf16[40,2432]{1,0:T(8,128)(2,1)S(1)}, u32[]{:S(2)}, u32[]{:S(2)}) collective-permute-start(bf16[40,2432]{1,0:T(8,128)(2,1)S(1)} %get-tuple-element.131), channel_id=1, source_target_pairs={{0,2},{1,3},{2,0},{3,1},{4,6},{5,7},{6,4},{7,5},{8,10},{9,11},{10,... | collective-permute-start | bytes 583688 | tf_op jit(solution)/shard_map/ppermute | solution.py:281
  48.1 1.3 %collective-permute-done.12.refs_2_.refs_4_ = bf16[40,4224]{1,0:T(8,128)(2,1)S(1)} collective-permute-done((bf16[40,4224]{1,0:T(8,128)(2,1)S(1)}, bf16[40,4224]{1,0:T(8,128)(2,1)S(1)}, u32[]{:S(2)}, u32[]{:S(2)}) %collective-permute-start.12) | collective-permute-done | bytes 337952 | tf_op jit(solution)/shard_map/ppermute | solution.py:281
  49.7 1.5 %collective-permute-start.17 = (bf16[40,4224]{1,0:T(8,128)(2,1)S(1)}, bf16[40,4224]{1,0:T(8,128)(2,1)S(1)}, u32[]{:S(2)}, u32[]{:S(2)}) collective-permute-start(bf16[40,4224]{1,0:T(8,128)(2,1)S(1)} %get-tuple-element.153), channel_id=1, source_target_pairs={{0,16},{8,24},{16,0},{24,8},{1,17},{9,25},{17,1},{25,9},{2,18},{10... | collective-permute-start | bytes 1013768 | tf_op jit(solution)/shard_map/ppermute | solution.py:281
  51.2 0.9 %collective-permute-done.11.refs_7_ = bf16[40,2432]{1,0:T(8,128)(2,1)S(1)} collective-permute-done((bf16[40,2432]{1,0:T(8,128)(2,1)S(1)}, bf16[40,2432]{1,0:T(8,128)(2,1)S(1)}, u32[]{:S(2)}, u32[]{:S(2)}) %collective-permute-start.11) | collective-permute-done | bytes 194592 | tf_op jit(solution)/shard_map/ppermute | solution.py:281
  52.1 1.0 %shard_map.104 = (bf16[128,1024]{1,0:T(8,128)(2,1)S(1)}, f32[128,1024]{1,0:T(8,128)S(1)}, f32[8,128]{1,0:T(8,128)S(1)}) custom-call(bf16[40,128]{1,0:T(8,128)(2,1)S(1)} %get-tuple-element.116.refs_4_.refs_0_, bf16[40,128]{1,0:T(8,128)(2,1)S(1)} %get-tuple-element.117.refs_5_.refs_1_, bf16[40,128]{1,0:T(8,128)(2,1)S(1)} %get-tuple-element.130.refs_2_, ...), custom_call_target="tpu_custom_call" | custom-call | flops 1 | bytes 1 | tf_op jit(solution)/shard_map/pallas_call | solution.py:39
  53.2 2.7 %collective-permute-start.14 = (bf16[128,1024]{1,0:T(8,128)(2,1)S(1)}, bf16[128,1024]{1,0:T(8,128)(2,1)S(1)}, u32[]{:S(2)}, u32[]{:S(2)}) collective-permute-start(bf16[128,1024]{1,0:T(8,128)(2,1)S(1)} %get-tuple-element.143), channel_id=1, source_target_pairs={{0,4},{1,5},{2,6},{3,7},{4,0},{5,1},{6,2},{7,3},{8,12},{9,13},{10,... | collective-permute-start | bytes 786440 | tf_op jit(solution)/shard_map/ppermute | solution.py:281
  56.7 1.0 %shard_map.106 = (f32[20,8192]{1,0:T(8,128)}, f32[8,128]{1,0:T(8,128)S(1)}) custom-call(f32[40,4096]{1,0:T(8,128)S(1)} %get-tuple-element.144.refs_0_, bf16[40,4096]{1,0:T(8,128)(2,1)S(1)} %collective-permute-done.15.refs_3_.refs_1_, bf16[40,4096]{1,0:T(8,128)(2,1)S(1)} %collective-permute-done.13.refs_3_.refs_2_, f32[8,128]{1,0:T(8,128)S(1)} %get-tuple-element.148.refs_3_), custom_call_target="tpu_custom_call" | custom-call | flops 1 | bytes 1 | tf_op jit(solution)/shard_map/pallas_call | solution.py:39
  57.7 7.0 %collective-permute-done.14.refs_1_ = bf16[128,1024]{1,0:T(8,128)(2,1)S(1)} collective-permute-done((bf16[128,1024]{1,0:T(8,128)(2,1)S(1)}, bf16[128,1024]{1,0:T(8,128)(2,1)S(1)}, u32[]{:S(2)}, u32[]{:S(2)}) %collective-permute-start.14) | collective-permute-done | bytes 262176 | tf_op jit(solution)/shard_map/ppermute | solution.py:281
  65.5 1.2 %collective-permute-done.19.refs_6_ = f32[128,128]{1,0:T(8,128)S(1)} collective-permute-done((f32[128,128]{1,0:T(8,128)S(1)}, f32[128,128]{1,0:T(8,128)S(1)}, u32[]{:S(2)}, u32[]{:S(2)}) %collective-permute-start.19) | collective-permute-done | bytes 65568 | tf_op jit(solution)/shard_map/ppermute | solution.py:281
  66.8 1.3 %shard_map.108 = (f32[20,8192]{1,0:T(8,128)}, f32[20,8192]{1,0:T(8,128)}, f32[8,128]{1,0:T(8,128)}) custom-call(f32[40,4224]{1,0:T(8,128)S(1)} %get-tuple-element.151.refs_0_, f32[40,3968]{1,0:T(8,128)S(1)} %get-tuple-element.152.refs_1_, bf16[40,4224]{1,0:T(8,128)(2,1)S(1)} %collective-permute-done.17.refs_2_, ...), custom_call_target="tpu_custom_call" | custom-call | flops 1 | bytes 1 | tf_op jit(solution)/shard_map/pallas_call | solution.py:39
  (33 shorter events, 6.5 us)
Async XLA Ops:
  2.4 3.1 %collective-permute-start = (bf16[20,4096]{1,0:T(8,128)(2,1)S(1)}, bf16[20,4096]{1,0:T(8,128)(2,1)S(1)}, u32[]{:S(2)}, u32[]{:S(2)}) collective-permute-start(bf16[20,4096]{1,0:T(8,128)(2,1)S(1)} %get-tuple-element.85), channel_id=1, source_target_pairs={{0,1},{1,0},{2,3},{3,2},{4,5},{5,4},{6,7},{7,6},{8,9},{9,8},{10,11... | collective-permute-start | bytes 491528 | tf_op jit(solution)/shard_map/ppermute | solution.py:281
  2.9 11.2 %collective-permute-start.2 = (bf16[40,4096]{1,0:T(8,128)(2,1)S(1)}, bf16[40,4096]{1,0:T(8,128)(2,1)S(1)}, u32[]{:S(2)}, u32[]{:S(2)}) collective-permute-start(bf16[40,4096]{1,0:T(8,128)(2,1)S(1)} %get-tuple-element.83.refs_3_.refs_1_), channel_id=1, source_target_pairs={{0,16},{8,24},{16,0},{24,8},{1,17},{9,25},{17,1},{25,9},{2,18},{10... | collective-permute-start | bytes 983048 | tf_op jit(solution)/shard_map/ppermute | solution.py:281
  5.8 10.2 %collective-permute-start.5 = (bf16[40,4096]{1,0:T(8,128)(2,1)S(1)}, bf16[40,4096]{1,0:T(8,128)(2,1)S(1)}, u32[]{:S(2)}, u32[]{:S(2)}) collective-permute-start(bf16[40,4096]{1,0:T(8,128)(2,1)S(1)} %get-tuple-element.90.refs_1_.refs_0_.refs_3_), channel_id=1, source_target_pairs={{0,8},{8,0},{16,24},{24,16},{1,9},{9,1},{17,25},{25,17},{2,10},{10... | collective-permute-start | bytes 983048 | tf_op jit(solution)/shard_map/ppermute | solution.py:281
  9.8 11.2 %collective-permute-start.1 = (bf16[40,4096]{1,0:T(8,128)(2,1)S(1)}, bf16[40,4096]{1,0:T(8,128)(2,1)S(1)}, u32[]{:S(2)}, u32[]{:S(2)}) collective-permute-start(bf16[40,4096]{1,0:T(8,128)(2,1)S(1)} %get-tuple-element.96.refs_2_.refs_1_), channel_id=1, source_target_pairs={{0,16},{8,24},{16,0},{24,8},{1,17},{9,25},{17,1},{25,9},{2,18},{10... | collective-permute-start | bytes 983048 | tf_op jit(solution)/shard_map/ppermute | solution.py:281
  14.1 10.1 %collective-permute-start.4 = (bf16[40,4096]{1,0:T(8,128)(2,1)S(1)}, bf16[40,4096]{1,0:T(8,128)(2,1)S(1)}, u32[]{:S(2)}, u32[]{:S(2)}) collective-permute-start(bf16[40,4096]{1,0:T(8,128)(2,1)S(1)} %get-tuple-element.100), channel_id=1, source_target_pairs={{0,8},{8,0},{16,24},{24,16},{1,9},{9,1},{17,25},{25,17},{2,10},{10... | collective-permute-start | bytes 983048 | tf_op jit(solution)/shard_map/ppermute | solution.py:281
  16.1 12.5 %collective-permute-start.6 = (bf16[40,4096]{1,0:T(8,128)(2,1)S(1)}, bf16[40,4096]{1,0:T(8,128)(2,1)S(1)}, u32[]{:S(2)}, u32[]{:S(2)}) collective-permute-start(bf16[40,4096]{1,0:T(8,128)(2,1)S(1)} %collective-permute-done.5.refs_0_), channel_id=1, source_target_pairs={{0,16},{16,0},{1,17},{17,1},{2,18},{18,2},{3,19},{19,3},{4,20},{20... | collective-permute-start | bytes 983048 | tf_op jit(solution)/shard_map/ppermute | solution.py:338
  21.1 9.7 %collective-permute-start.3 = (bf16[40,4096]{1,0:T(8,128)(2,1)S(1)}, bf16[40,4096]{1,0:T(8,128)(2,1)S(1)}, u32[]{:S(2)}, u32[]{:S(2)}) collective-permute-start(bf16[40,4096]{1,0:T(8,128)(2,1)S(1)} %get-tuple-element.99), channel_id=1, source_target_pairs={{0,8},{8,0},{16,24},{24,16},{1,9},{9,1},{17,25},{25,17},{2,10},{10... | collective-permute-start | bytes 983048 | tf_op jit(solution)/shard_map/ppermute | solution.py:281
  22.6 12.3 %collective-permute-start.8 = (bf16[40,4096]{1,0:T(8,128)(2,1)S(1)}, bf16[40,4096]{1,0:T(8,128)(2,1)S(1)}, u32[]{:S(2)}, u32[]{:S(2)}) collective-permute-start(bf16[40,4096]{1,0:T(8,128)(2,1)S(1)} %get-tuple-element.90.refs_1_.refs_0_.refs_3_), channel_id=1, source_target_pairs={{0,16},{8,24},{16,0},{24,8},{1,17},{9,25},{17,1},{25,9},{2,18},{10... | collective-permute-start | bytes 983048 | tf_op jit(solution)/shard_map/ppermute | solution.py:281
  29.2 8.6 %collective-permute-start.9 = (bf16[40,4096]{1,0:T(8,128)(2,1)S(1)}, bf16[40,4096]{1,0:T(8,128)(2,1)S(1)}, u32[]{:S(2)}, u32[]{:S(2)}) collective-permute-start(bf16[40,4096]{1,0:T(8,128)(2,1)S(1)} %get-tuple-element.120), channel_id=1, source_target_pairs={{0,2},{1,3},{2,0},{3,1},{4,6},{5,7},{6,4},{7,5},{8,10},{9,11},{10,... | collective-permute-start | bytes 983048 | tf_op jit(solution)/shard_map/ppermute | solution.py:281
  32.1 10.1 %collective-permute-start.13 = (bf16[40,4096]{1,0:T(8,128)(2,1)S(1)}, bf16[40,4096]{1,0:T(8,128)(2,1)S(1)}, u32[]{:S(2)}, u32[]{:S(2)}) collective-permute-start(bf16[40,4096]{1,0:T(8,128)(2,1)S(1)} %get-tuple-element.136), channel_id=1, source_target_pairs={{0,8},{8,0},{16,24},{24,16},{1,9},{9,1},{17,25},{25,17},{2,10},{10... | collective-permute-start | bytes 983048 | tf_op jit(solution)/shard_map/ppermute | solution.py:281
  33.2 1.2 %collective-permute-start.7 = (f32[80,128]{1,0:T(8,128)S(1)}, f32[80,128]{1,0:T(8,128)S(1)}, u32[]{:S(2)}, u32[]{:S(2)}) collective-permute-start(f32[80,128]{1,0:T(8,128)S(1)} %get-tuple-element.113), channel_id=1, source_target_pairs={{0,1},{1,0},{2,3},{3,2},{4,5},{5,4},{6,7},{7,6},{8,9},{9,8},{10,11... | collective-permute-start | bytes 122888 | tf_op jit(solution)/shard_map/ppermute | solution.py:281
  38.2 11.2 %collective-permute-start.12 = (bf16[40,4224]{1,0:T(8,128)(2,1)S(1)}, bf16[40,4224]{1,0:T(8,128)(2,1)S(1)}, u32[]{:S(2)}, u32[]{:S(2)}) collective-permute-start(bf16[40,4224]{1,0:T(8,128)(2,1)S(1)} %get-tuple-element.133), channel_id=1, source_target_pairs={{0,8},{8,0},{16,24},{24,16},{1,9},{9,1},{17,25},{25,17},{2,10},{10... | collective-permute-start | bytes 1013768 | tf_op jit(solution)/shard_map/ppermute | solution.py:281
  38.3 1.3 %collective-permute-start.10 = (f32[40,128]{1,0:T(8,128)S(1)}, f32[40,128]{1,0:T(8,128)S(1)}, u32[]{:S(2)}, u32[]{:S(2)}) collective-permute-start(f32[40,128]{1,0:T(8,128)S(1)} %get-tuple-element.125), channel_id=1, source_target_pairs={{0,1},{1,0},{2,3},{3,2},{4,5},{5,4},{6,7},{7,6},{8,9},{9,8},{10,11... | collective-permute-start | bytes 61448 | tf_op jit(solution)/shard_map/ppermute | solution.py:281
  42.6 13.2 %collective-permute-start.15 = (bf16[40,4096]{1,0:T(8,128)(2,1)S(1)}, bf16[40,4096]{1,0:T(8,128)(2,1)S(1)}, u32[]{:S(2)}, u32[]{:S(2)}) collective-permute-start(bf16[40,4096]{1,0:T(8,128)(2,1)S(1)} %get-tuple-element.145), channel_id=1, source_target_pairs={{0,16},{8,24},{16,0},{24,8},{1,17},{9,25},{17,1},{25,9},{2,18},{10... | collective-permute-start | bytes 983048 | tf_op jit(solution)/shard_map/ppermute | solution.py:281
  44.5 11.3 %collective-permute-start.16 = (bf16[40,3968]{1,0:T(8,128)(2,1)S(1)}, bf16[40,3968]{1,0:T(8,128)(2,1)S(1)}, u32[]{:S(2)}, u32[]{:S(2)}) collective-permute-start(bf16[40,3968]{1,0:T(8,128)(2,1)S(1)} %get-tuple-element.146), channel_id=1, source_target_pairs={{0,8},{8,0},{16,24},{24,16},{1,9},{9,1},{17,25},{25,17},{2,10},{10... | collective-permute-start | bytes 952328 | tf_op jit(solution)/shard_map/ppermute | solution.py:281
  46.5 5.6 %collective-permute-start.11 = (bf16[40,2432]{1,0:T(8,128)(2,1)S(1)}, bf16[40,2432]{1,0:T(8,128)(2,1)S(1)}, u32[]{:S(2)}, u32[]{:S(2)}) collective-permute-start(bf16[40,2432]{1,0:T(8,128)(2,1)S(1)} %get-tuple-element.131), channel_id=1, source_target_pairs={{0,2},{1,3},{2,0},{3,1},{4,6},{5,7},{6,4},{7,5},{8,10},{9,11},{10,... | collective-permute-start | bytes 583688 | tf_op jit(solution)/shard_map/ppermute | solution.py:281
  49.7 17.1 %collective-permute-start.17 = (bf16[40,4224]{1,0:T(8,128)(2,1)S(1)}, bf16[40,4224]{1,0:T(8,128)(2,1)S(1)}, u32[]{:S(2)}, u32[]{:S(2)}) collective-permute-start(bf16[40,4224]{1,0:T(8,128)(2,1)S(1)} %get-tuple-element.153), channel_id=1, source_target_pairs={{0,16},{8,24},{16,0},{24,8},{1,17},{9,25},{17,1},{25,9},{2,18},{10... | collective-permute-start | bytes 1013768 | tf_op jit(solution)/shard_map/ppermute | solution.py:281
  53.2 11.6 %collective-permute-start.14 = (bf16[128,1024]{1,0:T(8,128)(2,1)S(1)}, bf16[128,1024]{1,0:T(8,128)(2,1)S(1)}, u32[]{:S(2)}, u32[]{:S(2)}) collective-permute-start(bf16[128,1024]{1,0:T(8,128)(2,1)S(1)} %get-tuple-element.143), channel_id=1, source_target_pairs={{0,4},{1,5},{2,6},{3,7},{4,0},{5,1},{6,2},{7,3},{8,12},{9,13},{10,... | collective-permute-start | bytes 786440 | tf_op jit(solution)/shard_map/ppermute | solution.py:281
  56.1 9.4 %collective-permute-start.18 = (bf16[40,3968]{1,0:T(8,128)(2,1)S(1)}, bf16[40,3968]{1,0:T(8,128)(2,1)S(1)}, u32[]{:S(2)}, u32[]{:S(2)}) collective-permute-start(bf16[40,3968]{1,0:T(8,128)(2,1)S(1)} %get-tuple-element.154), channel_id=1, source_target_pairs={{0,16},{8,24},{16,0},{24,8},{1,17},{9,25},{17,1},{25,9},{2,18},{10... | collective-permute-start | bytes 952328 | tf_op jit(solution)/shard_map/ppermute | solution.py:281
  65.5 1.3 %collective-permute-start.19 = (f32[128,128]{1,0:T(8,128)S(1)}, f32[128,128]{1,0:T(8,128)S(1)}, u32[]{:S(2)}, u32[]{:S(2)}) collective-permute-start(f32[128,128]{1,0:T(8,128)S(1)} %get-tuple-element.155), channel_id=1, source_target_pairs={{0,1},{1,0},{2,3},{3,2},{4,5},{5,4},{6,7},{7,6},{8,9},{9,8},{10,11... | collective-permute-start | bytes 196616 | tf_op jit(solution)/shard_map/ppermute | solution.py:281

commit v11 on v10

--- a/solution.py
+++ b/solution.py
@@ -271,9 +271,8 @@
     either(tensor_bit(bit), run)
 
 
-def final_output(keep, got, out, end):
+def final_output(keep, got, out):
     out[...] = (keep[...] + got[...].astype(F32)).astype(BF)
-    end[...] = jnp.zeros_like(end)
 
 
 def exchanged(value, axis, bit):
@@ -379,6 +378,9 @@
     low_shape, high_shape = (both_rows, low_columns), (both_rows, wide - low_columns)
     low, high = step(sent_pair, [(low_shape, BF), (high_shape, BF)], [x, pair_second])
 
+    grads_f32 = [(low_shape, F32), (high_shape, F32), ((both_rows, half), F32)]
+    own_low, own_high, own_down = step(own_grads, grads_f32, [x, g, *hid_own, pair_own])
+
     def one_sent(gr, down, hid, part, out):
         shares(width, gr, down, part)
         out[...] = sent_share(part, hid)
@@ -386,7 +388,6 @@
     share_first, sent = step(one_sent, [small, small], [g, first[2], hid_first[1]], also=[two_theirs])
     got_one = exchanged(sent, "tensor", SWAP)
     side_low = outward(step.hold(low))
-    grads_f32 = [(low_shape, F32), (high_shape, F32), ((both_rows, half), F32)]
 
     def finish_last(both, share, got, hid, wide_a, wide_b, down, pair, wide_out, out):
         finish(both, share, got, hid, pair, wide_out)
@@ -416,7 +417,6 @@
         return body
 
     back_of_down = backward(step(back_down, piece, [g, *hid_first, side_down]))
-    own_low, own_high, own_down = step(own_grads, grads_f32, [x, g, *hid_own, pair_own])
     side_high = outward(step.hold(high))
     back_of_low = backward(step(back_pair(0), (low_shape, BF), [x, pair_first, side_low]))
     send, keep = step(
@@ -435,7 +435,24 @@
         send, keep = step(body, [((tokens, cols), BF), ((tokens, cols), F32)], [keep, got])
         return keep, exchanged(send, "tensor", bit)
 
-    back_of_high = backward(step(back_pair(low_columns), (high_shape, BF), [x, pair_first, side_high], also=[back_of_down]))
+    high_columns = wide - low_columns
+    cut_at = high_columns // 256 * 128
+    high_shapes = [(both_rows, cut_at), (both_rows, high_columns - cut_at)]
+
+    def back_last(xr, pair, side, out_a, out_b):
+        odd = is_odd()
+        for out, offset in ((out_a, 0), (out_b, cut_at)):
+            for cut in tiles(out.shape[1]):
+                value = dot(pair[...], xr[:, shifted(cut, low_columns + offset)], NN)
+                value += kept(side[:, shifted(cut, offset)], odd, four, True)
+                out[:, cut] = value.astype(BF)
+
+    backs_of_high = [
+        backward(value)
+        for value in step(
+            back_last, [(shape, BF) for shape in high_shapes], [x, pair_first, side_high], also=[back_of_down]
+        )
+    ]
     bit = 2 * BITS[0]
     while bit < count:
         keep, got = next_half(keep, got, bit)
@@ -453,23 +470,29 @@
             out[:, cut] = value[:rows]
             out[:, half + at : half + at + TILE] = value[rows:]
 
-    def final_pair(low_ref, high_ref, low_back, high_back, low_side, high_side, out_gate, out_up):
+    def final_pair(low_ref, high_ref, low_back, back_a, back_b, low_side, high_side, out_gate, out_up):
         odd = is_odd()
-        for offset, refs in ((0, (low_ref, low_back, low_side)), (low_columns, (high_ref, high_back, high_side))):
-            for cut in tiles(refs[0].shape[1]):
-                value = finished(*refs, odd, cut)
+        pieces = (
+            (low_ref, low_back, low_side, 0, 0, low_columns),
+            (high_ref, back_a, high_side, 0, low_columns, cut_at),
+            (high_ref, back_b, high_side, cut_at, low_columns + cut_at, high_columns - cut_at),
+        )
+        for own_ref, back, side, inside, offset, columns in pieces:
+            for cut in tiles(columns):
+                from_ = shifted(cut, inside)
+                value = own_ref[:, from_] + back[:, cut].astype(F32)
+                if four:
+                    value += kept(side[:, from_], odd, four, False)
                 out_gate[:, shifted(cut, offset)] = value[:rows]
                 out_up[:, shifted(cut, offset)] = value[rows:]
 
     whole = ((rows, wide), F32)
     grad_down = step(final_down, whole, [own_down, back_of_down, side_down])
-    output, end = step(final_output, [((tokens, width), BF), ((128, 128), F32)], [keep, got])
-    end = exchanged(end, "tensor", SWAP)
+    output = step(final_output, ((tokens, width), BF), [keep, got])
     grad_gate, grad_up = step(
         final_pair,
         [whole, whole],
-        [own_low, own_high, back_of_low, back_of_high, side_low, side_high],
-        also=[end],
+        [own_low, own_high, back_of_low, *backs_of_high, side_low, side_high],
     )
     return (output, grad_gate, grad_up, grad_down)
 

time: 68.3 us -> 66.3 us (0.971)
  waiting for transfers between devices: 25.8 us -> 22.1 us
  starting transfers between devices: 27 us -> 28.7 us
    ppermute x19, waiting for transfers between devices: 22.2 us -> 18.5 us  [exchanged(): lax.ppermute(value, axis, [(source, source ^ bit) for source in range(cou...]
    ppermute x19, starting transfers between devices: 23.6 us -> 25.3 us  [exchanged(): lax.ppermute(value, axis, [(source, source ^ bit) for source in range(cou...]
  transfers between devices with their start and end apart: 20 -> 20, of which waited for: 11 -> 9; matrix products, arithmetic and copies ran while one was open for 0% -> 0% of each run, Pallas kernels for 17% -> 17%
where the time goes in v11:
time: 66.3 us; the launch traced here: 66.1 us
  starting transfers between devices  28.7 us (43%)
  waiting for transfers between devices  22.1 us (33%)
  Pallas kernels  14.5 us (22%)
  between operations  0.82 us (1%)
    ppermute x19, starting transfers between devices, exchanged(): lax.ppermute(value, axis, [(source, source ^ bit) for source in range(cou...  25.3 us
    ppermute x19, waiting for transfers between devices, exchanged(): lax.ppermute(value, axis, [(source, source ^ bit) for source in range(cou...  18.5 us
    pallas_call x25, Pallas kernels, __call__(): pl.pallas_call(kernel, out_shape=[jax.ShapeDtypeStruct(*s) for s in shape...  14.5 us
    ppermute x1, waiting for transfers between devices, on_device(): lax.ppermute(crossed, 'section', [(source, source ^ 2) for source in (0,...  3.6 us
    ppermute x1, starting transfers between devices, on_device(): lax.ppermute(crossed, 'section', [(source, source ^ 2) for source in (0,...  3.41 us
  transfers between devices with their start and end apart: 20, of which 9 were waited for; matrix products, arithmetic and copies ran while one was open for 0% of the time, Pallas kernels for 17%

profile of v11, /device:TPU:0, one launch (start us, length us, event | category | flops | bytes accessed | tf_op | source)
XLA Modules:
  0.0 66.1 jit_solution(2246264186410652833)
XLA Ops:
  0.6 1.7 %shard_map.84 = (bf16[40,4096]{1,0:T(8,128)(2,1)S(1)}, bf16[40,4096]{1,0:T(8,128)(2,1)S(1)}, bf16[20,4096]{1,0:T(8,128)(2,1)S(1)}, bf16[20,4096]{1,0:T(8,128)(2,1)S(1)}, f32[8,128]{1,0:T(8,128)S(1)}) custom-call(bf16[20,8192]{1,0:T(8,128)(2,1)} %refs_0_.2, bf16[20,8192]{1,0:T(8,128)(2,1)} %refs_1_.2, bf16[20,8192]{1,0:T(8,128)(2,1)} %refs_2_.1), custom_call_target="tpu_custom_call" | custom-call | flops 1 | bytes 1 | tf_op jit(solution)/shard_map/pallas_call | solution.py:39
  2.9 2.6 %collective-permute-start.2 = (bf16[40,4096]{1,0:T(8,128)(2,1)S(1)}, bf16[40,4096]{1,0:T(8,128)(2,1)S(1)}, u32[]{:S(2)}, u32[]{:S(2)}) collective-permute-start(bf16[40,4096]{1,0:T(8,128)(2,1)S(1)} %get-tuple-element.83.refs_3_.refs_1_), channel_id=1, source_target_pairs={{0,16},{8,24},{16,0},{24,8},{1,17},{9,25},{17,1},{25,9},{2,18},{10... | collective-permute-start | bytes 983048 | tf_op jit(solution)/shard_map/ppermute | solution.py:280
  5.8 1.6 %collective-permute-start.5 = (bf16[40,4096]{1,0:T(8,128)(2,1)S(1)}, bf16[40,4096]{1,0:T(8,128)(2,1)S(1)}, u32[]{:S(2)}, u32[]{:S(2)}) collective-permute-start(bf16[40,4096]{1,0:T(8,128)(2,1)S(1)} %get-tuple-element.90.refs_1_.refs_0_.refs_3_), channel_id=1, source_target_pairs={{0,8},{8,0},{16,24},{24,16},{1,9},{9,1},{17,25},{25,17},{2,10},{10... | collective-permute-start | bytes 983048 | tf_op jit(solution)/shard_map/ppermute | solution.py:280
  7.4 2.4 %shard_map.86 = (bf16[128,8192]{1,0:T(8,128)(2,1)S(1)}, bf16[128,8192]{1,0:T(8,128)(2,1)S(1)}, f32[40,128]{1,0:T(8,128)S(1)}, bf16[40,128]{1,0:T(8,128)(2,1)S(1)...) custom-call(bf16[128,8192]{1,0:T(8,128)(2,1)} %refs_0_.3, bf16[128,8192]{1,0:T(8,128)(2,1)} %refs_1_.3, ...), custom_call_target="tpu_custom_call" | custom-call | flops 1 | bytes 1 | tf_op jit(solution)/shard_map/pallas_call | solution.py:39
  9.8 1.4 %collective-permute-start.1 = (bf16[40,4096]{1,0:T(8,128)(2,1)S(1)}, bf16[40,4096]{1,0:T(8,128)(2,1)S(1)}, u32[]{:S(2)}, u32[]{:S(2)}) collective-permute-start(bf16[40,4096]{1,0:T(8,128)(2,1)S(1)} %get-tuple-element.96.refs_2_.refs_1_), channel_id=1, source_target_pairs={{0,16},{8,24},{16,0},{24,8},{1,17},{9,25},{17,1},{25,9},{2,18},{10... | collective-permute-start | bytes 983048 | tf_op jit(solution)/shard_map/ppermute | solution.py:280
  11.7 2.3 %collective-permute-done.2.refs_0_.refs_2_ = bf16[40,4096]{1,0:T(8,128)(2,1)S(1)} collective-permute-done((bf16[40,4096]{1,0:T(8,128)(2,1)S(1)}, bf16[40,4096]{1,0:T(8,128)(2,1)S(1)}, u32[]{:S(2)}, u32[]{:S(2)}) %collective-permute-start.2) | collective-permute-done | bytes 327712 | tf_op jit(solution)/shard_map/ppermute | solution.py:280
  14.1 2.0 %collective-permute-start.4 = (bf16[40,4096]{1,0:T(8,128)(2,1)S(1)}, bf16[40,4096]{1,0:T(8,128)(2,1)S(1)}, u32[]{:S(2)}, u32[]{:S(2)}) collective-permute-start(bf16[40,4096]{1,0:T(8,128)(2,1)S(1)} %get-tuple-element.100), channel_id=1, source_target_pairs={{0,8},{8,0},{16,24},{24,16},{1,9},{9,1},{17,25},{25,17},{2,10},{10... | collective-permute-start | bytes 983048 | tf_op jit(solution)/shard_map/ppermute | solution.py:280
  16.1 3.4 %collective-permute-start.6 = (bf16[40,4096]{1,0:T(8,128)(2,1)S(1)}, bf16[40,4096]{1,0:T(8,128)(2,1)S(1)}, u32[]{:S(2)}, u32[]{:S(2)}) collective-permute-start(bf16[40,4096]{1,0:T(8,128)(2,1)S(1)} %collective-permute-done.5.refs_0_), channel_id=1, source_target_pairs={{0,16},{16,0},{1,17},{17,1},{2,18},{18,2},{3,19},{19,3},{4,20},{20... | collective-permute-start | bytes 983048 | tf_op jit(solution)/shard_map/ppermute | solution.py:337
  19.5 1.6 %collective-permute-done.1.refs_0_.refs_1_ = bf16[40,4096]{1,0:T(8,128)(2,1)S(1)} collective-permute-done((bf16[40,4096]{1,0:T(8,128)(2,1)S(1)}, bf16[40,4096]{1,0:T(8,128)(2,1)S(1)}, u32[]{:S(2)}, u32[]{:S(2)}) %collective-permute-start.1) | collective-permute-done | bytes 327712 | tf_op jit(solution)/shard_map/ppermute | solution.py:280
  21.1 1.5 %collective-permute-start.3 = (bf16[40,4096]{1,0:T(8,128)(2,1)S(1)}, bf16[40,4096]{1,0:T(8,128)(2,1)S(1)}, u32[]{:S(2)}, u32[]{:S(2)}) collective-permute-start(bf16[40,4096]{1,0:T(8,128)(2,1)S(1)} %get-tuple-element.99), channel_id=1, source_target_pairs={{0,8},{8,0},{16,24},{24,16},{1,9},{9,1},{17,25},{25,17},{2,10},{10... | collective-permute-start | bytes 983048 | tf_op jit(solution)/shard_map/ppermute | solution.py:280
  22.6 1.5 %collective-permute-start.8 = (bf16[40,4096]{1,0:T(8,128)(2,1)S(1)}, bf16[40,4096]{1,0:T(8,128)(2,1)S(1)}, u32[]{:S(2)}, u32[]{:S(2)}) collective-permute-start(bf16[40,4096]{1,0:T(8,128)(2,1)S(1)} %get-tuple-element.90.refs_1_.refs_0_.refs_3_), channel_id=1, source_target_pairs={{0,16},{8,24},{16,0},{24,8},{1,17},{9,25},{17,1},{25,9},{2,18},{10... | collective-permute-start | bytes 983048 | tf_op jit(solution)/shard_map/ppermute | solution.py:280
  24.1 0.8 %shard_map.90 = (f32[40,128]{1,0:T(8,128)S(1)}, bf16[40,128]{1,0:T(8,128)(2,1)S(1)}, bf16[40,128]{1,0:T(8,128)(2,1)S(1)}, f32[8,128]{1,0:T(8,128)S(1)}) custom-call(bf16[128,8192]{1,0:T(8,128)(2,1)S(1)} %get-tuple-element.95.refs_0_, bf16[40,4096]{1,0:T(8,128)(2,1)S(1)} %collective-permute-done.1.refs_0_.refs_1_, ...), custom_call_target="tpu_custom_call" | custom-call | flops 1 | bytes 1 | tf_op jit(solution)/shard_map/pallas_call | solution.py:39
  25.0 3.6 %collective-permute-done.6.refs_1_ = bf16[40,4096]{1,0:T(8,128)(2,1)S(1)} collective-permute-done((bf16[40,4096]{1,0:T(8,128)(2,1)S(1)}, bf16[40,4096]{1,0:T(8,128)(2,1)S(1)}, u32[]{:S(2)}, u32[]{:S(2)}) %collective-permute-start.6) | collective-permute-done | bytes 327712 | tf_op jit(solution)/shard_map/ppermute | solution.py:337
  29.2 1.6 %collective-permute-start.9 = (bf16[40,4096]{1,0:T(8,128)(2,1)S(1)}, bf16[40,4096]{1,0:T(8,128)(2,1)S(1)}, u32[]{:S(2)}, u32[]{:S(2)}) collective-permute-start(bf16[40,4096]{1,0:T(8,128)(2,1)S(1)} %get-tuple-element.120), channel_id=1, source_target_pairs={{0,2},{1,3},{2,0},{3,1},{4,6},{5,7},{6,4},{7,5},{8,10},{9,11},{10,... | collective-permute-start | bytes 983048 | tf_op jit(solution)/shard_map/ppermute | solution.py:280
  30.8 0.8 %shard_map.94 = (f32[40,128]{1,0:T(8,128)S(1)}, bf16[40,128]{1,0:T(8,128)(2,1)S(1)}, bf16[40,128]{1,0:T(8,128)(2,1)S(1)}, f32[8,128]{1,0:T(8,128)S(1)}) custom-call(bf16[128,8192]{1,0:T(8,128)(2,1)S(1)} %get-tuple-element.95.refs_0_, bf16[40,4096]{1,0:T(8,128)(2,1)S(1)} %collective-permute-done.3.refs_1_, ...), custom_call_target="tpu_custom_call" | custom-call | flops 1 | bytes 1 | tf_op jit(solution)/shard_map/pallas_call | solution.py:39
  32.1 1.2 %collective-permute-start.13 = (bf16[40,4096]{1,0:T(8,128)(2,1)S(1)}, bf16[40,4096]{1,0:T(8,128)(2,1)S(1)}, u32[]{:S(2)}, u32[]{:S(2)}) collective-permute-start(bf16[40,4096]{1,0:T(8,128)(2,1)S(1)} %get-tuple-element.137), channel_id=1, source_target_pairs={{0,8},{8,0},{16,24},{24,16},{1,9},{9,1},{17,25},{25,17},{2,10},{10... | collective-permute-start | bytes 983048 | tf_op jit(solution)/shard_map/ppermute | solution.py:280
  33.2 1.2 %collective-permute-done.7.refs_6_ = f32[80,128]{1,0:T(8,128)S(1)} collective-permute-done((f32[80,128]{1,0:T(8,128)S(1)}, f32[80,128]{1,0:T(8,128)S(1)}, u32[]{:S(2)}, u32[]{:S(2)}) %collective-permute-start.7) | collective-permute-done | bytes 40992 | tf_op jit(solution)/shard_map/ppermute | solution.py:280
  35.6 2.1 %collective-permute-done.9.refs_3_.refs_6_ = bf16[40,4096]{1,0:T(8,128)(2,1)S(1)} collective-permute-done((bf16[40,4096]{1,0:T(8,128)(2,1)S(1)}, bf16[40,4096]{1,0:T(8,128)(2,1)S(1)}, u32[]{:S(2)}, u32[]{:S(2)}) %collective-permute-start.9) | collective-permute-done | bytes 327712 | tf_op jit(solution)/shard_map/ppermute | solution.py:280
  38.4 1.2 %collective-permute-done.10.refs_2_ = f32[40,128]{1,0:T(8,128)S(1)} collective-permute-done((f32[40,128]{1,0:T(8,128)S(1)}, f32[40,128]{1,0:T(8,128)S(1)}, u32[]{:S(2)}, u32[]{:S(2)}) %collective-permute-start.10) | collective-permute-done | bytes 20512 | tf_op jit(solution)/shard_map/ppermute | solution.py:280
  39.6 2.4 %collective-permute-done.13.refs_3_.refs_2_ = bf16[40,4096]{1,0:T(8,128)(2,1)S(1)} collective-permute-done((bf16[40,4096]{1,0:T(8,128)(2,1)S(1)}, bf16[40,4096]{1,0:T(8,128)(2,1)S(1)}, u32[]{:S(2)}, u32[]{:S(2)}) %collective-permute-start.13) | collective-permute-done | bytes 327712 | tf_op jit(solution)/shard_map/ppermute | solution.py:280
  42.5 1.4 %collective-permute-start.15 = (bf16[40,4096]{1,0:T(8,128)(2,1)S(1)}, bf16[40,4096]{1,0:T(8,128)(2,1)S(1)}, u32[]{:S(2)}, u32[]{:S(2)}) collective-permute-start(bf16[40,4096]{1,0:T(8,128)(2,1)S(1)} %get-tuple-element.145), channel_id=1, source_target_pairs={{0,16},{8,24},{16,0},{24,8},{1,17},{9,25},{17,1},{25,9},{2,18},{10... | collective-permute-start | bytes 983048 | tf_op jit(solution)/shard_map/ppermute | solution.py:280
  43.8 1.4 %collective-permute-start.16 = (bf16[40,3968]{1,0:T(8,128)(2,1)S(1)}, bf16[40,3968]{1,0:T(8,128)(2,1)S(1)}, u32[]{:S(2)}, u32[]{:S(2)}) collective-permute-start(bf16[40,3968]{1,0:T(8,128)(2,1)S(1)} %get-tuple-element.146), channel_id=1, source_target_pairs={{0,8},{8,0},{16,24},{24,16},{1,9},{9,1},{17,25},{25,17},{2,10},{10... | collective-permute-start | bytes 952328 | tf_op jit(solution)/shard_map/ppermute | solution.py:280
  45.3 2.0 %collective-permute-start.11 = (bf16[40,2432]{1,0:T(8,128)(2,1)S(1)}, bf16[40,2432]{1,0:T(8,128)(2,1)S(1)}, u32[]{:S(2)}, u32[]{:S(2)}) collective-permute-start(bf16[40,2432]{1,0:T(8,128)(2,1)S(1)} %get-tuple-element.133), channel_id=1, source_target_pairs={{0,2},{1,3},{2,0},{3,1},{4,6},{5,7},{6,4},{7,5},{8,10},{9,11},{10,... | collective-permute-start | bytes 583688 | tf_op jit(solution)/shard_map/ppermute | solution.py:280
  47.3 2.0 %collective-permute-done.12.refs_2_.refs_5_ = bf16[40,4224]{1,0:T(8,128)(2,1)S(1)} collective-permute-done((bf16[40,4224]{1,0:T(8,128)(2,1)S(1)}, bf16[40,4224]{1,0:T(8,128)(2,1)S(1)}, u32[]{:S(2)}, u32[]{:S(2)}) %collective-permute-start.12) | collective-permute-done | bytes 337952 | tf_op jit(solution)/shard_map/ppermute | solution.py:280
  49.6 1.6 %collective-permute-start.17 = (bf16[40,4224]{1,0:T(8,128)(2,1)S(1)}, bf16[40,4224]{1,0:T(8,128)(2,1)S(1)}, u32[]{:S(2)}, u32[]{:S(2)}) collective-permute-start(bf16[40,4224]{1,0:T(8,128)(2,1)S(1)} %get-tuple-element.153), channel_id=1, source_target_pairs={{0,16},{8,24},{16,0},{24,8},{1,17},{9,25},{17,1},{25,9},{2,18},{10... | collective-permute-start | bytes 1013768 | tf_op jit(solution)/shard_map/ppermute | solution.py:280
  51.2 1.0 %shard_map.104 = (bf16[128,1024]{1,0:T(8,128)(2,1)S(1)}, f32[128,1024]{1,0:T(8,128)S(1)}, f32[8,128]{1,0:T(8,128)S(1)}) custom-call(bf16[40,128]{1,0:T(8,128)(2,1)S(1)} %get-tuple-element.116.refs_4_.refs_0_, bf16[40,128]{1,0:T(8,128)(2,1)S(1)} %get-tuple-element.117.refs_5_.refs_1_, bf16[40,128]{1,0:T(8,128)(2,1)S(1)} %get-tuple-element.132.refs_2_, ...), custom_call_target="tpu_custom_call" | custom-call | flops 1 | bytes 1 | tf_op jit(solution)/shard_map/pallas_call | solution.py:39
  52.2 2.6 %collective-permute-start.14 = (bf16[128,1024]{1,0:T(8,128)(2,1)S(1)}, bf16[128,1024]{1,0:T(8,128)(2,1)S(1)}, u32[]{:S(2)}, u32[]{:S(2)}) collective-permute-start(bf16[128,1024]{1,0:T(8,128)(2,1)S(1)} %get-tuple-element.143), channel_id=1, source_target_pairs={{0,4},{1,5},{2,6},{3,7},{4,0},{5,1},{6,2},{7,3},{8,12},{9,13},{10,... | collective-permute-start | bytes 786440 | tf_op jit(solution)/shard_map/ppermute | solution.py:280
  55.2 1.3 %collective-permute-start.19 = (bf16[40,2048]{1,0:T(8,128)(2,1)S(1)}, bf16[40,2048]{1,0:T(8,128)(2,1)S(1)}, u32[]{:S(2)}, u32[]{:S(2)}) collective-permute-start(bf16[40,2048]{1,0:T(8,128)(2,1)S(1)} %get-tuple-element.155), channel_id=1, source_target_pairs={{0,16},{8,24},{16,0},{24,8},{1,17},{9,25},{17,1},{25,9},{2,18},{10... | collective-permute-start | bytes 491528 | tf_op jit(solution)/shard_map/ppermute | solution.py:280
  56.5 0.8 %collective-permute-start.18 = (bf16[40,1920]{1,0:T(8,128)(2,1)S(1)}, bf16[40,1920]{1,0:T(8,128)(2,1)S(1)}, u32[]{:S(2)}, u32[]{:S(2)}) collective-permute-start(bf16[40,1920]{1,0:T(8,128)(2,1)S(1)} %get-tuple-element.154), channel_id=1, source_target_pairs={{0,16},{8,24},{16,0},{24,8},{1,17},{9,25},{17,1},{25,9},{2,18},{10... | collective-permute-start | bytes 460808 | tf_op jit(solution)/shard_map/ppermute | solution.py:280
  57.3 1.0 %shard_map.106 = (f32[20,8192]{1,0:T(8,128)}, f32[8,128]{1,0:T(8,128)S(1)}) custom-call(f32[40,4096]{1,0:T(8,128)S(1)} %get-tuple-element.144.refs_0_, bf16[40,4096]{1,0:T(8,128)(2,1)S(1)} %collective-permute-done.15.refs_3_.refs_1_, bf16[40,4096]{1,0:T(8,128)(2,1)S(1)} %collective-permute-done.13.refs_3_.refs_2_, f32[8,128]{1,0:T(8,128)S(1)} %get-tuple-element.148.refs_3_), custom_call_target="tpu_custom_call" | custom-call | flops 1 | bytes 1 | tf_op jit(solution)/shard_map/pallas_call | solution.py:39
  58.3 5.7 %collective-permute-done.14.refs_1_ = bf16[128,1024]{1,0:T(8,128)(2,1)S(1)} collective-permute-done((bf16[128,1024]{1,0:T(8,128)(2,1)S(1)}, bf16[128,1024]{1,0:T(8,128)(2,1)S(1)}, u32[]{:S(2)}, u32[]{:S(2)}) %collective-permute-start.14) | collective-permute-done | bytes 262176 | tf_op jit(solution)/shard_map/ppermute | solution.py:280
  64.7 1.4 %shard_map.108 = (f32[20,8192]{1,0:T(8,128)}, f32[20,8192]{1,0:T(8,128)}, f32[8,128]{1,0:T(8,128)}) custom-call(f32[40,4224]{1,0:T(8,128)S(1)} %get-tuple-element.151.refs_0_, f32[40,3968]{1,0:T(8,128)S(1)} %get-tuple-element.152.refs_1_, bf16[40,4224]{1,0:T(8,128)(2,1)S(1)} %collective-permute-done.17.refs_2_, ...), custom_call_target="tpu_custom_call" | custom-call | flops 1 | bytes 1 | tf_op jit(solution)/shard_map/pallas_call | solution.py:39
  (33 shorter events, 5.9 us)
Async XLA Ops:
  2.4 3.1 %collective-permute-start = (bf16[20,4096]{1,0:T(8,128)(2,1)S(1)}, bf16[20,4096]{1,0:T(8,128)(2,1)S(1)}, u32[]{:S(2)}, u32[]{:S(2)}) collective-permute-start(bf16[20,4096]{1,0:T(8,128)(2,1)S(1)} %get-tuple-element.85), channel_id=1, source_target_pairs={{0,1},{1,0},{2,3},{3,2},{4,5},{5,4},{6,7},{7,6},{8,9},{9,8},{10,11... | collective-permute-start | bytes 491528 | tf_op jit(solution)/shard_map/ppermute | solution.py:280
  2.9 11.2 %collective-permute-start.2 = (bf16[40,4096]{1,0:T(8,128)(2,1)S(1)}, bf16[40,4096]{1,0:T(8,128)(2,1)S(1)}, u32[]{:S(2)}, u32[]{:S(2)}) collective-permute-start(bf16[40,4096]{1,0:T(8,128)(2,1)S(1)} %get-tuple-element.83.refs_3_.refs_1_), channel_id=1, source_target_pairs={{0,16},{8,24},{16,0},{24,8},{1,17},{9,25},{17,1},{25,9},{2,18},{10... | collective-permute-start | bytes 983048 | tf_op jit(solution)/shard_map/ppermute | solution.py:280
  5.8 10.2 %collective-permute-start.5 = (bf16[40,4096]{1,0:T(8,128)(2,1)S(1)}, bf16[40,4096]{1,0:T(8,128)(2,1)S(1)}, u32[]{:S(2)}, u32[]{:S(2)}) collective-permute-start(bf16[40,4096]{1,0:T(8,128)(2,1)S(1)} %get-tuple-element.90.refs_1_.refs_0_.refs_3_), channel_id=1, source_target_pairs={{0,8},{8,0},{16,24},{24,16},{1,9},{9,1},{17,25},{25,17},{2,10},{10... | collective-permute-start | bytes 983048 | tf_op jit(solution)/shard_map/ppermute | solution.py:280
  9.8 11.2 %collective-permute-start.1 = (bf16[40,4096]{1,0:T(8,128)(2,1)S(1)}, bf16[40,4096]{1,0:T(8,128)(2,1)S(1)}, u32[]{:S(2)}, u32[]{:S(2)}) collective-permute-start(bf16[40,4096]{1,0:T(8,128)(2,1)S(1)} %get-tuple-element.96.refs_2_.refs_1_), channel_id=1, source_target_pairs={{0,16},{8,24},{16,0},{24,8},{1,17},{9,25},{17,1},{25,9},{2,18},{10... | collective-permute-start | bytes 983048 | tf_op jit(solution)/shard_map/ppermute | solution.py:280
  14.1 10.1 %collective-permute-start.4 = (bf16[40,4096]{1,0:T(8,128)(2,1)S(1)}, bf16[40,4096]{1,0:T(8,128)(2,1)S(1)}, u32[]{:S(2)}, u32[]{:S(2)}) collective-permute-start(bf16[40,4096]{1,0:T(8,128)(2,1)S(1)} %get-tuple-element.100), channel_id=1, source_target_pairs={{0,8},{8,0},{16,24},{24,16},{1,9},{9,1},{17,25},{25,17},{2,10},{10... | collective-permute-start | bytes 983048 | tf_op jit(solution)/shard_map/ppermute | solution.py:280
  16.1 12.5 %collective-permute-start.6 = (bf16[40,4096]{1,0:T(8,128)(2,1)S(1)}, bf16[40,4096]{1,0:T(8,128)(2,1)S(1)}, u32[]{:S(2)}, u32[]{:S(2)}) collective-permute-start(bf16[40,4096]{1,0:T(8,128)(2,1)S(1)} %collective-permute-done.5.refs_0_), channel_id=1, source_target_pairs={{0,16},{16,0},{1,17},{17,1},{2,18},{18,2},{3,19},{19,3},{4,20},{20... | collective-permute-start | bytes 983048 | tf_op jit(solution)/shard_map/ppermute | solution.py:337
  21.1 9.7 %collective-permute-start.3 = (bf16[40,4096]{1,0:T(8,128)(2,1)S(1)}, bf16[40,4096]{1,0:T(8,128)(2,1)S(1)}, u32[]{:S(2)}, u32[]{:S(2)}) collective-permute-start(bf16[40,4096]{1,0:T(8,128)(2,1)S(1)} %get-tuple-element.99), channel_id=1, source_target_pairs={{0,8},{8,0},{16,24},{24,16},{1,9},{9,1},{17,25},{25,17},{2,10},{10... | collective-permute-start | bytes 983048 | tf_op jit(solution)/shard_map/ppermute | solution.py:280
  22.6 13.0 %collective-permute-start.8 = (bf16[40,4096]{1,0:T(8,128)(2,1)S(1)}, bf16[40,4096]{1,0:T(8,128)(2,1)S(1)}, u32[]{:S(2)}, u32[]{:S(2)}) collective-permute-start(bf16[40,4096]{1,0:T(8,128)(2,1)S(1)} %get-tuple-element.90.refs_1_.refs_0_.refs_3_), channel_id=1, source_target_pairs={{0,16},{8,24},{16,0},{24,8},{1,17},{9,25},{17,1},{25,9},{2,18},{10... | collective-permute-start | bytes 983048 | tf_op jit(solution)/shard_map/ppermute | solution.py:280
  29.2 8.6 %collective-permute-start.9 = (bf16[40,4096]{1,0:T(8,128)(2,1)S(1)}, bf16[40,4096]{1,0:T(8,128)(2,1)S(1)}, u32[]{:S(2)}, u32[]{:S(2)}) collective-permute-start(bf16[40,4096]{1,0:T(8,128)(2,1)S(1)} %get-tuple-element.120), channel_id=1, source_target_pairs={{0,2},{1,3},{2,0},{3,1},{4,6},{5,7},{6,4},{7,5},{8,10},{9,11},{10,... | collective-permute-start | bytes 983048 | tf_op jit(solution)/shard_map/ppermute | solution.py:280
  32.1 10.0 %collective-permute-start.13 = (bf16[40,4096]{1,0:T(8,128)(2,1)S(1)}, bf16[40,4096]{1,0:T(8,128)(2,1)S(1)}, u32[]{:S(2)}, u32[]{:S(2)}) collective-permute-start(bf16[40,4096]{1,0:T(8,128)(2,1)S(1)} %get-tuple-element.137), channel_id=1, source_target_pairs={{0,8},{8,0},{16,24},{24,16},{1,9},{9,1},{17,25},{25,17},{2,10},{10... | collective-permute-start | bytes 983048 | tf_op jit(solution)/shard_map/ppermute | solution.py:280
  33.2 1.2 %collective-permute-start.7 = (f32[80,128]{1,0:T(8,128)S(1)}, f32[80,128]{1,0:T(8,128)S(1)}, u32[]{:S(2)}, u32[]{:S(2)}) collective-permute-start(f32[80,128]{1,0:T(8,128)S(1)} %get-tuple-element.113), channel_id=1, source_target_pairs={{0,1},{1,0},{2,3},{3,2},{4,5},{5,4},{6,7},{7,6},{8,9},{9,8},{10,11... | collective-permute-start | bytes 122888 | tf_op jit(solution)/shard_map/ppermute | solution.py:280
  38.2 11.1 %collective-permute-start.12 = (bf16[40,4224]{1,0:T(8,128)(2,1)S(1)}, bf16[40,4224]{1,0:T(8,128)(2,1)S(1)}, u32[]{:S(2)}, u32[]{:S(2)}) collective-permute-start(bf16[40,4224]{1,0:T(8,128)(2,1)S(1)} %get-tuple-element.135), channel_id=1, source_target_pairs={{0,8},{8,0},{16,24},{24,16},{1,9},{9,1},{17,25},{25,17},{2,10},{10... | collective-permute-start | bytes 1013768 | tf_op jit(solution)/shard_map/ppermute | solution.py:280
  38.3 1.3 %collective-permute-start.10 = (f32[40,128]{1,0:T(8,128)S(1)}, f32[40,128]{1,0:T(8,128)S(1)}, u32[]{:S(2)}, u32[]{:S(2)}) collective-permute-start(f32[40,128]{1,0:T(8,128)S(1)} %get-tuple-element.127), channel_id=1, source_target_pairs={{0,1},{1,0},{2,3},{3,2},{4,5},{5,4},{6,7},{7,6},{8,9},{9,8},{10,11... | collective-permute-start | bytes 61448 | tf_op jit(solution)/shard_map/ppermute | solution.py:280
  42.5 12.4 %collective-permute-start.15 = (bf16[40,4096]{1,0:T(8,128)(2,1)S(1)}, bf16[40,4096]{1,0:T(8,128)(2,1)S(1)}, u32[]{:S(2)}, u32[]{:S(2)}) collective-permute-start(bf16[40,4096]{1,0:T(8,128)(2,1)S(1)} %get-tuple-element.145), channel_id=1, source_target_pairs={{0,16},{8,24},{16,0},{24,8},{1,17},{9,25},{17,1},{25,9},{2,18},{10... | collective-permute-start | bytes 983048 | tf_op jit(solution)/shard_map/ppermute | solution.py:280
  43.8 11.0 %collective-permute-start.16 = (bf16[40,3968]{1,0:T(8,128)(2,1)S(1)}, bf16[40,3968]{1,0:T(8,128)(2,1)S(1)}, u32[]{:S(2)}, u32[]{:S(2)}) collective-permute-start(bf16[40,3968]{1,0:T(8,128)(2,1)S(1)} %get-tuple-element.146), channel_id=1, source_target_pairs={{0,8},{8,0},{16,24},{24,16},{1,9},{9,1},{17,25},{25,17},{2,10},{10... | collective-permute-start | bytes 952328 | tf_op jit(solution)/shard_map/ppermute | solution.py:280
  45.3 5.9 %collective-permute-start.11 = (bf16[40,2432]{1,0:T(8,128)(2,1)S(1)}, bf16[40,2432]{1,0:T(8,128)(2,1)S(1)}, u32[]{:S(2)}, u32[]{:S(2)}) collective-permute-start(bf16[40,2432]{1,0:T(8,128)(2,1)S(1)} %get-tuple-element.133), channel_id=1, source_target_pairs={{0,2},{1,3},{2,0},{3,1},{4,6},{5,7},{6,4},{7,5},{8,10},{9,11},{10,... | collective-permute-start | bytes 583688 | tf_op jit(solution)/shard_map/ppermute | solution.py:280
  49.6 15.2 %collective-permute-start.17 = (bf16[40,4224]{1,0:T(8,128)(2,1)S(1)}, bf16[40,4224]{1,0:T(8,128)(2,1)S(1)}, u32[]{:S(2)}, u32[]{:S(2)}) collective-permute-start(bf16[40,4224]{1,0:T(8,128)(2,1)S(1)} %get-tuple-element.153), channel_id=1, source_target_pairs={{0,16},{8,24},{16,0},{24,8},{1,17},{9,25},{17,1},{25,9},{2,18},{10... | collective-permute-start | bytes 1013768 | tf_op jit(solution)/shard_map/ppermute | solution.py:280
  52.2 11.7 %collective-permute-start.14 = (bf16[128,1024]{1,0:T(8,128)(2,1)S(1)}, bf16[128,1024]{1,0:T(8,128)(2,1)S(1)}, u32[]{:S(2)}, u32[]{:S(2)}) collective-permute-start(bf16[128,1024]{1,0:T(8,128)(2,1)S(1)} %get-tuple-element.143), channel_id=1, source_target_pairs={{0,4},{1,5},{2,6},{3,7},{4,0},{5,1},{6,2},{7,3},{8,12},{9,13},{10,... | collective-permute-start | bytes 786440 | tf_op jit(solution)/shard_map/ppermute | solution.py:280
  55.2 9.6 %collective-permute-start.19 = (bf16[40,2048]{1,0:T(8,128)(2,1)S(1)}, bf16[40,2048]{1,0:T(8,128)(2,1)S(1)}, u32[]{:S(2)}, u32[]{:S(2)}) collective-permute-start(bf16[40,2048]{1,0:T(8,128)(2,1)S(1)} %get-tuple-element.155), channel_id=1, source_target_pairs={{0,16},{8,24},{16,0},{24,8},{1,17},{9,25},{17,1},{25,9},{2,18},{10... | collective-permute-start | bytes 491528 | tf_op jit(solution)/shard_map/ppermute | solution.py:280
  56.5 8.3 %collective-permute-start.18 = (bf16[40,1920]{1,0:T(8,128)(2,1)S(1)}, bf16[40,1920]{1,0:T(8,128)(2,1)S(1)}, u32[]{:S(2)}, u32[]{:S(2)}) collective-permute-start(bf16[40,1920]{1,0:T(8,128)(2,1)S(1)} %get-tuple-element.154), channel_id=1, source_target_pairs={{0,16},{8,24},{16,0},{24,8},{1,17},{9,25},{17,1},{25,9},{2,18},{10... | collective-permute-start | bytes 460808 | tf_op jit(solution)/shard_map/ppermute | solution.py:280

commit v12 on v11

--- a/solution.py
+++ b/solution.py
@@ -470,29 +470,36 @@
             out[:, cut] = value[:rows]
             out[:, half + at : half + at + TILE] = value[rows:]
 
-    def final_pair(low_ref, high_ref, low_back, back_a, back_b, low_side, high_side, out_gate, out_up):
+    def ready_sums(low_ref, low_back, low_side, high_ref, high_side, gate_low, up_low, high_sum):
         odd = is_odd()
-        pieces = (
-            (low_ref, low_back, low_side, 0, 0, low_columns),
-            (high_ref, back_a, high_side, 0, low_columns, cut_at),
-            (high_ref, back_b, high_side, cut_at, low_columns + cut_at, high_columns - cut_at),
-        )
-        for own_ref, back, side, inside, offset, columns in pieces:
+        for cut in tiles(low_columns):
+            value = finished(low_ref, low_back, low_side, odd, cut)
+            gate_low[:, cut] = value[:rows]
+            up_low[:, cut] = value[rows:]
+        for cut in tiles(high_columns):
+            value = high_ref[:, cut]
+            high_sum[:, cut] = value + kept(high_side[:, cut], odd, four, False) if four else value
+
+    def final_pair(gate_low, up_low, high_sum, back_a, back_b, keep, got, out_gate, out_up, out):
+        for cut in tiles(low_columns):
+            out_gate[:, cut] = gate_low[:, cut]
+            out_up[:, cut] = up_low[:, cut]
+        for back, inside, columns in ((back_a, 0, cut_at), (back_b, cut_at, high_columns - cut_at)):
             for cut in tiles(columns):
-                from_ = shifted(cut, inside)
-                value = own_ref[:, from_] + back[:, cut].astype(F32)
-                if four:
-                    value += kept(side[:, from_], odd, four, False)
-                out_gate[:, shifted(cut, offset)] = value[:rows]
-                out_up[:, shifted(cut, offset)] = value[rows:]
+                value = high_sum[:, shifted(cut, inside)] + back[:, cut].astype(F32)
+                out_gate[:, shifted(cut, low_columns + inside)] = value[:rows]
+                out_up[:, shifted(cut, low_columns + inside)] = value[rows:]
+        final_output(keep, got, out)
 
     whole = ((rows, wide), F32)
     grad_down = step(final_down, whole, [own_down, back_of_down, side_down])
-    output = step(final_output, ((tokens, width), BF), [keep, got])
-    grad_gate, grad_up = step(
-        final_pair,
-        [whole, whole],
-        [own_low, own_high, back_of_low, *backs_of_high, side_low, side_high],
+    ready = step(
+        ready_sums,
+        [((rows, low_columns), F32)] * 2 + [((both_rows, high_columns), F32)],
+        [own_low, back_of_low, side_low, own_high, side_high],
+    )
+    grad_gate, grad_up, output = step(
+        final_pair, [whole, whole, ((tokens, width), BF)], [*ready, *backs_of_high, keep, got]
     )
     return (output, grad_gate, grad_up, grad_down)
 

time: 66.3 us -> 65.5 us (0.988)
  no operation moved by 1% of the time
where the time goes in v12:
time: 65.5 us; the launch traced here: 65.4 us
  starting transfers between devices  28.7 us (44%)
  waiting for transfers between devices  21.9 us (33%)
  Pallas kernels  14 us (21%)
  between operations  0.82 us (1%)
    ppermute x19, starting transfers between devices, exchanged(): lax.ppermute(value, axis, [(source, source ^ bit) for source in range(cou...  25.3 us
    ppermute x19, waiting for transfers between devices, exchanged(): lax.ppermute(value, axis, [(source, source ^ bit) for source in range(cou...  18.3 us
    pallas_call x25, Pallas kernels, __call__(): pl.pallas_call(kernel, out_shape=[jax.ShapeDtypeStruct(*s) for s in shape...  14 us
    ppermute x1, waiting for transfers between devices, on_device(): lax.ppermute(crossed, 'section', [(source, source ^ 2) for source in (0,...  3.6 us
    ppermute x1, starting transfers between devices, on_device(): lax.ppermute(crossed, 'section', [(source, source ^ 2) for source in (0,...  3.41 us
  transfers between devices with their start and end apart: 20, of which 9 were waited for; matrix products, arithmetic and copies ran while one was open for 0% of the time, Pallas kernels for 17%

profile of v12, /device:TPU:0, one launch (start us, length us, event | category | flops | bytes accessed | tf_op | source)
XLA Modules:
  0.0 65.4 jit_solution(14310017066415358011)
XLA Ops:
  0.6 1.7 %shard_map.84 = (bf16[40,4096]{1,0:T(8,128)(2,1)S(1)}, bf16[40,4096]{1,0:T(8,128)(2,1)S(1)}, bf16[20,4096]{1,0:T(8,128)(2,1)S(1)}, bf16[20,4096]{1,0:T(8,128)(2,1)S(1)}, f32[8,128]{1,0:T(8,128)S(1)}) custom-call(bf16[20,8192]{1,0:T(8,128)(2,1)} %refs_0_.2, bf16[20,8192]{1,0:T(8,128)(2,1)} %refs_1_.2, bf16[20,8192]{1,0:T(8,128)(2,1)} %refs_2_.1), custom_call_target="tpu_custom_call" | custom-call | flops 1 | bytes 1 | tf_op jit(solution)/shard_map/pallas_call | solution.py:39
  2.9 2.6 %collective-permute-start.2 = (bf16[40,4096]{1,0:T(8,128)(2,1)S(1)}, bf16[40,4096]{1,0:T(8,128)(2,1)S(1)}, u32[]{:S(2)}, u32[]{:S(2)}) collective-permute-start(bf16[40,4096]{1,0:T(8,128)(2,1)S(1)} %get-tuple-element.86.refs_3_.refs_1_), channel_id=1, source_target_pairs={{0,16},{8,24},{16,0},{24,8},{1,17},{9,25},{17,1},{25,9},{2,18},{10... | collective-permute-start | bytes 983048 | tf_op jit(solution)/shard_map/ppermute | solution.py:280
  5.8 1.6 %collective-permute-start.5 = (bf16[40,4096]{1,0:T(8,128)(2,1)S(1)}, bf16[40,4096]{1,0:T(8,128)(2,1)S(1)}, u32[]{:S(2)}, u32[]{:S(2)}) collective-permute-start(bf16[40,4096]{1,0:T(8,128)(2,1)S(1)} %get-tuple-element.96.refs_1_.refs_0_.refs_3_), channel_id=1, source_target_pairs={{0,8},{8,0},{16,24},{24,16},{1,9},{9,1},{17,25},{25,17},{2,10},{10... | collective-permute-start | bytes 983048 | tf_op jit(solution)/shard_map/ppermute | solution.py:280
  7.4 2.4 %shard_map.86 = (bf16[128,8192]{1,0:T(8,128)(2,1)S(1)}, bf16[128,8192]{1,0:T(8,128)(2,1)S(1)}, f32[40,128]{1,0:T(8,128)S(1)}, bf16[40,128]{1,0:T(8,128)(2,1)S(1)...) custom-call(bf16[128,8192]{1,0:T(8,128)(2,1)} %refs_0_.3, bf16[128,8192]{1,0:T(8,128)(2,1)} %refs_1_.3, ...), custom_call_target="tpu_custom_call" | custom-call | flops 1 | bytes 1 | tf_op jit(solution)/shard_map/pallas_call | solution.py:39
  9.8 1.4 %collective-permute-start.1 = (bf16[40,4096]{1,0:T(8,128)(2,1)S(1)}, bf16[40,4096]{1,0:T(8,128)(2,1)S(1)}, u32[]{:S(2)}, u32[]{:S(2)}) collective-permute-start(bf16[40,4096]{1,0:T(8,128)(2,1)S(1)} %get-tuple-element.100.refs_2_.refs_1_), channel_id=1, source_target_pairs={{0,16},{8,24},{16,0},{24,8},{1,17},{9,25},{17,1},{25,9},{2,18},{10... | collective-permute-start | bytes 983048 | tf_op jit(solution)/shard_map/ppermute | solution.py:280
  11.7 2.3 %collective-permute-done.2.refs_0_.refs_2_ = bf16[40,4096]{1,0:T(8,128)(2,1)S(1)} collective-permute-done((bf16[40,4096]{1,0:T(8,128)(2,1)S(1)}, bf16[40,4096]{1,0:T(8,128)(2,1)S(1)}, u32[]{:S(2)}, u32[]{:S(2)}) %collective-permute-start.2) | collective-permute-done | bytes 327712 | tf_op jit(solution)/shard_map/ppermute | solution.py:280
  14.1 2.0 %collective-permute-start.4 = (bf16[40,4096]{1,0:T(8,128)(2,1)S(1)}, bf16[40,4096]{1,0:T(8,128)(2,1)S(1)}, u32[]{:S(2)}, u32[]{:S(2)}) collective-permute-start(bf16[40,4096]{1,0:T(8,128)(2,1)S(1)} %get-tuple-element.104), channel_id=1, source_target_pairs={{0,8},{8,0},{16,24},{24,16},{1,9},{9,1},{17,25},{25,17},{2,10},{10... | collective-permute-start | bytes 983048 | tf_op jit(solution)/shard_map/ppermute | solution.py:280
  16.1 3.4 %collective-permute-start.6 = (bf16[40,4096]{1,0:T(8,128)(2,1)S(1)}, bf16[40,4096]{1,0:T(8,128)(2,1)S(1)}, u32[]{:S(2)}, u32[]{:S(2)}) collective-permute-start(bf16[40,4096]{1,0:T(8,128)(2,1)S(1)} %collective-permute-done.5.refs_0_), channel_id=1, source_target_pairs={{0,16},{16,0},{1,17},{17,1},{2,18},{18,2},{3,19},{19,3},{4,20},{20... | collective-permute-start | bytes 983048 | tf_op jit(solution)/shard_map/ppermute | solution.py:337
  19.5 1.6 %collective-permute-done.1.refs_0_.refs_1_ = bf16[40,4096]{1,0:T(8,128)(2,1)S(1)} collective-permute-done((bf16[40,4096]{1,0:T(8,128)(2,1)S(1)}, bf16[40,4096]{1,0:T(8,128)(2,1)S(1)}, u32[]{:S(2)}, u32[]{:S(2)}) %collective-permute-start.1) | collective-permute-done | bytes 327712 | tf_op jit(solution)/shard_map/ppermute | solution.py:280
  21.1 1.5 %collective-permute-start.3 = (bf16[40,4096]{1,0:T(8,128)(2,1)S(1)}, bf16[40,4096]{1,0:T(8,128)(2,1)S(1)}, u32[]{:S(2)}, u32[]{:S(2)}) collective-permute-start(bf16[40,4096]{1,0:T(8,128)(2,1)S(1)} %get-tuple-element.103), channel_id=1, source_target_pairs={{0,8},{8,0},{16,24},{24,16},{1,9},{9,1},{17,25},{25,17},{2,10},{10... | collective-permute-start | bytes 983048 | tf_op jit(solution)/shard_map/ppermute | solution.py:280
  22.6 1.5 %collective-permute-start.8 = (bf16[40,4096]{1,0:T(8,128)(2,1)S(1)}, bf16[40,4096]{1,0:T(8,128)(2,1)S(1)}, u32[]{:S(2)}, u32[]{:S(2)}) collective-permute-start(bf16[40,4096]{1,0:T(8,128)(2,1)S(1)} %get-tuple-element.96.refs_1_.refs_0_.refs_3_), channel_id=1, source_target_pairs={{0,16},{8,24},{16,0},{24,8},{1,17},{9,25},{17,1},{25,9},{2,18},{10... | collective-permute-start | bytes 983048 | tf_op jit(solution)/shard_map/ppermute | solution.py:280
  24.1 0.8 %shard_map.90 = (f32[40,128]{1,0:T(8,128)S(1)}, bf16[40,128]{1,0:T(8,128)(2,1)S(1)}, bf16[40,128]{1,0:T(8,128)(2,1)S(1)}, f32[8,128]{1,0:T(8,128)S(1)}) custom-call(bf16[128,8192]{1,0:T(8,128)(2,1)S(1)} %get-tuple-element.91.refs_0_, bf16[40,4096]{1,0:T(8,128)(2,1)S(1)} %collective-permute-done.1.refs_0_.refs_1_, ...), custom_call_target="tpu_custom_call" | custom-call | flops 1 | bytes 1 | tf_op jit(solution)/shard_map/pallas_call | solution.py:39
  25.0 3.6 %collective-permute-done.6.refs_1_ = bf16[40,4096]{1,0:T(8,128)(2,1)S(1)} collective-permute-done((bf16[40,4096]{1,0:T(8,128)(2,1)S(1)}, bf16[40,4096]{1,0:T(8,128)(2,1)S(1)}, u32[]{:S(2)}, u32[]{:S(2)}) %collective-permute-start.6) | collective-permute-done | bytes 327712 | tf_op jit(solution)/shard_map/ppermute | solution.py:337
  29.2 1.6 %collective-permute-start.9 = (bf16[40,4096]{1,0:T(8,128)(2,1)S(1)}, bf16[40,4096]{1,0:T(8,128)(2,1)S(1)}, u32[]{:S(2)}, u32[]{:S(2)}) collective-permute-start(bf16[40,4096]{1,0:T(8,128)(2,1)S(1)} %get-tuple-element.126), channel_id=1, source_target_pairs={{0,2},{1,3},{2,0},{3,1},{4,6},{5,7},{6,4},{7,5},{8,10},{9,11},{10,... | collective-permute-start | bytes 983048 | tf_op jit(solution)/shard_map/ppermute | solution.py:280
  30.8 0.8 %shard_map.94 = (f32[40,128]{1,0:T(8,128)S(1)}, bf16[40,128]{1,0:T(8,128)(2,1)S(1)}, bf16[40,128]{1,0:T(8,128)(2,1)S(1)}, f32[8,128]{1,0:T(8,128)S(1)}) custom-call(bf16[128,8192]{1,0:T(8,128)(2,1)S(1)} %get-tuple-element.91.refs_0_, bf16[40,4096]{1,0:T(8,128)(2,1)S(1)} %collective-permute-done.3.refs_1_, ...), custom_call_target="tpu_custom_call" | custom-call | flops 1 | bytes 1 | tf_op jit(solution)/shard_map/pallas_call | solution.py:39
  32.1 1.2 %collective-permute-start.12 = (bf16[40,4096]{1,0:T(8,128)(2,1)S(1)}, bf16[40,4096]{1,0:T(8,128)(2,1)S(1)}, u32[]{:S(2)}, u32[]{:S(2)}) collective-permute-start(bf16[40,4096]{1,0:T(8,128)(2,1)S(1)} %get-tuple-element.139), channel_id=1, source_target_pairs={{0,8},{8,0},{16,24},{24,16},{1,9},{9,1},{17,25},{25,17},{2,10},{10... | collective-permute-start | bytes 983048 | tf_op jit(solution)/shard_map/ppermute | solution.py:280
  33.2 1.2 %collective-permute-done.7.refs_6_ = f32[80,128]{1,0:T(8,128)S(1)} collective-permute-done((f32[80,128]{1,0:T(8,128)S(1)}, f32[80,128]{1,0:T(8,128)S(1)}, u32[]{:S(2)}, u32[]{:S(2)}) %collective-permute-start.7) | collective-permute-done | bytes 40992 | tf_op jit(solution)/shard_map/ppermute | solution.py:280
  35.6 2.1 %collective-permute-done.9.refs_3_.refs_6_ = bf16[40,4096]{1,0:T(8,128)(2,1)S(1)} collective-permute-done((bf16[40,4096]{1,0:T(8,128)(2,1)S(1)}, bf16[40,4096]{1,0:T(8,128)(2,1)S(1)}, u32[]{:S(2)}, u32[]{:S(2)}) %collective-permute-start.9) | collective-permute-done | bytes 327712 | tf_op jit(solution)/shard_map/ppermute | solution.py:280
  38.4 1.2 %collective-permute-done.10.refs_2_ = f32[40,128]{1,0:T(8,128)S(1)} collective-permute-done((f32[40,128]{1,0:T(8,128)S(1)}, f32[40,128]{1,0:T(8,128)S(1)}, u32[]{:S(2)}, u32[]{:S(2)}) %collective-permute-start.10) | collective-permute-done | bytes 20512 | tf_op jit(solution)/shard_map/ppermute | solution.py:280
  39.6 2.4 %collective-permute-done.12.refs_3_.refs_2_ = bf16[40,4096]{1,0:T(8,128)(2,1)S(1)} collective-permute-done((bf16[40,4096]{1,0:T(8,128)(2,1)S(1)}, bf16[40,4096]{1,0:T(8,128)(2,1)S(1)}, u32[]{:S(2)}, u32[]{:S(2)}) %collective-permute-start.12) | collective-permute-done | bytes 327712 | tf_op jit(solution)/shard_map/ppermute | solution.py:280
  42.5 1.4 %collective-permute-start.15 = (bf16[40,4096]{1,0:T(8,128)(2,1)S(1)}, bf16[40,4096]{1,0:T(8,128)(2,1)S(1)}, u32[]{:S(2)}, u32[]{:S(2)}) collective-permute-start(bf16[40,4096]{1,0:T(8,128)(2,1)S(1)} %get-tuple-element.147), channel_id=1, source_target_pairs={{0,16},{8,24},{16,0},{24,8},{1,17},{9,25},{17,1},{25,9},{2,18},{10... | collective-permute-start | bytes 983048 | tf_op jit(solution)/shard_map/ppermute | solution.py:280
  43.8 1.4 %collective-permute-start.14 = (bf16[40,3968]{1,0:T(8,128)(2,1)S(1)}, bf16[40,3968]{1,0:T(8,128)(2,1)S(1)}, u32[]{:S(2)}, u32[]{:S(2)}) collective-permute-start(bf16[40,3968]{1,0:T(8,128)(2,1)S(1)} %get-tuple-element.145), channel_id=1, source_target_pairs={{0,8},{8,0},{16,24},{24,16},{1,9},{9,1},{17,25},{25,17},{2,10},{10... | collective-permute-start | bytes 952328 | tf_op jit(solution)/shard_map/ppermute | solution.py:280
  45.3 2.0 %collective-permute-start.16 = (bf16[40,2432]{1,0:T(8,128)(2,1)S(1)}, bf16[40,2432]{1,0:T(8,128)(2,1)S(1)}, u32[]{:S(2)}, u32[]{:S(2)}) collective-permute-start(bf16[40,2432]{1,0:T(8,128)(2,1)S(1)} %get-tuple-element.149), channel_id=1, source_target_pairs={{0,2},{1,3},{2,0},{3,1},{4,6},{5,7},{6,4},{7,5},{8,10},{9,11},{10,... | collective-permute-start | bytes 583688 | tf_op jit(solution)/shard_map/ppermute | solution.py:280
  47.3 2.0 %collective-permute-done.11.refs_2_ = bf16[40,4224]{1,0:T(8,128)(2,1)S(1)} collective-permute-done((bf16[40,4224]{1,0:T(8,128)(2,1)S(1)}, bf16[40,4224]{1,0:T(8,128)(2,1)S(1)}, u32[]{:S(2)}, u32[]{:S(2)}) %collective-permute-start.11) | collective-permute-done | bytes 337952 | tf_op jit(solution)/shard_map/ppermute | solution.py:280
  49.6 1.6 %collective-permute-start.13 = (bf16[40,4224]{1,0:T(8,128)(2,1)S(1)}, bf16[40,4224]{1,0:T(8,128)(2,1)S(1)}, u32[]{:S(2)}, u32[]{:S(2)}) collective-permute-start(bf16[40,4224]{1,0:T(8,128)(2,1)S(1)} %get-tuple-element.143), channel_id=1, source_target_pairs={{0,16},{8,24},{16,0},{24,8},{1,17},{9,25},{17,1},{25,9},{2,18},{10... | collective-permute-start | bytes 1013768 | tf_op jit(solution)/shard_map/ppermute | solution.py:280
  51.2 1.0 %shard_map.104 = (bf16[128,1024]{1,0:T(8,128)(2,1)S(1)}, f32[128,1024]{1,0:T(8,128)S(1)}, f32[8,128]{1,0:T(8,128)S(1)}) custom-call(bf16[40,128]{1,0:T(8,128)(2,1)S(1)} %get-tuple-element.131.refs_4_.refs_0_, bf16[40,128]{1,0:T(8,128)(2,1)S(1)} %get-tuple-element.132.refs_5_.refs_1_, bf16[40,128]{1,0:T(8,128)(2,1)S(1)} %get-tuple-element.148.refs_2_, ...), custom_call_target="tpu_custom_call" | custom-call | flops 1 | bytes 1 | tf_op jit(solution)/shard_map/pallas_call | solution.py:39
  52.2 2.6 %collective-permute-start.19 = (bf16[128,1024]{1,0:T(8,128)(2,1)S(1)}, bf16[128,1024]{1,0:T(8,128)(2,1)S(1)}, u32[]{:S(2)}, u32[]{:S(2)}) collective-permute-start(bf16[128,1024]{1,0:T(8,128)(2,1)S(1)} %get-tuple-element.160), channel_id=1, source_target_pairs={{0,4},{1,5},{2,6},{3,7},{4,0},{5,1},{6,2},{7,3},{8,12},{9,13},{10,... | collective-permute-start | bytes 786440 | tf_op jit(solution)/shard_map/ppermute | solution.py:280
  55.2 1.3 %collective-permute-start.18 = (bf16[40,2048]{1,0:T(8,128)(2,1)S(1)}, bf16[40,2048]{1,0:T(8,128)(2,1)S(1)}, u32[]{:S(2)}, u32[]{:S(2)}) collective-permute-start(bf16[40,2048]{1,0:T(8,128)(2,1)S(1)} %get-tuple-element.158), channel_id=1, source_target_pairs={{0,16},{8,24},{16,0},{24,8},{1,17},{9,25},{17,1},{25,9},{2,18},{10... | collective-permute-start | bytes 491528 | tf_op jit(solution)/shard_map/ppermute | solution.py:280
  56.5 0.8 %collective-permute-start.17 = (bf16[40,1920]{1,0:T(8,128)(2,1)S(1)}, bf16[40,1920]{1,0:T(8,128)(2,1)S(1)}, u32[]{:S(2)}, u32[]{:S(2)}) collective-permute-start(bf16[40,1920]{1,0:T(8,128)(2,1)S(1)} %get-tuple-element.157), channel_id=1, source_target_pairs={{0,16},{8,24},{16,0},{24,8},{1,17},{9,25},{17,1},{25,9},{2,18},{10... | collective-permute-start | bytes 460808 | tf_op jit(solution)/shard_map/ppermute | solution.py:280
  57.3 1.0 %shard_map.106 = (f32[20,8192]{1,0:T(8,128)}, f32[8,128]{1,0:T(8,128)S(1)}) custom-call(f32[40,4096]{1,0:T(8,128)S(1)} %get-tuple-element.146.refs_0_, bf16[40,4096]{1,0:T(8,128)(2,1)S(1)} %collective-permute-done.15.refs_3_.refs_1_, bf16[40,4096]{1,0:T(8,128)(2,1)S(1)} %collective-permute-done.12.refs_3_.refs_2_, f32[8,128]{1,0:T(8,128)S(1)} %get-tuple-element.152.refs_3_), custom_call_target="tpu_custom_call" | custom-call | flops 1 | bytes 1 | tf_op jit(solution)/shard_map/pallas_call | solution.py:39
  58.5 5.4 %collective-permute-done.17.refs_3_ = bf16[40,1920]{1,0:T(8,128)(2,1)S(1)} collective-permute-done((bf16[40,1920]{1,0:T(8,128)(2,1)S(1)}, bf16[40,1920]{1,0:T(8,128)(2,1)S(1)}, u32[]{:S(2)}, u32[]{:S(2)}) %collective-permute-start.17) | collective-permute-done | bytes 153632 | tf_op jit(solution)/shard_map/ppermute | solution.py:280
  64.0 1.4 %shard_map.108 = (f32[20,8192]{1,0:T(8,128)}, f32[20,8192]{1,0:T(8,128)}, bf16[128,1024]{1,0:T(8,128)(2,1)}, f32[8,128]{1,0:T(8,128)}) custom-call(f32[20,4224]{1,0:T(8,128)S(1)} %get-tuple-element.154.refs_0_, f32[20,4224]{1,0:T(8,128)S(1)} %get-tuple-element.155.refs_1_, f32[40,3968]{1,0:T(8,128)S(1)} %get-tuple-element.156.refs_2_, ...), custom_call_target="tpu_custom_call" | custom-call | flops 1 | bytes 1 | tf_op jit(solution)/shard_map/pallas_call | solution.py:39
  (33 shorter events, 5.4 us)
Async XLA Ops:
  2.4 3.1 %collective-permute-start = (bf16[20,4096]{1,0:T(8,128)(2,1)S(1)}, bf16[20,4096]{1,0:T(8,128)(2,1)S(1)}, u32[]{:S(2)}, u32[]{:S(2)}) collective-permute-start(bf16[20,4096]{1,0:T(8,128)(2,1)S(1)} %get-tuple-element.88), channel_id=1, source_target_pairs={{0,1},{1,0},{2,3},{3,2},{4,5},{5,4},{6,7},{7,6},{8,9},{9,8},{10,11... | collective-permute-start | bytes 491528 | tf_op jit(solution)/shard_map/ppermute | solution.py:280
  2.9 11.2 %collective-permute-start.2 = (bf16[40,4096]{1,0:T(8,128)(2,1)S(1)}, bf16[40,4096]{1,0:T(8,128)(2,1)S(1)}, u32[]{:S(2)}, u32[]{:S(2)}) collective-permute-start(bf16[40,4096]{1,0:T(8,128)(2,1)S(1)} %get-tuple-element.86.refs_3_.refs_1_), channel_id=1, source_target_pairs={{0,16},{8,24},{16,0},{24,8},{1,17},{9,25},{17,1},{25,9},{2,18},{10... | collective-permute-start | bytes 983048 | tf_op jit(solution)/shard_map/ppermute | solution.py:280
  5.8 10.2 %collective-permute-start.5 = (bf16[40,4096]{1,0:T(8,128)(2,1)S(1)}, bf16[40,4096]{1,0:T(8,128)(2,1)S(1)}, u32[]{:S(2)}, u32[]{:S(2)}) collective-permute-start(bf16[40,4096]{1,0:T(8,128)(2,1)S(1)} %get-tuple-element.96.refs_1_.refs_0_.refs_3_), channel_id=1, source_target_pairs={{0,8},{8,0},{16,24},{24,16},{1,9},{9,1},{17,25},{25,17},{2,10},{10... | collective-permute-start | bytes 983048 | tf_op jit(solution)/shard_map/ppermute | solution.py:280
  9.8 11.2 %collective-permute-start.1 = (bf16[40,4096]{1,0:T(8,128)(2,1)S(1)}, bf16[40,4096]{1,0:T(8,128)(2,1)S(1)}, u32[]{:S(2)}, u32[]{:S(2)}) collective-permute-start(bf16[40,4096]{1,0:T(8,128)(2,1)S(1)} %get-tuple-element.100.refs_2_.refs_1_), channel_id=1, source_target_pairs={{0,16},{8,24},{16,0},{24,8},{1,17},{9,25},{17,1},{25,9},{2,18},{10... | collective-permute-start | bytes 983048 | tf_op jit(solution)/shard_map/ppermute | solution.py:280
  14.1 10.1 %collective-permute-start.4 = (bf16[40,4096]{1,0:T(8,128)(2,1)S(1)}, bf16[40,4096]{1,0:T(8,128)(2,1)S(1)}, u32[]{:S(2)}, u32[]{:S(2)}) collective-permute-start(bf16[40,4096]{1,0:T(8,128)(2,1)S(1)} %get-tuple-element.104), channel_id=1, source_target_pairs={{0,8},{8,0},{16,24},{24,16},{1,9},{9,1},{17,25},{25,17},{2,10},{10... | collective-permute-start | bytes 983048 | tf_op jit(solution)/shard_map/ppermute | solution.py:280
  16.1 12.5 %collective-permute-start.6 = (bf16[40,4096]{1,0:T(8,128)(2,1)S(1)}, bf16[40,4096]{1,0:T(8,128)(2,1)S(1)}, u32[]{:S(2)}, u32[]{:S(2)}) collective-permute-start(bf16[40,4096]{1,0:T(8,128)(2,1)S(1)} %collective-permute-done.5.refs_0_), channel_id=1, source_target_pairs={{0,16},{16,0},{1,17},{17,1},{2,18},{18,2},{3,19},{19,3},{4,20},{20... | collective-permute-start | bytes 983048 | tf_op jit(solution)/shard_map/ppermute | solution.py:337
  21.1 9.7 %collective-permute-start.3 = (bf16[40,4096]{1,0:T(8,128)(2,1)S(1)}, bf16[40,4096]{1,0:T(8,128)(2,1)S(1)}, u32[]{:S(2)}, u32[]{:S(2)}) collective-permute-start(bf16[40,4096]{1,0:T(8,128)(2,1)S(1)} %get-tuple-element.103), channel_id=1, source_target_pairs={{0,8},{8,0},{16,24},{24,16},{1,9},{9,1},{17,25},{25,17},{2,10},{10... | collective-permute-start | bytes 983048 | tf_op jit(solution)/shard_map/ppermute | solution.py:280
  22.6 13.0 %collective-permute-start.8 = (bf16[40,4096]{1,0:T(8,128)(2,1)S(1)}, bf16[40,4096]{1,0:T(8,128)(2,1)S(1)}, u32[]{:S(2)}, u32[]{:S(2)}) collective-permute-start(bf16[40,4096]{1,0:T(8,128)(2,1)S(1)} %get-tuple-element.96.refs_1_.refs_0_.refs_3_), channel_id=1, source_target_pairs={{0,16},{8,24},{16,0},{24,8},{1,17},{9,25},{17,1},{25,9},{2,18},{10... | collective-permute-start | bytes 983048 | tf_op jit(solution)/shard_map/ppermute | solution.py:280
  29.2 8.6 %collective-permute-start.9 = (bf16[40,4096]{1,0:T(8,128)(2,1)S(1)}, bf16[40,4096]{1,0:T(8,128)(2,1)S(1)}, u32[]{:S(2)}, u32[]{:S(2)}) collective-permute-start(bf16[40,4096]{1,0:T(8,128)(2,1)S(1)} %get-tuple-element.126), channel_id=1, source_target_pairs={{0,2},{1,3},{2,0},{3,1},{4,6},{5,7},{6,4},{7,5},{8,10},{9,11},{10,... | collective-permute-start | bytes 983048 | tf_op jit(solution)/shard_map/ppermute | solution.py:280
  32.1 10.0 %collective-permute-start.12 = (bf16[40,4096]{1,0:T(8,128)(2,1)S(1)}, bf16[40,4096]{1,0:T(8,128)(2,1)S(1)}, u32[]{:S(2)}, u32[]{:S(2)}) collective-permute-start(bf16[40,4096]{1,0:T(8,128)(2,1)S(1)} %get-tuple-element.139), channel_id=1, source_target_pairs={{0,8},{8,0},{16,24},{24,16},{1,9},{9,1},{17,25},{25,17},{2,10},{10... | collective-permute-start | bytes 983048 | tf_op jit(solution)/shard_map/ppermute | solution.py:280
  33.2 1.2 %collective-permute-start.7 = (f32[80,128]{1,0:T(8,128)S(1)}, f32[80,128]{1,0:T(8,128)S(1)}, u32[]{:S(2)}, u32[]{:S(2)}) collective-permute-start(f32[80,128]{1,0:T(8,128)S(1)} %get-tuple-element.116), channel_id=1, source_target_pairs={{0,1},{1,0},{2,3},{3,2},{4,5},{5,4},{6,7},{7,6},{8,9},{9,8},{10,11... | collective-permute-start | bytes 122888 | tf_op jit(solution)/shard_map/ppermute | solution.py:280
  38.2 11.1 %collective-permute-start.11 = (bf16[40,4224]{1,0:T(8,128)(2,1)S(1)}, bf16[40,4224]{1,0:T(8,128)(2,1)S(1)}, u32[]{:S(2)}, u32[]{:S(2)}) collective-permute-start(bf16[40,4224]{1,0:T(8,128)(2,1)S(1)} %get-tuple-element.137), channel_id=1, source_target_pairs={{0,8},{8,0},{16,24},{24,16},{1,9},{9,1},{17,25},{25,17},{2,10},{10... | collective-permute-start | bytes 1013768 | tf_op jit(solution)/shard_map/ppermute | solution.py:280
  38.3 1.3 %collective-permute-start.10 = (f32[40,128]{1,0:T(8,128)S(1)}, f32[40,128]{1,0:T(8,128)S(1)}, u32[]{:S(2)}, u32[]{:S(2)}) collective-permute-start(f32[40,128]{1,0:T(8,128)S(1)} %get-tuple-element.129), channel_id=1, source_target_pairs={{0,1},{1,0},{2,3},{3,2},{4,5},{5,4},{6,7},{7,6},{8,9},{9,8},{10,11... | collective-permute-start | bytes 61448 | tf_op jit(solution)/shard_map/ppermute | solution.py:280
  42.5 12.4 %collective-permute-start.15 = (bf16[40,4096]{1,0:T(8,128)(2,1)S(1)}, bf16[40,4096]{1,0:T(8,128)(2,1)S(1)}, u32[]{:S(2)}, u32[]{:S(2)}) collective-permute-start(bf16[40,4096]{1,0:T(8,128)(2,1)S(1)} %get-tuple-element.147), channel_id=1, source_target_pairs={{0,16},{8,24},{16,0},{24,8},{1,17},{9,25},{17,1},{25,9},{2,18},{10... | collective-permute-start | bytes 983048 | tf_op jit(solution)/shard_map/ppermute | solution.py:280
  43.8 11.0 %collective-permute-start.14 = (bf16[40,3968]{1,0:T(8,128)(2,1)S(1)}, bf16[40,3968]{1,0:T(8,128)(2,1)S(1)}, u32[]{:S(2)}, u32[]{:S(2)}) collective-permute-start(bf16[40,3968]{1,0:T(8,128)(2,1)S(1)} %get-tuple-element.145), channel_id=1, source_target_pairs={{0,8},{8,0},{16,24},{24,16},{1,9},{9,1},{17,25},{25,17},{2,10},{10... | collective-permute-start | bytes 952328 | tf_op jit(solution)/shard_map/ppermute | solution.py:280
  45.3 5.9 %collective-permute-start.16 = (bf16[40,2432]{1,0:T(8,128)(2,1)S(1)}, bf16[40,2432]{1,0:T(8,128)(2,1)S(1)}, u32[]{:S(2)}, u32[]{:S(2)}) collective-permute-start(bf16[40,2432]{1,0:T(8,128)(2,1)S(1)} %get-tuple-element.149), channel_id=1, source_target_pairs={{0,2},{1,3},{2,0},{3,1},{4,6},{5,7},{6,4},{7,5},{8,10},{9,11},{10,... | collective-permute-start | bytes 583688 | tf_op jit(solution)/shard_map/ppermute | solution.py:280
  49.6 8.7 %collective-permute-start.13 = (bf16[40,4224]{1,0:T(8,128)(2,1)S(1)}, bf16[40,4224]{1,0:T(8,128)(2,1)S(1)}, u32[]{:S(2)}, u32[]{:S(2)}) collective-permute-start(bf16[40,4224]{1,0:T(8,128)(2,1)S(1)} %get-tuple-element.143), channel_id=1, source_target_pairs={{0,16},{8,24},{16,0},{24,8},{1,17},{9,25},{17,1},{25,9},{2,18},{10... | collective-permute-start | bytes 1013768 | tf_op jit(solution)/shard_map/ppermute | solution.py:280
  52.2 11.7 %collective-permute-start.19 = (bf16[128,1024]{1,0:T(8,128)(2,1)S(1)}, bf16[128,1024]{1,0:T(8,128)(2,1)S(1)}, u32[]{:S(2)}, u32[]{:S(2)}) collective-permute-start(bf16[128,1024]{1,0:T(8,128)(2,1)S(1)} %get-tuple-element.160), channel_id=1, source_target_pairs={{0,4},{1,5},{2,6},{3,7},{4,0},{5,1},{6,2},{7,3},{8,12},{9,13},{10,... | collective-permute-start | bytes 786440 | tf_op jit(solution)/shard_map/ppermute | solution.py:280
  55.2 8.8 %collective-permute-start.18 = (bf16[40,2048]{1,0:T(8,128)(2,1)S(1)}, bf16[40,2048]{1,0:T(8,128)(2,1)S(1)}, u32[]{:S(2)}, u32[]{:S(2)}) collective-permute-start(bf16[40,2048]{1,0:T(8,128)(2,1)S(1)} %get-tuple-element.158), channel_id=1, source_target_pairs={{0,16},{8,24},{16,0},{24,8},{1,17},{9,25},{17,1},{25,9},{2,18},{10... | collective-permute-start | bytes 491528 | tf_op jit(solution)/shard_map/ppermute | solution.py:280
  56.5 7.5 %collective-permute-start.17 = (bf16[40,1920]{1,0:T(8,128)(2,1)S(1)}, bf16[40,1920]{1,0:T(8,128)(2,1)S(1)}, u32[]{:S(2)}, u32[]{:S(2)}) collective-permute-start(bf16[40,1920]{1,0:T(8,128)(2,1)S(1)} %get-tuple-element.157), channel_id=1, source_target_pairs={{0,16},{8,24},{16,0},{24,8},{1,17},{9,25},{17,1},{25,9},{2,18},{10... | collective-permute-start | bytes 460808 | tf_op jit(solution)/shard_map/ppermute | solution.py:280

commit v13 on v12

--- a/solution.py
+++ b/solution.py
@@ -91,7 +91,7 @@
     return [(SWAP * width * j, 2 * SWAP * width * j) for j in range(wide // (2 * SWAP * width))]
 
 
-def packed(width, gate, up, down, high, low, keep, send, gate_here, up_here, down_here, sems):
+def packed(width, gate, up, down, high, keep, send, gate_here, up_here, down_here, sems):
     copies = [
         pltpu.make_async_copy(there, here, sems.at[k])
         for k, (there, here) in enumerate(((gate, gate_here), (up, up_here), (down, down_here)))
@@ -102,7 +102,6 @@
     copies[0].wait()
     copies[1].wait()
     stacked(high, gate_here, up_here, half, half)
-    stacked(low, gate_here, up_here)
     copies[2].wait()
 
     def run(mine):
@@ -235,26 +234,37 @@
     either(tensor_bit(SECOND), run)
 
 
-def output_sums(width, *refs):
-    hids, downs, (two, last, send, keep) = refs[:3], refs[3:6], refs[6:]
-    tokens, quarter = send.shape[0], downs[0].shape[1] // 2
+def near_sums(width, *refs):
+    hids, downs, outs = refs[:3], refs[3:6], refs[6:]
+    tile = min(width, TILE)
+
+    def run(here, mine):
+        for block in range(2 * outs[0].shape[1] // width):
+            for at in range(0, width, tile):
+                near, column = (2 * block + here) * width + at, block // 2 * width + at
+                total = sum(dot(hid[...], down[:, near : near + tile], TN) for hid, down in zip(hids, downs))
+                outs[int(block % 2 == mine)][:, column : column + tile] = total
+
+    both_bits(run)
+
+
+def output_sums(width, send_sum, keep_sum, two, last, send, keep):
+    tokens, quarter = send.shape[0], two.shape[1] // 2
+    tile = min(width, TILE)
     gots = ((two, 0), (two, quarter), (last, 0))
-    tile = min(width, TILE)
-
-    def run(here, mine):
+
+    def run(mine):
         for block in range(2 * keep.shape[1] // width):
-            out = keep if block % 2 == mine else send
             for at in range(0, width, tile):
-                near, far = (2 * block + here) * width + at, block * width + at
-                total = 0.0
-                for k, (hid, down, (got, offset)) in enumerate(zip(hids, downs, gots)):
-                    total += dot(hid[...], down[:, near : near + tile], TN)
+                far, column = block * width + at, block // 2 * width + at
+                out, sums = (keep, keep_sum) if block % 2 == mine else (send, send_sum)
+                total = sums[:, column : column + tile]
+                for k, (got, offset) in enumerate(gots):
                     other = last[:, quarter + k * tokens : quarter + (k + 1) * tokens]
                     total += dot(other, got[:, offset + far : offset + far + tile], TN)
-                column = block // 2 * width + at
                 out[:, column : column + tile] = total.astype(out.dtype)
 
-    both_bits(run)
+    either(tensor_bit(BITS[0]), run)
 
 
 def halved(bit, width, keep, got, send, left):
@@ -317,13 +327,12 @@
         return exchanged(value, "section", 2) if four else ring_passed(value, -1)
 
     own, first, second = [None] * 3, [None] * 3, [None] * 3
-    held = pltpu.VMEM((rows, wide), BF)
-    own[1], own[0], down_keep, down_send = step(
+    own[1], down_keep, down_send, gate_here, up_here = step(
         with_width(packed),
-        [piece, piece, narrow, narrow],
+        [piece, narrow, narrow, ((rows, wide), BF), ((rows, wide), BF)],
         [gate_weight, up_weight, down_weight],
         far=3,
-        scratch=[held, held, held, pltpu.SemaphoreType.DMA((3,))],
+        scratch=[pltpu.VMEM((rows, wide), BF), pltpu.SemaphoreType.DMA((3,))],
     )
     first[1] = one_hop(own[1])
     down_got = exchanged(down_send, "tensor", SWAP)
@@ -336,6 +345,7 @@
         crossed = exchanged(own[2], "section", 1)
         onward = lax.ppermute(crossed, "section", [(source, source ^ 2) for source in (0, 2)])
     first[2] = one_hop(own[2])
+    own[0] = step(joined, piece, [gate_here, up_here])
     x, g, both_own, *hid_own = step(
         project_first,
         [(x.shape, BF), (g.shape, BF), small, small_bf, small_bf],
@@ -401,6 +411,11 @@
         [both_first, share_first, got_one, hid_first[0], wide_own, wide_second, first[2]],
     )
     last_theirs = exchanged(sent, "tensor", SECOND)
+    near = step(
+        with_width(near_sums),
+        [((tokens, wide // 8), F32)] * 2,
+        [wide_own, wide_second, wide_first, own[2], second[2], first[2]],
+    )
     def back_down(gr, a, b, side, out):
         odd = is_odd()
         for at in range(0, half, TILE):
@@ -422,7 +437,7 @@
     send, keep = step(
         with_width(output_sums),
         [((tokens, wide // 8), BF), ((tokens, wide // 8), F32)],
-        [wide_own, wide_second, wide_first, own[2], second[2], first[2], two_theirs, last_theirs],
+        [*near, two_theirs, last_theirs],
     )
     got = exchanged(send, "tensor", BITS[0])
 

time: 65.5 us -> 65.9 us (level)
    pallas_call x25 -> x27, Pallas kernels: 14 us -> 14.3 us  [__call__(): pl.pallas_call(kernel, out_shape=[jax.ShapeDtypeStruct(*s) for s in shape...]
  transfers between devices with their start and end apart: 20 -> 20, of which waited for: 9 -> 11; matrix products, arithmetic and copies ran while one was open for 0% -> 0% of each run, Pallas kernels for 17% -> 17%
where the time goes in v13:
time: 65.9 us; the launch traced here: 65.7 us
  starting transfers between devices  28.7 us (44%)
  waiting for transfers between devices  21.9 us (33%)
  Pallas kernels  14.3 us (22%)
  between operations  0.83 us (1%)
    ppermute x19, starting transfers between devices, exchanged(): lax.ppermute(value, axis, [(source, source ^ bit) for source in range(cou...  25.2 us
    ppermute x19, waiting for transfers between devices, exchanged(): lax.ppermute(value, axis, [(source, source ^ bit) for source in range(cou...  18.3 us
    pallas_call x27, Pallas kernels, __call__(): pl.pallas_call(kernel, out_shape=[jax.ShapeDtypeStruct(*s) for s in shape...  14.3 us
    ppermute x1, waiting for transfers between devices, on_device(): lax.ppermute(crossed, 'section', [(source, source ^ 2) for source in (0,...  3.6 us
    ppermute x1, starting transfers between devices, on_device(): lax.ppermute(crossed, 'section', [(source, source ^ 2) for source in (0,...  3.41 us
  transfers between devices with their start and end apart: 20, of which 11 were waited for; matrix products, arithmetic and copies ran while one was open for 0% of the time, Pallas kernels for 17%

profile of v13, /device:TPU:0, one launch (start us, length us, event | category | flops | bytes accessed | tf_op | source)
XLA Modules:
  0.0 65.7 jit_solution(5725106835355790335)
XLA Ops:
  0.6 1.5 %shard_map.84 = (bf16[40,4096]{1,0:T(8,128)(2,1)S(1)}, bf16[20,4096]{1,0:T(8,128)(2,1)S(1)}, bf16[20,4096]{1,0:T(8,128)(2,1)S(1)}, bf16[20,8192]{1,0:T(8,128)(2,...) custom-call(bf16[20,8192]{1,0:T(8,128)(2,1)} %refs_0_.2, bf16[20,8192]{1,0:T(8,128)(2,1)} %refs_1_.2, ...), custom_call_target="tpu_custom_call" | custom-call | flops 1 | bytes 1 | tf_op jit(solution)/shard_map/pallas_call | solution.py:39
  2.7 2.6 %collective-permute-start.2 = (bf16[40,4096]{1,0:T(8,128)(2,1)S(1)}, bf16[40,4096]{1,0:T(8,128)(2,1)S(1)}, u32[]{:S(2)}, u32[]{:S(2)}) collective-permute-start(bf16[40,4096]{1,0:T(8,128)(2,1)S(1)} %get-tuple-element.98.refs_3_.refs_1_), channel_id=1, source_target_pairs={{0,16},{8,24},{16,0},{24,8},{1,17},{9,25},{17,1},{25,9},{2,18},{10... | collective-permute-start | bytes 983048 | tf_op jit(solution)/shard_map/ppermute | solution.py:290
  5.6 1.6 %collective-permute-start.5 = (bf16[40,4096]{1,0:T(8,128)(2,1)S(1)}, bf16[40,4096]{1,0:T(8,128)(2,1)S(1)}, u32[]{:S(2)}, u32[]{:S(2)}) collective-permute-start(bf16[40,4096]{1,0:T(8,128)(2,1)S(1)} %get-tuple-element.105.refs_1_.refs_0_.refs_3_), channel_id=1, source_target_pairs={{0,8},{8,0},{16,24},{24,16},{1,9},{9,1},{17,25},{25,17},{2,10},{10... | collective-permute-start | bytes 983048 | tf_op jit(solution)/shard_map/ppermute | solution.py:290
  7.5 2.5 %shard_map.87 = (bf16[128,8192]{1,0:T(8,128)(2,1)S(1)}, bf16[128,8192]{1,0:T(8,128)(2,1)S(1)}, f32[40,128]{1,0:T(8,128)S(1)}, bf16[40,128]{1,0:T(8,128)(2,1)S(1)...) custom-call(bf16[128,8192]{1,0:T(8,128)(2,1)} %refs_0_.3, bf16[128,8192]{1,0:T(8,128)(2,1)} %refs_1_.3, ...), custom_call_target="tpu_custom_call" | custom-call | flops 1 | bytes 1 | tf_op jit(solution)/shard_map/pallas_call | solution.py:39
  10.0 1.4 %collective-permute-start.1 = (bf16[40,4096]{1,0:T(8,128)(2,1)S(1)}, bf16[40,4096]{1,0:T(8,128)(2,1)S(1)}, u32[]{:S(2)}, u32[]{:S(2)}) collective-permute-start(bf16[40,4096]{1,0:T(8,128)(2,1)S(1)} %get-tuple-element.109.refs_2_.refs_1_), channel_id=1, source_target_pairs={{0,16},{8,24},{16,0},{24,8},{1,17},{9,25},{17,1},{25,9},{2,18},{10... | collective-permute-start | bytes 983048 | tf_op jit(solution)/shard_map/ppermute | solution.py:290
  11.9 2.0 %collective-permute-done.2.refs_0_.refs_2_ = bf16[40,4096]{1,0:T(8,128)(2,1)S(1)} collective-permute-done((bf16[40,4096]{1,0:T(8,128)(2,1)S(1)}, bf16[40,4096]{1,0:T(8,128)(2,1)S(1)}, u32[]{:S(2)}, u32[]{:S(2)}) %collective-permute-start.2) | collective-permute-done | bytes 327712 | tf_op jit(solution)/shard_map/ppermute | solution.py:290
  13.9 2.0 %collective-permute-start.4 = (bf16[40,4096]{1,0:T(8,128)(2,1)S(1)}, bf16[40,4096]{1,0:T(8,128)(2,1)S(1)}, u32[]{:S(2)}, u32[]{:S(2)}) collective-permute-start(bf16[40,4096]{1,0:T(8,128)(2,1)S(1)} %get-tuple-element.113), channel_id=1, source_target_pairs={{0,8},{8,0},{16,24},{24,16},{1,9},{9,1},{17,25},{25,17},{2,10},{10... | collective-permute-start | bytes 983048 | tf_op jit(solution)/shard_map/ppermute | solution.py:290
  15.9 3.4 %collective-permute-start.6 = (bf16[40,4096]{1,0:T(8,128)(2,1)S(1)}, bf16[40,4096]{1,0:T(8,128)(2,1)S(1)}, u32[]{:S(2)}, u32[]{:S(2)}) collective-permute-start(bf16[40,4096]{1,0:T(8,128)(2,1)S(1)} %collective-permute-done.5.refs_0_), channel_id=1, source_target_pairs={{0,16},{16,0},{1,17},{17,1},{2,18},{18,2},{3,19},{19,3},{4,20},{20... | collective-permute-start | bytes 983048 | tf_op jit(solution)/shard_map/ppermute | solution.py:346
  19.3 1.6 %collective-permute-done.1.refs_0_.refs_1_ = bf16[40,4096]{1,0:T(8,128)(2,1)S(1)} collective-permute-done((bf16[40,4096]{1,0:T(8,128)(2,1)S(1)}, bf16[40,4096]{1,0:T(8,128)(2,1)S(1)}, u32[]{:S(2)}, u32[]{:S(2)}) %collective-permute-start.1) | collective-permute-done | bytes 327712 | tf_op jit(solution)/shard_map/ppermute | solution.py:290
  20.9 1.5 %collective-permute-start.3 = (bf16[40,4096]{1,0:T(8,128)(2,1)S(1)}, bf16[40,4096]{1,0:T(8,128)(2,1)S(1)}, u32[]{:S(2)}, u32[]{:S(2)}) collective-permute-start(bf16[40,4096]{1,0:T(8,128)(2,1)S(1)} %get-tuple-element.112), channel_id=1, source_target_pairs={{0,8},{8,0},{16,24},{24,16},{1,9},{9,1},{17,25},{25,17},{2,10},{10... | collective-permute-start | bytes 983048 | tf_op jit(solution)/shard_map/ppermute | solution.py:290
  22.4 1.5 %collective-permute-start.8 = (bf16[40,4096]{1,0:T(8,128)(2,1)S(1)}, bf16[40,4096]{1,0:T(8,128)(2,1)S(1)}, u32[]{:S(2)}, u32[]{:S(2)}) collective-permute-start(bf16[40,4096]{1,0:T(8,128)(2,1)S(1)} %get-tuple-element.105.refs_1_.refs_0_.refs_3_), channel_id=1, source_target_pairs={{0,16},{8,24},{16,0},{24,8},{1,17},{9,25},{17,1},{25,9},{2,18},{10... | collective-permute-start | bytes 983048 | tf_op jit(solution)/shard_map/ppermute | solution.py:290
  23.9 0.8 %shard_map.91 = (f32[40,128]{1,0:T(8,128)S(1)}, bf16[40,128]{1,0:T(8,128)(2,1)S(1)}, bf16[40,128]{1,0:T(8,128)(2,1)S(1)}, f32[8,128]{1,0:T(8,128)S(1)}) custom-call(bf16[128,8192]{1,0:T(8,128)(2,1)S(1)} %get-tuple-element.100.refs_0_, bf16[40,4096]{1,0:T(8,128)(2,1)S(1)} %collective-permute-done.1.refs_0_.refs_1_, ...), custom_call_target="tpu_custom_call" | custom-call | flops 1 | bytes 1 | tf_op jit(solution)/shard_map/pallas_call | solution.py:39
  24.8 3.6 %collective-permute-done.6.refs_1_ = bf16[40,4096]{1,0:T(8,128)(2,1)S(1)} collective-permute-done((bf16[40,4096]{1,0:T(8,128)(2,1)S(1)}, bf16[40,4096]{1,0:T(8,128)(2,1)S(1)}, u32[]{:S(2)}, u32[]{:S(2)}) %collective-permute-start.6) | collective-permute-done | bytes 327712 | tf_op jit(solution)/shard_map/ppermute | solution.py:346
  29.0 1.6 %collective-permute-start.9 = (bf16[40,4096]{1,0:T(8,128)(2,1)S(1)}, bf16[40,4096]{1,0:T(8,128)(2,1)S(1)}, u32[]{:S(2)}, u32[]{:S(2)}) collective-permute-start(bf16[40,4096]{1,0:T(8,128)(2,1)S(1)} %get-tuple-element.135), channel_id=1, source_target_pairs={{0,2},{1,3},{2,0},{3,1},{4,6},{5,7},{6,4},{7,5},{8,10},{9,11},{10,... | collective-permute-start | bytes 983048 | tf_op jit(solution)/shard_map/ppermute | solution.py:290
  30.6 0.8 %shard_map.95 = (f32[40,128]{1,0:T(8,128)S(1)}, bf16[40,128]{1,0:T(8,128)(2,1)S(1)}, bf16[40,128]{1,0:T(8,128)(2,1)S(1)}, f32[8,128]{1,0:T(8,128)S(1)}) custom-call(bf16[128,8192]{1,0:T(8,128)(2,1)S(1)} %get-tuple-element.100.refs_0_, bf16[40,4096]{1,0:T(8,128)(2,1)S(1)} %collective-permute-done.3.refs_1_, ...), custom_call_target="tpu_custom_call" | custom-call | flops 1 | bytes 1 | tf_op jit(solution)/shard_map/pallas_call | solution.py:39
  31.9 1.2 %collective-permute-start.12 = (bf16[40,4096]{1,0:T(8,128)(2,1)S(1)}, bf16[40,4096]{1,0:T(8,128)(2,1)S(1)}, u32[]{:S(2)}, u32[]{:S(2)}) collective-permute-start(bf16[40,4096]{1,0:T(8,128)(2,1)S(1)} %get-tuple-element.148), channel_id=1, source_target_pairs={{0,8},{8,0},{16,24},{24,16},{1,9},{9,1},{17,25},{25,17},{2,10},{10... | collective-permute-start | bytes 983048 | tf_op jit(solution)/shard_map/ppermute | solution.py:290
  33.0 1.2 %collective-permute-done.7.refs_6_ = f32[80,128]{1,0:T(8,128)S(1)} collective-permute-done((f32[80,128]{1,0:T(8,128)S(1)}, f32[80,128]{1,0:T(8,128)S(1)}, u32[]{:S(2)}, u32[]{:S(2)}) %collective-permute-start.7) | collective-permute-done | bytes 40992 | tf_op jit(solution)/shard_map/ppermute | solution.py:290
  34.7 0.7 %shard_map.100 = (f32[40,4224]{1,0:T(8,128)S(1)}, f32[40,3968]{1,0:T(8,128)S(1)}, f32[40,4096]{1,0:T(8,128)S(1)}, f32[8,128]{1,0:T(8,128)S(1)}) custom-call(bf16[128,8192]{1,0:T(8,128)(2,1)S(1)} %get-tuple-element.100.refs_0_, bf16[128,8192]{1,0:T(8,128)(2,1)S(1)} %get-tuple-element.101.refs_0_.refs_1_, bf16[40,128]{1,0:T(8,128)(2,1)S(1)} %get-tuple-element.102.refs_2_, ...), custom_call_target="tpu_custom_call" | custom-call | flops 1 | bytes 1 | tf_op jit(solution)/shard_map/pallas_call | solution.py:39
  35.4 2.1 %collective-permute-done.9.refs_3_.refs_2_ = bf16[40,4096]{1,0:T(8,128)(2,1)S(1)} collective-permute-done((bf16[40,4096]{1,0:T(8,128)(2,1)S(1)}, bf16[40,4096]{1,0:T(8,128)(2,1)S(1)}, u32[]{:S(2)}, u32[]{:S(2)}) %collective-permute-start.9) | collective-permute-done | bytes 327712 | tf_op jit(solution)/shard_map/ppermute | solution.py:290
  38.2 1.2 %collective-permute-done.10.refs_2_ = f32[40,128]{1,0:T(8,128)S(1)} collective-permute-done((f32[40,128]{1,0:T(8,128)S(1)}, f32[40,128]{1,0:T(8,128)S(1)}, u32[]{:S(2)}, u32[]{:S(2)}) %collective-permute-start.10) | collective-permute-done | bytes 20512 | tf_op jit(solution)/shard_map/ppermute | solution.py:290
  40.0 1.8 %collective-permute-done.12.refs_3_.refs_2_ = bf16[40,4096]{1,0:T(8,128)(2,1)S(1)} collective-permute-done((bf16[40,4096]{1,0:T(8,128)(2,1)S(1)}, bf16[40,4096]{1,0:T(8,128)(2,1)S(1)}, u32[]{:S(2)}, u32[]{:S(2)}) %collective-permute-start.12) | collective-permute-done | bytes 327712 | tf_op jit(solution)/shard_map/ppermute | solution.py:290
  42.3 1.4 %collective-permute-start.15 = (bf16[40,4096]{1,0:T(8,128)(2,1)S(1)}, bf16[40,4096]{1,0:T(8,128)(2,1)S(1)}, u32[]{:S(2)}, u32[]{:S(2)}) collective-permute-start(bf16[40,4096]{1,0:T(8,128)(2,1)S(1)} %get-tuple-element.158), channel_id=1, source_target_pairs={{0,16},{8,24},{16,0},{24,8},{1,17},{9,25},{17,1},{25,9},{2,18},{10... | collective-permute-start | bytes 983048 | tf_op jit(solution)/shard_map/ppermute | solution.py:290
  43.6 1.4 %collective-permute-start.14 = (bf16[40,3968]{1,0:T(8,128)(2,1)S(1)}, bf16[40,3968]{1,0:T(8,128)(2,1)S(1)}, u32[]{:S(2)}, u32[]{:S(2)}) collective-permute-start(bf16[40,3968]{1,0:T(8,128)(2,1)S(1)} %get-tuple-element.156), channel_id=1, source_target_pairs={{0,8},{8,0},{16,24},{24,16},{1,9},{9,1},{17,25},{25,17},{2,10},{10... | collective-permute-start | bytes 952328 | tf_op jit(solution)/shard_map/ppermute | solution.py:290
  45.1 2.0 %collective-permute-start.16 = (bf16[40,2432]{1,0:T(8,128)(2,1)S(1)}, bf16[40,2432]{1,0:T(8,128)(2,1)S(1)}, u32[]{:S(2)}, u32[]{:S(2)}) collective-permute-start(bf16[40,2432]{1,0:T(8,128)(2,1)S(1)} %get-tuple-element.161), channel_id=1, source_target_pairs={{0,2},{1,3},{2,0},{3,1},{4,6},{5,7},{6,4},{7,5},{8,10},{9,11},{10,... | collective-permute-start | bytes 583688 | tf_op jit(solution)/shard_map/ppermute | solution.py:290
  47.0 2.0 %collective-permute-done.11.refs_2_ = bf16[40,4224]{1,0:T(8,128)(2,1)S(1)} collective-permute-done((bf16[40,4224]{1,0:T(8,128)(2,1)S(1)}, bf16[40,4224]{1,0:T(8,128)(2,1)S(1)}, u32[]{:S(2)}, u32[]{:S(2)}) %collective-permute-start.11) | collective-permute-done | bytes 337952 | tf_op jit(solution)/shard_map/ppermute | solution.py:290
  49.4 1.6 %collective-permute-start.13 = (bf16[40,4224]{1,0:T(8,128)(2,1)S(1)}, bf16[40,4224]{1,0:T(8,128)(2,1)S(1)}, u32[]{:S(2)}, u32[]{:S(2)}) collective-permute-start(bf16[40,4224]{1,0:T(8,128)(2,1)S(1)} %get-tuple-element.154), channel_id=1, source_target_pairs={{0,16},{8,24},{16,0},{24,8},{1,17},{9,25},{17,1},{25,9},{2,18},{10... | collective-permute-start | bytes 1013768 | tf_op jit(solution)/shard_map/ppermute | solution.py:290
  51.6 2.7 %collective-permute-start.19 = (bf16[128,1024]{1,0:T(8,128)(2,1)S(1)}, bf16[128,1024]{1,0:T(8,128)(2,1)S(1)}, u32[]{:S(2)}, u32[]{:S(2)}) collective-permute-start(bf16[128,1024]{1,0:T(8,128)(2,1)S(1)} %get-tuple-element.172), channel_id=1, source_target_pairs={{0,4},{1,5},{2,6},{3,7},{4,0},{5,1},{6,2},{7,3},{8,12},{9,13},{10,... | collective-permute-start | bytes 786440 | tf_op jit(solution)/shard_map/ppermute | solution.py:290
  54.7 1.6 %collective-permute-start.18 = (bf16[40,2048]{1,0:T(8,128)(2,1)S(1)}, bf16[40,2048]{1,0:T(8,128)(2,1)S(1)}, u32[]{:S(2)}, u32[]{:S(2)}) collective-permute-start(bf16[40,2048]{1,0:T(8,128)(2,1)S(1)} %get-tuple-element.170), channel_id=1, source_target_pairs={{0,16},{8,24},{16,0},{24,8},{1,17},{9,25},{17,1},{25,9},{2,18},{10... | collective-permute-start | bytes 491528 | tf_op jit(solution)/shard_map/ppermute | solution.py:290
  56.8 1.0 %shard_map.108 = (f32[20,8192]{1,0:T(8,128)}, f32[8,128]{1,0:T(8,128)S(1)}) custom-call(f32[40,4096]{1,0:T(8,128)S(1)} %get-tuple-element.157.refs_0_, bf16[40,4096]{1,0:T(8,128)(2,1)S(1)} %collective-permute-done.15.refs_3_.refs_1_, bf16[40,4096]{1,0:T(8,128)(2,1)S(1)} %collective-permute-done.12.refs_3_.refs_2_, f32[8,128]{1,0:T(8,128)S(1)} %get-tuple-element.164.refs_3_), custom_call_target="tpu_custom_call" | custom-call | flops 1 | bytes 1 | tf_op jit(solution)/shard_map/pallas_call | solution.py:39
  57.8 1.3 %collective-permute-done.13.refs_1_ = bf16[40,4224]{1,0:T(8,128)(2,1)S(1)} collective-permute-done((bf16[40,4224]{1,0:T(8,128)(2,1)S(1)}, bf16[40,4224]{1,0:T(8,128)(2,1)S(1)}, u32[]{:S(2)}, u32[]{:S(2)}) %collective-permute-start.13) | collective-permute-done | bytes 337952 | tf_op jit(solution)/shard_map/ppermute | solution.py:290
  59.3 5.0 %collective-permute-done.17.refs_3_ = bf16[40,1920]{1,0:T(8,128)(2,1)S(1)} collective-permute-done((bf16[40,1920]{1,0:T(8,128)(2,1)S(1)}, bf16[40,1920]{1,0:T(8,128)(2,1)S(1)}, u32[]{:S(2)}, u32[]{:S(2)}) %collective-permute-start.17) | collective-permute-done | bytes 153632 | tf_op jit(solution)/shard_map/ppermute | solution.py:290
  64.4 1.4 %shard_map.110 = (f32[20,8192]{1,0:T(8,128)}, f32[20,8192]{1,0:T(8,128)}, bf16[128,1024]{1,0:T(8,128)(2,1)}, f32[8,128]{1,0:T(8,128)}) custom-call(f32[20,4224]{1,0:T(8,128)S(1)} %get-tuple-element.166.refs_0_, f32[20,4224]{1,0:T(8,128)S(1)} %get-tuple-element.167.refs_1_, f32[40,3968]{1,0:T(8,128)S(1)} %get-tuple-element.168.refs_2_, ...), custom_call_target="tpu_custom_call" | custom-call | flops 1 | bytes 1 | tf_op jit(solution)/shard_map/pallas_call | solution.py:39
  (35 shorter events, 6.9 us)
Async XLA Ops:
  2.2 3.1 %collective-permute-start = (bf16[20,4096]{1,0:T(8,128)(2,1)S(1)}, bf16[20,4096]{1,0:T(8,128)(2,1)S(1)}, u32[]{:S(2)}, u32[]{:S(2)}) collective-permute-start(bf16[20,4096]{1,0:T(8,128)(2,1)S(1)} %get-tuple-element.94), channel_id=1, source_target_pairs={{0,1},{1,0},{2,3},{3,2},{4,5},{5,4},{6,7},{7,6},{8,9},{9,8},{10,11... | collective-permute-start | bytes 491528 | tf_op jit(solution)/shard_map/ppermute | solution.py:290
  2.7 11.2 %collective-permute-start.2 = (bf16[40,4096]{1,0:T(8,128)(2,1)S(1)}, bf16[40,4096]{1,0:T(8,128)(2,1)S(1)}, u32[]{:S(2)}, u32[]{:S(2)}) collective-permute-start(bf16[40,4096]{1,0:T(8,128)(2,1)S(1)} %get-tuple-element.98.refs_3_.refs_1_), channel_id=1, source_target_pairs={{0,16},{8,24},{16,0},{24,8},{1,17},{9,25},{17,1},{25,9},{2,18},{10... | collective-permute-start | bytes 983048 | tf_op jit(solution)/shard_map/ppermute | solution.py:290
  5.6 10.2 %collective-permute-start.5 = (bf16[40,4096]{1,0:T(8,128)(2,1)S(1)}, bf16[40,4096]{1,0:T(8,128)(2,1)S(1)}, u32[]{:S(2)}, u32[]{:S(2)}) collective-permute-start(bf16[40,4096]{1,0:T(8,128)(2,1)S(1)} %get-tuple-element.105.refs_1_.refs_0_.refs_3_), channel_id=1, source_target_pairs={{0,8},{8,0},{16,24},{24,16},{1,9},{9,1},{17,25},{25,17},{2,10},{10... | collective-permute-start | bytes 983048 | tf_op jit(solution)/shard_map/ppermute | solution.py:290
  10.0 10.9 %collective-permute-start.1 = (bf16[40,4096]{1,0:T(8,128)(2,1)S(1)}, bf16[40,4096]{1,0:T(8,128)(2,1)S(1)}, u32[]{:S(2)}, u32[]{:S(2)}) collective-permute-start(bf16[40,4096]{1,0:T(8,128)(2,1)S(1)} %get-tuple-element.109.refs_2_.refs_1_), channel_id=1, source_target_pairs={{0,16},{8,24},{16,0},{24,8},{1,17},{9,25},{17,1},{25,9},{2,18},{10... | collective-permute-start | bytes 983048 | tf_op jit(solution)/shard_map/ppermute | solution.py:290
  13.9 10.1 %collective-permute-start.4 = (bf16[40,4096]{1,0:T(8,128)(2,1)S(1)}, bf16[40,4096]{1,0:T(8,128)(2,1)S(1)}, u32[]{:S(2)}, u32[]{:S(2)}) collective-permute-start(bf16[40,4096]{1,0:T(8,128)(2,1)S(1)} %get-tuple-element.113), channel_id=1, source_target_pairs={{0,8},{8,0},{16,24},{24,16},{1,9},{9,1},{17,25},{25,17},{2,10},{10... | collective-permute-start | bytes 983048 | tf_op jit(solution)/shard_map/ppermute | solution.py:290
  15.9 12.5 %collective-permute-start.6 = (bf16[40,4096]{1,0:T(8,128)(2,1)S(1)}, bf16[40,4096]{1,0:T(8,128)(2,1)S(1)}, u32[]{:S(2)}, u32[]{:S(2)}) collective-permute-start(bf16[40,4096]{1,0:T(8,128)(2,1)S(1)} %collective-permute-done.5.refs_0_), channel_id=1, source_target_pairs={{0,16},{16,0},{1,17},{17,1},{2,18},{18,2},{3,19},{19,3},{4,20},{20... | collective-permute-start | bytes 983048 | tf_op jit(solution)/shard_map/ppermute | solution.py:346
  20.9 9.7 %collective-permute-start.3 = (bf16[40,4096]{1,0:T(8,128)(2,1)S(1)}, bf16[40,4096]{1,0:T(8,128)(2,1)S(1)}, u32[]{:S(2)}, u32[]{:S(2)}) collective-permute-start(bf16[40,4096]{1,0:T(8,128)(2,1)S(1)} %get-tuple-element.112), channel_id=1, source_target_pairs={{0,8},{8,0},{16,24},{24,16},{1,9},{9,1},{17,25},{25,17},{2,10},{10... | collective-permute-start | bytes 983048 | tf_op jit(solution)/shard_map/ppermute | solution.py:290
  22.4 13.0 %collective-permute-start.8 = (bf16[40,4096]{1,0:T(8,128)(2,1)S(1)}, bf16[40,4096]{1,0:T(8,128)(2,1)S(1)}, u32[]{:S(2)}, u32[]{:S(2)}) collective-permute-start(bf16[40,4096]{1,0:T(8,128)(2,1)S(1)} %get-tuple-element.105.refs_1_.refs_0_.refs_3_), channel_id=1, source_target_pairs={{0,16},{8,24},{16,0},{24,8},{1,17},{9,25},{17,1},{25,9},{2,18},{10... | collective-permute-start | bytes 983048 | tf_op jit(solution)/shard_map/ppermute | solution.py:290
  29.0 8.6 %collective-permute-start.9 = (bf16[40,4096]{1,0:T(8,128)(2,1)S(1)}, bf16[40,4096]{1,0:T(8,128)(2,1)S(1)}, u32[]{:S(2)}, u32[]{:S(2)}) collective-permute-start(bf16[40,4096]{1,0:T(8,128)(2,1)S(1)} %get-tuple-element.135), channel_id=1, source_target_pairs={{0,2},{1,3},{2,0},{3,1},{4,6},{5,7},{6,4},{7,5},{8,10},{9,11},{10,... | collective-permute-start | bytes 983048 | tf_op jit(solution)/shard_map/ppermute | solution.py:290
  31.9 10.0 %collective-permute-start.12 = (bf16[40,4096]{1,0:T(8,128)(2,1)S(1)}, bf16[40,4096]{1,0:T(8,128)(2,1)S(1)}, u32[]{:S(2)}, u32[]{:S(2)}) collective-permute-start(bf16[40,4096]{1,0:T(8,128)(2,1)S(1)} %get-tuple-element.148), channel_id=1, source_target_pairs={{0,8},{8,0},{16,24},{24,16},{1,9},{9,1},{17,25},{25,17},{2,10},{10... | collective-permute-start | bytes 983048 | tf_op jit(solution)/shard_map/ppermute | solution.py:290
  33.0 1.2 %collective-permute-start.7 = (f32[80,128]{1,0:T(8,128)S(1)}, f32[80,128]{1,0:T(8,128)S(1)}, u32[]{:S(2)}, u32[]{:S(2)}) collective-permute-start(f32[80,128]{1,0:T(8,128)S(1)} %get-tuple-element.125), channel_id=1, source_target_pairs={{0,1},{1,0},{2,3},{3,2},{4,5},{5,4},{6,7},{7,6},{8,9},{9,8},{10,11... | collective-permute-start | bytes 122888 | tf_op jit(solution)/shard_map/ppermute | solution.py:290
  38.0 11.1 %collective-permute-start.11 = (bf16[40,4224]{1,0:T(8,128)(2,1)S(1)}, bf16[40,4224]{1,0:T(8,128)(2,1)S(1)}, u32[]{:S(2)}, u32[]{:S(2)}) collective-permute-start(bf16[40,4224]{1,0:T(8,128)(2,1)S(1)} %get-tuple-element.146), channel_id=1, source_target_pairs={{0,8},{8,0},{16,24},{24,16},{1,9},{9,1},{17,25},{25,17},{2,10},{10... | collective-permute-start | bytes 1013768 | tf_op jit(solution)/shard_map/ppermute | solution.py:290
  38.1 1.3 %collective-permute-start.10 = (f32[40,128]{1,0:T(8,128)S(1)}, f32[40,128]{1,0:T(8,128)S(1)}, u32[]{:S(2)}, u32[]{:S(2)}) collective-permute-start(f32[40,128]{1,0:T(8,128)S(1)} %get-tuple-element.138), channel_id=1, source_target_pairs={{0,1},{1,0},{2,3},{3,2},{4,5},{5,4},{6,7},{7,6},{8,9},{9,8},{10,11... | collective-permute-start | bytes 61448 | tf_op jit(solution)/shard_map/ppermute | solution.py:290
  42.3 12.1 %collective-permute-start.15 = (bf16[40,4096]{1,0:T(8,128)(2,1)S(1)}, bf16[40,4096]{1,0:T(8,128)(2,1)S(1)}, u32[]{:S(2)}, u32[]{:S(2)}) collective-permute-start(bf16[40,4096]{1,0:T(8,128)(2,1)S(1)} %get-tuple-element.158), channel_id=1, source_target_pairs={{0,16},{8,24},{16,0},{24,8},{1,17},{9,25},{17,1},{25,9},{2,18},{10... | collective-permute-start | bytes 983048 | tf_op jit(solution)/shard_map/ppermute | solution.py:290
  43.6 10.7 %collective-permute-start.14 = (bf16[40,3968]{1,0:T(8,128)(2,1)S(1)}, bf16[40,3968]{1,0:T(8,128)(2,1)S(1)}, u32[]{:S(2)}, u32[]{:S(2)}) collective-permute-start(bf16[40,3968]{1,0:T(8,128)(2,1)S(1)} %get-tuple-element.156), channel_id=1, source_target_pairs={{0,8},{8,0},{16,24},{24,16},{1,9},{9,1},{17,25},{25,17},{2,10},{10... | collective-permute-start | bytes 952328 | tf_op jit(solution)/shard_map/ppermute | solution.py:290
  45.1 5.9 %collective-permute-start.16 = (bf16[40,2432]{1,0:T(8,128)(2,1)S(1)}, bf16[40,2432]{1,0:T(8,128)(2,1)S(1)}, u32[]{:S(2)}, u32[]{:S(2)}) collective-permute-start(bf16[40,2432]{1,0:T(8,128)(2,1)S(1)} %get-tuple-element.161), channel_id=1, source_target_pairs={{0,2},{1,3},{2,0},{3,1},{4,6},{5,7},{6,4},{7,5},{8,10},{9,11},{10,... | collective-permute-start | bytes 583688 | tf_op jit(solution)/shard_map/ppermute | solution.py:290
  49.4 9.7 %collective-permute-start.13 = (bf16[40,4224]{1,0:T(8,128)(2,1)S(1)}, bf16[40,4224]{1,0:T(8,128)(2,1)S(1)}, u32[]{:S(2)}, u32[]{:S(2)}) collective-permute-start(bf16[40,4224]{1,0:T(8,128)(2,1)S(1)} %get-tuple-element.154), channel_id=1, source_target_pairs={{0,16},{8,24},{16,0},{24,8},{1,17},{9,25},{17,1},{25,9},{2,18},{10... | collective-permute-start | bytes 1013768 | tf_op jit(solution)/shard_map/ppermute | solution.py:290
  51.6 12.8 %collective-permute-start.19 = (bf16[128,1024]{1,0:T(8,128)(2,1)S(1)}, bf16[128,1024]{1,0:T(8,128)(2,1)S(1)}, u32[]{:S(2)}, u32[]{:S(2)}) collective-permute-start(bf16[128,1024]{1,0:T(8,128)(2,1)S(1)} %get-tuple-element.172), channel_id=1, source_target_pairs={{0,4},{1,5},{2,6},{3,7},{4,0},{5,1},{6,2},{7,3},{8,12},{9,13},{10,... | collective-permute-start | bytes 786440 | tf_op jit(solution)/shard_map/ppermute | solution.py:290
  54.7 9.7 %collective-permute-start.18 = (bf16[40,2048]{1,0:T(8,128)(2,1)S(1)}, bf16[40,2048]{1,0:T(8,128)(2,1)S(1)}, u32[]{:S(2)}, u32[]{:S(2)}) collective-permute-start(bf16[40,2048]{1,0:T(8,128)(2,1)S(1)} %get-tuple-element.170), channel_id=1, source_target_pairs={{0,16},{8,24},{16,0},{24,8},{1,17},{9,25},{17,1},{25,9},{2,18},{10... | collective-permute-start | bytes 491528 | tf_op jit(solution)/shard_map/ppermute | solution.py:290
  56.2 8.1 %collective-permute-start.17 = (bf16[40,1920]{1,0:T(8,128)(2,1)S(1)}, bf16[40,1920]{1,0:T(8,128)(2,1)S(1)}, u32[]{:S(2)}, u32[]{:S(2)}) collective-permute-start(bf16[40,1920]{1,0:T(8,128)(2,1)S(1)} %get-tuple-element.169), channel_id=1, source_target_pairs={{0,16},{8,24},{16,0},{24,8},{1,17},{9,25},{17,1},{25,9},{2,18},{10... | collective-permute-start | bytes 460808 | tf_op jit(solution)/shard_map/ppermute | solution.py:290

commit v14 on v13

--- a/solution.py
+++ b/solution.py
@@ -416,24 +416,19 @@
         [((tokens, wide // 8), F32)] * 2,
         [wide_own, wide_second, wide_first, own[2], second[2], first[2]],
     )
-    def back_down(gr, a, b, side, out):
-        odd = is_odd()
-        for at in range(0, half, TILE):
-            value = down_columns(gr, a, b, at, half) + kept(side[:, at : at + TILE], odd, four, True)
-            out[:, at : at + TILE] = value.astype(BF)
-
-    def back_pair(offset):
-        def body(xr, pair, side, out):
-            odd = is_odd()
+    first_low, first_high, first_down = step(own_grads, grads_f32, [x, g, *hid_first, pair_first])
+
+    def added(own_ref, side, *outs):
+        odd, at = is_odd(), 0
+        for out in outs:
             for cut in tiles(out.shape[1]):
-                value = dot(pair[...], xr[:, shifted(cut, offset)], NN)
-                out[:, cut] = (value + kept(side[:, cut], odd, four, True)).astype(BF)
-
-        return body
-
-    back_of_down = backward(step(back_down, piece, [g, *hid_first, side_down]))
+                from_ = shifted(cut, at)
+                out[:, cut] = (own_ref[:, from_] + kept(side[:, from_], odd, four, True)).astype(BF)
+            at += out.shape[1]
+
+    back_of_down = backward(step(added, piece, [first_down, side_down]))
     side_high = outward(step.hold(high))
-    back_of_low = backward(step(back_pair(0), (low_shape, BF), [x, pair_first, side_low]))
+    back_of_low = backward(step(added, (low_shape, BF), [first_low, side_low]))
     send, keep = step(
         with_width(output_sums),
         [((tokens, wide // 8), BF), ((tokens, wide // 8), F32)],
@@ -454,18 +449,10 @@
     cut_at = high_columns // 256 * 128
     high_shapes = [(both_rows, cut_at), (both_rows, high_columns - cut_at)]
 
-    def back_last(xr, pair, side, out_a, out_b):
-        odd = is_odd()
-        for out, offset in ((out_a, 0), (out_b, cut_at)):
-            for cut in tiles(out.shape[1]):
-                value = dot(pair[...], xr[:, shifted(cut, low_columns + offset)], NN)
-                value += kept(side[:, shifted(cut, offset)], odd, four, True)
-                out[:, cut] = value.astype(BF)
-
     backs_of_high = [
         backward(value)
         for value in step(
-            back_last, [(shape, BF) for shape in high_shapes], [x, pair_first, side_high], also=[back_of_down]
+            added, [(shape, BF) for shape in high_shapes], [first_high, side_high], also=[back_of_down]
         )
     ]
     bit = 2 * BITS[0]

time: 65.9 us -> 66.4 us (level)
    pallas_call x27 -> x28, Pallas kernels: 14.3 us -> 14.3 us  [__call__(): pl.pallas_call(kernel, out_shape=[jax.ShapeDtypeStruct(*s) for s in shape...]
  transfers between devices with their start and end apart: 20 -> 20, of which waited for: 11 -> 13; matrix products, arithmetic and copies ran while one was open for 0% -> 0% of each run, Pallas kernels for 17% -> 17%
where the time goes in v14:
time: 66.4 us; the launch traced here: 66.2 us
  starting transfers between devices  28.6 us (43%)
  waiting for transfers between devices  22.4 us (34%)
  Pallas kernels  14.3 us (22%)
  between operations  0.84 us (1%)
    ppermute x19, starting transfers between devices, exchanged(): lax.ppermute(value, axis, [(source, source ^ bit) for source in range(cou...  25.2 us
    ppermute x19, waiting for transfers between devices, exchanged(): lax.ppermute(value, axis, [(source, source ^ bit) for source in range(cou...  18.8 us
    pallas_call x28, Pallas kernels, __call__(): pl.pallas_call(kernel, out_shape=[jax.ShapeDtypeStruct(*s) for s in shape...  14.3 us
    ppermute x1, waiting for transfers between devices, on_device(): lax.ppermute(crossed, 'section', [(source, source ^ 2) for source in (0,...  3.6 us
    ppermute x1, starting transfers between devices, on_device(): lax.ppermute(crossed, 'section', [(source, source ^ 2) for source in (0,...  3.41 us
  transfers between devices with their start and end apart: 20, of which 13 were waited for; matrix products, arithmetic and copies ran while one was open for 0% of the time, Pallas kernels for 17%

profile of v14, /device:TPU:0, one launch (start us, length us, event | category | flops | bytes accessed | tf_op | source)
XLA Modules:
  0.0 66.2 jit_solution(12812529787103972892)
XLA Ops:
  0.6 1.5 %shard_map.84 = (bf16[40,4096]{1,0:T(8,128)(2,1)S(1)}, bf16[20,4096]{1,0:T(8,128)(2,1)S(1)}, bf16[20,4096]{1,0:T(8,128)(2,1)S(1)}, bf16[20,8192]{1,0:T(8,128)(2,...) custom-call(bf16[20,8192]{1,0:T(8,128)(2,1)} %refs_0_.2, bf16[20,8192]{1,0:T(8,128)(2,1)} %refs_1_.2, ...), custom_call_target="tpu_custom_call" | custom-call | flops 1 | bytes 1 | tf_op jit(solution)/shard_map/pallas_call | solution.py:39
  2.7 2.6 %collective-permute-start.2 = (bf16[40,4096]{1,0:T(8,128)(2,1)S(1)}, bf16[40,4096]{1,0:T(8,128)(2,1)S(1)}, u32[]{:S(2)}, u32[]{:S(2)}) collective-permute-start(bf16[40,4096]{1,0:T(8,128)(2,1)S(1)} %get-tuple-element.102.refs_3_.refs_1_), channel_id=1, source_target_pairs={{0,16},{8,24},{16,0},{24,8},{1,17},{9,25},{17,1},{25,9},{2,18},{10... | collective-permute-start | bytes 983048 | tf_op jit(solution)/shard_map/ppermute | solution.py:290
  5.6 1.6 %collective-permute-start.5 = (bf16[40,4096]{1,0:T(8,128)(2,1)S(1)}, bf16[40,4096]{1,0:T(8,128)(2,1)S(1)}, u32[]{:S(2)}, u32[]{:S(2)}) collective-permute-start(bf16[40,4096]{1,0:T(8,128)(2,1)S(1)} %get-tuple-element.109.refs_1_.refs_0_.refs_3_), channel_id=1, source_target_pairs={{0,8},{8,0},{16,24},{24,16},{1,9},{9,1},{17,25},{25,17},{2,10},{10... | collective-permute-start | bytes 983048 | tf_op jit(solution)/shard_map/ppermute | solution.py:290
  7.5 2.5 %shard_map.87 = (bf16[128,8192]{1,0:T(8,128)(2,1)S(1)}, bf16[128,8192]{1,0:T(8,128)(2,1)S(1)}, f32[40,128]{1,0:T(8,128)S(1)}, bf16[40,128]{1,0:T(8,128)(2,1)S(1)...) custom-call(bf16[128,8192]{1,0:T(8,128)(2,1)} %refs_0_.3, bf16[128,8192]{1,0:T(8,128)(2,1)} %refs_1_.3, ...), custom_call_target="tpu_custom_call" | custom-call | flops 1 | bytes 1 | tf_op jit(solution)/shard_map/pallas_call | solution.py:39
  10.0 1.4 %collective-permute-start.1 = (bf16[40,4096]{1,0:T(8,128)(2,1)S(1)}, bf16[40,4096]{1,0:T(8,128)(2,1)S(1)}, u32[]{:S(2)}, u32[]{:S(2)}) collective-permute-start(bf16[40,4096]{1,0:T(8,128)(2,1)S(1)} %get-tuple-element.113.refs_2_.refs_1_), channel_id=1, source_target_pairs={{0,16},{8,24},{16,0},{24,8},{1,17},{9,25},{17,1},{25,9},{2,18},{10... | collective-permute-start | bytes 983048 | tf_op jit(solution)/shard_map/ppermute | solution.py:290
  11.9 2.0 %collective-permute-done.2.refs_0_.refs_2_ = bf16[40,4096]{1,0:T(8,128)(2,1)S(1)} collective-permute-done((bf16[40,4096]{1,0:T(8,128)(2,1)S(1)}, bf16[40,4096]{1,0:T(8,128)(2,1)S(1)}, u32[]{:S(2)}, u32[]{:S(2)}) %collective-permute-start.2) | collective-permute-done | bytes 327712 | tf_op jit(solution)/shard_map/ppermute | solution.py:290
  13.9 2.0 %collective-permute-start.4 = (bf16[40,4096]{1,0:T(8,128)(2,1)S(1)}, bf16[40,4096]{1,0:T(8,128)(2,1)S(1)}, u32[]{:S(2)}, u32[]{:S(2)}) collective-permute-start(bf16[40,4096]{1,0:T(8,128)(2,1)S(1)} %get-tuple-element.117), channel_id=1, source_target_pairs={{0,8},{8,0},{16,24},{24,16},{1,9},{9,1},{17,25},{25,17},{2,10},{10... | collective-permute-start | bytes 983048 | tf_op jit(solution)/shard_map/ppermute | solution.py:290
  15.9 3.4 %collective-permute-start.6 = (bf16[40,4096]{1,0:T(8,128)(2,1)S(1)}, bf16[40,4096]{1,0:T(8,128)(2,1)S(1)}, u32[]{:S(2)}, u32[]{:S(2)}) collective-permute-start(bf16[40,4096]{1,0:T(8,128)(2,1)S(1)} %collective-permute-done.5.refs_0_), channel_id=1, source_target_pairs={{0,16},{16,0},{1,17},{17,1},{2,18},{18,2},{3,19},{19,3},{4,20},{20... | collective-permute-start | bytes 983048 | tf_op jit(solution)/shard_map/ppermute | solution.py:346
  19.3 1.6 %collective-permute-done.1.refs_0_.refs_1_ = bf16[40,4096]{1,0:T(8,128)(2,1)S(1)} collective-permute-done((bf16[40,4096]{1,0:T(8,128)(2,1)S(1)}, bf16[40,4096]{1,0:T(8,128)(2,1)S(1)}, u32[]{:S(2)}, u32[]{:S(2)}) %collective-permute-start.1) | collective-permute-done | bytes 327712 | tf_op jit(solution)/shard_map/ppermute | solution.py:290
  20.9 1.5 %collective-permute-start.3 = (bf16[40,4096]{1,0:T(8,128)(2,1)S(1)}, bf16[40,4096]{1,0:T(8,128)(2,1)S(1)}, u32[]{:S(2)}, u32[]{:S(2)}) collective-permute-start(bf16[40,4096]{1,0:T(8,128)(2,1)S(1)} %get-tuple-element.116), channel_id=1, source_target_pairs={{0,8},{8,0},{16,24},{24,16},{1,9},{9,1},{17,25},{25,17},{2,10},{10... | collective-permute-start | bytes 983048 | tf_op jit(solution)/shard_map/ppermute | solution.py:290
  22.4 1.5 %collective-permute-start.8 = (bf16[40,4096]{1,0:T(8,128)(2,1)S(1)}, bf16[40,4096]{1,0:T(8,128)(2,1)S(1)}, u32[]{:S(2)}, u32[]{:S(2)}) collective-permute-start(bf16[40,4096]{1,0:T(8,128)(2,1)S(1)} %get-tuple-element.109.refs_1_.refs_0_.refs_3_), channel_id=1, source_target_pairs={{0,16},{8,24},{16,0},{24,8},{1,17},{9,25},{17,1},{25,9},{2,18},{10... | collective-permute-start | bytes 983048 | tf_op jit(solution)/shard_map/ppermute | solution.py:290
  23.9 0.8 %shard_map.91 = (f32[40,128]{1,0:T(8,128)S(1)}, bf16[40,128]{1,0:T(8,128)(2,1)S(1)}, bf16[40,128]{1,0:T(8,128)(2,1)S(1)}, f32[8,128]{1,0:T(8,128)S(1)}) custom-call(bf16[128,8192]{1,0:T(8,128)(2,1)S(1)} %get-tuple-element.104.refs_0_, bf16[40,4096]{1,0:T(8,128)(2,1)S(1)} %collective-permute-done.1.refs_0_.refs_1_, ...), custom_call_target="tpu_custom_call" | custom-call | flops 1 | bytes 1 | tf_op jit(solution)/shard_map/pallas_call | solution.py:39
  24.8 3.6 %collective-permute-done.6.refs_1_ = bf16[40,4096]{1,0:T(8,128)(2,1)S(1)} collective-permute-done((bf16[40,4096]{1,0:T(8,128)(2,1)S(1)}, bf16[40,4096]{1,0:T(8,128)(2,1)S(1)}, u32[]{:S(2)}, u32[]{:S(2)}) %collective-permute-start.6) | collective-permute-done | bytes 327712 | tf_op jit(solution)/shard_map/ppermute | solution.py:346
  29.0 1.6 %collective-permute-start.9 = (bf16[40,4096]{1,0:T(8,128)(2,1)S(1)}, bf16[40,4096]{1,0:T(8,128)(2,1)S(1)}, u32[]{:S(2)}, u32[]{:S(2)}) collective-permute-start(bf16[40,4096]{1,0:T(8,128)(2,1)S(1)} %get-tuple-element.140), channel_id=1, source_target_pairs={{0,2},{1,3},{2,0},{3,1},{4,6},{5,7},{6,4},{7,5},{8,10},{9,11},{10,... | collective-permute-start | bytes 983048 | tf_op jit(solution)/shard_map/ppermute | solution.py:290
  30.6 0.8 %shard_map.95 = (f32[40,128]{1,0:T(8,128)S(1)}, bf16[40,128]{1,0:T(8,128)(2,1)S(1)}, bf16[40,128]{1,0:T(8,128)(2,1)S(1)}, f32[8,128]{1,0:T(8,128)S(1)}) custom-call(bf16[128,8192]{1,0:T(8,128)(2,1)S(1)} %get-tuple-element.104.refs_0_, bf16[40,4096]{1,0:T(8,128)(2,1)S(1)} %collective-permute-done.3.refs_1_, ...), custom_call_target="tpu_custom_call" | custom-call | flops 1 | bytes 1 | tf_op jit(solution)/shard_map/pallas_call | solution.py:39
  31.9 1.2 %collective-permute-start.12 = (bf16[40,4096]{1,0:T(8,128)(2,1)S(1)}, bf16[40,4096]{1,0:T(8,128)(2,1)S(1)}, u32[]{:S(2)}, u32[]{:S(2)}) collective-permute-start(bf16[40,4096]{1,0:T(8,128)(2,1)S(1)} %get-tuple-element.157), channel_id=1, source_target_pairs={{0,8},{8,0},{16,24},{24,16},{1,9},{9,1},{17,25},{25,17},{2,10},{10... | collective-permute-start | bytes 983048 | tf_op jit(solution)/shard_map/ppermute | solution.py:290
  33.0 1.2 %collective-permute-done.7.refs_6_ = f32[80,128]{1,0:T(8,128)S(1)} collective-permute-done((f32[80,128]{1,0:T(8,128)S(1)}, f32[80,128]{1,0:T(8,128)S(1)}, u32[]{:S(2)}, u32[]{:S(2)}) %collective-permute-start.7) | collective-permute-done | bytes 40992 | tf_op jit(solution)/shard_map/ppermute | solution.py:290
  34.7 0.7 %shard_map.100 = (f32[40,4224]{1,0:T(8,128)S(1)}, f32[40,3968]{1,0:T(8,128)S(1)}, f32[40,4096]{1,0:T(8,128)S(1)}, f32[8,128]{1,0:T(8,128)S(1)}) custom-call(bf16[128,8192]{1,0:T(8,128)(2,1)S(1)} %get-tuple-element.104.refs_0_, bf16[128,8192]{1,0:T(8,128)(2,1)S(1)} %get-tuple-element.105.refs_0_.refs_1_, bf16[40,128]{1,0:T(8,128)(2,1)S(1)} %get-tuple-element.106.refs_2_, ...), custom_call_target="tpu_custom_call" | custom-call | flops 1 | bytes 1 | tf_op jit(solution)/shard_map/pallas_call | solution.py:39
  35.4 2.1 %collective-permute-done.9.refs_3_.refs_2_ = bf16[40,4096]{1,0:T(8,128)(2,1)S(1)} collective-permute-done((bf16[40,4096]{1,0:T(8,128)(2,1)S(1)}, bf16[40,4096]{1,0:T(8,128)(2,1)S(1)}, u32[]{:S(2)}, u32[]{:S(2)}) %collective-permute-start.9) | collective-permute-done | bytes 327712 | tf_op jit(solution)/shard_map/ppermute | solution.py:290
  38.2 1.2 %collective-permute-done.10.refs_2_ = f32[40,128]{1,0:T(8,128)S(1)} collective-permute-done((f32[40,128]{1,0:T(8,128)S(1)}, f32[40,128]{1,0:T(8,128)S(1)}, u32[]{:S(2)}, u32[]{:S(2)}) %collective-permute-start.10) | collective-permute-done | bytes 20512 | tf_op jit(solution)/shard_map/ppermute | solution.py:290
  40.7 1.1 %collective-permute-done.12.refs_1_.refs_2_ = bf16[40,4096]{1,0:T(8,128)(2,1)S(1)} collective-permute-done((bf16[40,4096]{1,0:T(8,128)(2,1)S(1)}, bf16[40,4096]{1,0:T(8,128)(2,1)S(1)}, u32[]{:S(2)}, u32[]{:S(2)}) %collective-permute-start.12) | collective-permute-done | bytes 327712 | tf_op jit(solution)/shard_map/ppermute | solution.py:290
  41.9 1.4 %collective-permute-start.15 = (bf16[40,4096]{1,0:T(8,128)(2,1)S(1)}, bf16[40,4096]{1,0:T(8,128)(2,1)S(1)}, u32[]{:S(2)}, u32[]{:S(2)}) collective-permute-start(bf16[40,4096]{1,0:T(8,128)(2,1)S(1)} %get-tuple-element.165), channel_id=1, source_target_pairs={{0,16},{8,24},{16,0},{24,8},{1,17},{9,25},{17,1},{25,9},{2,18},{10... | collective-permute-start | bytes 983048 | tf_op jit(solution)/shard_map/ppermute | solution.py:290
  43.3 1.4 %collective-permute-start.14 = (bf16[40,3968]{1,0:T(8,128)(2,1)S(1)}, bf16[40,3968]{1,0:T(8,128)(2,1)S(1)}, u32[]{:S(2)}, u32[]{:S(2)}) collective-permute-start(bf16[40,3968]{1,0:T(8,128)(2,1)S(1)} %get-tuple-element.163), channel_id=1, source_target_pairs={{0,8},{8,0},{16,24},{24,16},{1,9},{9,1},{17,25},{25,17},{2,10},{10... | collective-permute-start | bytes 952328 | tf_op jit(solution)/shard_map/ppermute | solution.py:290
  44.7 2.0 %collective-permute-start.16 = (bf16[40,2432]{1,0:T(8,128)(2,1)S(1)}, bf16[40,2432]{1,0:T(8,128)(2,1)S(1)}, u32[]{:S(2)}, u32[]{:S(2)}) collective-permute-start(bf16[40,2432]{1,0:T(8,128)(2,1)S(1)} %get-tuple-element.169), channel_id=1, source_target_pairs={{0,2},{1,3},{2,0},{3,1},{4,6},{5,7},{6,4},{7,5},{8,10},{9,11},{10,... | collective-permute-start | bytes 583688 | tf_op jit(solution)/shard_map/ppermute | solution.py:290
  46.7 2.4 %collective-permute-done.11.refs_1_.refs_2_ = bf16[40,4224]{1,0:T(8,128)(2,1)S(1)} collective-permute-done((bf16[40,4224]{1,0:T(8,128)(2,1)S(1)}, bf16[40,4224]{1,0:T(8,128)(2,1)S(1)}, u32[]{:S(2)}, u32[]{:S(2)}) %collective-permute-start.11) | collective-permute-done | bytes 337952 | tf_op jit(solution)/shard_map/ppermute | solution.py:290
  49.2 1.6 %collective-permute-start.13 = (bf16[40,4224]{1,0:T(8,128)(2,1)S(1)}, bf16[40,4224]{1,0:T(8,128)(2,1)S(1)}, u32[]{:S(2)}, u32[]{:S(2)}) collective-permute-start(bf16[40,4224]{1,0:T(8,128)(2,1)S(1)} %get-tuple-element.161), channel_id=1, source_target_pairs={{0,16},{8,24},{16,0},{24,8},{1,17},{9,25},{17,1},{25,9},{2,18},{10... | collective-permute-start | bytes 1013768 | tf_op jit(solution)/shard_map/ppermute | solution.py:290
  51.5 2.6 %collective-permute-start.19 = (bf16[128,1024]{1,0:T(8,128)(2,1)S(1)}, bf16[128,1024]{1,0:T(8,128)(2,1)S(1)}, u32[]{:S(2)}, u32[]{:S(2)}) collective-permute-start(bf16[128,1024]{1,0:T(8,128)(2,1)S(1)} %get-tuple-element.180), channel_id=1, source_target_pairs={{0,4},{1,5},{2,6},{3,7},{4,0},{5,1},{6,2},{7,3},{8,12},{9,13},{10,... | collective-permute-start | bytes 786440 | tf_op jit(solution)/shard_map/ppermute | solution.py:290
  54.5 1.6 %collective-permute-start.18 = (bf16[40,2048]{1,0:T(8,128)(2,1)S(1)}, bf16[40,2048]{1,0:T(8,128)(2,1)S(1)}, u32[]{:S(2)}, u32[]{:S(2)}) collective-permute-start(bf16[40,2048]{1,0:T(8,128)(2,1)S(1)} %get-tuple-element.178), channel_id=1, source_target_pairs={{0,16},{8,24},{16,0},{24,8},{1,17},{9,25},{17,1},{25,9},{2,18},{10... | collective-permute-start | bytes 491528 | tf_op jit(solution)/shard_map/ppermute | solution.py:290
  56.6 1.0 %shard_map.109 = (f32[20,8192]{1,0:T(8,128)}, f32[8,128]{1,0:T(8,128)S(1)}) custom-call(f32[40,4096]{1,0:T(8,128)S(1)} %get-tuple-element.164.refs_0_, bf16[40,4096]{1,0:T(8,128)(2,1)S(1)} %collective-permute-done.15.refs_2_.refs_1_, bf16[40,4096]{1,0:T(8,128)(2,1)S(1)} %collective-permute-done.12.refs_1_.refs_2_, f32[8,128]{1,0:T(8,128)S(1)} %get-tuple-element.172.refs_3_), custom_call_target="tpu_custom_call" | custom-call | flops 1 | bytes 1 | tf_op jit(solution)/shard_map/pallas_call | solution.py:39
  57.6 2.5 %collective-permute-done.13.refs_1_ = bf16[40,4224]{1,0:T(8,128)(2,1)S(1)} collective-permute-done((bf16[40,4224]{1,0:T(8,128)(2,1)S(1)}, bf16[40,4224]{1,0:T(8,128)(2,1)S(1)}, u32[]{:S(2)}, u32[]{:S(2)}) %collective-permute-start.13) | collective-permute-done | bytes 337952 | tf_op jit(solution)/shard_map/ppermute | solution.py:290
  60.3 4.4 %collective-permute-done.17.refs_3_ = bf16[40,1920]{1,0:T(8,128)(2,1)S(1)} collective-permute-done((bf16[40,1920]{1,0:T(8,128)(2,1)S(1)}, bf16[40,1920]{1,0:T(8,128)(2,1)S(1)}, u32[]{:S(2)}, u32[]{:S(2)}) %collective-permute-start.17) | collective-permute-done | bytes 153632 | tf_op jit(solution)/shard_map/ppermute | solution.py:290
  64.8 1.4 %shard_map.111 = (f32[20,8192]{1,0:T(8,128)}, f32[20,8192]{1,0:T(8,128)}, bf16[128,1024]{1,0:T(8,128)(2,1)}, f32[8,128]{1,0:T(8,128)}) custom-call(f32[20,4224]{1,0:T(8,128)S(1)} %get-tuple-element.174.refs_0_, f32[20,4224]{1,0:T(8,128)S(1)} %get-tuple-element.175.refs_1_, f32[40,3968]{1,0:T(8,128)S(1)} %get-tuple-element.176.refs_2_, ...), custom_call_target="tpu_custom_call" | custom-call | flops 1 | bytes 1 | tf_op jit(solution)/shard_map/pallas_call | solution.py:39
  (36 shorter events, 7.1 us)
Async XLA Ops:
  2.2 3.1 %collective-permute-start = (bf16[20,4096]{1,0:T(8,128)(2,1)S(1)}, bf16[20,4096]{1,0:T(8,128)(2,1)S(1)}, u32[]{:S(2)}, u32[]{:S(2)}) collective-permute-start(bf16[20,4096]{1,0:T(8,128)(2,1)S(1)} %get-tuple-element.98), channel_id=1, source_target_pairs={{0,1},{1,0},{2,3},{3,2},{4,5},{5,4},{6,7},{7,6},{8,9},{9,8},{10,11... | collective-permute-start | bytes 491528 | tf_op jit(solution)/shard_map/ppermute | solution.py:290
  2.7 11.2 %collective-permute-start.2 = (bf16[40,4096]{1,0:T(8,128)(2,1)S(1)}, bf16[40,4096]{1,0:T(8,128)(2,1)S(1)}, u32[]{:S(2)}, u32[]{:S(2)}) collective-permute-start(bf16[40,4096]{1,0:T(8,128)(2,1)S(1)} %get-tuple-element.102.refs_3_.refs_1_), channel_id=1, source_target_pairs={{0,16},{8,24},{16,0},{24,8},{1,17},{9,25},{17,1},{25,9},{2,18},{10... | collective-permute-start | bytes 983048 | tf_op jit(solution)/shard_map/ppermute | solution.py:290
  5.6 10.2 %collective-permute-start.5 = (bf16[40,4096]{1,0:T(8,128)(2,1)S(1)}, bf16[40,4096]{1,0:T(8,128)(2,1)S(1)}, u32[]{:S(2)}, u32[]{:S(2)}) collective-permute-start(bf16[40,4096]{1,0:T(8,128)(2,1)S(1)} %get-tuple-element.109.refs_1_.refs_0_.refs_3_), channel_id=1, source_target_pairs={{0,8},{8,0},{16,24},{24,16},{1,9},{9,1},{17,25},{25,17},{2,10},{10... | collective-permute-start | bytes 983048 | tf_op jit(solution)/shard_map/ppermute | solution.py:290
  10.0 10.9 %collective-permute-start.1 = (bf16[40,4096]{1,0:T(8,128)(2,1)S(1)}, bf16[40,4096]{1,0:T(8,128)(2,1)S(1)}, u32[]{:S(2)}, u32[]{:S(2)}) collective-permute-start(bf16[40,4096]{1,0:T(8,128)(2,1)S(1)} %get-tuple-element.113.refs_2_.refs_1_), channel_id=1, source_target_pairs={{0,16},{8,24},{16,0},{24,8},{1,17},{9,25},{17,1},{25,9},{2,18},{10... | collective-permute-start | bytes 983048 | tf_op jit(solution)/shard_map/ppermute | solution.py:290
  13.9 10.1 %collective-permute-start.4 = (bf16[40,4096]{1,0:T(8,128)(2,1)S(1)}, bf16[40,4096]{1,0:T(8,128)(2,1)S(1)}, u32[]{:S(2)}, u32[]{:S(2)}) collective-permute-start(bf16[40,4096]{1,0:T(8,128)(2,1)S(1)} %get-tuple-element.117), channel_id=1, source_target_pairs={{0,8},{8,0},{16,24},{24,16},{1,9},{9,1},{17,25},{25,17},{2,10},{10... | collective-permute-start | bytes 983048 | tf_op jit(solution)/shard_map/ppermute | solution.py:290
  15.9 12.5 %collective-permute-start.6 = (bf16[40,4096]{1,0:T(8,128)(2,1)S(1)}, bf16[40,4096]{1,0:T(8,128)(2,1)S(1)}, u32[]{:S(2)}, u32[]{:S(2)}) collective-permute-start(bf16[40,4096]{1,0:T(8,128)(2,1)S(1)} %collective-permute-done.5.refs_0_), channel_id=1, source_target_pairs={{0,16},{16,0},{1,17},{17,1},{2,18},{18,2},{3,19},{19,3},{4,20},{20... | collective-permute-start | bytes 983048 | tf_op jit(solution)/shard_map/ppermute | solution.py:346
  20.9 9.7 %collective-permute-start.3 = (bf16[40,4096]{1,0:T(8,128)(2,1)S(1)}, bf16[40,4096]{1,0:T(8,128)(2,1)S(1)}, u32[]{:S(2)}, u32[]{:S(2)}) collective-permute-start(bf16[40,4096]{1,0:T(8,128)(2,1)S(1)} %get-tuple-element.116), channel_id=1, source_target_pairs={{0,8},{8,0},{16,24},{24,16},{1,9},{9,1},{17,25},{25,17},{2,10},{10... | collective-permute-start | bytes 983048 | tf_op jit(solution)/shard_map/ppermute | solution.py:290
  22.4 13.0 %collective-permute-start.8 = (bf16[40,4096]{1,0:T(8,128)(2,1)S(1)}, bf16[40,4096]{1,0:T(8,128)(2,1)S(1)}, u32[]{:S(2)}, u32[]{:S(2)}) collective-permute-start(bf16[40,4096]{1,0:T(8,128)(2,1)S(1)} %get-tuple-element.109.refs_1_.refs_0_.refs_3_), channel_id=1, source_target_pairs={{0,16},{8,24},{16,0},{24,8},{1,17},{9,25},{17,1},{25,9},{2,18},{10... | collective-permute-start | bytes 983048 | tf_op jit(solution)/shard_map/ppermute | solution.py:290
  29.0 8.6 %collective-permute-start.9 = (bf16[40,4096]{1,0:T(8,128)(2,1)S(1)}, bf16[40,4096]{1,0:T(8,128)(2,1)S(1)}, u32[]{:S(2)}, u32[]{:S(2)}) collective-permute-start(bf16[40,4096]{1,0:T(8,128)(2,1)S(1)} %get-tuple-element.140), channel_id=1, source_target_pairs={{0,2},{1,3},{2,0},{3,1},{4,6},{5,7},{6,4},{7,5},{8,10},{9,11},{10,... | collective-permute-start | bytes 983048 | tf_op jit(solution)/shard_map/ppermute | solution.py:290
  31.9 10.0 %collective-permute-start.12 = (bf16[40,4096]{1,0:T(8,128)(2,1)S(1)}, bf16[40,4096]{1,0:T(8,128)(2,1)S(1)}, u32[]{:S(2)}, u32[]{:S(2)}) collective-permute-start(bf16[40,4096]{1,0:T(8,128)(2,1)S(1)} %get-tuple-element.157), channel_id=1, source_target_pairs={{0,8},{8,0},{16,24},{24,16},{1,9},{9,1},{17,25},{25,17},{2,10},{10... | collective-permute-start | bytes 983048 | tf_op jit(solution)/shard_map/ppermute | solution.py:290
  33.0 1.2 %collective-permute-start.7 = (f32[80,128]{1,0:T(8,128)S(1)}, f32[80,128]{1,0:T(8,128)S(1)}, u32[]{:S(2)}, u32[]{:S(2)}) collective-permute-start(f32[80,128]{1,0:T(8,128)S(1)} %get-tuple-element.129), channel_id=1, source_target_pairs={{0,1},{1,0},{2,3},{3,2},{4,5},{5,4},{6,7},{7,6},{8,9},{9,8},{10,11... | collective-permute-start | bytes 122888 | tf_op jit(solution)/shard_map/ppermute | solution.py:290
  38.0 11.1 %collective-permute-start.11 = (bf16[40,4224]{1,0:T(8,128)(2,1)S(1)}, bf16[40,4224]{1,0:T(8,128)(2,1)S(1)}, u32[]{:S(2)}, u32[]{:S(2)}) collective-permute-start(bf16[40,4224]{1,0:T(8,128)(2,1)S(1)} %get-tuple-element.154), channel_id=1, source_target_pairs={{0,8},{8,0},{16,24},{24,16},{1,9},{9,1},{17,25},{25,17},{2,10},{10... | collective-permute-start | bytes 1013768 | tf_op jit(solution)/shard_map/ppermute | solution.py:290
  38.1 1.3 %collective-permute-start.10 = (f32[40,128]{1,0:T(8,128)S(1)}, f32[40,128]{1,0:T(8,128)S(1)}, u32[]{:S(2)}, u32[]{:S(2)}) collective-permute-start(f32[40,128]{1,0:T(8,128)S(1)} %get-tuple-element.143), channel_id=1, source_target_pairs={{0,1},{1,0},{2,3},{3,2},{4,5},{5,4},{6,7},{7,6},{8,9},{9,8},{10,11... | collective-permute-start | bytes 61448 | tf_op jit(solution)/shard_map/ppermute | solution.py:290
  41.9 12.5 %collective-permute-start.15 = (bf16[40,4096]{1,0:T(8,128)(2,1)S(1)}, bf16[40,4096]{1,0:T(8,128)(2,1)S(1)}, u32[]{:S(2)}, u32[]{:S(2)}) collective-permute-start(bf16[40,4096]{1,0:T(8,128)(2,1)S(1)} %get-tuple-element.165), channel_id=1, source_target_pairs={{0,16},{8,24},{16,0},{24,8},{1,17},{9,25},{17,1},{25,9},{2,18},{10... | collective-permute-start | bytes 983048 | tf_op jit(solution)/shard_map/ppermute | solution.py:290
  43.3 11.1 %collective-permute-start.14 = (bf16[40,3968]{1,0:T(8,128)(2,1)S(1)}, bf16[40,3968]{1,0:T(8,128)(2,1)S(1)}, u32[]{:S(2)}, u32[]{:S(2)}) collective-permute-start(bf16[40,3968]{1,0:T(8,128)(2,1)S(1)} %get-tuple-element.163), channel_id=1, source_target_pairs={{0,8},{8,0},{16,24},{24,16},{1,9},{9,1},{17,25},{25,17},{2,10},{10... | collective-permute-start | bytes 952328 | tf_op jit(solution)/shard_map/ppermute | solution.py:290
  44.7 6.2 %collective-permute-start.16 = (bf16[40,2432]{1,0:T(8,128)(2,1)S(1)}, bf16[40,2432]{1,0:T(8,128)(2,1)S(1)}, u32[]{:S(2)}, u32[]{:S(2)}) collective-permute-start(bf16[40,2432]{1,0:T(8,128)(2,1)S(1)} %get-tuple-element.169), channel_id=1, source_target_pairs={{0,2},{1,3},{2,0},{3,1},{4,6},{5,7},{6,4},{7,5},{8,10},{9,11},{10,... | collective-permute-start | bytes 583688 | tf_op jit(solution)/shard_map/ppermute | solution.py:290
  49.2 10.9 %collective-permute-start.13 = (bf16[40,4224]{1,0:T(8,128)(2,1)S(1)}, bf16[40,4224]{1,0:T(8,128)(2,1)S(1)}, u32[]{:S(2)}, u32[]{:S(2)}) collective-permute-start(bf16[40,4224]{1,0:T(8,128)(2,1)S(1)} %get-tuple-element.161), channel_id=1, source_target_pairs={{0,16},{8,24},{16,0},{24,8},{1,17},{9,25},{17,1},{25,9},{2,18},{10... | collective-permute-start | bytes 1013768 | tf_op jit(solution)/shard_map/ppermute | solution.py:290
  51.5 13.3 %collective-permute-start.19 = (bf16[128,1024]{1,0:T(8,128)(2,1)S(1)}, bf16[128,1024]{1,0:T(8,128)(2,1)S(1)}, u32[]{:S(2)}, u32[]{:S(2)}) collective-permute-start(bf16[128,1024]{1,0:T(8,128)(2,1)S(1)} %get-tuple-element.180), channel_id=1, source_target_pairs={{0,4},{1,5},{2,6},{3,7},{4,0},{5,1},{6,2},{7,3},{8,12},{9,13},{10,... | collective-permute-start | bytes 786440 | tf_op jit(solution)/shard_map/ppermute | solution.py:290
  54.5 10.3 %collective-permute-start.18 = (bf16[40,2048]{1,0:T(8,128)(2,1)S(1)}, bf16[40,2048]{1,0:T(8,128)(2,1)S(1)}, u32[]{:S(2)}, u32[]{:S(2)}) collective-permute-start(bf16[40,2048]{1,0:T(8,128)(2,1)S(1)} %get-tuple-element.178), channel_id=1, source_target_pairs={{0,16},{8,24},{16,0},{24,8},{1,17},{9,25},{17,1},{25,9},{2,18},{10... | collective-permute-start | bytes 491528 | tf_op jit(solution)/shard_map/ppermute | solution.py:290
  56.1 8.7 %collective-permute-start.17 = (bf16[40,1920]{1,0:T(8,128)(2,1)S(1)}, bf16[40,1920]{1,0:T(8,128)(2,1)S(1)}, u32[]{:S(2)}, u32[]{:S(2)}) collective-permute-start(bf16[40,1920]{1,0:T(8,128)(2,1)S(1)} %get-tuple-element.177), channel_id=1, source_target_pairs={{0,16},{8,24},{16,0},{24,8},{1,17},{9,25},{17,1},{25,9},{2,18},{10... | collective-permute-start | bytes 460808 | tf_op jit(solution)/shard_map/ppermute | solution.py:290

commit v15 on v14

--- a/solution.py
+++ b/solution.py
@@ -189,11 +189,18 @@
     return slice(cut.start + offset, cut.stop + offset)
 
 
-def own_grads(x, g, hid_a, hid_b, pair, low, high, down):
+def pair_columns(x, pair, outs):
+    at = 0
+    for out in outs:
+        for cut in tiles(out.shape[1]):
+            out[:, cut] = dot(pair[...], x[:, shifted(cut, at)], NN).astype(out.dtype)
+        at += out.shape[1]
+
+
+def own_grads(x, g, hid_a, hid_b, pair, *refs):
+    *outs, down = refs
     half = down.shape[1]
-    for out, offset in ((low, 0), (high, low.shape[1])):
-        for cut in tiles(out.shape[1]):
-            out[:, cut] = dot(pair[...], x[:, shifted(cut, offset)], NN)
+    pair_columns(x, pair, outs)
     for at in range(0, half, TILE):
         down[:, at : at + TILE] = down_columns(g, hid_a, hid_b, at, half)
 
@@ -204,10 +211,8 @@
         out[:, at : at + TILE] = down_columns(g, hid_a, hid_b, at, half).astype(BF)
 
 
-def sent_pair(x, pair, low, high):
-    for out, offset in ((low, 0), (high, low.shape[1])):
-        for cut in tiles(out.shape[1]):
-            out[:, cut] = dot(pair[...], x[:, shifted(cut, offset)], NN).astype(BF)
+def sent_pair(x, pair, *outs):
+    pair_columns(x, pair, outs)
 
 
 def kept(side, odd, four, wanted):
@@ -385,11 +390,14 @@
         finish_two, [small_bf] * 4, [both_own, share_own, hid_own[0], both_second, share_second, hid_second[0], got_two]
     )
     low_columns = half + 128
-    low_shape, high_shape = (both_rows, low_columns), (both_rows, wide - low_columns)
-    low, high = step(sent_pair, [(low_shape, BF), (high_shape, BF)], [x, pair_second])
-
-    grads_f32 = [(low_shape, F32), (high_shape, F32), ((both_rows, half), F32)]
-    own_low, own_high, own_down = step(own_grads, grads_f32, [x, g, *hid_own, pair_own])
+    high_columns = wide - low_columns
+    cut_at = high_columns // 256 * 128 + 128
+    low_shape = (both_rows, low_columns)
+    high_shapes = [(both_rows, cut_at), (both_rows, high_columns - cut_at)]
+    low, *highs = step(sent_pair, [(shape, BF) for shape in (low_shape, *high_shapes)], [x, pair_second])
+
+    grads_f32 = [(shape, F32) for shape in (low_shape, *high_shapes, (both_rows, half))]
+    own_low, *own_highs, own_down = step(own_grads, grads_f32, [x, g, *hid_own, pair_own])
 
     def one_sent(gr, down, hid, part, out):
         shares(width, gr, down, part)
@@ -416,7 +424,7 @@
         [((tokens, wide // 8), F32)] * 2,
         [wide_own, wide_second, wide_first, own[2], second[2], first[2]],
     )
-    first_low, first_high, first_down = step(own_grads, grads_f32, [x, g, *hid_first, pair_first])
+    first_low, *first_highs, first_down = step(own_grads, grads_f32, [x, g, *hid_first, pair_first])
 
     def added(own_ref, side, *outs):
         odd, at = is_odd(), 0
@@ -427,7 +435,8 @@
             at += out.shape[1]
 
     back_of_down = backward(step(added, piece, [first_down, side_down]))
-    side_high = outward(step.hold(high))
+    highs[0] = step.hold(highs[0])
+    side_highs = [outward(value) for value in highs]
     back_of_low = backward(step(added, (low_shape, BF), [first_low, side_low]))
     send, keep = step(
         with_width(output_sums),
@@ -445,15 +454,9 @@
         send, keep = step(body, [((tokens, cols), BF), ((tokens, cols), F32)], [keep, got])
         return keep, exchanged(send, "tensor", bit)
 
-    high_columns = wide - low_columns
-    cut_at = high_columns // 256 * 128
-    high_shapes = [(both_rows, cut_at), (both_rows, high_columns - cut_at)]
-
     backs_of_high = [
-        backward(value)
-        for value in step(
-            added, [(shape, BF) for shape in high_shapes], [first_high, side_high], also=[back_of_down]
-        )
+        backward(step(added, (shape, BF), [first, side], also=also))
+        for shape, first, side, also in zip(high_shapes, first_highs, side_highs, ([], [back_of_down]))
     ]
     bit = 2 * BITS[0]
     while bit < count:
@@ -472,33 +475,34 @@
             out[:, cut] = value[:rows]
             out[:, half + at : half + at + TILE] = value[rows:]
 
-    def ready_sums(low_ref, low_back, low_side, high_ref, high_side, gate_low, up_low, high_sum):
+    def ready_sums(low_ref, low_back, low_side, high_a, high_b, side_a, side_b, gate_low, up_low, sum_a, sum_b):
         odd = is_odd()
         for cut in tiles(low_columns):
             value = finished(low_ref, low_back, low_side, odd, cut)
             gate_low[:, cut] = value[:rows]
             up_low[:, cut] = value[rows:]
-        for cut in tiles(high_columns):
-            value = high_ref[:, cut]
-            high_sum[:, cut] = value + kept(high_side[:, cut], odd, four, False) if four else value
-
-    def final_pair(gate_low, up_low, high_sum, back_a, back_b, keep, got, out_gate, out_up, out):
+        for own_ref, side, out in ((high_a, side_a, sum_a), (high_b, side_b, sum_b)):
+            for cut in tiles(out.shape[1]):
+                value = own_ref[:, cut]
+                out[:, cut] = value + kept(side[:, cut], odd, four, False) if four else value
+
+    def final_pair(gate_low, up_low, sum_a, sum_b, back_a, back_b, keep, got, out_gate, out_up, out):
         for cut in tiles(low_columns):
             out_gate[:, cut] = gate_low[:, cut]
             out_up[:, cut] = up_low[:, cut]
-        for back, inside, columns in ((back_a, 0, cut_at), (back_b, cut_at, high_columns - cut_at)):
-            for cut in tiles(columns):
-                value = high_sum[:, shifted(cut, inside)] + back[:, cut].astype(F32)
-                out_gate[:, shifted(cut, low_columns + inside)] = value[:rows]
-                out_up[:, shifted(cut, low_columns + inside)] = value[rows:]
+        for own_sum, back, offset in ((sum_a, back_a, low_columns), (sum_b, back_b, low_columns + cut_at)):
+            for cut in tiles(back.shape[1]):
+                value = own_sum[:, cut] + back[:, cut].astype(F32)
+                out_gate[:, shifted(cut, offset)] = value[:rows]
+                out_up[:, shifted(cut, offset)] = value[rows:]
         final_output(keep, got, out)
 
     whole = ((rows, wide), F32)
     grad_down = step(final_down, whole, [own_down, back_of_down, side_down])
     ready = step(
         ready_sums,
-        [((rows, low_columns), F32)] * 2 + [((both_rows, high_columns), F32)],
-        [own_low, back_of_low, side_low, own_high, side_high],
+        [((rows, low_columns), F32)] * 2 + [(shape, F32) for shape in high_shapes],
+        [own_low, back_of_low, side_low, *own_highs, *side_highs],
     )
     grad_gate, grad_up, output = step(
         final_pair, [whole, whole, ((tokens, width), BF)], [*ready, *backs_of_high, keep, got]

time: 66.4 us -> 66.3 us (level)
  starting transfers between devices: 28.6 us -> 27.3 us
  waiting for transfers between devices: 22.4 us -> 23.7 us
    ppermute x19 -> x20, starting transfers between devices: 25.2 us -> 23.9 us  [exchanged(): lax.ppermute(value, axis, [(source, source ^ bit) for source in range(cou...]
    ppermute x19 -> x20, waiting for transfers between devices: 18.8 us -> 20.1 us  [exchanged(): lax.ppermute(value, axis, [(source, source ^ bit) for source in range(cou...]
    pallas_call x28 -> x29, Pallas kernels: 14.3 us -> 14.3 us  [__call__(): pl.pallas_call(kernel, out_shape=[jax.ShapeDtypeStruct(*s) for s in shape...]
  transfers between devices with their start and end apart: 20 -> 21, of which waited for: 13 -> 12; matrix products, arithmetic and copies ran while one was open for 0% -> 0% of each run, Pallas kernels for 17% -> 17%
where the time goes in v15:
time: 66.3 us; the launch traced here: 66.1 us
  starting transfers between devices  27.3 us (41%)
  waiting for transfers between devices  23.7 us (36%)
  Pallas kernels  14.3 us (22%)
  between operations  0.85 us (1%)
    ppermute x20, starting transfers between devices, exchanged(): lax.ppermute(value, axis, [(source, source ^ bit) for source in range(cou...  23.9 us
    ppermute x20, waiting for transfers between devices, exchanged(): lax.ppermute(value, axis, [(source, source ^ bit) for source in range(cou...  20.1 us
    pallas_call x29, Pallas kernels, __call__(): pl.pallas_call(kernel, out_shape=[jax.ShapeDtypeStruct(*s) for s in shape...  14.3 us
    ppermute x1, waiting for transfers between devices, on_device(): lax.ppermute(crossed, 'section', [(source, source ^ 2) for source in (0,...  3.6 us
    ppermute x1, starting transfers between devices, on_device(): lax.ppermute(crossed, 'section', [(source, source ^ 2) for source in (0,...  3.41 us
  transfers between devices with their start and end apart: 21, of which 12 were waited for; matrix products, arithmetic and copies ran while one was open for 0% of the time, Pallas kernels for 17%

profile of v15, /device:TPU:0, one launch (start us, length us, event | category | flops | bytes accessed | tf_op | source)
XLA Modules:
  0.0 66.1 jit_solution(16703737079398610604)
XLA Ops:
  0.6 1.5 %shard_map.84 = (bf16[40,4096]{1,0:T(8,128)(2,1)S(1)}, bf16[20,4096]{1,0:T(8,128)(2,1)S(1)}, bf16[20,4096]{1,0:T(8,128)(2,1)S(1)}, bf16[20,8192]{1,0:T(8,128)(2,...) custom-call(bf16[20,8192]{1,0:T(8,128)(2,1)} %refs_0_.2, bf16[20,8192]{1,0:T(8,128)(2,1)} %refs_1_.2, ...), custom_call_target="tpu_custom_call" | custom-call | flops 1 | bytes 1 | tf_op jit(solution)/shard_map/pallas_call | solution.py:39
  2.7 2.6 %collective-permute-start.2 = (bf16[40,4096]{1,0:T(8,128)(2,1)S(1)}, bf16[40,4096]{1,0:T(8,128)(2,1)S(1)}, u32[]{:S(2)}, u32[]{:S(2)}) collective-permute-start(bf16[40,4096]{1,0:T(8,128)(2,1)S(1)} %get-tuple-element.107.refs_3_.refs_1_), channel_id=1, source_target_pairs={{0,16},{8,24},{16,0},{24,8},{1,17},{9,25},{17,1},{25,9},{2,18},{10... | collective-permute-start | bytes 983048 | tf_op jit(solution)/shard_map/ppermute | solution.py:295
  5.6 1.6 %collective-permute-start.5 = (bf16[40,4096]{1,0:T(8,128)(2,1)S(1)}, bf16[40,4096]{1,0:T(8,128)(2,1)S(1)}, u32[]{:S(2)}, u32[]{:S(2)}) collective-permute-start(bf16[40,4096]{1,0:T(8,128)(2,1)S(1)} %get-tuple-element.114.refs_1_.refs_0_.refs_3_), channel_id=1, source_target_pairs={{0,8},{8,0},{16,24},{24,16},{1,9},{9,1},{17,25},{25,17},{2,10},{10... | collective-permute-start | bytes 983048 | tf_op jit(solution)/shard_map/ppermute | solution.py:295
  7.5 2.5 %shard_map.87 = (bf16[128,8192]{1,0:T(8,128)(2,1)S(1)}, bf16[128,8192]{1,0:T(8,128)(2,1)S(1)}, f32[40,128]{1,0:T(8,128)S(1)}, bf16[40,128]{1,0:T(8,128)(2,1)S(1)...) custom-call(bf16[128,8192]{1,0:T(8,128)(2,1)} %refs_0_.3, bf16[128,8192]{1,0:T(8,128)(2,1)} %refs_1_.3, ...), custom_call_target="tpu_custom_call" | custom-call | flops 1 | bytes 1 | tf_op jit(solution)/shard_map/pallas_call | solution.py:39
  10.0 1.4 %collective-permute-start.1 = (bf16[40,4096]{1,0:T(8,128)(2,1)S(1)}, bf16[40,4096]{1,0:T(8,128)(2,1)S(1)}, u32[]{:S(2)}, u32[]{:S(2)}) collective-permute-start(bf16[40,4096]{1,0:T(8,128)(2,1)S(1)} %get-tuple-element.118.refs_2_.refs_1_), channel_id=1, source_target_pairs={{0,16},{8,24},{16,0},{24,8},{1,17},{9,25},{17,1},{25,9},{2,18},{10... | collective-permute-start | bytes 983048 | tf_op jit(solution)/shard_map/ppermute | solution.py:295
  11.9 2.0 %collective-permute-done.2.refs_0_.refs_2_ = bf16[40,4096]{1,0:T(8,128)(2,1)S(1)} collective-permute-done((bf16[40,4096]{1,0:T(8,128)(2,1)S(1)}, bf16[40,4096]{1,0:T(8,128)(2,1)S(1)}, u32[]{:S(2)}, u32[]{:S(2)}) %collective-permute-start.2) | collective-permute-done | bytes 327712 | tf_op jit(solution)/shard_map/ppermute | solution.py:295
  13.9 2.0 %collective-permute-start.4 = (bf16[40,4096]{1,0:T(8,128)(2,1)S(1)}, bf16[40,4096]{1,0:T(8,128)(2,1)S(1)}, u32[]{:S(2)}, u32[]{:S(2)}) collective-permute-start(bf16[40,4096]{1,0:T(8,128)(2,1)S(1)} %get-tuple-element.122), channel_id=1, source_target_pairs={{0,8},{8,0},{16,24},{24,16},{1,9},{9,1},{17,25},{25,17},{2,10},{10... | collective-permute-start | bytes 983048 | tf_op jit(solution)/shard_map/ppermute | solution.py:295
  15.9 3.4 %collective-permute-start.6 = (bf16[40,4096]{1,0:T(8,128)(2,1)S(1)}, bf16[40,4096]{1,0:T(8,128)(2,1)S(1)}, u32[]{:S(2)}, u32[]{:S(2)}) collective-permute-start(bf16[40,4096]{1,0:T(8,128)(2,1)S(1)} %collective-permute-done.5.refs_0_), channel_id=1, source_target_pairs={{0,16},{16,0},{1,17},{17,1},{2,18},{18,2},{3,19},{19,3},{4,20},{20... | collective-permute-start | bytes 983048 | tf_op jit(solution)/shard_map/ppermute | solution.py:351
  19.3 1.6 %collective-permute-done.1.refs_0_.refs_1_ = bf16[40,4096]{1,0:T(8,128)(2,1)S(1)} collective-permute-done((bf16[40,4096]{1,0:T(8,128)(2,1)S(1)}, bf16[40,4096]{1,0:T(8,128)(2,1)S(1)}, u32[]{:S(2)}, u32[]{:S(2)}) %collective-permute-start.1) | collective-permute-done | bytes 327712 | tf_op jit(solution)/shard_map/ppermute | solution.py:295
  20.9 1.5 %collective-permute-start.3 = (bf16[40,4096]{1,0:T(8,128)(2,1)S(1)}, bf16[40,4096]{1,0:T(8,128)(2,1)S(1)}, u32[]{:S(2)}, u32[]{:S(2)}) collective-permute-start(bf16[40,4096]{1,0:T(8,128)(2,1)S(1)} %get-tuple-element.121), channel_id=1, source_target_pairs={{0,8},{8,0},{16,24},{24,16},{1,9},{9,1},{17,25},{25,17},{2,10},{10... | collective-permute-start | bytes 983048 | tf_op jit(solution)/shard_map/ppermute | solution.py:295
  22.4 1.5 %collective-permute-start.8 = (bf16[40,4096]{1,0:T(8,128)(2,1)S(1)}, bf16[40,4096]{1,0:T(8,128)(2,1)S(1)}, u32[]{:S(2)}, u32[]{:S(2)}) collective-permute-start(bf16[40,4096]{1,0:T(8,128)(2,1)S(1)} %get-tuple-element.114.refs_1_.refs_0_.refs_3_), channel_id=1, source_target_pairs={{0,16},{8,24},{16,0},{24,8},{1,17},{9,25},{17,1},{25,9},{2,18},{10... | collective-permute-start | bytes 983048 | tf_op jit(solution)/shard_map/ppermute | solution.py:295
  23.9 0.8 %shard_map.91 = (f32[40,128]{1,0:T(8,128)S(1)}, bf16[40,128]{1,0:T(8,128)(2,1)S(1)}, bf16[40,128]{1,0:T(8,128)(2,1)S(1)}, f32[8,128]{1,0:T(8,128)S(1)}) custom-call(bf16[128,8192]{1,0:T(8,128)(2,1)S(1)} %get-tuple-element.109.refs_0_, bf16[40,4096]{1,0:T(8,128)(2,1)S(1)} %collective-permute-done.1.refs_0_.refs_1_, ...), custom_call_target="tpu_custom_call" | custom-call | flops 1 | bytes 1 | tf_op jit(solution)/shard_map/pallas_call | solution.py:39
  24.8 3.6 %collective-permute-done.6.refs_1_ = bf16[40,4096]{1,0:T(8,128)(2,1)S(1)} collective-permute-done((bf16[40,4096]{1,0:T(8,128)(2,1)S(1)}, bf16[40,4096]{1,0:T(8,128)(2,1)S(1)}, u32[]{:S(2)}, u32[]{:S(2)}) %collective-permute-start.6) | collective-permute-done | bytes 327712 | tf_op jit(solution)/shard_map/ppermute | solution.py:351
  29.0 1.6 %collective-permute-start.9 = (bf16[40,4096]{1,0:T(8,128)(2,1)S(1)}, bf16[40,4096]{1,0:T(8,128)(2,1)S(1)}, u32[]{:S(2)}, u32[]{:S(2)}) collective-permute-start(bf16[40,4096]{1,0:T(8,128)(2,1)S(1)} %get-tuple-element.145), channel_id=1, source_target_pairs={{0,2},{1,3},{2,0},{3,1},{4,6},{5,7},{6,4},{7,5},{8,10},{9,11},{10,... | collective-permute-start | bytes 983048 | tf_op jit(solution)/shard_map/ppermute | solution.py:295
  30.6 0.8 %shard_map.95 = (f32[40,128]{1,0:T(8,128)S(1)}, bf16[40,128]{1,0:T(8,128)(2,1)S(1)}, bf16[40,128]{1,0:T(8,128)(2,1)S(1)}, f32[8,128]{1,0:T(8,128)S(1)}) custom-call(bf16[128,8192]{1,0:T(8,128)(2,1)S(1)} %get-tuple-element.109.refs_0_, bf16[40,4096]{1,0:T(8,128)(2,1)S(1)} %collective-permute-done.3.refs_1_, ...), custom_call_target="tpu_custom_call" | custom-call | flops 1 | bytes 1 | tf_op jit(solution)/shard_map/pallas_call | solution.py:39
  31.9 1.2 %collective-permute-start.12 = (bf16[40,4096]{1,0:T(8,128)(2,1)S(1)}, bf16[40,4096]{1,0:T(8,128)(2,1)S(1)}, u32[]{:S(2)}, u32[]{:S(2)}) collective-permute-start(bf16[40,4096]{1,0:T(8,128)(2,1)S(1)} %get-tuple-element.162), channel_id=1, source_target_pairs={{0,8},{8,0},{16,24},{24,16},{1,9},{9,1},{17,25},{25,17},{2,10},{10... | collective-permute-start | bytes 983048 | tf_op jit(solution)/shard_map/ppermute | solution.py:295
  33.0 1.2 %collective-permute-done.7.refs_6_ = f32[80,128]{1,0:T(8,128)S(1)} collective-permute-done((f32[80,128]{1,0:T(8,128)S(1)}, f32[80,128]{1,0:T(8,128)S(1)}, u32[]{:S(2)}, u32[]{:S(2)}) %collective-permute-start.7) | collective-permute-done | bytes 40992 | tf_op jit(solution)/shard_map/ppermute | solution.py:295
  35.4 2.1 %collective-permute-done.9.refs_3_.refs_2_ = bf16[40,4096]{1,0:T(8,128)(2,1)S(1)} collective-permute-done((bf16[40,4096]{1,0:T(8,128)(2,1)S(1)}, bf16[40,4096]{1,0:T(8,128)(2,1)S(1)}, u32[]{:S(2)}, u32[]{:S(2)}) %collective-permute-start.9) | collective-permute-done | bytes 327712 | tf_op jit(solution)/shard_map/ppermute | solution.py:295
  38.2 1.2 %collective-permute-done.10.refs_2_ = f32[40,128]{1,0:T(8,128)S(1)} collective-permute-done((f32[40,128]{1,0:T(8,128)S(1)}, f32[40,128]{1,0:T(8,128)S(1)}, u32[]{:S(2)}, u32[]{:S(2)}) %collective-permute-start.10) | collective-permute-done | bytes 20512 | tf_op jit(solution)/shard_map/ppermute | solution.py:295
  40.7 1.1 %collective-permute-done.12.refs_1_.refs_2_ = bf16[40,4096]{1,0:T(8,128)(2,1)S(1)} collective-permute-done((bf16[40,4096]{1,0:T(8,128)(2,1)S(1)}, bf16[40,4096]{1,0:T(8,128)(2,1)S(1)}, u32[]{:S(2)}, u32[]{:S(2)}) %collective-permute-start.12) | collective-permute-done | bytes 327712 | tf_op jit(solution)/shard_map/ppermute | solution.py:295
  41.9 1.4 %collective-permute-start.16 = (bf16[40,4096]{1,0:T(8,128)(2,1)S(1)}, bf16[40,4096]{1,0:T(8,128)(2,1)S(1)}, u32[]{:S(2)}, u32[]{:S(2)}) collective-permute-start(bf16[40,4096]{1,0:T(8,128)(2,1)S(1)} %get-tuple-element.172), channel_id=1, source_target_pairs={{0,16},{8,24},{16,0},{24,8},{1,17},{9,25},{17,1},{25,9},{2,18},{10... | collective-permute-start | bytes 983048 | tf_op jit(solution)/shard_map/ppermute | solution.py:295
  43.3 0.9 %collective-permute-start.17 = (bf16[40,2432]{1,0:T(8,128)(2,1)S(1)}, bf16[40,2432]{1,0:T(8,128)(2,1)S(1)}, u32[]{:S(2)}, u32[]{:S(2)}) collective-permute-start(bf16[40,2432]{1,0:T(8,128)(2,1)S(1)} %get-tuple-element.177), channel_id=1, source_target_pairs={{0,2},{1,3},{2,0},{3,1},{4,6},{5,7},{6,4},{7,5},{8,10},{9,11},{10,... | collective-permute-start | bytes 583688 | tf_op jit(solution)/shard_map/ppermute | solution.py:295
  44.2 3.4 %collective-permute-done.11.refs_1_.refs_2_ = bf16[40,4224]{1,0:T(8,128)(2,1)S(1)} collective-permute-done((bf16[40,4224]{1,0:T(8,128)(2,1)S(1)}, bf16[40,4224]{1,0:T(8,128)(2,1)S(1)}, u32[]{:S(2)}, u32[]{:S(2)}) %collective-permute-start.11) | collective-permute-done | bytes 337952 | tf_op jit(solution)/shard_map/ppermute | solution.py:295
  47.7 1.6 %collective-permute-start.13 = (bf16[40,4224]{1,0:T(8,128)(2,1)S(1)}, bf16[40,4224]{1,0:T(8,128)(2,1)S(1)}, u32[]{:S(2)}, u32[]{:S(2)}) collective-permute-start(bf16[40,4224]{1,0:T(8,128)(2,1)S(1)} %get-tuple-element.166), channel_id=1, source_target_pairs={{0,16},{8,24},{16,0},{24,8},{1,17},{9,25},{17,1},{25,9},{2,18},{10... | collective-permute-start | bytes 1013768 | tf_op jit(solution)/shard_map/ppermute | solution.py:295
  49.2 1.1 %collective-permute-start.14 = (bf16[40,2048]{1,0:T(8,128)(2,1)S(1)}, bf16[40,2048]{1,0:T(8,128)(2,1)S(1)}, u32[]{:S(2)}, u32[]{:S(2)}) collective-permute-start(bf16[40,2048]{1,0:T(8,128)(2,1)S(1)} %get-tuple-element.169), channel_id=1, source_target_pairs={{0,8},{8,0},{16,24},{24,16},{1,9},{9,1},{17,25},{25,17},{2,10},{10... | collective-permute-start | bytes 491528 | tf_op jit(solution)/shard_map/ppermute | solution.py:295
  50.3 0.9 %collective-permute-start.15 = (bf16[40,1920]{1,0:T(8,128)(2,1)S(1)}, bf16[40,1920]{1,0:T(8,128)(2,1)S(1)}, u32[]{:S(2)}, u32[]{:S(2)}) collective-permute-start(bf16[40,1920]{1,0:T(8,128)(2,1)S(1)} %get-tuple-element.170), channel_id=1, source_target_pairs={{0,8},{8,0},{16,24},{24,16},{1,9},{9,1},{17,25},{25,17},{2,10},{10... | collective-permute-start | bytes 460808 | tf_op jit(solution)/shard_map/ppermute | solution.py:295
  51.9 2.6 %collective-permute-start.20 = (bf16[128,1024]{1,0:T(8,128)(2,1)S(1)}, bf16[128,1024]{1,0:T(8,128)(2,1)S(1)}, u32[]{:S(2)}, u32[]{:S(2)}) collective-permute-start(bf16[128,1024]{1,0:T(8,128)(2,1)S(1)} %get-tuple-element.190), channel_id=1, source_target_pairs={{0,4},{1,5},{2,6},{3,7},{4,0},{5,1},{6,2},{7,3},{8,12},{9,13},{10,... | collective-permute-start | bytes 786440 | tf_op jit(solution)/shard_map/ppermute | solution.py:295
  56.0 1.0 %collective-permute-done.15.refs_1_.refs_6_ = bf16[40,1920]{1,0:T(8,128)(2,1)S(1)} collective-permute-done((bf16[40,1920]{1,0:T(8,128)(2,1)S(1)}, bf16[40,1920]{1,0:T(8,128)(2,1)S(1)}, u32[]{:S(2)}, u32[]{:S(2)}) %collective-permute-start.15) | collective-permute-done | bytes 153632 | tf_op jit(solution)/shard_map/ppermute | solution.py:295
  57.6 1.0 %shard_map.110 = (f32[20,8192]{1,0:T(8,128)}, f32[8,128]{1,0:T(8,128)S(1)}) custom-call(f32[40,4096]{1,0:T(8,128)S(1)} %get-tuple-element.171.refs_0_, bf16[40,4096]{1,0:T(8,128)(2,1)S(1)} %collective-permute-done.16.refs_2_.refs_1_, bf16[40,4096]{1,0:T(8,128)(2,1)S(1)} %collective-permute-done.12.refs_1_.refs_2_, f32[8,128]{1,0:T(8,128)S(1)} %get-tuple-element.181.refs_3_), custom_call_target="tpu_custom_call" | custom-call | flops 1 | bytes 1 | tf_op jit(solution)/shard_map/pallas_call | solution.py:39
  58.6 1.0 %collective-permute-done.13.refs_1_ = bf16[40,4224]{1,0:T(8,128)(2,1)S(1)} collective-permute-done((bf16[40,4224]{1,0:T(8,128)(2,1)S(1)}, bf16[40,4224]{1,0:T(8,128)(2,1)S(1)}, u32[]{:S(2)}, u32[]{:S(2)}) %collective-permute-start.13) | collective-permute-done | bytes 337952 | tf_op jit(solution)/shard_map/ppermute | solution.py:295
  59.8 4.9 %collective-permute-done.19.refs_5_ = bf16[40,1920]{1,0:T(8,128)(2,1)S(1)} collective-permute-done((bf16[40,1920]{1,0:T(8,128)(2,1)S(1)}, bf16[40,1920]{1,0:T(8,128)(2,1)S(1)}, u32[]{:S(2)}, u32[]{:S(2)}) %collective-permute-start.19) | collective-permute-done | bytes 153632 | tf_op jit(solution)/shard_map/ppermute | solution.py:295
  64.7 1.4 %shard_map.112 = (f32[20,8192]{1,0:T(8,128)}, f32[20,8192]{1,0:T(8,128)}, bf16[128,1024]{1,0:T(8,128)(2,1)}, f32[8,128]{1,0:T(8,128)}) custom-call(f32[20,4224]{1,0:T(8,128)S(1)} %get-tuple-element.183.refs_0_, f32[20,4224]{1,0:T(8,128)S(1)} %get-tuple-element.184.refs_1_, f32[40,2048]{1,0:T(8,128)S(1)} %get-tuple-element.185.refs_2_, ...), custom_call_target="tpu_custom_call" | custom-call | flops 1 | bytes 1 | tf_op jit(solution)/shard_map/pallas_call | solution.py:39
  (39 shorter events, 8.9 us)
Async XLA Ops:
  2.2 3.1 %collective-permute-start = (bf16[20,4096]{1,0:T(8,128)(2,1)S(1)}, bf16[20,4096]{1,0:T(8,128)(2,1)S(1)}, u32[]{:S(2)}, u32[]{:S(2)}) collective-permute-start(bf16[20,4096]{1,0:T(8,128)(2,1)S(1)} %get-tuple-element.103), channel_id=1, source_target_pairs={{0,1},{1,0},{2,3},{3,2},{4,5},{5,4},{6,7},{7,6},{8,9},{9,8},{10,11... | collective-permute-start | bytes 491528 | tf_op jit(solution)/shard_map/ppermute | solution.py:295
  2.7 11.2 %collective-permute-start.2 = (bf16[40,4096]{1,0:T(8,128)(2,1)S(1)}, bf16[40,4096]{1,0:T(8,128)(2,1)S(1)}, u32[]{:S(2)}, u32[]{:S(2)}) collective-permute-start(bf16[40,4096]{1,0:T(8,128)(2,1)S(1)} %get-tuple-element.107.refs_3_.refs_1_), channel_id=1, source_target_pairs={{0,16},{8,24},{16,0},{24,8},{1,17},{9,25},{17,1},{25,9},{2,18},{10... | collective-permute-start | bytes 983048 | tf_op jit(solution)/shard_map/ppermute | solution.py:295
  5.6 10.2 %collective-permute-start.5 = (bf16[40,4096]{1,0:T(8,128)(2,1)S(1)}, bf16[40,4096]{1,0:T(8,128)(2,1)S(1)}, u32[]{:S(2)}, u32[]{:S(2)}) collective-permute-start(bf16[40,4096]{1,0:T(8,128)(2,1)S(1)} %get-tuple-element.114.refs_1_.refs_0_.refs_3_), channel_id=1, source_target_pairs={{0,8},{8,0},{16,24},{24,16},{1,9},{9,1},{17,25},{25,17},{2,10},{10... | collective-permute-start | bytes 983048 | tf_op jit(solution)/shard_map/ppermute | solution.py:295
  10.0 10.9 %collective-permute-start.1 = (bf16[40,4096]{1,0:T(8,128)(2,1)S(1)}, bf16[40,4096]{1,0:T(8,128)(2,1)S(1)}, u32[]{:S(2)}, u32[]{:S(2)}) collective-permute-start(bf16[40,4096]{1,0:T(8,128)(2,1)S(1)} %get-tuple-element.118.refs_2_.refs_1_), channel_id=1, source_target_pairs={{0,16},{8,24},{16,0},{24,8},{1,17},{9,25},{17,1},{25,9},{2,18},{10... | collective-permute-start | bytes 983048 | tf_op jit(solution)/shard_map/ppermute | solution.py:295
  13.9 10.1 %collective-permute-start.4 = (bf16[40,4096]{1,0:T(8,128)(2,1)S(1)}, bf16[40,4096]{1,0:T(8,128)(2,1)S(1)}, u32[]{:S(2)}, u32[]{:S(2)}) collective-permute-start(bf16[40,4096]{1,0:T(8,128)(2,1)S(1)} %get-tuple-element.122), channel_id=1, source_target_pairs={{0,8},{8,0},{16,24},{24,16},{1,9},{9,1},{17,25},{25,17},{2,10},{10... | collective-permute-start | bytes 983048 | tf_op jit(solution)/shard_map/ppermute | solution.py:295
  15.9 12.5 %collective-permute-start.6 = (bf16[40,4096]{1,0:T(8,128)(2,1)S(1)}, bf16[40,4096]{1,0:T(8,128)(2,1)S(1)}, u32[]{:S(2)}, u32[]{:S(2)}) collective-permute-start(bf16[40,4096]{1,0:T(8,128)(2,1)S(1)} %collective-permute-done.5.refs_0_), channel_id=1, source_target_pairs={{0,16},{16,0},{1,17},{17,1},{2,18},{18,2},{3,19},{19,3},{4,20},{20... | collective-permute-start | bytes 983048 | tf_op jit(solution)/shard_map/ppermute | solution.py:351
  20.9 9.7 %collective-permute-start.3 = (bf16[40,4096]{1,0:T(8,128)(2,1)S(1)}, bf16[40,4096]{1,0:T(8,128)(2,1)S(1)}, u32[]{:S(2)}, u32[]{:S(2)}) collective-permute-start(bf16[40,4096]{1,0:T(8,128)(2,1)S(1)} %get-tuple-element.121), channel_id=1, source_target_pairs={{0,8},{8,0},{16,24},{24,16},{1,9},{9,1},{17,25},{25,17},{2,10},{10... | collective-permute-start | bytes 983048 | tf_op jit(solution)/shard_map/ppermute | solution.py:295
  22.4 13.0 %collective-permute-start.8 = (bf16[40,4096]{1,0:T(8,128)(2,1)S(1)}, bf16[40,4096]{1,0:T(8,128)(2,1)S(1)}, u32[]{:S(2)}, u32[]{:S(2)}) collective-permute-start(bf16[40,4096]{1,0:T(8,128)(2,1)S(1)} %get-tuple-element.114.refs_1_.refs_0_.refs_3_), channel_id=1, source_target_pairs={{0,16},{8,24},{16,0},{24,8},{1,17},{9,25},{17,1},{25,9},{2,18},{10... | collective-permute-start | bytes 983048 | tf_op jit(solution)/shard_map/ppermute | solution.py:295
  29.0 8.6 %collective-permute-start.9 = (bf16[40,4096]{1,0:T(8,128)(2,1)S(1)}, bf16[40,4096]{1,0:T(8,128)(2,1)S(1)}, u32[]{:S(2)}, u32[]{:S(2)}) collective-permute-start(bf16[40,4096]{1,0:T(8,128)(2,1)S(1)} %get-tuple-element.145), channel_id=1, source_target_pairs={{0,2},{1,3},{2,0},{3,1},{4,6},{5,7},{6,4},{7,5},{8,10},{9,11},{10,... | collective-permute-start | bytes 983048 | tf_op jit(solution)/shard_map/ppermute | solution.py:295
  31.9 10.0 %collective-permute-start.12 = (bf16[40,4096]{1,0:T(8,128)(2,1)S(1)}, bf16[40,4096]{1,0:T(8,128)(2,1)S(1)}, u32[]{:S(2)}, u32[]{:S(2)}) collective-permute-start(bf16[40,4096]{1,0:T(8,128)(2,1)S(1)} %get-tuple-element.162), channel_id=1, source_target_pairs={{0,8},{8,0},{16,24},{24,16},{1,9},{9,1},{17,25},{25,17},{2,10},{10... | collective-permute-start | bytes 983048 | tf_op jit(solution)/shard_map/ppermute | solution.py:295
  33.0 1.2 %collective-permute-start.7 = (f32[80,128]{1,0:T(8,128)S(1)}, f32[80,128]{1,0:T(8,128)S(1)}, u32[]{:S(2)}, u32[]{:S(2)}) collective-permute-start(f32[80,128]{1,0:T(8,128)S(1)} %get-tuple-element.134), channel_id=1, source_target_pairs={{0,1},{1,0},{2,3},{3,2},{4,5},{5,4},{6,7},{7,6},{8,9},{9,8},{10,11... | collective-permute-start | bytes 122888 | tf_op jit(solution)/shard_map/ppermute | solution.py:295
  38.0 9.6 %collective-permute-start.11 = (bf16[40,4224]{1,0:T(8,128)(2,1)S(1)}, bf16[40,4224]{1,0:T(8,128)(2,1)S(1)}, u32[]{:S(2)}, u32[]{:S(2)}) collective-permute-start(bf16[40,4224]{1,0:T(8,128)(2,1)S(1)} %get-tuple-element.159), channel_id=1, source_target_pairs={{0,8},{8,0},{16,24},{24,16},{1,9},{9,1},{17,25},{25,17},{2,10},{10... | collective-permute-start | bytes 1013768 | tf_op jit(solution)/shard_map/ppermute | solution.py:295
  38.1 1.3 %collective-permute-start.10 = (f32[40,128]{1,0:T(8,128)S(1)}, f32[40,128]{1,0:T(8,128)S(1)}, u32[]{:S(2)}, u32[]{:S(2)}) collective-permute-start(f32[40,128]{1,0:T(8,128)S(1)} %get-tuple-element.148), channel_id=1, source_target_pairs={{0,1},{1,0},{2,3},{3,2},{4,5},{5,4},{6,7},{7,6},{8,9},{9,8},{10,11... | collective-permute-start | bytes 61448 | tf_op jit(solution)/shard_map/ppermute | solution.py:295
  41.9 15.0 %collective-permute-start.16 = (bf16[40,4096]{1,0:T(8,128)(2,1)S(1)}, bf16[40,4096]{1,0:T(8,128)(2,1)S(1)}, u32[]{:S(2)}, u32[]{:S(2)}) collective-permute-start(bf16[40,4096]{1,0:T(8,128)(2,1)S(1)} %get-tuple-element.172), channel_id=1, source_target_pairs={{0,16},{8,24},{16,0},{24,8},{1,17},{9,25},{17,1},{25,9},{2,18},{10... | collective-permute-start | bytes 983048 | tf_op jit(solution)/shard_map/ppermute | solution.py:295
  43.3 8.0 %collective-permute-start.17 = (bf16[40,2432]{1,0:T(8,128)(2,1)S(1)}, bf16[40,2432]{1,0:T(8,128)(2,1)S(1)}, u32[]{:S(2)}, u32[]{:S(2)}) collective-permute-start(bf16[40,2432]{1,0:T(8,128)(2,1)S(1)} %get-tuple-element.177), channel_id=1, source_target_pairs={{0,2},{1,3},{2,0},{3,1},{4,6},{5,7},{6,4},{7,5},{8,10},{9,11},{10,... | collective-permute-start | bytes 583688 | tf_op jit(solution)/shard_map/ppermute | solution.py:295
  47.7 11.9 %collective-permute-start.13 = (bf16[40,4224]{1,0:T(8,128)(2,1)S(1)}, bf16[40,4224]{1,0:T(8,128)(2,1)S(1)}, u32[]{:S(2)}, u32[]{:S(2)}) collective-permute-start(bf16[40,4224]{1,0:T(8,128)(2,1)S(1)} %get-tuple-element.166), channel_id=1, source_target_pairs={{0,16},{8,24},{16,0},{24,8},{1,17},{9,25},{17,1},{25,9},{2,18},{10... | collective-permute-start | bytes 1013768 | tf_op jit(solution)/shard_map/ppermute | solution.py:295
  49.2 6.0 %collective-permute-start.14 = (bf16[40,2048]{1,0:T(8,128)(2,1)S(1)}, bf16[40,2048]{1,0:T(8,128)(2,1)S(1)}, u32[]{:S(2)}, u32[]{:S(2)}) collective-permute-start(bf16[40,2048]{1,0:T(8,128)(2,1)S(1)} %get-tuple-element.169), channel_id=1, source_target_pairs={{0,8},{8,0},{16,24},{24,16},{1,9},{9,1},{17,25},{25,17},{2,10},{10... | collective-permute-start | bytes 491528 | tf_op jit(solution)/shard_map/ppermute | solution.py:295
  50.3 6.6 %collective-permute-start.15 = (bf16[40,1920]{1,0:T(8,128)(2,1)S(1)}, bf16[40,1920]{1,0:T(8,128)(2,1)S(1)}, u32[]{:S(2)}, u32[]{:S(2)}) collective-permute-start(bf16[40,1920]{1,0:T(8,128)(2,1)S(1)} %get-tuple-element.170), channel_id=1, source_target_pairs={{0,8},{8,0},{16,24},{24,16},{1,9},{9,1},{17,25},{25,17},{2,10},{10... | collective-permute-start | bytes 460808 | tf_op jit(solution)/shard_map/ppermute | solution.py:295
  51.9 12.8 %collective-permute-start.20 = (bf16[128,1024]{1,0:T(8,128)(2,1)S(1)}, bf16[128,1024]{1,0:T(8,128)(2,1)S(1)}, u32[]{:S(2)}, u32[]{:S(2)}) collective-permute-start(bf16[128,1024]{1,0:T(8,128)(2,1)S(1)} %get-tuple-element.190), channel_id=1, source_target_pairs={{0,4},{1,5},{2,6},{3,7},{4,0},{5,1},{6,2},{7,3},{8,12},{9,13},{10,... | collective-permute-start | bytes 786440 | tf_op jit(solution)/shard_map/ppermute | solution.py:295
  55.3 9.4 %collective-permute-start.18 = (bf16[40,2048]{1,0:T(8,128)(2,1)S(1)}, bf16[40,2048]{1,0:T(8,128)(2,1)S(1)}, u32[]{:S(2)}, u32[]{:S(2)}) collective-permute-start(bf16[40,2048]{1,0:T(8,128)(2,1)S(1)} %get-tuple-element.187), channel_id=1, source_target_pairs={{0,16},{8,24},{16,0},{24,8},{1,17},{9,25},{17,1},{25,9},{2,18},{10... | collective-permute-start | bytes 491528 | tf_op jit(solution)/shard_map/ppermute | solution.py:295
  57.0 7.7 %collective-permute-start.19 = (bf16[40,1920]{1,0:T(8,128)(2,1)S(1)}, bf16[40,1920]{1,0:T(8,128)(2,1)S(1)}, u32[]{:S(2)}, u32[]{:S(2)}) collective-permute-start(bf16[40,1920]{1,0:T(8,128)(2,1)S(1)} %get-tuple-element.188), channel_id=1, source_target_pairs={{0,16},{8,24},{16,0},{24,8},{1,17},{9,25},{17,1},{25,9},{2,18},{10... | collective-permute-start | bytes 460808 | tf_op jit(solution)/shard_map/ppermute | solution.py:295

commit v16 on v12

--- a/solution.py
+++ b/solution.py
@@ -91,7 +91,7 @@
     return [(SWAP * width * j, 2 * SWAP * width * j) for j in range(wide // (2 * SWAP * width))]
 
 
-def packed(width, gate, up, down, high, low, keep, send, gate_here, up_here, down_here, sems):
+def packed(width, gate, up, down, high, keep, send, gate_here, up_here, down_here, sems):
     copies = [
         pltpu.make_async_copy(there, here, sems.at[k])
         for k, (there, here) in enumerate(((gate, gate_here), (up, up_here), (down, down_here)))
@@ -102,7 +102,6 @@
     copies[0].wait()
     copies[1].wait()
     stacked(high, gate_here, up_here, half, half)
-    stacked(low, gate_here, up_here)
     copies[2].wait()
 
     def run(mine):
@@ -317,13 +316,12 @@
         return exchanged(value, "section", 2) if four else ring_passed(value, -1)
 
     own, first, second = [None] * 3, [None] * 3, [None] * 3
-    held = pltpu.VMEM((rows, wide), BF)
-    own[1], own[0], down_keep, down_send = step(
+    own[1], down_keep, down_send, gate_here, up_here = step(
         with_width(packed),
-        [piece, piece, narrow, narrow],
+        [piece, narrow, narrow, ((rows, wide), BF), ((rows, wide), BF)],
         [gate_weight, up_weight, down_weight],
         far=3,
-        scratch=[held, held, held, pltpu.SemaphoreType.DMA((3,))],
+        scratch=[pltpu.VMEM((rows, wide), BF), pltpu.SemaphoreType.DMA((3,))],
     )
     first[1] = one_hop(own[1])
     down_got = exchanged(down_send, "tensor", SWAP)
@@ -336,6 +334,7 @@
         crossed = exchanged(own[2], "section", 1)
         onward = lax.ppermute(crossed, "section", [(source, source ^ 2) for source in (0, 2)])
     first[2] = one_hop(own[2])
+    own[0] = step(joined, piece, [gate_here, up_here])
     x, g, both_own, *hid_own = step(
         project_first,
         [(x.shape, BF), (g.shape, BF), small, small_bf, small_bf],

time: 65.5 us -> 65.3 us (level)
    pallas_call x25 -> x26, Pallas kernels: 14 us -> 14.1 us  [__call__(): pl.pallas_call(kernel, out_shape=[jax.ShapeDtypeStruct(*s) for s in shape...]
where the time goes in v16:
time: 65.3 us; the launch traced here: 65.2 us
  starting transfers between devices  28.6 us (44%)
  waiting for transfers between devices  21.5 us (33%)
  Pallas kernels  14.1 us (22%)
  between operations  0.83 us (1%)
    ppermute x19, starting transfers between devices, exchanged(): lax.ppermute(value, axis, [(source, source ^ bit) for source in range(cou...  25.2 us
    ppermute x19, waiting for transfers between devices, exchanged(): lax.ppermute(value, axis, [(source, source ^ bit) for source in range(cou...  18 us
    pallas_call x26, Pallas kernels, __call__(): pl.pallas_call(kernel, out_shape=[jax.ShapeDtypeStruct(*s) for s in shape...  14.1 us
    ppermute x1, waiting for transfers between devices, on_device(): lax.ppermute(crossed, 'section', [(source, source ^ 2) for source in (0,...  3.6 us
    ppermute x1, starting transfers between devices, on_device(): lax.ppermute(crossed, 'section', [(source, source ^ 2) for source in (0,...  3.41 us
  transfers between devices with their start and end apart: 20, of which 9 were waited for; matrix products, arithmetic and copies ran while one was open for 0% of the time, Pallas kernels for 17%

profile of v16, /device:TPU:0, one launch (start us, length us, event | category | flops | bytes accessed | tf_op | source)
XLA Modules:
  0.0 65.2 jit_solution(8041499797604789760)
XLA Ops:
  0.6 1.5 %shard_map.84 = (bf16[40,4096]{1,0:T(8,128)(2,1)S(1)}, bf16[20,4096]{1,0:T(8,128)(2,1)S(1)}, bf16[20,4096]{1,0:T(8,128)(2,1)S(1)}, bf16[20,8192]{1,0:T(8,128)(2,...) custom-call(bf16[20,8192]{1,0:T(8,128)(2,1)} %refs_0_.2, bf16[20,8192]{1,0:T(8,128)(2,1)} %refs_1_.2, ...), custom_call_target="tpu_custom_call" | custom-call | flops 1 | bytes 1 | tf_op jit(solution)/shard_map/pallas_call | solution.py:39
  2.7 2.6 %collective-permute-start.2 = (bf16[40,4096]{1,0:T(8,128)(2,1)S(1)}, bf16[40,4096]{1,0:T(8,128)(2,1)S(1)}, u32[]{:S(2)}, u32[]{:S(2)}) collective-permute-start(bf16[40,4096]{1,0:T(8,128)(2,1)S(1)} %get-tuple-element.95.refs_3_.refs_1_), channel_id=1, source_target_pairs={{0,16},{8,24},{16,0},{24,8},{1,17},{9,25},{17,1},{25,9},{2,18},{10... | collective-permute-start | bytes 983048 | tf_op jit(solution)/shard_map/ppermute | solution.py:279
  5.6 1.6 %collective-permute-start.5 = (bf16[40,4096]{1,0:T(8,128)(2,1)S(1)}, bf16[40,4096]{1,0:T(8,128)(2,1)S(1)}, u32[]{:S(2)}, u32[]{:S(2)}) collective-permute-start(bf16[40,4096]{1,0:T(8,128)(2,1)S(1)} %get-tuple-element.102.refs_1_.refs_0_.refs_3_), channel_id=1, source_target_pairs={{0,8},{8,0},{16,24},{24,16},{1,9},{9,1},{17,25},{25,17},{2,10},{10... | collective-permute-start | bytes 983048 | tf_op jit(solution)/shard_map/ppermute | solution.py:279
  7.5 2.5 %shard_map.87 = (bf16[128,8192]{1,0:T(8,128)(2,1)S(1)}, bf16[128,8192]{1,0:T(8,128)(2,1)S(1)}, f32[40,128]{1,0:T(8,128)S(1)}, bf16[40,128]{1,0:T(8,128)(2,1)S(1)...) custom-call(bf16[128,8192]{1,0:T(8,128)(2,1)} %refs_0_.3, bf16[128,8192]{1,0:T(8,128)(2,1)} %refs_1_.3, ...), custom_call_target="tpu_custom_call" | custom-call | flops 1 | bytes 1 | tf_op jit(solution)/shard_map/pallas_call | solution.py:39
  10.0 1.4 %collective-permute-start.1 = (bf16[40,4096]{1,0:T(8,128)(2,1)S(1)}, bf16[40,4096]{1,0:T(8,128)(2,1)S(1)}, u32[]{:S(2)}, u32[]{:S(2)}) collective-permute-start(bf16[40,4096]{1,0:T(8,128)(2,1)S(1)} %get-tuple-element.106.refs_2_.refs_1_), channel_id=1, source_target_pairs={{0,16},{8,24},{16,0},{24,8},{1,17},{9,25},{17,1},{25,9},{2,18},{10... | collective-permute-start | bytes 983048 | tf_op jit(solution)/shard_map/ppermute | solution.py:279
  11.9 2.0 %collective-permute-done.2.refs_0_.refs_2_ = bf16[40,4096]{1,0:T(8,128)(2,1)S(1)} collective-permute-done((bf16[40,4096]{1,0:T(8,128)(2,1)S(1)}, bf16[40,4096]{1,0:T(8,128)(2,1)S(1)}, u32[]{:S(2)}, u32[]{:S(2)}) %collective-permute-start.2) | collective-permute-done | bytes 327712 | tf_op jit(solution)/shard_map/ppermute | solution.py:279
  13.9 2.0 %collective-permute-start.4 = (bf16[40,4096]{1,0:T(8,128)(2,1)S(1)}, bf16[40,4096]{1,0:T(8,128)(2,1)S(1)}, u32[]{:S(2)}, u32[]{:S(2)}) collective-permute-start(bf16[40,4096]{1,0:T(8,128)(2,1)S(1)} %get-tuple-element.110), channel_id=1, source_target_pairs={{0,8},{8,0},{16,24},{24,16},{1,9},{9,1},{17,25},{25,17},{2,10},{10... | collective-permute-start | bytes 983048 | tf_op jit(solution)/shard_map/ppermute | solution.py:279
  15.9 3.4 %collective-permute-start.6 = (bf16[40,4096]{1,0:T(8,128)(2,1)S(1)}, bf16[40,4096]{1,0:T(8,128)(2,1)S(1)}, u32[]{:S(2)}, u32[]{:S(2)}) collective-permute-start(bf16[40,4096]{1,0:T(8,128)(2,1)S(1)} %collective-permute-done.5.refs_0_), channel_id=1, source_target_pairs={{0,16},{16,0},{1,17},{17,1},{2,18},{18,2},{3,19},{19,3},{4,20},{20... | collective-permute-start | bytes 983048 | tf_op jit(solution)/shard_map/ppermute | solution.py:335
  19.3 1.6 %collective-permute-done.1.refs_0_.refs_1_ = bf16[40,4096]{1,0:T(8,128)(2,1)S(1)} collective-permute-done((bf16[40,4096]{1,0:T(8,128)(2,1)S(1)}, bf16[40,4096]{1,0:T(8,128)(2,1)S(1)}, u32[]{:S(2)}, u32[]{:S(2)}) %collective-permute-start.1) | collective-permute-done | bytes 327712 | tf_op jit(solution)/shard_map/ppermute | solution.py:279
  20.9 1.5 %collective-permute-start.3 = (bf16[40,4096]{1,0:T(8,128)(2,1)S(1)}, bf16[40,4096]{1,0:T(8,128)(2,1)S(1)}, u32[]{:S(2)}, u32[]{:S(2)}) collective-permute-start(bf16[40,4096]{1,0:T(8,128)(2,1)S(1)} %get-tuple-element.109), channel_id=1, source_target_pairs={{0,8},{8,0},{16,24},{24,16},{1,9},{9,1},{17,25},{25,17},{2,10},{10... | collective-permute-start | bytes 983048 | tf_op jit(solution)/shard_map/ppermute | solution.py:279
  22.4 1.5 %collective-permute-start.8 = (bf16[40,4096]{1,0:T(8,128)(2,1)S(1)}, bf16[40,4096]{1,0:T(8,128)(2,1)S(1)}, u32[]{:S(2)}, u32[]{:S(2)}) collective-permute-start(bf16[40,4096]{1,0:T(8,128)(2,1)S(1)} %get-tuple-element.102.refs_1_.refs_0_.refs_3_), channel_id=1, source_target_pairs={{0,16},{8,24},{16,0},{24,8},{1,17},{9,25},{17,1},{25,9},{2,18},{10... | collective-permute-start | bytes 983048 | tf_op jit(solution)/shard_map/ppermute | solution.py:279
  23.9 0.8 %shard_map.91 = (f32[40,128]{1,0:T(8,128)S(1)}, bf16[40,128]{1,0:T(8,128)(2,1)S(1)}, bf16[40,128]{1,0:T(8,128)(2,1)S(1)}, f32[8,128]{1,0:T(8,128)S(1)}) custom-call(bf16[128,8192]{1,0:T(8,128)(2,1)S(1)} %get-tuple-element.97.refs_0_, bf16[40,4096]{1,0:T(8,128)(2,1)S(1)} %collective-permute-done.1.refs_0_.refs_1_, ...), custom_call_target="tpu_custom_call" | custom-call | flops 1 | bytes 1 | tf_op jit(solution)/shard_map/pallas_call | solution.py:39
  24.8 3.6 %collective-permute-done.6.refs_1_ = bf16[40,4096]{1,0:T(8,128)(2,1)S(1)} collective-permute-done((bf16[40,4096]{1,0:T(8,128)(2,1)S(1)}, bf16[40,4096]{1,0:T(8,128)(2,1)S(1)}, u32[]{:S(2)}, u32[]{:S(2)}) %collective-permute-start.6) | collective-permute-done | bytes 327712 | tf_op jit(solution)/shard_map/ppermute | solution.py:335
  29.0 1.6 %collective-permute-start.9 = (bf16[40,4096]{1,0:T(8,128)(2,1)S(1)}, bf16[40,4096]{1,0:T(8,128)(2,1)S(1)}, u32[]{:S(2)}, u32[]{:S(2)}) collective-permute-start(bf16[40,4096]{1,0:T(8,128)(2,1)S(1)} %get-tuple-element.132), channel_id=1, source_target_pairs={{0,2},{1,3},{2,0},{3,1},{4,6},{5,7},{6,4},{7,5},{8,10},{9,11},{10,... | collective-permute-start | bytes 983048 | tf_op jit(solution)/shard_map/ppermute | solution.py:279
  30.6 0.8 %shard_map.95 = (f32[40,128]{1,0:T(8,128)S(1)}, bf16[40,128]{1,0:T(8,128)(2,1)S(1)}, bf16[40,128]{1,0:T(8,128)(2,1)S(1)}, f32[8,128]{1,0:T(8,128)S(1)}) custom-call(bf16[128,8192]{1,0:T(8,128)(2,1)S(1)} %get-tuple-element.97.refs_0_, bf16[40,4096]{1,0:T(8,128)(2,1)S(1)} %collective-permute-done.3.refs_1_, ...), custom_call_target="tpu_custom_call" | custom-call | flops 1 | bytes 1 | tf_op jit(solution)/shard_map/pallas_call | solution.py:39
  31.9 1.2 %collective-permute-start.12 = (bf16[40,4096]{1,0:T(8,128)(2,1)S(1)}, bf16[40,4096]{1,0:T(8,128)(2,1)S(1)}, u32[]{:S(2)}, u32[]{:S(2)}) collective-permute-start(bf16[40,4096]{1,0:T(8,128)(2,1)S(1)} %get-tuple-element.145), channel_id=1, source_target_pairs={{0,8},{8,0},{16,24},{24,16},{1,9},{9,1},{17,25},{25,17},{2,10},{10... | collective-permute-start | bytes 983048 | tf_op jit(solution)/shard_map/ppermute | solution.py:279
  33.0 1.2 %collective-permute-done.7.refs_6_ = f32[80,128]{1,0:T(8,128)S(1)} collective-permute-done((f32[80,128]{1,0:T(8,128)S(1)}, f32[80,128]{1,0:T(8,128)S(1)}, u32[]{:S(2)}, u32[]{:S(2)}) %collective-permute-start.7) | collective-permute-done | bytes 40992 | tf_op jit(solution)/shard_map/ppermute | solution.py:279
  35.4 2.1 %collective-permute-done.9.refs_3_.refs_6_ = bf16[40,4096]{1,0:T(8,128)(2,1)S(1)} collective-permute-done((bf16[40,4096]{1,0:T(8,128)(2,1)S(1)}, bf16[40,4096]{1,0:T(8,128)(2,1)S(1)}, u32[]{:S(2)}, u32[]{:S(2)}) %collective-permute-start.9) | collective-permute-done | bytes 327712 | tf_op jit(solution)/shard_map/ppermute | solution.py:279
  38.2 1.2 %collective-permute-done.10.refs_2_ = f32[40,128]{1,0:T(8,128)S(1)} collective-permute-done((f32[40,128]{1,0:T(8,128)S(1)}, f32[40,128]{1,0:T(8,128)S(1)}, u32[]{:S(2)}, u32[]{:S(2)}) %collective-permute-start.10) | collective-permute-done | bytes 20512 | tf_op jit(solution)/shard_map/ppermute | solution.py:279
  39.4 2.4 %collective-permute-done.12.refs_3_.refs_2_ = bf16[40,4096]{1,0:T(8,128)(2,1)S(1)} collective-permute-done((bf16[40,4096]{1,0:T(8,128)(2,1)S(1)}, bf16[40,4096]{1,0:T(8,128)(2,1)S(1)}, u32[]{:S(2)}, u32[]{:S(2)}) %collective-permute-start.12) | collective-permute-done | bytes 327712 | tf_op jit(solution)/shard_map/ppermute | solution.py:279
  42.3 1.4 %collective-permute-start.15 = (bf16[40,4096]{1,0:T(8,128)(2,1)S(1)}, bf16[40,4096]{1,0:T(8,128)(2,1)S(1)}, u32[]{:S(2)}, u32[]{:S(2)}) collective-permute-start(bf16[40,4096]{1,0:T(8,128)(2,1)S(1)} %get-tuple-element.153), channel_id=1, source_target_pairs={{0,16},{8,24},{16,0},{24,8},{1,17},{9,25},{17,1},{25,9},{2,18},{10... | collective-permute-start | bytes 983048 | tf_op jit(solution)/shard_map/ppermute | solution.py:279
  43.6 1.4 %collective-permute-start.14 = (bf16[40,3968]{1,0:T(8,128)(2,1)S(1)}, bf16[40,3968]{1,0:T(8,128)(2,1)S(1)}, u32[]{:S(2)}, u32[]{:S(2)}) collective-permute-start(bf16[40,3968]{1,0:T(8,128)(2,1)S(1)} %get-tuple-element.151), channel_id=1, source_target_pairs={{0,8},{8,0},{16,24},{24,16},{1,9},{9,1},{17,25},{25,17},{2,10},{10... | collective-permute-start | bytes 952328 | tf_op jit(solution)/shard_map/ppermute | solution.py:279
  45.1 2.0 %collective-permute-start.16 = (bf16[40,2432]{1,0:T(8,128)(2,1)S(1)}, bf16[40,2432]{1,0:T(8,128)(2,1)S(1)}, u32[]{:S(2)}, u32[]{:S(2)}) collective-permute-start(bf16[40,2432]{1,0:T(8,128)(2,1)S(1)} %get-tuple-element.155), channel_id=1, source_target_pairs={{0,2},{1,3},{2,0},{3,1},{4,6},{5,7},{6,4},{7,5},{8,10},{9,11},{10,... | collective-permute-start | bytes 583688 | tf_op jit(solution)/shard_map/ppermute | solution.py:279
  47.0 2.0 %collective-permute-done.11.refs_2_ = bf16[40,4224]{1,0:T(8,128)(2,1)S(1)} collective-permute-done((bf16[40,4224]{1,0:T(8,128)(2,1)S(1)}, bf16[40,4224]{1,0:T(8,128)(2,1)S(1)}, u32[]{:S(2)}, u32[]{:S(2)}) %collective-permute-start.11) | collective-permute-done | bytes 337952 | tf_op jit(solution)/shard_map/ppermute | solution.py:279
  49.4 1.6 %collective-permute-start.13 = (bf16[40,4224]{1,0:T(8,128)(2,1)S(1)}, bf16[40,4224]{1,0:T(8,128)(2,1)S(1)}, u32[]{:S(2)}, u32[]{:S(2)}) collective-permute-start(bf16[40,4224]{1,0:T(8,128)(2,1)S(1)} %get-tuple-element.149), channel_id=1, source_target_pairs={{0,16},{8,24},{16,0},{24,8},{1,17},{9,25},{17,1},{25,9},{2,18},{10... | collective-permute-start | bytes 1013768 | tf_op jit(solution)/shard_map/ppermute | solution.py:279
  51.0 1.0 %shard_map.105 = (bf16[128,1024]{1,0:T(8,128)(2,1)S(1)}, f32[128,1024]{1,0:T(8,128)S(1)}, f32[8,128]{1,0:T(8,128)S(1)}) custom-call(bf16[40,128]{1,0:T(8,128)(2,1)S(1)} %get-tuple-element.137.refs_4_.refs_0_, bf16[40,128]{1,0:T(8,128)(2,1)S(1)} %get-tuple-element.138.refs_5_.refs_1_, bf16[40,128]{1,0:T(8,128)(2,1)S(1)} %get-tuple-element.154.refs_2_, ...), custom_call_target="tpu_custom_call" | custom-call | flops 1 | bytes 1 | tf_op jit(solution)/shard_map/pallas_call | solution.py:39
  52.0 2.6 %collective-permute-start.19 = (bf16[128,1024]{1,0:T(8,128)(2,1)S(1)}, bf16[128,1024]{1,0:T(8,128)(2,1)S(1)}, u32[]{:S(2)}, u32[]{:S(2)}) collective-permute-start(bf16[128,1024]{1,0:T(8,128)(2,1)S(1)} %get-tuple-element.166), channel_id=1, source_target_pairs={{0,4},{1,5},{2,6},{3,7},{4,0},{5,1},{6,2},{7,3},{8,12},{9,13},{10,... | collective-permute-start | bytes 786440 | tf_op jit(solution)/shard_map/ppermute | solution.py:279
  55.0 1.3 %collective-permute-start.18 = (bf16[40,2048]{1,0:T(8,128)(2,1)S(1)}, bf16[40,2048]{1,0:T(8,128)(2,1)S(1)}, u32[]{:S(2)}, u32[]{:S(2)}) collective-permute-start(bf16[40,2048]{1,0:T(8,128)(2,1)S(1)} %get-tuple-element.164), channel_id=1, source_target_pairs={{0,16},{8,24},{16,0},{24,8},{1,17},{9,25},{17,1},{25,9},{2,18},{10... | collective-permute-start | bytes 491528 | tf_op jit(solution)/shard_map/ppermute | solution.py:279
  56.3 0.8 %collective-permute-start.17 = (bf16[40,1920]{1,0:T(8,128)(2,1)S(1)}, bf16[40,1920]{1,0:T(8,128)(2,1)S(1)}, u32[]{:S(2)}, u32[]{:S(2)}) collective-permute-start(bf16[40,1920]{1,0:T(8,128)(2,1)S(1)} %get-tuple-element.163), channel_id=1, source_target_pairs={{0,16},{8,24},{16,0},{24,8},{1,17},{9,25},{17,1},{25,9},{2,18},{10... | collective-permute-start | bytes 460808 | tf_op jit(solution)/shard_map/ppermute | solution.py:279
  57.1 1.0 %shard_map.107 = (f32[20,8192]{1,0:T(8,128)}, f32[8,128]{1,0:T(8,128)S(1)}) custom-call(f32[40,4096]{1,0:T(8,128)S(1)} %get-tuple-element.152.refs_0_, bf16[40,4096]{1,0:T(8,128)(2,1)S(1)} %collective-permute-done.15.refs_3_.refs_1_, bf16[40,4096]{1,0:T(8,128)(2,1)S(1)} %collective-permute-done.12.refs_3_.refs_2_, f32[8,128]{1,0:T(8,128)S(1)} %get-tuple-element.158.refs_3_), custom_call_target="tpu_custom_call" | custom-call | flops 1 | bytes 1 | tf_op jit(solution)/shard_map/pallas_call | solution.py:39
  58.3 5.4 %collective-permute-done.17.refs_3_ = bf16[40,1920]{1,0:T(8,128)(2,1)S(1)} collective-permute-done((bf16[40,1920]{1,0:T(8,128)(2,1)S(1)}, bf16[40,1920]{1,0:T(8,128)(2,1)S(1)}, u32[]{:S(2)}, u32[]{:S(2)}) %collective-permute-start.17) | collective-permute-done | bytes 153632 | tf_op jit(solution)/shard_map/ppermute | solution.py:279
  63.8 1.4 %shard_map.109 = (f32[20,8192]{1,0:T(8,128)}, f32[20,8192]{1,0:T(8,128)}, bf16[128,1024]{1,0:T(8,128)(2,1)}, f32[8,128]{1,0:T(8,128)}) custom-call(f32[20,4224]{1,0:T(8,128)S(1)} %get-tuple-element.160.refs_0_, f32[20,4224]{1,0:T(8,128)S(1)} %get-tuple-element.161.refs_1_, f32[40,3968]{1,0:T(8,128)S(1)} %get-tuple-element.162.refs_2_, ...), custom_call_target="tpu_custom_call" | custom-call | flops 1 | bytes 1 | tf_op jit(solution)/shard_map/pallas_call | solution.py:39
  (34 shorter events, 5.7 us)
Async XLA Ops:
  2.2 3.1 %collective-permute-start = (bf16[20,4096]{1,0:T(8,128)(2,1)S(1)}, bf16[20,4096]{1,0:T(8,128)(2,1)S(1)}, u32[]{:S(2)}, u32[]{:S(2)}) collective-permute-start(bf16[20,4096]{1,0:T(8,128)(2,1)S(1)} %get-tuple-element.91), channel_id=1, source_target_pairs={{0,1},{1,0},{2,3},{3,2},{4,5},{5,4},{6,7},{7,6},{8,9},{9,8},{10,11... | collective-permute-start | bytes 491528 | tf_op jit(solution)/shard_map/ppermute | solution.py:279
  2.7 11.2 %collective-permute-start.2 = (bf16[40,4096]{1,0:T(8,128)(2,1)S(1)}, bf16[40,4096]{1,0:T(8,128)(2,1)S(1)}, u32[]{:S(2)}, u32[]{:S(2)}) collective-permute-start(bf16[40,4096]{1,0:T(8,128)(2,1)S(1)} %get-tuple-element.95.refs_3_.refs_1_), channel_id=1, source_target_pairs={{0,16},{8,24},{16,0},{24,8},{1,17},{9,25},{17,1},{25,9},{2,18},{10... | collective-permute-start | bytes 983048 | tf_op jit(solution)/shard_map/ppermute | solution.py:279
  5.6 10.2 %collective-permute-start.5 = (bf16[40,4096]{1,0:T(8,128)(2,1)S(1)}, bf16[40,4096]{1,0:T(8,128)(2,1)S(1)}, u32[]{:S(2)}, u32[]{:S(2)}) collective-permute-start(bf16[40,4096]{1,0:T(8,128)(2,1)S(1)} %get-tuple-element.102.refs_1_.refs_0_.refs_3_), channel_id=1, source_target_pairs={{0,8},{8,0},{16,24},{24,16},{1,9},{9,1},{17,25},{25,17},{2,10},{10... | collective-permute-start | bytes 983048 | tf_op jit(solution)/shard_map/ppermute | solution.py:279
  10.0 10.9 %collective-permute-start.1 = (bf16[40,4096]{1,0:T(8,128)(2,1)S(1)}, bf16[40,4096]{1,0:T(8,128)(2,1)S(1)}, u32[]{:S(2)}, u32[]{:S(2)}) collective-permute-start(bf16[40,4096]{1,0:T(8,128)(2,1)S(1)} %get-tuple-element.106.refs_2_.refs_1_), channel_id=1, source_target_pairs={{0,16},{8,24},{16,0},{24,8},{1,17},{9,25},{17,1},{25,9},{2,18},{10... | collective-permute-start | bytes 983048 | tf_op jit(solution)/shard_map/ppermute | solution.py:279
  13.9 10.1 %collective-permute-start.4 = (bf16[40,4096]{1,0:T(8,128)(2,1)S(1)}, bf16[40,4096]{1,0:T(8,128)(2,1)S(1)}, u32[]{:S(2)}, u32[]{:S(2)}) collective-permute-start(bf16[40,4096]{1,0:T(8,128)(2,1)S(1)} %get-tuple-element.110), channel_id=1, source_target_pairs={{0,8},{8,0},{16,24},{24,16},{1,9},{9,1},{17,25},{25,17},{2,10},{10... | collective-permute-start | bytes 983048 | tf_op jit(solution)/shard_map/ppermute | solution.py:279
  15.9 12.5 %collective-permute-start.6 = (bf16[40,4096]{1,0:T(8,128)(2,1)S(1)}, bf16[40,4096]{1,0:T(8,128)(2,1)S(1)}, u32[]{:S(2)}, u32[]{:S(2)}) collective-permute-start(bf16[40,4096]{1,0:T(8,128)(2,1)S(1)} %collective-permute-done.5.refs_0_), channel_id=1, source_target_pairs={{0,16},{16,0},{1,17},{17,1},{2,18},{18,2},{3,19},{19,3},{4,20},{20... | collective-permute-start | bytes 983048 | tf_op jit(solution)/shard_map/ppermute | solution.py:335
  20.9 9.7 %collective-permute-start.3 = (bf16[40,4096]{1,0:T(8,128)(2,1)S(1)}, bf16[40,4096]{1,0:T(8,128)(2,1)S(1)}, u32[]{:S(2)}, u32[]{:S(2)}) collective-permute-start(bf16[40,4096]{1,0:T(8,128)(2,1)S(1)} %get-tuple-element.109), channel_id=1, source_target_pairs={{0,8},{8,0},{16,24},{24,16},{1,9},{9,1},{17,25},{25,17},{2,10},{10... | collective-permute-start | bytes 983048 | tf_op jit(solution)/shard_map/ppermute | solution.py:279
  22.4 13.0 %collective-permute-start.8 = (bf16[40,4096]{1,0:T(8,128)(2,1)S(1)}, bf16[40,4096]{1,0:T(8,128)(2,1)S(1)}, u32[]{:S(2)}, u32[]{:S(2)}) collective-permute-start(bf16[40,4096]{1,0:T(8,128)(2,1)S(1)} %get-tuple-element.102.refs_1_.refs_0_.refs_3_), channel_id=1, source_target_pairs={{0,16},{8,24},{16,0},{24,8},{1,17},{9,25},{17,1},{25,9},{2,18},{10... | collective-permute-start | bytes 983048 | tf_op jit(solution)/shard_map/ppermute | solution.py:279
  29.0 8.6 %collective-permute-start.9 = (bf16[40,4096]{1,0:T(8,128)(2,1)S(1)}, bf16[40,4096]{1,0:T(8,128)(2,1)S(1)}, u32[]{:S(2)}, u32[]{:S(2)}) collective-permute-start(bf16[40,4096]{1,0:T(8,128)(2,1)S(1)} %get-tuple-element.132), channel_id=1, source_target_pairs={{0,2},{1,3},{2,0},{3,1},{4,6},{5,7},{6,4},{7,5},{8,10},{9,11},{10,... | collective-permute-start | bytes 983048 | tf_op jit(solution)/shard_map/ppermute | solution.py:279
  31.9 10.0 %collective-permute-start.12 = (bf16[40,4096]{1,0:T(8,128)(2,1)S(1)}, bf16[40,4096]{1,0:T(8,128)(2,1)S(1)}, u32[]{:S(2)}, u32[]{:S(2)}) collective-permute-start(bf16[40,4096]{1,0:T(8,128)(2,1)S(1)} %get-tuple-element.145), channel_id=1, source_target_pairs={{0,8},{8,0},{16,24},{24,16},{1,9},{9,1},{17,25},{25,17},{2,10},{10... | collective-permute-start | bytes 983048 | tf_op jit(solution)/shard_map/ppermute | solution.py:279
  33.0 1.2 %collective-permute-start.7 = (f32[80,128]{1,0:T(8,128)S(1)}, f32[80,128]{1,0:T(8,128)S(1)}, u32[]{:S(2)}, u32[]{:S(2)}) collective-permute-start(f32[80,128]{1,0:T(8,128)S(1)} %get-tuple-element.122), channel_id=1, source_target_pairs={{0,1},{1,0},{2,3},{3,2},{4,5},{5,4},{6,7},{7,6},{8,9},{9,8},{10,11... | collective-permute-start | bytes 122888 | tf_op jit(solution)/shard_map/ppermute | solution.py:279
  38.0 11.1 %collective-permute-start.11 = (bf16[40,4224]{1,0:T(8,128)(2,1)S(1)}, bf16[40,4224]{1,0:T(8,128)(2,1)S(1)}, u32[]{:S(2)}, u32[]{:S(2)}) collective-permute-start(bf16[40,4224]{1,0:T(8,128)(2,1)S(1)} %get-tuple-element.143), channel_id=1, source_target_pairs={{0,8},{8,0},{16,24},{24,16},{1,9},{9,1},{17,25},{25,17},{2,10},{10... | collective-permute-start | bytes 1013768 | tf_op jit(solution)/shard_map/ppermute | solution.py:279
  38.1 1.3 %collective-permute-start.10 = (f32[40,128]{1,0:T(8,128)S(1)}, f32[40,128]{1,0:T(8,128)S(1)}, u32[]{:S(2)}, u32[]{:S(2)}) collective-permute-start(f32[40,128]{1,0:T(8,128)S(1)} %get-tuple-element.135), channel_id=1, source_target_pairs={{0,1},{1,0},{2,3},{3,2},{4,5},{5,4},{6,7},{7,6},{8,9},{9,8},{10,11... | collective-permute-start | bytes 61448 | tf_op jit(solution)/shard_map/ppermute | solution.py:279
  42.3 12.4 %collective-permute-start.15 = (bf16[40,4096]{1,0:T(8,128)(2,1)S(1)}, bf16[40,4096]{1,0:T(8,128)(2,1)S(1)}, u32[]{:S(2)}, u32[]{:S(2)}) collective-permute-start(bf16[40,4096]{1,0:T(8,128)(2,1)S(1)} %get-tuple-element.153), channel_id=1, source_target_pairs={{0,16},{8,24},{16,0},{24,8},{1,17},{9,25},{17,1},{25,9},{2,18},{10... | collective-permute-start | bytes 983048 | tf_op jit(solution)/shard_map/ppermute | solution.py:279
  43.6 11.0 %collective-permute-start.14 = (bf16[40,3968]{1,0:T(8,128)(2,1)S(1)}, bf16[40,3968]{1,0:T(8,128)(2,1)S(1)}, u32[]{:S(2)}, u32[]{:S(2)}) collective-permute-start(bf16[40,3968]{1,0:T(8,128)(2,1)S(1)} %get-tuple-element.151), channel_id=1, source_target_pairs={{0,8},{8,0},{16,24},{24,16},{1,9},{9,1},{17,25},{25,17},{2,10},{10... | collective-permute-start | bytes 952328 | tf_op jit(solution)/shard_map/ppermute | solution.py:279
  45.1 5.9 %collective-permute-start.16 = (bf16[40,2432]{1,0:T(8,128)(2,1)S(1)}, bf16[40,2432]{1,0:T(8,128)(2,1)S(1)}, u32[]{:S(2)}, u32[]{:S(2)}) collective-permute-start(bf16[40,2432]{1,0:T(8,128)(2,1)S(1)} %get-tuple-element.155), channel_id=1, source_target_pairs={{0,2},{1,3},{2,0},{3,1},{4,6},{5,7},{6,4},{7,5},{8,10},{9,11},{10,... | collective-permute-start | bytes 583688 | tf_op jit(solution)/shard_map/ppermute | solution.py:279
  49.4 8.7 %collective-permute-start.13 = (bf16[40,4224]{1,0:T(8,128)(2,1)S(1)}, bf16[40,4224]{1,0:T(8,128)(2,1)S(1)}, u32[]{:S(2)}, u32[]{:S(2)}) collective-permute-start(bf16[40,4224]{1,0:T(8,128)(2,1)S(1)} %get-tuple-element.149), channel_id=1, source_target_pairs={{0,16},{8,24},{16,0},{24,8},{1,17},{9,25},{17,1},{25,9},{2,18},{10... | collective-permute-start | bytes 1013768 | tf_op jit(solution)/shard_map/ppermute | solution.py:279
  52.0 11.7 %collective-permute-start.19 = (bf16[128,1024]{1,0:T(8,128)(2,1)S(1)}, bf16[128,1024]{1,0:T(8,128)(2,1)S(1)}, u32[]{:S(2)}, u32[]{:S(2)}) collective-permute-start(bf16[128,1024]{1,0:T(8,128)(2,1)S(1)} %get-tuple-element.166), channel_id=1, source_target_pairs={{0,4},{1,5},{2,6},{3,7},{4,0},{5,1},{6,2},{7,3},{8,12},{9,13},{10,... | collective-permute-start | bytes 786440 | tf_op jit(solution)/shard_map/ppermute | solution.py:279
  55.0 8.8 %collective-permute-start.18 = (bf16[40,2048]{1,0:T(8,128)(2,1)S(1)}, bf16[40,2048]{1,0:T(8,128)(2,1)S(1)}, u32[]{:S(2)}, u32[]{:S(2)}) collective-permute-start(bf16[40,2048]{1,0:T(8,128)(2,1)S(1)} %get-tuple-element.164), channel_id=1, source_target_pairs={{0,16},{8,24},{16,0},{24,8},{1,17},{9,25},{17,1},{25,9},{2,18},{10... | collective-permute-start | bytes 491528 | tf_op jit(solution)/shard_map/ppermute | solution.py:279
  56.3 7.5 %collective-permute-start.17 = (bf16[40,1920]{1,0:T(8,128)(2,1)S(1)}, bf16[40,1920]{1,0:T(8,128)(2,1)S(1)}, u32[]{:S(2)}, u32[]{:S(2)}) collective-permute-start(bf16[40,1920]{1,0:T(8,128)(2,1)S(1)} %get-tuple-element.163), channel_id=1, source_target_pairs={{0,16},{8,24},{16,0},{24,8},{1,17},{9,25},{17,1},{25,9},{2,18},{10... | collective-permute-start | bytes 460808 | tf_op jit(solution)/shard_map/ppermute | solution.py:279
